TPU v7x, 512 devices: a whole 4x8x8 slice. The times are simulated.
512 devices in a mesh: out: 32 (over z, y_lo, core), inp: 16 (over x, y_hi).
Axes of the slice: x: 4, y: 8 (y_hi: 4, y_lo: 2; y = y_hi * 2 + y_lo), z: 8, core: 2. Of those that a mesh axis runs over, the one named last changes fastest.
Arguments:
- grads: bfloat16 [1024, 8192], P('out', 'inp'), may hold values from -6 to 6
- acts: bfloat16 [1024, 28672], P('inp', 'out'), may hold values from -6 to 6
- grad_basis: bfloat16 [8192, 8192], P('inp', 'out'), may hold values from -0.0625 to 0.0625
- act_basis: bfloat16 [28672, 14336], P('out', 'inp'), may hold values from -0.03125 to 0.03125
Outputs:
- eigenvalues: float32 [8192, 14336], P('out', 'inp')
All inputs are finite; a program needn't handle non-finite values.
Results may differ from a plain program's by a relative error of at most 0.0041.
Values may be sent and summed in bfloat16 or wider, within the bound.
No kernel may reach another device: no remote copies, remote signals or barrier semaphores. Data moves between devices by JAX's collectives and lax.ppermute only.
A program may use at most 64 MiB of HBM per device.

v0:
```python
import jax
import jax.numpy as jnp
from jax import lax
from jax.sharding import PartitionSpec as P

SEQS = 2
SEQ_LEN = 512


def shards(grads, acts, grad_basis, act_basis):
    partial_grad = jnp.dot(
        lax.all_gather(grads, "out", axis=0, tiled=True),
        grad_basis,
        preferred_element_type=jnp.float32,
    )
    grad_rot = lax.psum(partial_grad, "inp").astype(jnp.bfloat16)
    partial_act = jnp.dot(
        lax.all_gather(acts, "inp", axis=0, tiled=True),
        act_basis,
        preferred_element_type=jnp.float32,
    )
    act_rot = lax.psum(partial_act, "out").astype(jnp.bfloat16)
    seq_grads = grad_rot.reshape(SEQS, SEQ_LEN, grad_rot.shape[1])
    seq_acts = act_rot.reshape(SEQS, SEQ_LEN, act_rot.shape[1])
    rotated = jnp.einsum("stk,stj->skj", seq_grads, seq_acts, preferred_element_type=jnp.float32)
    return jnp.sum(rotated * rotated, axis=0) / (SEQS * SEQ_LEN)


def solution(mesh):
    return jax.shard_map(
        shards,
        mesh=mesh,
        in_specs=(P("out", "inp"), P("inp", "out"), P("inp", "out"), P("out", "inp")),
        out_specs=P("out", "inp"),
        check_vma=False,
    )
```

profile of v0, /device:TPU:1, one launch (start us, length us, event | category | flops | bytes accessed | tf_op | source)
XLA Modules:
  0.0 344.2 jit_solution(6301069832977269073)
XLA Ops:
  6.5 0.0 copy-start
  6.5 0.0 all-gather.3.cloned.1.call-start
  6.5 0.7 all-gather.3.cloned.1.call-update
  7.3 0.0 all-gather.5.cloned.1.call-start
  7.3 0.7 all-gather.5.cloned.1.call-update
  8.0 74.2 %all-gather.3.cloned.1.call-done = bf16[1024,512]{1,0:T(8,128)(2,1)} async-done(((bf16[32,512]{1,0:T(8,128)(2,1)}), bf16[1024,512]{1,0:T(8,128)(2,1)}) %all-gather.3.cloned.1.call-update) | async-done | bytes 1048592 | tf_op jit(solution)/shard_map/all_gather | solution.py:12
  82.2 1.7 fusion
  83.9 95.2 %all-reduce.3 = bf16[1024,256]{1,0:T(8,128)(2,1)} all-reduce(f32[1024,256]{1,0:T(8,128)S(1)} %fusion), channel_id=1, replica_groups=mesh['out'=32,'inp'=16] {'inp'}, use_global_device_ids=true, to_apply=%region_0.0 | all-reduce | flops 262144 | bytes 1572864 | tf_op jit(solution)/shard_map/psum | solution.py:16
  179.2 0.0 all-gather.5.cloned.1.call-done
  179.2 0.0 copy-done
  179.2 5.5 %fusion.1 = f32[1024,896]{1,0:T(8,128)} fusion(bf16[1024,896]{1,0:T(8,128)(2,1)} %all-gather.5.cloned.1.call-done, bf16[896,896]{1,0:T(8,128)(2,1)S(1)} %copy-done), kind=kOutput, calls=%fused_computation.3 | convolution fusion | flops 1644167168 | bytes 7110656 | tf_op jit(solution)/shard_map/dot_general | solution.py:17
  184.7 149.8 %all-reduce.2 = bf16[1024,896]{1,0:T(8,128)(2,1)S(1)} all-reduce(f32[1024,896]{1,0:T(8,128)} %fusion.1), channel_id=1, replica_groups=mesh['out'=32,'inp'=16] {'out'}, use_global_device_ids=true, to_apply=%region_1.0 | all-reduce | flops 917504 | bytes 5505024 | tf_op jit(solution)/shard_map/psum | solution.py:22
  334.5 1.9 multiply_reduce_fusion
  336.4 1.0 broadcast_multiply_fusion
Async XLA Ops:
  6.5 172.6 %copy-start = (bf16[896,896]{1,0:T(8,128)(2,1)S(1)}, bf16[896,896]{1,0:T(8,128)(2,1)}, u32[]{:S(2)}) copy-start(bf16[896,896]{1,0:T(8,128)(2,1)} %param.7) | copy-start | bytes 4816900
  6.5 75.7 %all-gather.3.cloned.1.call-start = ((), (), s32[]{:S(2)}) async-start(), calls=%async_computation | async-start | bytes 1081344 | tf_op jit(solution)/shard_map/all_gather | solution.py:12
  7.3 171.9 %all-gather.5.cloned.1.call-start = ((), (), s32[]{:S(2)}) async-start(), calls=%async_computation.1 | async-start | bytes 1949696 | tf_op jit(solution)/shard_map/all_gather | solution.py:18
Sparse Core Ops, SparseCore 0:
  9.5 72.6 all-gather.2
  85.3 71.4 all-gather.4
where the time goes:
time: 344 us
  blocking collectives  245 us (71%)
  waiting for transfers between devices  75.6 us (22%)
  between operations  13.4 us (4%)
  matrix products  9.11 us (3%)
    psum x1, blocking collectives, shards(): act_rot = lax.psum(partial_act, 'out').astype(jnp.bfloat16)  150 us
    psum x1, blocking collectives, shards(): grad_rot = lax.psum(partial_grad, 'inp').astype(jnp.bfloat16)  95.2 us
    all_gather x1, waiting for transfers between devices, shards(): lax.all_gather(grads, 'out', axis=0, tiled=True)  74.2 us
  transfers between devices with their start and end apart: 2, of which 1 were waited for; matrix products, arithmetic and copies ran while one was open for 0% of the time, Pallas kernels for 0%

commit v1 on v0

v1 whole, which is shorter than its diff:
```python
import jax
import jax.numpy as jnp
from jax import lax
from jax.experimental import pallas as pl
from jax.experimental.pallas import tpu as pltpu
from jax.sharding import Mesh, PartitionSpec as P

SEQS = 2
SEQ_LEN = 512
OUT = ("z", "ylo", "core")
INP = ("x", "yhi")
CHIPS = ("z", "ylo")
BF16 = jnp.bfloat16
F32 = jnp.float32
VMEM = pl.BlockSpec(memory_space=pltpu.VMEM)


def kernel_call(body, shapes, args, flops=0):
    moved = sum(a.size * a.dtype.itemsize for a in args) + sum(s.size * s.dtype.itemsize for s in shapes)
    many = len(shapes) > 1
    return pl.pallas_call(
        body,
        out_shape=shapes if many else shapes[0],
        in_specs=[VMEM] * len(args),
        out_specs=[VMEM] * len(shapes) if many else VMEM,
        compiler_params=pltpu.CompilerParams(vmem_limit_bytes=40 * 2**20),
        cost_estimate=pl.CostEstimate(flops=flops, bytes_accessed=moved, transcendentals=0),
    )(*args)


def swap(value, axis, flip):
    size = lax.axis_size(axis)
    return lax.ppermute(value, axis, [(s, s ^ flip) for s in range(size)])


def stack_kernel(*refs):
    blocks, outs, row = refs[:4], refs[4:], 0
    for block in blocks:
        height = outs[0].shape[0]
        outs[row // height][row % height:row % height + block.shape[0], :] = block[...]
        row += block.shape[0]


def gather_yhi(mine, parts):
    blocks = [mine, swap(mine, "yhi", 1), swap(mine, "yhi", 2), swap(mine, "yhi", 3)]
    rows, columns = mine.shape
    shapes = [jax.ShapeDtypeStruct((4 * rows // parts, columns), mine.dtype)] * parts
    return kernel_call(stack_kernel, shapes, blocks)


def gather_chips(copies):
    return lax.all_to_all(copies, CHIPS, 0, 0, tiled=True)


def act_dot_kernel(top, bottom, top1, bottom1, top2, bottom2, top3, bottom3, own, other, out):
    features = own.shape[0]
    for pair in range(4):
        first, second = ((top, bottom), (top1, bottom1), (top2, bottom2), (top3, bottom3))[pair]
        rows = jnp.concatenate([first[...], second[...]])
        total = jnp.dot(rows[:, :features], own[...], preferred_element_type=F32)
        total += jnp.dot(rows[:, features:], other[...], preferred_element_type=F32)
        block = out.shape[1]
        for part in range(rows.shape[0] // block):
            at = pair * (rows.shape[0] // block) + part
            out[at] = total[part * block:(part + 1) * block].astype(BF16)


def sum_copies_kernel(parts, out):
    total = parts[0].astype(F32)
    for index in range(1, parts.shape[0]):
        total += parts[index].astype(F32)
    rounded = total.astype(BF16)
    for index in range(out.shape[0]):
        out[index] = rounded


def sum_split_kernel(parts, mine, give):
    total = parts[0].astype(F32)
    for index in range(1, parts.shape[0]):
        total += parts[index].astype(F32)
    rounded = total.astype(BF16)
    columns = mine.shape[1]
    mine[...] = rounded[:, :columns]
    give[...] = rounded[:, columns:]


def square_kernel(g0, g1, g2, g3, act_mine, act_theirs, out):
    columns = out.shape[0]
    half = act_mine.shape[0] // SEQS
    grads = (jnp.concatenate([g0[...], g1[...]]), jnp.concatenate([g2[...], g3[...]]))
    total = 0.0
    for seq in range(SEQS):
        rows = slice(seq * half, (seq + 1) * half)
        contract = (((0,), (0,)), ((), ()))
        rotated = lax.dot_general(grads[seq][:, :columns], act_mine[rows, :], contract, preferred_element_type=F32)
        rotated += lax.dot_general(grads[seq][:, columns:], act_theirs[rows, :], contract, preferred_element_type=F32)
        total = total + rotated * rotated
    out[...] = total * (1.0 / (SEQS * SEQ_LEN))


def shards(grads, acts, grad_basis, act_basis):
    core = lax.axis_index("core")
    half = acts.shape[0] // 2
    keep = lax.dynamic_slice_in_dim(acts, core * half, half)
    give = lax.dynamic_slice_in_dim(acts, (1 - core) * half, half)
    act_own = jnp.concatenate([keep, swap(give, "core", 1)], axis=1)
    act_basis_other = swap(act_basis, "core", 1)
    grad_basis_both = jnp.concatenate([grad_basis, swap(grad_basis, "core", 1)], axis=1)

    top, bottom = gather_yhi(act_own, 2)
    top3, bottom1 = swap(top, "x", 3), swap(bottom, "x", 1)
    bottom3, top1 = swap(bottom, "x", 3), swap(top, "x", 1)
    top2, bottom2 = swap(top3, "x", 1), swap(bottom1, "x", 3)

    rows = grads.shape[0]
    grad_rows = gather_chips(jnp.broadcast_to(grads[None], (16, *grads.shape)))
    grad_partial = jnp.dot(
        grad_rows.reshape(16 * rows, -1), grad_basis_both, preferred_element_type=F32
    ).astype(BF16)
    grad_parts = lax.all_to_all(grad_partial.reshape(16, rows, -1), INP, 0, 0, tiled=True)
    columns = grad_basis.shape[1]
    narrow = jax.ShapeDtypeStruct((rows, columns), BF16)
    grad_mine, grad_give = kernel_call(sum_split_kernel, [narrow, narrow], [grad_parts])
    grad_own = jnp.concatenate([grad_mine, swap(grad_give, "core", 1)], axis=1)
    top2, bottom2, grad_own = lax.optimization_barrier((top2, bottom2, grad_own))
    g0 = gather_yhi(grad_own, 1)

    tokens, eig = 16 * half, act_basis.shape[1]
    blocks = jax.ShapeDtypeStruct((16, half, eig), BF16)
    act_partial = kernel_call(
        act_dot_kernel,
        [blocks],
        [top, bottom, top1, bottom1, top2, bottom2, top3, bottom3, act_basis, act_basis_other],
        flops=2 * tokens * 2 * act_basis.shape[0] * eig,
    )
    act_parts = lax.all_to_all(act_partial, CHIPS, 0, 0, tiled=True)
    act_parts, g0 = lax.optimization_barrier((act_parts, g0))
    g1, g2, g3 = swap(g0, "x", 1), swap(g0, "x", 2), swap(g0, "x", 3)
    act_mine = gather_chips(kernel_call(sum_copies_kernel, [blocks], [act_parts])).reshape(tokens, eig)
    act_theirs = swap(act_mine, "core", 1)

    return kernel_call(
        square_kernel,
        [jax.ShapeDtypeStruct((columns, eig), F32)],
        [g0, g1, g2, g3, act_mine, act_theirs],
        flops=2 * 2 * tokens * columns * eig,
    )


def solution(mesh):
    split = Mesh(mesh.devices.reshape(8, 2, 2, 4, 4), OUT + INP)
    return jax.shard_map(
        shards,
        mesh=split,
        in_specs=(P(OUT, INP), P(INP, OUT), P(INP, OUT), P(OUT, INP)),
        out_specs=P(OUT, INP),
        check_vma=False,
    )
```

time: 344 us -> 176 us (0.51)
  blocking collectives: 245 us -> 29.4 us
  starting transfers between devices: 0.04 us -> 96.1 us
  waiting for transfers between devices: 75.6 us -> 39.2 us
  between operations: 13.4 us -> 0.31 us
  matrix products: 9.11 us -> 1.23 us
  Pallas kernels: 0 us -> 6.63 us
    psum x2 -> x0, blocking collectives: 245 us -> none  [the longest x1 150 us: shards(): act_rot = lax.psum(partial_act, 'out').astype(jnp.bfloat16)]
    all_gather x2 -> x0, waiting for transfers between devices: 74.2 us -> none  [the longest x1 74.2 us: shards(): lax.all_gather(grads, 'out', axis=0, tiled=True)]
    ppermute x0 -> x20, starting transfers between devices: none -> 69.9 us  [swap(): return lax.ppermute(value, axis, [(s, s ^ flip) for s in range(size)])]
    all_to_all x0 -> x1, blocking collectives: none -> 29.4 us  [gather_chips(): return lax.all_to_all(copies, CHIPS, 0, 0, tiled=True)]
    all_to_all x0 -> x3, starting transfers between devices: none -> 26.2 us  [the longest x1 12 us: gather_chips(): return lax.all_to_all(copies, CHIPS, 0, 0, tiled=True)]
    ppermute x0 -> x20, waiting for transfers between devices: none -> 20.9 us  [swap(): return lax.ppermute(value, axis, [(s, s ^ flip) for s in range(size)])]
    all_to_all x0 -> x3, waiting for transfers between devices: none -> 18.3 us  [the longest x1 9.96 us: gather_chips(): return lax.all_to_all(copies, CHIPS, 0, 0, tiled=True)]
    dot_general x3 -> x1, matrix products: 9.11 us -> 1.23 us  [shards(): jnp.dot(grad_rows.reshape(16 * rows, -1), grad_basis_both, preferred_elem...]
  transfers between devices with their start and end apart: 2 -> 23, of which waited for: 1 -> 10; matrix products, arithmetic and copies ran while one was open for 0% -> 1% of each run, Pallas kernels for 0% -> 0%
where the time goes in v1:
time: 176 us; the launch traced here: 175 us
  starting transfers between devices  96.1 us (55%)
  waiting for transfers between devices  39.2 us (22%)
  blocking collectives  29.4 us (17%)
  Pallas kernels  6.63 us (4%)
    ppermute x20, starting transfers between devices, swap(): return lax.ppermute(value, axis, [(s, s ^ flip) for s in range(size)])  69.9 us
    all_to_all x1, blocking collectives, gather_chips(): return lax.all_to_all(copies, CHIPS, 0, 0, tiled=True)  29.4 us
    ppermute x20, waiting for transfers between devices, swap(): return lax.ppermute(value, axis, [(s, s ^ flip) for s in range(size)])  20.9 us
    all_to_all x1, starting transfers between devices, gather_chips(): return lax.all_to_all(copies, CHIPS, 0, 0, tiled=True)  12 us
    all_to_all x1, waiting for transfers between devices, gather_chips(): return lax.all_to_all(copies, CHIPS, 0, 0, tiled=True)  9.96 us
    all_to_all x1, starting transfers between devices, shards(): lax.all_to_all(grad_partial.reshape(16, rows, -1), INP, 0, 0, tiled=True)  8.62 us
    all_to_all x1, waiting for transfers between devices, shards(): act_parts = lax.all_to_all(act_partial, CHIPS, 0, 0, tiled=True)  8.36 us
    pallas_call x6, Pallas kernels, kernel_call(): pl.pallas_call(body, out_shape=shapes if many else shapes[0], in_specs=[V...  6.63 us
  transfers between devices with their start and end apart: 23, of which 10 were waited for; matrix products, arithmetic and copies ran while one was open for 1% of the time, Pallas kernels for 0%

profile of v1, /device:TPU:1, one launch (start us, length us, event | category | flops | bytes accessed | tf_op | source)
XLA Modules:
  0.0 174.6 jit_solution(9801545190213738916)
XLA Ops:
  0.0 0.0 copy-start.2
  0.0 1.6 broadcast_in_dim.2
  1.6 12.0 %all-to-all-start = ((bf16[16,32,512]{2,1,0:T(8,128)(2,1)}), bf16[16,32,512]{2,1,0:T(8,128)(2,1)S(1)}, u32[]{:S(2)}, u32[]{:S(2)}) async-start(bf16[16,32,512]{2,1,0:T(8,128)(2,1)} %broadcast_in_dim.2), calls=%async_computation | async-start | bytes 1048576 | tf_op jit(solution)/shard_map/all_to_all | solution.py:52
  13.6 0.0 copy-start.1
  13.6 3.0 %collective-permute-start.9 = (bf16[512,256]{1,0:T(8,128)(2,1)}, bf16[512,256]{1,0:T(8,128)(2,1)S(1)}, u32[]{:S(2)}, u32[]{:S(2)}) collective-permute-start(bf16[512,256]{1,0:T(8,128)(2,1)} %param.6), channel_id=1, source_target_pairs={{0,16},{16,0},{1,17},{17,1},{2,18},{18,2},{3,19},{19,3},{4,20},{20... | collective-permute-start | bytes 786440 | tf_op jit(solution)/shard_map/ppermute | solution.py:33
  16.7 1.9 %collective-permute-start.12 = (bf16[896,896]{1,0:T(8,128)(2,1)}, bf16[896,896]{1,0:T(8,128)(2,1)}, u32[]{:S(2)}, u32[]{:S(2)}) collective-permute-start(bf16[896,896]{1,0:T(8,128)(2,1)} %own.1), channel_id=1, source_target_pairs={{0,16},{16,0},{1,17},{17,1},{2,18},{18,2},{3,19},{19,3},{4,20},{20... | collective-permute-start | bytes 4816904 | tf_op jit(solution)/shard_map/ppermute | solution.py:33
  18.6 0.0 collective-permute-done.9
  18.6 10.0 %all-to-all-done = bf16[16,32,512]{2,1,0:T(8,128)(2,1)S(1)} async-done(((bf16[16,32,512]{2,1,0:T(8,128)(2,1)}), bf16[16,32,512]{2,1,0:T(8,128)(2,1)S(1)}, u32[]{:S(2)}, u32[]{:S(2)}) %all-to-all-start) | async-done | bytes 524320 | tf_op jit(solution)/shard_map/all_to_all | solution.py:52
  28.6 0.0 copy-done.2
  28.6 1.2 convolution_convert_fusion
  29.8 0.0 copy-start
  29.8 8.6 %all-to-all-start.1 = ((bf16[16,32,512]{2,1,0:T(8,128)(2,1)}), bf16[16,32,512]{2,1,0:T(8,128)(2,1)S(1)}, u32[]{:S(2)}, u32[]{:S(2)}) async-start(bf16[16,32,512]{2,1,0:T(8,128)(2,1)} %bitcast.2), calls=%async_computation.1 | async-start | bytes 1048576 | tf_op jit(solution)/shard_map/all_to_all | solution.py:120
  38.4 0.0 copy-done.1
  38.5 5.1 %collective-permute-start = (bf16[32,896]{1,0:T(8,128)(2,1)S(1)}, bf16[32,896]{1,0:T(8,128)(2,1)S(1)}, u32[]{:S(2)}, u32[]{:S(2)}) collective-permute-start(bf16[32,896]{1,0:T(8,128)(2,1)S(1)} %get-tuple-element.24), channel_id=1, source_target_pairs={{0,16},{16,0},{1,17},{17,1},{2,18},{18,2},{3,19},{19,3},{4,20},{20... | collective-permute-start | bytes 172040 | tf_op jit(solution)/shard_map/ppermute | solution.py:33
  43.6 0.9 collective-permute-done
  44.5 4.4 %collective-permute-start.1 = (bf16[32,1792]{1,0:T(8,128)(2,1)S(1)}, bf16[32,1792]{1,0:T(8,128)(2,1)S(1)}, u32[]{:S(2)}, u32[]{:S(2)}) collective-permute-start(bf16[32,1792]{1,0:T(8,128)(2,1)S(1)} %pad_maximum_fusion.refs_0_), channel_id=1, source_target_pairs={{0,1},{1,0},{2,3},{3,2},{4,5},{5,4},{6,7},{7,6},{8,9},{9,8},{10,11... | collective-permute-start | bytes 344072 | tf_op jit(solution)/shard_map/ppermute | solution.py:33
  48.9 5.2 %collective-permute-start.2 = (bf16[32,1792]{1,0:T(8,128)(2,1)S(1)}, bf16[32,1792]{1,0:T(8,128)(2,1)S(1)}, u32[]{:S(2)}, u32[]{:S(2)}) collective-permute-start(bf16[32,1792]{1,0:T(8,128)(2,1)S(1)} %pad_maximum_fusion.refs_0_), channel_id=1, source_target_pairs={{0,2},{1,3},{2,0},{3,1},{4,6},{5,7},{6,4},{7,5},{8,10},{9,11},{10,... | collective-permute-start | bytes 344072 | tf_op jit(solution)/shard_map/ppermute | solution.py:33
  54.2 1.9 %collective-permute-start.3 = (bf16[32,1792]{1,0:T(8,128)(2,1)S(1)}, bf16[32,1792]{1,0:T(8,128)(2,1)S(1)}, u32[]{:S(2)}, u32[]{:S(2)}) collective-permute-start(bf16[32,1792]{1,0:T(8,128)(2,1)S(1)} %pad_maximum_fusion.refs_0_), channel_id=1, source_target_pairs={{0,3},{1,2},{2,1},{3,0},{4,7},{5,6},{6,5},{7,4},{8,11},{9,10},{10,... | collective-permute-start | bytes 344072 | tf_op jit(solution)/shard_map/ppermute | solution.py:33
  56.1 7.5 %collective-permute-done.1.refs_1_ = bf16[32,1792]{1,0:T(8,128)(2,1)S(1)} collective-permute-done((bf16[32,1792]{1,0:T(8,128)(2,1)S(1)}, bf16[32,1792]{1,0:T(8,128)(2,1)S(1)}, u32[]{:S(2)}, u32[]{:S(2)}) %collective-permute-start.1) | collective-permute-done | bytes 114720 | tf_op jit(solution)/shard_map/ppermute | solution.py:33
  63.6 0.0 collective-permute-done.2.refs_2_
  63.6 0.0 collective-permute-done.3.refs_3_
  63.6 4.3 %collective-permute-start.6 = (bf16[64,1792]{1,0:T(8,128)(2,1)S(1)}, bf16[64,1792]{1,0:T(8,128)(2,1)S(1)}, u32[]{:S(2)}, u32[]{:S(2)}) collective-permute-start(bf16[64,1792]{1,0:T(8,128)(2,1)S(1)} %get-tuple-element.14.top), channel_id=1, source_target_pairs={{0,12},{4,8},{8,4},{12,0},{1,13},{5,9},{9,5},{13,1},{2,14},{6,10},... | collective-permute-start | bytes 688136 | tf_op jit(solution)/shard_map/ppermute | solution.py:33
  68.0 1.9 %collective-permute-start.5 = (bf16[64,1792]{1,0:T(8,128)(2,1)S(1)}, bf16[64,1792]{1,0:T(8,128)(2,1)S(1)}, u32[]{:S(2)}, u32[]{:S(2)}) collective-permute-start(bf16[64,1792]{1,0:T(8,128)(2,1)S(1)} %get-tuple-element.15.bottom), channel_id=1, source_target_pairs={{0,4},{4,0},{8,12},{12,8},{1,5},{5,1},{9,13},{13,9},{2,6},{6,2},{1... | collective-permute-start | bytes 688136 | tf_op jit(solution)/shard_map/ppermute | solution.py:33
  69.9 0.0 all-to-all-done.1.parts
  69.9 0.1 shard_map.47
  70.0 5.7 %collective-permute-start.10 = (bf16[32,256]{1,0:T(8,128)(2,1)S(1)}, bf16[32,256]{1,0:T(8,128)(2,1)S(1)}, u32[]{:S(2)}, u32[]{:S(2)}) collective-permute-start(bf16[32,256]{1,0:T(8,128)(2,1)S(1)} %get-tuple-element.17), channel_id=1, source_target_pairs={{0,16},{16,0},{1,17},{17,1},{2,18},{18,2},{3,19},{19,3},{4,20},{20... | collective-permute-start | bytes 49160 | tf_op jit(solution)/shard_map/ppermute | solution.py:33
  75.8 0.0 collective-permute-done.6.top3
  75.8 3.4 %collective-permute-start.7 = (bf16[64,1792]{1,0:T(8,128)(2,1)S(1)}, bf16[64,1792]{1,0:T(8,128)(2,1)S(1)}, u32[]{:S(2)}, u32[]{:S(2)}) collective-permute-start(bf16[64,1792]{1,0:T(8,128)(2,1)S(1)} %collective-permute-done.6.top3), channel_id=1, source_target_pairs={{0,4},{4,0},{8,12},{12,8},{1,5},{5,1},{9,13},{13,9},{2,6},{6,2},{1... | collective-permute-start | bytes 688136 | tf_op jit(solution)/shard_map/ppermute | solution.py:33
  79.2 0.0 collective-permute-done.5.bottom1
  79.2 2.2 %collective-permute-start.8 = (bf16[64,1792]{1,0:T(8,128)(2,1)S(1)}, bf16[64,1792]{1,0:T(8,128)(2,1)S(1)}, u32[]{:S(2)}, u32[]{:S(2)}) collective-permute-start(bf16[64,1792]{1,0:T(8,128)(2,1)S(1)} %collective-permute-done.5.bottom1), channel_id=1, source_target_pairs={{0,12},{4,8},{8,4},{12,0},{1,13},{5,9},{9,5},{13,1},{2,14},{6,10},... | collective-permute-start | bytes 688136 | tf_op jit(solution)/shard_map/ppermute | solution.py:33
  81.4 1.9 %collective-permute-start.4 = (bf16[64,1792]{1,0:T(8,128)(2,1)S(1)}, bf16[64,1792]{1,0:T(8,128)(2,1)S(1)}, u32[]{:S(2)}, u32[]{:S(2)}) collective-permute-start(bf16[64,1792]{1,0:T(8,128)(2,1)S(1)} %get-tuple-element.14.top), channel_id=1, source_target_pairs={{0,4},{4,0},{8,12},{12,8},{1,5},{5,1},{9,13},{13,9},{2,6},{6,2},{1... | collective-permute-start | bytes 688136 | tf_op jit(solution)/shard_map/ppermute | solution.py:33
  83.3 0.0 collective-permute-done.10
  83.3 4.3 %collective-permute-start.11 = (bf16[64,1792]{1,0:T(8,128)(2,1)S(1)}, bf16[64,1792]{1,0:T(8,128)(2,1)S(1)}, u32[]{:S(2)}, u32[]{:S(2)}) collective-permute-start(bf16[64,1792]{1,0:T(8,128)(2,1)S(1)} %get-tuple-element.15.bottom), channel_id=1, source_target_pairs={{0,12},{4,8},{8,4},{12,0},{1,13},{5,9},{9,5},{13,1},{2,14},{6,10},... | collective-permute-start | bytes 688136 | tf_op jit(solution)/shard_map/ppermute | solution.py:33
  87.6 0.0 collective-permute-done.7.top2
  87.7 1.5 collective-permute-done.8.bottom2
  89.2 0.0 collective-permute-done.4.top1
  89.2 3.2 %collective-permute-done.11.bottom3 = bf16[64,1792]{1,0:T(8,128)(2,1)S(1)} collective-permute-done((bf16[64,1792]{1,0:T(8,128)(2,1)S(1)}, bf16[64,1792]{1,0:T(8,128)(2,1)S(1)}, u32[]{:S(2)}, u32[]{:S(2)}) %collective-permute-start.11) | collective-permute-done | bytes 229408 | tf_op jit(solution)/shard_map/ppermute | solution.py:33
  92.4 0.0 collective-permute-done.12.other
  92.4 0.0 copy-done
  92.4 4.7 %shard_map.48 = bf16[16,32,896]{2,1,0:T(8,128)(2,1)} custom-call(bf16[64,1792]{1,0:T(8,128)(2,1)S(1)} %get-tuple-element.14.top, bf16[64,1792]{1,0:T(8,128)(2,1)S(1)} %get-tuple-element.15.bottom, bf16[64,1792]{1,0:T(8,128)(2,1)S(1)} %collective-permute-done.4.top1, bf16[64,1792]{1,0:T(8,128)(2,1)S(1)} %collective-permute-done.5.bottom1, ...), custom_call_target="tpu_custom_call" | custom-call | flops 1644167168 | bytes 5963776 | tf_op jit(solution)/shard_map/pallas_call | solution.py:21
  97.2 5.6 %all-to-all-start.2 = ((bf16[16,32,896]{2,1,0:T(8,128)(2,1)}), bf16[16,32,896]{2,1,0:T(8,128)(2,1)S(1)}, u32[]{:S(2)}, u32[]{:S(2)}) async-start(bf16[16,32,896]{2,1,0:T(8,128)(2,1)} %shard_map.48), calls=%async_computation.2 | async-start | bytes 1835008 | tf_op jit(solution)/shard_map/all_to_all | solution.py:136
  102.7 2.3 %collective-permute-start.13 = (bf16[32,512]{1,0:T(8,128)(2,1)S(1)}, bf16[32,512]{1,0:T(8,128)(2,1)S(1)}, u32[]{:S(2)}, u32[]{:S(2)}) collective-permute-start(bf16[32,512]{1,0:T(8,128)(2,1)S(1)} %pad_maximum_fusion.1.refs_0_), channel_id=1, source_target_pairs={{0,1},{1,0},{2,3},{3,2},{4,5},{5,4},{6,7},{7,6},{8,9},{9,8},{10,11... | collective-permute-start | bytes 98312 | tf_op jit(solution)/shard_map/ppermute | solution.py:33
  105.0 5.0 %collective-permute-start.14 = (bf16[32,512]{1,0:T(8,128)(2,1)S(1)}, bf16[32,512]{1,0:T(8,128)(2,1)S(1)}, u32[]{:S(2)}, u32[]{:S(2)}) collective-permute-start(bf16[32,512]{1,0:T(8,128)(2,1)S(1)} %pad_maximum_fusion.1.refs_0_), channel_id=1, source_target_pairs={{0,2},{1,3},{2,0},{3,1},{4,6},{5,7},{6,4},{7,5},{8,10},{9,11},{10,... | collective-permute-start | bytes 98312 | tf_op jit(solution)/shard_map/ppermute | solution.py:33
  110.0 4.1 %collective-permute-start.15 = (bf16[32,512]{1,0:T(8,128)(2,1)S(1)}, bf16[32,512]{1,0:T(8,128)(2,1)S(1)}, u32[]{:S(2)}, u32[]{:S(2)}) collective-permute-start(bf16[32,512]{1,0:T(8,128)(2,1)S(1)} %pad_maximum_fusion.1.refs_0_), channel_id=1, source_target_pairs={{0,3},{1,2},{2,1},{3,0},{4,7},{5,6},{6,5},{7,4},{8,11},{9,10},{10,... | collective-permute-start | bytes 98312 | tf_op jit(solution)/shard_map/ppermute | solution.py:33
  114.1 0.0 collective-permute-done.13.refs_1_
  114.1 0.6 collective-permute-done.14.refs_2_
  114.7 2.7 %collective-permute-done.15.refs_3_ = bf16[32,512]{1,0:T(8,128)(2,1)S(1)} collective-permute-done((bf16[32,512]{1,0:T(8,128)(2,1)S(1)}, bf16[32,512]{1,0:T(8,128)(2,1)S(1)}, u32[]{:S(2)}, u32[]{:S(2)}) %collective-permute-start.15) | collective-permute-done | bytes 32800 | tf_op jit(solution)/shard_map/ppermute | solution.py:33
  117.5 8.4 %all-to-all-done.2.parts = bf16[16,32,896]{2,1,0:T(8,128)(2,1)S(1)} async-done(((bf16[16,32,896]{2,1,0:T(8,128)(2,1)}), bf16[16,32,896]{2,1,0:T(8,128)(2,1)S(1)}, u32[]{:S(2)}, u32[]{:S(2)}) %all-to-all-start.2) | async-done | bytes 917536 | tf_op jit(solution)/shard_map/all_to_all | solution.py:136
  125.8 0.1 shard_map.50
  126.0 29.4 %all_to_all.20 = bf16[16,32,896]{2,1,0:T(8,128)(2,1)S(1)} all-to-all(bf16[16,32,896]{2,1,0:T(8,128)(2,1)S(1)} %shard_map.50), channel_id=1, replica_groups=mesh['z'=8,'ylo'=2,'core'=2,'x'=4,'yhi'=4] {'z','ylo'}, dimensions={0} | all-to-all | bytes 1835008 | tf_op jit(solution)/shard_map/all_to_all | solution.py:52
  155.3 3.5 %collective-permute-start.19 = (bf16[512,896]{1,0:T(8,128)(2,1)S(1)}, bf16[512,896]{1,0:T(8,128)(2,1)S(1)}, u32[]{:S(2)}, u32[]{:S(2)}) collective-permute-start(bf16[512,896]{1,0:T(8,128)(2,1)S(1)} %bitcast.6), channel_id=1, source_target_pairs={{0,16},{16,0},{1,17},{17,1},{2,18},{18,2},{3,19},{19,3},{4,20},{20... | collective-permute-start | bytes 2752520 | tf_op jit(solution)/shard_map/ppermute | solution.py:33
  158.8 1.9 %collective-permute-start.16 = (bf16[128,512]{1,0:T(8,128)(2,1)S(1)}, bf16[128,512]{1,0:T(8,128)(2,1)S(1)}, u32[]{:S(2)}, u32[]{:S(2)}) collective-permute-start(bf16[128,512]{1,0:T(8,128)(2,1)S(1)} %shard_map.49.g0), channel_id=1, source_target_pairs={{0,4},{4,0},{8,12},{12,8},{1,5},{5,1},{9,13},{13,9},{2,6},{6,2},{1... | collective-permute-start | bytes 393224 | tf_op jit(solution)/shard_map/ppermute | solution.py:33
  160.8 4.5 %collective-permute-start.17 = (bf16[128,512]{1,0:T(8,128)(2,1)S(1)}, bf16[128,512]{1,0:T(8,128)(2,1)S(1)}, u32[]{:S(2)}, u32[]{:S(2)}) collective-permute-start(bf16[128,512]{1,0:T(8,128)(2,1)S(1)} %shard_map.49.g0), channel_id=1, source_target_pairs={{0,8},{4,12},{8,0},{12,4},{1,9},{5,13},{9,1},{13,5},{2,10},{6,14},... | collective-permute-start | bytes 393224 | tf_op jit(solution)/shard_map/ppermute | solution.py:33
  165.3 3.1 %collective-permute-start.18 = (bf16[128,512]{1,0:T(8,128)(2,1)S(1)}, bf16[128,512]{1,0:T(8,128)(2,1)S(1)}, u32[]{:S(2)}, u32[]{:S(2)}) collective-permute-start(bf16[128,512]{1,0:T(8,128)(2,1)S(1)} %shard_map.49.g0), channel_id=1, source_target_pairs={{0,12},{4,8},{8,4},{12,0},{1,13},{5,9},{9,5},{13,1},{2,14},{6,10},... | collective-permute-start | bytes 393224 | tf_op jit(solution)/shard_map/ppermute | solution.py:33
  168.4 0.0 collective-permute-done.16.g1
  168.4 1.4 collective-permute-done.17.g2
  169.8 3.1 %collective-permute-done.18.g3 = bf16[128,512]{1,0:T(8,128)(2,1)S(1)} collective-permute-done((bf16[128,512]{1,0:T(8,128)(2,1)S(1)}, bf16[128,512]{1,0:T(8,128)(2,1)S(1)}, u32[]{:S(2)}, u32[]{:S(2)}) %collective-permute-start.18) | collective-permute-done | bytes 131104 | tf_op jit(solution)/shard_map/ppermute | solution.py:33
  172.9 0.0 collective-permute-done.19.act_theirs
  172.9 1.7 shard_map.51
  (5 shorter events, 0.1 us)
Async XLA Ops:
  0.0 28.6 %copy-start.2 = (bf16[512,256]{1,0:T(8,128)(2,1)S(1)}, bf16[512,256]{1,0:T(8,128)(2,1)}, u32[]{:S(2)}) copy-start(bf16[512,256]{1,0:T(8,128)(2,1)} %param.6) | copy-start | bytes 786436
  1.6 26.9 %all-to-all-start = ((bf16[16,32,512]{2,1,0:T(8,128)(2,1)}), bf16[16,32,512]{2,1,0:T(8,128)(2,1)S(1)}, u32[]{:S(2)}, u32[]{:S(2)}) async-start(bf16[16,32,512]{2,1,0:T(8,128)(2,1)} %broadcast_in_dim.2), calls=%async_computation | async-start | bytes 1048576 | tf_op jit(solution)/shard_map/all_to_all | solution.py:52
  13.6 24.8 %copy-start.1 = (bf16[64,896]{1,0:T(8,128)(2,1)S(1)}, bf16[64,896]{1,0:T(8,128)(2,1)}, u32[]{:S(2)}) copy-start(bf16[64,896]{1,0:T(8,128)(2,1)} %param.5) | copy-start | bytes 344068
  13.6 4.9 %collective-permute-start.9 = (bf16[512,256]{1,0:T(8,128)(2,1)}, bf16[512,256]{1,0:T(8,128)(2,1)S(1)}, u32[]{:S(2)}, u32[]{:S(2)}) collective-permute-start(bf16[512,256]{1,0:T(8,128)(2,1)} %param.6), channel_id=1, source_target_pairs={{0,16},{16,0},{1,17},{17,1},{2,18},{18,2},{3,19},{19,3},{4,20},{20... | collective-permute-start | bytes 786440 | tf_op jit(solution)/shard_map/ppermute | solution.py:33
  16.7 75.8 %collective-permute-start.12 = (bf16[896,896]{1,0:T(8,128)(2,1)}, bf16[896,896]{1,0:T(8,128)(2,1)}, u32[]{:S(2)}, u32[]{:S(2)}) collective-permute-start(bf16[896,896]{1,0:T(8,128)(2,1)} %own.1), channel_id=1, source_target_pairs={{0,16},{16,0},{1,17},{17,1},{2,18},{18,2},{3,19},{19,3},{4,20},{20... | collective-permute-start | bytes 4816904 | tf_op jit(solution)/shard_map/ppermute | solution.py:33
  29.8 62.6 %copy-start = (bf16[896,896]{1,0:T(8,128)(2,1)S(1)}, bf16[896,896]{1,0:T(8,128)(2,1)}, u32[]{:S(2)}) copy-start(bf16[896,896]{1,0:T(8,128)(2,1)} %own.1) | copy-start | bytes 4816900
  29.8 40.1 %all-to-all-start.1 = ((bf16[16,32,512]{2,1,0:T(8,128)(2,1)}), bf16[16,32,512]{2,1,0:T(8,128)(2,1)S(1)}, u32[]{:S(2)}, u32[]{:S(2)}) async-start(bf16[16,32,512]{2,1,0:T(8,128)(2,1)} %bitcast.2), calls=%async_computation.1 | async-start | bytes 1048576 | tf_op jit(solution)/shard_map/all_to_all | solution.py:120
  38.5 6.0 %collective-permute-start = (bf16[32,896]{1,0:T(8,128)(2,1)S(1)}, bf16[32,896]{1,0:T(8,128)(2,1)S(1)}, u32[]{:S(2)}, u32[]{:S(2)}) collective-permute-start(bf16[32,896]{1,0:T(8,128)(2,1)S(1)} %get-tuple-element.24), channel_id=1, source_target_pairs={{0,16},{16,0},{1,17},{17,1},{2,18},{18,2},{3,19},{19,3},{4,20},{20... | collective-permute-start | bytes 172040 | tf_op jit(solution)/shard_map/ppermute | solution.py:33
  44.5 19.1 %collective-permute-start.1 = (bf16[32,1792]{1,0:T(8,128)(2,1)S(1)}, bf16[32,1792]{1,0:T(8,128)(2,1)S(1)}, u32[]{:S(2)}, u32[]{:S(2)}) collective-permute-start(bf16[32,1792]{1,0:T(8,128)(2,1)S(1)} %pad_maximum_fusion.refs_0_), channel_id=1, source_target_pairs={{0,1},{1,0},{2,3},{3,2},{4,5},{5,4},{6,7},{7,6},{8,9},{9,8},{10,11... | collective-permute-start | bytes 344072 | tf_op jit(solution)/shard_map/ppermute | solution.py:33
  48.9 14.6 %collective-permute-start.2 = (bf16[32,1792]{1,0:T(8,128)(2,1)S(1)}, bf16[32,1792]{1,0:T(8,128)(2,1)S(1)}, u32[]{:S(2)}, u32[]{:S(2)}) collective-permute-start(bf16[32,1792]{1,0:T(8,128)(2,1)S(1)} %pad_maximum_fusion.refs_0_), channel_id=1, source_target_pairs={{0,2},{1,3},{2,0},{3,1},{4,6},{5,7},{6,4},{7,5},{8,10},{9,11},{10,... | collective-permute-start | bytes 344072 | tf_op jit(solution)/shard_map/ppermute | solution.py:33
  54.2 9.4 %collective-permute-start.3 = (bf16[32,1792]{1,0:T(8,128)(2,1)S(1)}, bf16[32,1792]{1,0:T(8,128)(2,1)S(1)}, u32[]{:S(2)}, u32[]{:S(2)}) collective-permute-start(bf16[32,1792]{1,0:T(8,128)(2,1)S(1)} %pad_maximum_fusion.refs_0_), channel_id=1, source_target_pairs={{0,3},{1,2},{2,1},{3,0},{4,7},{5,6},{6,5},{7,4},{8,11},{9,10},{10,... | collective-permute-start | bytes 344072 | tf_op jit(solution)/shard_map/ppermute | solution.py:33
  63.6 12.1 %collective-permute-start.6 = (bf16[64,1792]{1,0:T(8,128)(2,1)S(1)}, bf16[64,1792]{1,0:T(8,128)(2,1)S(1)}, u32[]{:S(2)}, u32[]{:S(2)}) collective-permute-start(bf16[64,1792]{1,0:T(8,128)(2,1)S(1)} %get-tuple-element.14.top), channel_id=1, source_target_pairs={{0,12},{4,8},{8,4},{12,0},{1,13},{5,9},{9,5},{13,1},{2,14},{6,10},... | collective-permute-start | bytes 688136 | tf_op jit(solution)/shard_map/ppermute | solution.py:33
  68.0 11.2 %collective-permute-start.5 = (bf16[64,1792]{1,0:T(8,128)(2,1)S(1)}, bf16[64,1792]{1,0:T(8,128)(2,1)S(1)}, u32[]{:S(2)}, u32[]{:S(2)}) collective-permute-start(bf16[64,1792]{1,0:T(8,128)(2,1)S(1)} %get-tuple-element.15.bottom), channel_id=1, source_target_pairs={{0,4},{4,0},{8,12},{12,8},{1,5},{5,1},{9,13},{13,9},{2,6},{6,2},{1... | collective-permute-start | bytes 688136 | tf_op jit(solution)/shard_map/ppermute | solution.py:33
  70.0 13.3 %collective-permute-start.10 = (bf16[32,256]{1,0:T(8,128)(2,1)S(1)}, bf16[32,256]{1,0:T(8,128)(2,1)S(1)}, u32[]{:S(2)}, u32[]{:S(2)}) collective-permute-start(bf16[32,256]{1,0:T(8,128)(2,1)S(1)} %get-tuple-element.17), channel_id=1, source_target_pairs={{0,16},{16,0},{1,17},{17,1},{2,18},{18,2},{3,19},{19,3},{4,20},{20... | collective-permute-start | bytes 49160 | tf_op jit(solution)/shard_map/ppermute | solution.py:33
  75.8 11.9 %collective-permute-start.7 = (bf16[64,1792]{1,0:T(8,128)(2,1)S(1)}, bf16[64,1792]{1,0:T(8,128)(2,1)S(1)}, u32[]{:S(2)}, u32[]{:S(2)}) collective-permute-start(bf16[64,1792]{1,0:T(8,128)(2,1)S(1)} %collective-permute-done.6.top3), channel_id=1, source_target_pairs={{0,4},{4,0},{8,12},{12,8},{1,5},{5,1},{9,13},{13,9},{2,6},{6,2},{1... | collective-permute-start | bytes 688136 | tf_op jit(solution)/shard_map/ppermute | solution.py:33
  79.2 10.0 %collective-permute-start.8 = (bf16[64,1792]{1,0:T(8,128)(2,1)S(1)}, bf16[64,1792]{1,0:T(8,128)(2,1)S(1)}, u32[]{:S(2)}, u32[]{:S(2)}) collective-permute-start(bf16[64,1792]{1,0:T(8,128)(2,1)S(1)} %collective-permute-done.5.bottom1), channel_id=1, source_target_pairs={{0,12},{4,8},{8,4},{12,0},{1,13},{5,9},{9,5},{13,1},{2,14},{6,10},... | collective-permute-start | bytes 688136 | tf_op jit(solution)/shard_map/ppermute | solution.py:33
  81.4 7.8 %collective-permute-start.4 = (bf16[64,1792]{1,0:T(8,128)(2,1)S(1)}, bf16[64,1792]{1,0:T(8,128)(2,1)S(1)}, u32[]{:S(2)}, u32[]{:S(2)}) collective-permute-start(bf16[64,1792]{1,0:T(8,128)(2,1)S(1)} %get-tuple-element.14.top), channel_id=1, source_target_pairs={{0,4},{4,0},{8,12},{12,8},{1,5},{5,1},{9,13},{13,9},{2,6},{6,2},{1... | collective-permute-start | bytes 688136 | tf_op jit(solution)/shard_map/ppermute | solution.py:33
  83.3 9.1 %collective-permute-start.11 = (bf16[64,1792]{1,0:T(8,128)(2,1)S(1)}, bf16[64,1792]{1,0:T(8,128)(2,1)S(1)}, u32[]{:S(2)}, u32[]{:S(2)}) collective-permute-start(bf16[64,1792]{1,0:T(8,128)(2,1)S(1)} %get-tuple-element.15.bottom), channel_id=1, source_target_pairs={{0,12},{4,8},{8,4},{12,0},{1,13},{5,9},{9,5},{13,1},{2,14},{6,10},... | collective-permute-start | bytes 688136 | tf_op jit(solution)/shard_map/ppermute | solution.py:33
  97.2 28.7 %all-to-all-start.2 = ((bf16[16,32,896]{2,1,0:T(8,128)(2,1)}), bf16[16,32,896]{2,1,0:T(8,128)(2,1)S(1)}, u32[]{:S(2)}, u32[]{:S(2)}) async-start(bf16[16,32,896]{2,1,0:T(8,128)(2,1)} %shard_map.48), calls=%async_computation.2 | async-start | bytes 1835008 | tf_op jit(solution)/shard_map/all_to_all | solution.py:136
  102.7 11.4 %collective-permute-start.13 = (bf16[32,512]{1,0:T(8,128)(2,1)S(1)}, bf16[32,512]{1,0:T(8,128)(2,1)S(1)}, u32[]{:S(2)}, u32[]{:S(2)}) collective-permute-start(bf16[32,512]{1,0:T(8,128)(2,1)S(1)} %pad_maximum_fusion.1.refs_0_), channel_id=1, source_target_pairs={{0,1},{1,0},{2,3},{3,2},{4,5},{5,4},{6,7},{7,6},{8,9},{9,8},{10,11... | collective-permute-start | bytes 98312 | tf_op jit(solution)/shard_map/ppermute | solution.py:33
  105.0 9.7 %collective-permute-start.14 = (bf16[32,512]{1,0:T(8,128)(2,1)S(1)}, bf16[32,512]{1,0:T(8,128)(2,1)S(1)}, u32[]{:S(2)}, u32[]{:S(2)}) collective-permute-start(bf16[32,512]{1,0:T(8,128)(2,1)S(1)} %pad_maximum_fusion.1.refs_0_), channel_id=1, source_target_pairs={{0,2},{1,3},{2,0},{3,1},{4,6},{5,7},{6,4},{7,5},{8,10},{9,11},{10,... | collective-permute-start | bytes 98312 | tf_op jit(solution)/shard_map/ppermute | solution.py:33
  110.0 7.5 %collective-permute-start.15 = (bf16[32,512]{1,0:T(8,128)(2,1)S(1)}, bf16[32,512]{1,0:T(8,128)(2,1)S(1)}, u32[]{:S(2)}, u32[]{:S(2)}) collective-permute-start(bf16[32,512]{1,0:T(8,128)(2,1)S(1)} %pad_maximum_fusion.1.refs_0_), channel_id=1, source_target_pairs={{0,3},{1,2},{2,1},{3,0},{4,7},{5,6},{6,5},{7,4},{8,11},{9,10},{10,... | collective-permute-start | bytes 98312 | tf_op jit(solution)/shard_map/ppermute | solution.py:33
  155.3 17.6 %collective-permute-start.19 = (bf16[512,896]{1,0:T(8,128)(2,1)S(1)}, bf16[512,896]{1,0:T(8,128)(2,1)S(1)}, u32[]{:S(2)}, u32[]{:S(2)}) collective-permute-start(bf16[512,896]{1,0:T(8,128)(2,1)S(1)} %bitcast.6), channel_id=1, source_target_pairs={{0,16},{16,0},{1,17},{17,1},{2,18},{18,2},{3,19},{19,3},{4,20},{20... | collective-permute-start | bytes 2752520 | tf_op jit(solution)/shard_map/ppermute | solution.py:33
  158.8 9.6 %collective-permute-start.16 = (bf16[128,512]{1,0:T(8,128)(2,1)S(1)}, bf16[128,512]{1,0:T(8,128)(2,1)S(1)}, u32[]{:S(2)}, u32[]{:S(2)}) collective-permute-start(bf16[128,512]{1,0:T(8,128)(2,1)S(1)} %shard_map.49.g0), channel_id=1, source_target_pairs={{0,4},{4,0},{8,12},{12,8},{1,5},{5,1},{9,13},{13,9},{2,6},{6,2},{1... | collective-permute-start | bytes 393224 | tf_op jit(solution)/shard_map/ppermute | solution.py:33
  160.8 9.1 %collective-permute-start.17 = (bf16[128,512]{1,0:T(8,128)(2,1)S(1)}, bf16[128,512]{1,0:T(8,128)(2,1)S(1)}, u32[]{:S(2)}, u32[]{:S(2)}) collective-permute-start(bf16[128,512]{1,0:T(8,128)(2,1)S(1)} %shard_map.49.g0), channel_id=1, source_target_pairs={{0,8},{4,12},{8,0},{12,4},{1,9},{5,13},{9,1},{13,5},{2,10},{6,14},... | collective-permute-start | bytes 393224 | tf_op jit(solution)/shard_map/ppermute | solution.py:33
  165.3 7.6 %collective-permute-start.18 = (bf16[128,512]{1,0:T(8,128)(2,1)S(1)}, bf16[128,512]{1,0:T(8,128)(2,1)S(1)}, u32[]{:S(2)}, u32[]{:S(2)}) collective-permute-start(bf16[128,512]{1,0:T(8,128)(2,1)S(1)} %shard_map.49.g0), channel_id=1, source_target_pairs={{0,12},{4,8},{8,4},{12,0},{1,13},{5,9},{9,5},{13,1},{2,14},{6,10},... | collective-permute-start | bytes 393224 | tf_op jit(solution)/shard_map/ppermute | solution.py:33

commit v2 on v0

v2 whole, which is shorter than its diff:
```python
import jax
import jax.numpy as jnp
from jax import lax
from jax.experimental import pallas as pl
from jax.experimental.pallas import tpu as pltpu
from jax.sharding import Mesh, PartitionSpec as P

SEQS = 2
SEQ_LEN = 512
OUT = ("z", "ylo", "core")
INP = ("x", "yhi")
CHIPS = ("z", "ylo")
BF16 = jnp.bfloat16
F32 = jnp.float32
VMEM = pl.BlockSpec(memory_space=pltpu.VMEM)


def kernel_call(body, shapes, args, flops=0):
    moved = sum(a.size * a.dtype.itemsize for a in args) + sum(s.size * s.dtype.itemsize for s in shapes)
    many = len(shapes) > 1
    return pl.pallas_call(
        body,
        out_shape=shapes if many else shapes[0],
        in_specs=[VMEM] * len(args),
        out_specs=[VMEM] * len(shapes) if many else VMEM,
        compiler_params=pltpu.CompilerParams(vmem_limit_bytes=40 * 2**20),
        cost_estimate=pl.CostEstimate(flops=flops, bytes_accessed=moved, transcendentals=0),
    )(*args)


def swap(value, axis, flip):
    size = lax.axis_size(axis)
    return lax.ppermute(value, axis, [(s, s ^ flip) for s in range(size)])


def dot_kernel(*refs):
    pieces, (basis0, basis1, out) = refs[:4], refs[4:]
    features = basis0.shape[0]
    blocks, block = out.shape[0], out.shape[1]
    each = blocks // 4
    total = 0.0
    for core, basis in ((0, basis0), (1, basis1)):
        rows = jnp.concatenate([piece[core * each:(core + 1) * each] for piece in pieces])
        total += jnp.dot(rows.reshape(blocks * block, features), basis[...], preferred_element_type=F32)
    out[...] = total.astype(BF16).reshape(out.shape)


def sum_parts(parts):
    total = parts[0].astype(F32)
    for index in range(1, parts.shape[0]):
        total += parts[index].astype(F32)
    return total.astype(BF16)


def sum_copies_kernel(parts, out):
    rounded = sum_parts(parts)
    for index in range(out.shape[0]):
        out[index] = rounded


def sum_split_kernel(parts, out):
    rounded = sum_parts(parts)
    copies, columns = out.shape[0] // 2, out.shape[2]
    for index in range(out.shape[0]):
        core = index // copies
        out[index] = rounded[:, core * columns:(core + 1) * columns]


def square_kernel(grad_mine, grad_theirs, act_mine, act_theirs, out):
    half = act_mine.shape[0] // SEQS
    total = 0.0
    for seq in range(SEQS):
        rows = slice(seq * half, (seq + 1) * half)
        contract = (((0,), (0,)), ((), ()))
        rotated = lax.dot_general(grad_mine[rows, :], act_mine[rows, :], contract, preferred_element_type=F32)
        rotated += lax.dot_general(grad_theirs[rows, :], act_theirs[rows, :], contract, preferred_element_type=F32)
        total = total + rotated * rotated
    out[...] = total * (1.0 / (SEQS * SEQ_LEN))


def both_cores(core, own):
    other = swap(own, "core", 1)
    return jnp.where(core == 0, own, other), jnp.where(core == 0, other, own)


def shards(grads, acts, grad_basis, act_basis):
    core, x = lax.axis_index("core"), lax.axis_index("x")
    half, features = acts.shape[0] // 2, acts.shape[1]
    tokens, eig = 16 * half, act_basis.shape[1]
    rows, columns = grads.shape[0], grad_basis.shape[1]

    copies = jnp.broadcast_to(acts.reshape(2, 1, half, features), (2, 4, half, features))
    act0 = lax.all_to_all(copies.reshape(8, half, features), ("core", "yhi"), 0, 0, tiled=True)
    act_basis0, act_basis1 = both_cores(core, act_basis)
    grad_basis_both = jnp.concatenate(both_cores(core, grad_basis), axis=1)

    act0, grads = lax.optimization_barrier((act0, grads))
    act1, act3, act2 = swap(act0, "x", 1), swap(act0, "x", 3), swap(act0, "x", 2)
    grad_copies = jnp.broadcast_to(grads[None], (16, *grads.shape))
    grad_rows = lax.all_to_all(grad_copies, CHIPS, 0, 0, tiled=True)

    blocks = jax.ShapeDtypeStruct((16, half, eig), BF16)
    act_partial = kernel_call(
        dot_kernel,
        [blocks],
        [act0, act1, act2, act3, act_basis0, act_basis1],
        flops=2 * tokens * 2 * features * eig,
    )
    act_partial, grad_rows = lax.optimization_barrier((act_partial, grad_rows))
    act_parts = lax.all_to_all(act_partial, CHIPS, 0, 0, tiled=True)
    grad_partial = jnp.dot(
        grad_rows.reshape(16 * rows, -1), grad_basis_both, preferred_element_type=F32
    ).astype(BF16)
    grad_parts = lax.all_to_all(grad_partial.reshape(16, rows, -1), INP, 0, 0, tiled=True)

    act_copies = kernel_call(sum_copies_kernel, [blocks], [act_parts])
    act_copies, grad_parts = lax.optimization_barrier((act_copies, grad_parts))
    act_mine = lax.all_to_all(act_copies, CHIPS, 0, 0, tiled=True).reshape(tokens, eig)
    split = jax.ShapeDtypeStruct((32, rows, columns), BF16)
    grad_split = kernel_call(sum_split_kernel, [split], [grad_parts])
    grad_all = lax.all_to_all(grad_split, ("core", *INP), 0, 0, tiled=True).reshape(2, 4, 4 * rows, columns)
    grad_mine, grad_theirs = (
        jnp.concatenate([grad_all[core ^ other, x ^ flip] for flip in range(4)]) for other in range(2)
    )
    act_theirs = swap(act_mine, "core", 1)

    return kernel_call(
        square_kernel,
        [jax.ShapeDtypeStruct((columns, eig), F32)],
        [grad_mine, grad_theirs, act_mine, act_theirs],
        flops=2 * 2 * tokens * columns * eig,
    )


def solution(mesh):
    split = Mesh(mesh.devices.reshape(8, 2, 2, 4, 4), OUT + INP)
    return jax.shard_map(
        shards,
        mesh=split,
        in_specs=(P(OUT, INP), P(INP, OUT), P(INP, OUT), P(OUT, INP)),
        out_specs=P(OUT, INP),
        check_vma=False,
    )
```

time: 344 us -> 181 us (0.53)
  the two profiles are of different devices: /device:TPU:1 before, /device:TPU:9 now
where the time goes in v2:
time: 181 us; the launch traced here: 180 us
  waiting for transfers between devices  88.4 us (49%)
  starting transfers between devices  58.2 us (32%)
  blocking collectives  19.5 us (11%)
  Pallas kernels  6.8 us (4%)
  local copies, waits for them, and re-layouts  2.57 us (1%)
  matrix products  2.29 us (1%)
  other arithmetic  1.82 us (1%)
    all_to_all x1, waiting for transfers between devices, shards(): lax.all_to_all(act_copies, CHIPS, 0, 0, tiled=True).reshape(tokens, eig)  21.8 us
    ppermute x6, waiting for transfers between devices, swap(): return lax.ppermute(value, axis, [(s, s ^ flip) for s in range(size)])  20.9 us
    all_to_all x1, blocking collectives, shards(): lax.all_to_all(copies.reshape(8, half, features), ('core', 'yhi'), 0, 0,...  19.5 us
    ppermute x6, starting transfers between devices, swap(): return lax.ppermute(value, axis, [(s, s ^ flip) for s in range(size)])  19.1 us
    all_to_all x1, waiting for transfers between devices, shards(): lax.all_to_all(grad_split, ('core', *INP), 0, 0, tiled=True)  15.8 us
    all_to_all x1, waiting for transfers between devices, shards(): lax.all_to_all(grad_partial.reshape(16, rows, -1), INP, 0, 0, tiled=True)  15 us
    all_to_all x1, waiting for transfers between devices, shards(): act_parts = lax.all_to_all(act_partial, CHIPS, 0, 0, tiled=True)  14.9 us
    all_to_all x1, starting transfers between devices, shards(): grad_rows = lax.all_to_all(grad_copies, CHIPS, 0, 0, tiled=True)  12.6 us
  transfers between devices with their start and end apart: 11, of which 8 were waited for; matrix products, arithmetic and copies ran while one was open for 4% of the time, Pallas kernels for 3%

profile of v2, /device:TPU:9, one launch (start us, length us, event | category | flops | bytes accessed | tf_op | source)
XLA Modules:
  0.0 179.8 jit_solution(8133894966778672315)
XLA Ops:
  0.0 0.0 copy-start
  0.0 2.7 %collective-permute-start.3 = (bf16[896,896]{1,0:T(8,128)(2,1)}, bf16[896,896]{1,0:T(8,128)(2,1)}, u32[]{:S(2)}, u32[]{:S(2)}) collective-permute-start(bf16[896,896]{1,0:T(8,128)(2,1)} %param.7), channel_id=1, source_target_pairs={{0,16},{16,0},{1,17},{17,1},{2,18},{18,2},{3,19},{19,3},{4,20},{20... | collective-permute-start | bytes 4816904 | tf_op jit(solution)/shard_map/ppermute | solution.py:33
  2.7 0.9 broadcast_in_dim.14
  3.7 19.5 %all_to_all.30.refs_0_ = bf16[8,32,896]{2,1,0:T(8,128)(2,1)S(1)} all-to-all(bf16[8,32,896]{2,1,0:T(8,128)(2,1)S(1)} %bitcast.26), channel_id=1, replica_groups=mesh['z'=8,'ylo'=2,'core'=2,'x'=4,'yhi'=4] {'core','yhi'}, dimensions={0} | all-to-all | bytes 917504 | tf_op jit(solution)/shard_map/all_to_all | solution.py:93
  23.2 1.6 broadcast_in_dim.15
  24.8 12.6 %all-to-all-start.1 = ((bf16[16,32,512]{2,1,0:T(8,128)(2,1)}), bf16[16,32,512]{2,1,0:T(8,128)(2,1)}, u32[]{:S(2)}, u32[]{:S(2)}) async-start(bf16[16,32,512]{2,1,0:T(8,128)(2,1)} %broadcast_in_dim.15), calls=%async_computation.1 | async-start | bytes 1048576 | tf_op jit(solution)/shard_map/all_to_all | solution.py:100
  37.3 3.1 %collective-permute-start = (bf16[8,32,896]{2,1,0:T(8,128)(2,1)S(1)}, bf16[8,32,896]{2,1,0:T(8,128)(2,1)S(1)}, u32[]{:S(2)}, u32[]{:S(2)}) collective-permute-start(bf16[8,32,896]{2,1,0:T(8,128)(2,1)S(1)} %all_to_all.30.refs_0_), channel_id=1, source_target_pairs={{0,4},{4,0},{8,12},{12,8},{1,5},{5,1},{9,13},{13,9},{2,6},{6,2},{1... | collective-permute-start | bytes 1376264 | tf_op jit(solution)/shard_map/ppermute | solution.py:33
  40.5 4.4 %collective-permute-start.1 = (bf16[8,32,896]{2,1,0:T(8,128)(2,1)S(1)}, bf16[8,32,896]{2,1,0:T(8,128)(2,1)S(1)}, u32[]{:S(2)}, u32[]{:S(2)}) collective-permute-start(bf16[8,32,896]{2,1,0:T(8,128)(2,1)S(1)} %all_to_all.30.refs_0_), channel_id=1, source_target_pairs={{0,8},{4,12},{8,0},{12,4},{1,9},{5,13},{9,1},{13,5},{2,10},{6,14},... | collective-permute-start | bytes 1376264 | tf_op jit(solution)/shard_map/ppermute | solution.py:33
  44.8 2.1 %collective-permute-start.2 = (bf16[8,32,896]{2,1,0:T(8,128)(2,1)S(1)}, bf16[8,32,896]{2,1,0:T(8,128)(2,1)S(1)}, u32[]{:S(2)}, u32[]{:S(2)}) collective-permute-start(bf16[8,32,896]{2,1,0:T(8,128)(2,1)S(1)} %all_to_all.30.refs_0_), channel_id=1, source_target_pairs={{0,12},{4,8},{8,4},{12,0},{1,13},{5,9},{9,5},{13,1},{2,14},{6,10},... | collective-permute-start | bytes 1376264 | tf_op jit(solution)/shard_map/ppermute | solution.py:33
  46.9 0.0 collective-permute-done.3
  47.0 0.0 copy-done
  47.0 1.7 broadcast_select_fusion
  48.7 2.0 %collective-permute-done.refs_1_ = bf16[8,32,896]{2,1,0:T(8,128)(2,1)S(1)} collective-permute-done((bf16[8,32,896]{2,1,0:T(8,128)(2,1)S(1)}, bf16[8,32,896]{2,1,0:T(8,128)(2,1)S(1)}, u32[]{:S(2)}, u32[]{:S(2)}) %collective-permute-start) | collective-permute-done | bytes 458784 | tf_op jit(solution)/shard_map/ppermute | solution.py:33
  50.7 12.0 %collective-permute-done.1.refs_2_ = bf16[8,32,896]{2,1,0:T(8,128)(2,1)S(1)} collective-permute-done((bf16[8,32,896]{2,1,0:T(8,128)(2,1)S(1)}, bf16[8,32,896]{2,1,0:T(8,128)(2,1)S(1)}, u32[]{:S(2)}, u32[]{:S(2)}) %collective-permute-start.1) | collective-permute-done | bytes 458784 | tf_op jit(solution)/shard_map/ppermute | solution.py:33
  62.6 5.9 %collective-permute-done.2.refs_3_ = bf16[8,32,896]{2,1,0:T(8,128)(2,1)S(1)} collective-permute-done((bf16[8,32,896]{2,1,0:T(8,128)(2,1)S(1)}, bf16[8,32,896]{2,1,0:T(8,128)(2,1)S(1)}, u32[]{:S(2)}, u32[]{:S(2)}) %collective-permute-start.2) | collective-permute-done | bytes 458784 | tf_op jit(solution)/shard_map/ppermute | solution.py:33
  68.5 3.2 %shard_map.46 = bf16[16,32,896]{2,1,0:T(8,128)(2,1)} custom-call(bf16[8,32,896]{2,1,0:T(8,128)(2,1)S(1)} %all_to_all.30.refs_0_, bf16[8,32,896]{2,1,0:T(8,128)(2,1)S(1)} %collective-permute-done.refs_1_, bf16[8,32,896]{2,1,0:T(8,128)(2,1)S(1)} %collective-permute-done.1.refs_2_, bf16[8,32,896]{2,1,0:T(8,128)(2,1)S(1)} %collective-permute-done.2.refs_3_, ...), custom_call_target="tpu_custom_call" | custom-call | flops 1644167168 | bytes 5963776 | tf_op jit(solution)/shard_map/pallas_call | solution.py:21
  71.7 0.0 copy-start.1
  71.7 0.0 all-to-all-done.1
  71.7 7.7 %all-to-all-start.2 = ((bf16[16,32,896]{2,1,0:T(8,128)(2,1)}), bf16[16,32,896]{2,1,0:T(8,128)(2,1)S(1)}, u32[]{:S(2)}, u32[]{:S(2)}) async-start(bf16[16,32,896]{2,1,0:T(8,128)(2,1)} %shard_map.46), calls=%async_computation.2 | async-start | bytes 1835008 | tf_op jit(solution)/shard_map/all_to_all | solution.py:110
  79.4 0.0 copy-done.1
  79.4 4.7 %collective-permute-start.4 = (bf16[512,256]{1,0:T(8,128)(2,1)S(1)}, bf16[512,256]{1,0:T(8,128)(2,1)S(1)}, u32[]{:S(2)}, u32[]{:S(2)}) collective-permute-start(bf16[512,256]{1,0:T(8,128)(2,1)S(1)} %copy-done.1), channel_id=1, source_target_pairs={{0,16},{16,0},{1,17},{17,1},{2,18},{18,2},{3,19},{19,3},{4,20},{20... | collective-permute-start | bytes 786440 | tf_op jit(solution)/shard_map/ppermute | solution.py:33
  84.1 1.1 collective-permute-done.4
  85.2 0.1 broadcast_select_fusion.3
  85.3 2.3 %convolution_convert_fusion = bf16[512,512]{1,0:T(8,128)(2,1)} fusion(bf16[512,512]{1,0:T(8,128)(2,1)} %bitcast.2, bf16[512,256]{1,0:T(8,128)(2,1)S(1)} %get-tuple-element.28, bf16[512,256]{1,0:T(8,128)(2,1)S(1)} %get-tuple-element.27), kind=kOutput, calls=%fused_computation.2 | convolution fusion | flops 269746176 | bytes 1572864 | tf_op jit(solution)/shard_map/dot_general | solution.py:111
  87.5 14.9 %all-to-all-done.2.parts = bf16[16,32,896]{2,1,0:T(8,128)(2,1)S(1)} async-done(((bf16[16,32,896]{2,1,0:T(8,128)(2,1)}), bf16[16,32,896]{2,1,0:T(8,128)(2,1)S(1)}, u32[]{:S(2)}, u32[]{:S(2)}) %all-to-all-start.2) | async-done | bytes 917536 | tf_op jit(solution)/shard_map/all_to_all | solution.py:110
  102.5 3.6 %all-to-all-start.3 = ((bf16[16,32,512]{2,1,0:T(8,128)(2,1)}), bf16[16,32,512]{2,1,0:T(8,128)(2,1)S(1)}, u32[]{:S(2)}, u32[]{:S(2)}) async-start(bf16[16,32,512]{2,1,0:T(8,128)(2,1)} %bitcast.3), calls=%async_computation.3 | async-start | bytes 1048576 | tf_op jit(solution)/shard_map/all_to_all | solution.py:114
  106.0 1.1 shard_map.47
  107.1 15.0 %all-to-all-done.3.parts = bf16[16,32,512]{2,1,0:T(8,128)(2,1)S(1)} async-done(((bf16[16,32,512]{2,1,0:T(8,128)(2,1)}), bf16[16,32,512]{2,1,0:T(8,128)(2,1)S(1)}, u32[]{:S(2)}, u32[]{:S(2)}) %all-to-all-start.3) | async-done | bytes 524320 | tf_op jit(solution)/shard_map/all_to_all | solution.py:114
  122.1 7.5 %all-to-all-start.5 = ((bf16[16,32,896]{2,1,0:T(8,128)(2,1)}), bf16[16,32,896]{2,1,0:T(8,128)(2,1)S(1)}, u32[]{:S(2)}, u32[]{:S(2)}) async-start(bf16[16,32,896]{2,1,0:T(8,128)(2,1)} %shard_map.47), calls=%async_computation.5 | async-start | bytes 1835008 | tf_op jit(solution)/shard_map/all_to_all | solution.py:118
  129.7 0.9 shard_map.48
  130.6 21.8 %all-to-all-done.5 = bf16[16,32,896]{2,1,0:T(8,128)(2,1)S(1)} async-done(((bf16[16,32,896]{2,1,0:T(8,128)(2,1)}), bf16[16,32,896]{2,1,0:T(8,128)(2,1)S(1)}, u32[]{:S(2)}, u32[]{:S(2)}) %all-to-all-start.5) | async-done | bytes 917536 | tf_op jit(solution)/shard_map/all_to_all | solution.py:118
  152.3 7.7 %all-to-all-start.4 = ((bf16[32,32,256]{2,1,0:T(8,128)(2,1)}), bf16[32,32,256]{2,1,0:T(8,128)(2,1)S(1)}, u32[]{:S(2)}, u32[]{:S(2)}) async-start(bf16[32,32,256]{2,1,0:T(8,128)(2,1)} %shard_map.48), calls=%async_computation.4 | async-start | bytes 1048576 | tf_op jit(solution)/shard_map/all_to_all | solution.py:121
  160.1 2.1 %collective-permute-start.5 = (bf16[512,896]{1,0:T(8,128)(2,1)S(1)}, bf16[512,896]{1,0:T(8,128)(2,1)S(1)}, u32[]{:S(2)}, u32[]{:S(2)}) collective-permute-start(bf16[512,896]{1,0:T(8,128)(2,1)S(1)} %bitcast.23), channel_id=1, source_target_pairs={{0,16},{16,0},{1,17},{17,1},{2,18},{18,2},{3,19},{19,3},{4,20},{20... | collective-permute-start | bytes 2752520 | tf_op jit(solution)/shard_map/ppermute | solution.py:33
  162.2 15.8 %all-to-all-done.4 = bf16[32,32,256]{2,1,0:T(8,128)(2,1)S(1)} async-done(((bf16[32,32,256]{2,1,0:T(8,128)(2,1)}), bf16[32,32,256]{2,1,0:T(8,128)(2,1)S(1)}, u32[]{:S(2)}, u32[]{:S(2)}) %all-to-all-start.4) | async-done | bytes 524320 | tf_op jit(solution)/shard_map/all_to_all | solution.py:121
  178.1 0.0 collective-permute-done.5.act_theirs
  178.1 1.7 shard_map.49
  (2 shorter events, 0.1 us)
Async XLA Ops:
  0.0 47.0 %copy-start = (bf16[896,896]{1,0:T(8,128)(2,1)S(1)}, bf16[896,896]{1,0:T(8,128)(2,1)}, u32[]{:S(2)}) copy-start(bf16[896,896]{1,0:T(8,128)(2,1)} %param.7) | copy-start | bytes 4816900
  0.0 46.9 %collective-permute-start.3 = (bf16[896,896]{1,0:T(8,128)(2,1)}, bf16[896,896]{1,0:T(8,128)(2,1)}, u32[]{:S(2)}, u32[]{:S(2)}) collective-permute-start(bf16[896,896]{1,0:T(8,128)(2,1)} %param.7), channel_id=1, source_target_pairs={{0,16},{16,0},{1,17},{17,1},{2,18},{18,2},{3,19},{19,3},{4,20},{20... | collective-permute-start | bytes 4816904 | tf_op jit(solution)/shard_map/ppermute | solution.py:33
  24.8 46.9 %all-to-all-start.1 = ((bf16[16,32,512]{2,1,0:T(8,128)(2,1)}), bf16[16,32,512]{2,1,0:T(8,128)(2,1)}, u32[]{:S(2)}, u32[]{:S(2)}) async-start(bf16[16,32,512]{2,1,0:T(8,128)(2,1)} %broadcast_in_dim.15), calls=%async_computation.1 | async-start | bytes 1048576 | tf_op jit(solution)/shard_map/all_to_all | solution.py:100
  37.3 13.3 %collective-permute-start = (bf16[8,32,896]{2,1,0:T(8,128)(2,1)S(1)}, bf16[8,32,896]{2,1,0:T(8,128)(2,1)S(1)}, u32[]{:S(2)}, u32[]{:S(2)}) collective-permute-start(bf16[8,32,896]{2,1,0:T(8,128)(2,1)S(1)} %all_to_all.30.refs_0_), channel_id=1, source_target_pairs={{0,4},{4,0},{8,12},{12,8},{1,5},{5,1},{9,13},{13,9},{2,6},{6,2},{1... | collective-permute-start | bytes 1376264 | tf_op jit(solution)/shard_map/ppermute | solution.py:33
  40.5 22.2 %collective-permute-start.1 = (bf16[8,32,896]{2,1,0:T(8,128)(2,1)S(1)}, bf16[8,32,896]{2,1,0:T(8,128)(2,1)S(1)}, u32[]{:S(2)}, u32[]{:S(2)}) collective-permute-start(bf16[8,32,896]{2,1,0:T(8,128)(2,1)S(1)} %all_to_all.30.refs_0_), channel_id=1, source_target_pairs={{0,8},{4,12},{8,0},{12,4},{1,9},{5,13},{9,1},{13,5},{2,10},{6,14},... | collective-permute-start | bytes 1376264 | tf_op jit(solution)/shard_map/ppermute | solution.py:33
  44.8 23.7 %collective-permute-start.2 = (bf16[8,32,896]{2,1,0:T(8,128)(2,1)S(1)}, bf16[8,32,896]{2,1,0:T(8,128)(2,1)S(1)}, u32[]{:S(2)}, u32[]{:S(2)}) collective-permute-start(bf16[8,32,896]{2,1,0:T(8,128)(2,1)S(1)} %all_to_all.30.refs_0_), channel_id=1, source_target_pairs={{0,12},{4,8},{8,4},{12,0},{1,13},{5,9},{9,5},{13,1},{2,14},{6,10},... | collective-permute-start | bytes 1376264 | tf_op jit(solution)/shard_map/ppermute | solution.py:33
  71.7 7.7 %copy-start.1 = (bf16[512,256]{1,0:T(8,128)(2,1)S(1)}, bf16[512,256]{1,0:T(8,128)(2,1)}, u32[]{:S(2)}) copy-start(bf16[512,256]{1,0:T(8,128)(2,1)} %param.6) | copy-start | bytes 786436
  71.7 30.8 %all-to-all-start.2 = ((bf16[16,32,896]{2,1,0:T(8,128)(2,1)}), bf16[16,32,896]{2,1,0:T(8,128)(2,1)S(1)}, u32[]{:S(2)}, u32[]{:S(2)}) async-start(bf16[16,32,896]{2,1,0:T(8,128)(2,1)} %shard_map.46), calls=%async_computation.2 | async-start | bytes 1835008 | tf_op jit(solution)/shard_map/all_to_all | solution.py:110
  79.4 5.8 %collective-permute-start.4 = (bf16[512,256]{1,0:T(8,128)(2,1)S(1)}, bf16[512,256]{1,0:T(8,128)(2,1)S(1)}, u32[]{:S(2)}, u32[]{:S(2)}) collective-permute-start(bf16[512,256]{1,0:T(8,128)(2,1)S(1)} %copy-done.1), channel_id=1, source_target_pairs={{0,16},{16,0},{1,17},{17,1},{2,18},{18,2},{3,19},{19,3},{4,20},{20... | collective-permute-start | bytes 786440 | tf_op jit(solution)/shard_map/ppermute | solution.py:33
  102.5 19.7 %all-to-all-start.3 = ((bf16[16,32,512]{2,1,0:T(8,128)(2,1)}), bf16[16,32,512]{2,1,0:T(8,128)(2,1)S(1)}, u32[]{:S(2)}, u32[]{:S(2)}) async-start(bf16[16,32,512]{2,1,0:T(8,128)(2,1)} %bitcast.3), calls=%async_computation.3 | async-start | bytes 1048576 | tf_op jit(solution)/shard_map/all_to_all | solution.py:114
  122.1 30.2 %all-to-all-start.5 = ((bf16[16,32,896]{2,1,0:T(8,128)(2,1)}), bf16[16,32,896]{2,1,0:T(8,128)(2,1)S(1)}, u32[]{:S(2)}, u32[]{:S(2)}) async-start(bf16[16,32,896]{2,1,0:T(8,128)(2,1)} %shard_map.47), calls=%async_computation.5 | async-start | bytes 1835008 | tf_op jit(solution)/shard_map/all_to_all | solution.py:118
  152.3 25.7 %all-to-all-start.4 = ((bf16[32,32,256]{2,1,0:T(8,128)(2,1)}), bf16[32,32,256]{2,1,0:T(8,128)(2,1)S(1)}, u32[]{:S(2)}, u32[]{:S(2)}) async-start(bf16[32,32,256]{2,1,0:T(8,128)(2,1)} %shard_map.48), calls=%async_computation.4 | async-start | bytes 1048576 | tf_op jit(solution)/shard_map/all_to_all | solution.py:121
  160.1 18.0 %collective-permute-start.5 = (bf16[512,896]{1,0:T(8,128)(2,1)S(1)}, bf16[512,896]{1,0:T(8,128)(2,1)S(1)}, u32[]{:S(2)}, u32[]{:S(2)}) collective-permute-start(bf16[512,896]{1,0:T(8,128)(2,1)S(1)} %bitcast.23), channel_id=1, source_target_pairs={{0,16},{16,0},{1,17},{17,1},{2,18},{18,2},{3,19},{19,3},{4,20},{20... | collective-permute-start | bytes 2752520 | tf_op jit(solution)/shard_map/ppermute | solution.py:33

commit v3 on v2

v3 whole, which is shorter than its diff:
```python
import jax
import jax.numpy as jnp
from jax import lax
from jax.experimental import pallas as pl
from jax.experimental.pallas import tpu as pltpu
from jax.sharding import Mesh, PartitionSpec as P

SEQS = 2
SEQ_LEN = 512
OUT = ("z", "ylo", "core")
INP = ("x", "yhi")
CHIPS = ("z", "ylo")
BF16 = jnp.bfloat16
F32 = jnp.float32
VMEM = pl.BlockSpec(memory_space=pltpu.VMEM)


def kernel_call(body, shapes, args, flops=0):
    moved = sum(a.size * a.dtype.itemsize for a in args) + sum(s.size * s.dtype.itemsize for s in shapes)
    many = len(shapes) > 1
    return pl.pallas_call(
        body,
        out_shape=shapes if many else shapes[0],
        in_specs=[VMEM] * len(args),
        out_specs=[VMEM] * len(shapes) if many else VMEM,
        compiler_params=pltpu.CompilerParams(vmem_limit_bytes=40 * 2**20),
        cost_estimate=pl.CostEstimate(flops=flops, bytes_accessed=moved, transcendentals=0),
    )(*args)


def swap(value, axis, flip):
    size = lax.axis_size(axis)
    return lax.ppermute(value, axis, [(s, s ^ flip) for s in range(size)])


def dot_kernel(act0, act1, low2, high2, act3, basis0, basis1, out, done):
    features = basis0.shape[0]
    blocks, block = out.shape[0], out.shape[1]
    each = blocks // 4
    first = [act0[:each], act1[:each], low2[...], act3[:each]]
    second = [act0[each:], act1[each:], high2[...], act3[each:]]
    total = 0.0
    for pieces, basis in ((first, basis0), (second, basis1)):
        rows = jnp.concatenate(pieces).reshape(blocks * block, features)
        total += jnp.dot(rows, basis[...], preferred_element_type=F32)
    out[...] = total.astype(BF16).reshape(out.shape)
    done[...] = jnp.zeros_like(done)


def grad_dot_kernel(done, rows, own, other, out):
    columns = own.shape[1]
    out[:, :columns] = jnp.dot(rows[...], own[...], preferred_element_type=F32)
    out[:, columns:] = jnp.dot(rows[...], other[...], preferred_element_type=F32)


def sum_kernel(parts, out):
    total = parts[0].astype(F32)
    for index in range(1, parts.shape[0]):
        total += parts[index].astype(F32)
    out[...] = total.astype(BF16)


def square_kernel(grad_mine, grad_theirs, act_mine, act_theirs, out):
    half = act_mine.shape[0] // SEQS
    total = 0.0
    for seq in range(SEQS):
        rows = slice(seq * half, (seq + 1) * half)
        contract = (((0,), (0,)), ((), ()))
        rotated = lax.dot_general(grad_mine[rows, :], act_mine[rows, :], contract, preferred_element_type=F32)
        rotated += lax.dot_general(grad_theirs[rows, :], act_theirs[rows, :], contract, preferred_element_type=F32)
        total = total + rotated * rotated
    out[...] = total * (1.0 / (SEQS * SEQ_LEN))


def both(index, axis, own):
    other = swap(own, axis, 1)
    return jnp.where(index == 0, own, other), jnp.where(index == 0, other, own)


def shards(grads, acts, grad_basis, act_basis):
    core, ylo, x = lax.axis_index("core"), lax.axis_index("ylo"), lax.axis_index("x")
    half, features = acts.shape[0] // 2, acts.shape[1]
    tokens, eig = 16 * half, act_basis.shape[1]
    columns = grad_basis.shape[1]

    copies = jnp.broadcast_to(acts.reshape(2, 1, half, features), (2, 4, half, features))
    act0 = lax.all_to_all(copies.reshape(8, half, features), ("core", "yhi"), 0, 0, tiled=True)
    act_basis0, act_basis1 = both(core, "core", act_basis)
    grad_basis_other = swap(grad_basis, "core", 1)
    grad_rows = lax.all_gather(lax.all_gather(grads, "ylo", axis=0, tiled=True), "z", axis=0, tiled=True)

    act1, act3 = swap(act0, "x", 1), swap(act0, "x", 3)
    low2, high2 = swap(act3[:4], "x", 1), swap(act1[4:], "x", 3)

    blocks = jax.ShapeDtypeStruct((16, half, eig), BF16)
    act_partial, done = kernel_call(
        dot_kernel,
        [blocks, jax.ShapeDtypeStruct((8, 128), F32)],
        [act0, act1, low2, high2, act3, act_basis0, act_basis1],
        flops=2 * tokens * 2 * features * eig,
    )
    act_parts = lax.all_to_all(act_partial, CHIPS, 0, 0, tiled=True)

    grad_partial = kernel_call(
        grad_dot_kernel,
        [jax.ShapeDtypeStruct((tokens, 2 * columns), F32)],
        [done, grad_rows, grad_basis, grad_basis_other],
        flops=2 * tokens * grads.shape[1] * 2 * columns,
    )
    grad_sum = lax.psum_scatter(grad_partial, "x", scatter_dimension=0, tiled=True)
    grad_sum = lax.psum_scatter(grad_sum, "yhi", scatter_dimension=0, tiled=True).astype(BF16)

    act_sum = kernel_call(sum_kernel, [jax.ShapeDtypeStruct((half, eig), BF16)], [act_parts])
    act_pair = jnp.concatenate(both(ylo, "ylo", act_sum))
    act_mine = lax.all_gather(act_pair, "z", axis=0, tiled=True)

    grad_all = lax.all_gather(lax.all_gather(grad_sum, "yhi", axis=0, tiled=True), "x", axis=0, tiled=True)
    grad_all = grad_all.reshape(4, tokens // 4, 2 * columns)
    grad_all = jnp.concatenate([grad_all[x ^ flip] for flip in range(4)])
    grad_mine, grad_theirs = grad_all[:, :columns], swap(grad_all[:, columns:], "core", 1)
    act_theirs = swap(act_mine, "core", 1)

    return kernel_call(
        square_kernel,
        [jax.ShapeDtypeStruct((columns, eig), F32)],
        [grad_mine, grad_theirs, act_mine, act_theirs],
        flops=2 * 2 * tokens * columns * eig,
    )


def solution(mesh):
    split = Mesh(mesh.devices.reshape(8, 2, 2, 4, 4), OUT + INP)
    return jax.shard_map(
        shards,
        mesh=split,
        in_specs=(P(OUT, INP), P(INP, OUT), P(INP, OUT), P(OUT, INP)),
        out_specs=P(OUT, INP),
        check_vma=False,
    )
```

time: 181 us -> 191 us (1.055)
  the two profiles are of different devices: /device:TPU:9 before, /device:TPU:1 now
where the time goes in v3:
time: 191 us; the launch traced here: 190 us
  blocking collectives  111 us (58%)
  starting transfers between devices  49.9 us (26%)
  between operations  13.6 us (7%)
  waiting for transfers between devices  7.1 us (4%)
  Pallas kernels  5.46 us (3%)
  other arithmetic  2.64 us (1%)
    ppermute x9, starting transfers between devices, swap(): return lax.ppermute(value, axis, [(s, s ^ flip) for s in range(size)])  49.9 us
    all_gather x1, blocking collectives, shards(): lax.all_gather(lax.all_gather(grads, 'ylo', axis=0, tiled=True), 'z', axi...  25.8 us
    all_gather x1, blocking collectives, shards(): act_mine = lax.all_gather(act_pair, 'z', axis=0, tiled=True)  21.9 us
    all_to_all x1, blocking collectives, shards(): act_parts = lax.all_to_all(act_partial, CHIPS, 0, 0, tiled=True)  19.9 us
    all_to_all x1, blocking collectives, shards(): lax.all_to_all(copies.reshape(8, half, features), ('core', 'yhi'), 0, 0,...  16.8 us
    all_gather x1, blocking collectives, shards(): lax.all_gather(lax.all_gather(grad_sum, 'yhi', axis=0, tiled=True), 'x',...  11.3 us
    all_gather x1, blocking collectives, shards(): lax.all_gather(grad_sum, 'yhi', axis=0, tiled=True)  10.9 us
    ppermute x9, waiting for transfers between devices, swap(): return lax.ppermute(value, axis, [(s, s ^ flip) for s in range(size)])  6.43 us
  transfers between devices with their start and end apart: 11, of which 4 were waited for; matrix products, arithmetic and copies ran while one was open for 2% of the time, Pallas kernels for 1%

profile of v3, /device:TPU:1, one launch (start us, length us, event | category | flops | bytes accessed | tf_op | source)
XLA Modules:
  0.0 190.4 jit_solution(2287430758606846751)
XLA Ops:
  6.5 0.0 copy-start.1
  6.5 0.0 reduce-scatter.3.cloned.1.call-start
  6.5 8.9 %collective-permute-start.4 = (bf16[896,896]{1,0:T(8,128)(2,1)}, bf16[896,896]{1,0:T(8,128)(2,1)}, u32[]{:S(2)}, u32[]{:S(2)}) collective-permute-start(bf16[896,896]{1,0:T(8,128)(2,1)} %param.7), channel_id=1, source_target_pairs={{0,16},{16,0},{1,17},{17,1},{2,18},{18,2},{3,19},{19,3},{4,20},{20... | collective-permute-start | bytes 4816904 | tf_op jit(solution)/shard_map/ppermute | solution.py:33
  15.5 0.9 broadcast_in_dim.8
  16.4 16.8 %all_to_all.10.act0 = bf16[8,32,896]{2,1,0:T(8,128)(2,1)S(1)} all-to-all(bf16[8,32,896]{2,1,0:T(8,128)(2,1)S(1)} %bitcast.12), channel_id=1, replica_groups=mesh['z'=8,'ylo'=2,'core'=2,'x'=4,'yhi'=4] {'core','yhi'}, dimensions={0} | all-to-all | bytes 917504 | tf_op jit(solution)/shard_map/all_to_all | solution.py:87
  33.2 4.0 %collective-permute-start.1 = (bf16[8,32,896]{2,1,0:T(8,128)(2,1)S(1)}, bf16[8,32,896]{2,1,0:T(8,128)(2,1)S(1)}, u32[]{:S(2)}, u32[]{:S(2)}) collective-permute-start(bf16[8,32,896]{2,1,0:T(8,128)(2,1)S(1)} %all_to_all.10.act0), channel_id=1, source_target_pairs={{0,12},{4,8},{8,4},{12,0},{1,13},{5,9},{9,5},{13,1},{2,14},{6,10},... | collective-permute-start | bytes 1376264 | tf_op jit(solution)/shard_map/ppermute | solution.py:33
  37.3 1.9 %collective-permute-start = (bf16[8,32,896]{2,1,0:T(8,128)(2,1)S(1)}, bf16[8,32,896]{2,1,0:T(8,128)(2,1)S(1)}, u32[]{:S(2)}, u32[]{:S(2)}) collective-permute-start(bf16[8,32,896]{2,1,0:T(8,128)(2,1)S(1)} %all_to_all.10.act0), channel_id=1, source_target_pairs={{0,4},{4,0},{8,12},{12,8},{1,5},{5,1},{9,13},{13,9},{2,6},{6,2},{1... | collective-permute-start | bytes 1376264 | tf_op jit(solution)/shard_map/ppermute | solution.py:33
  39.2 2.6 %collective-permute-start.5 = (bf16[512,256]{1,0:T(8,128)(2,1)}, bf16[512,256]{1,0:T(8,128)(2,1)S(1)}, u32[]{:S(2)}, u32[]{:S(2)}) collective-permute-start(bf16[512,256]{1,0:T(8,128)(2,1)} %own.1), channel_id=1, source_target_pairs={{0,16},{16,0},{1,17},{17,1},{2,18},{18,2},{3,19},{19,3},{4,20},{20... | collective-permute-start | bytes 786440 | tf_op jit(solution)/shard_map/ppermute | solution.py:33
  41.8 3.9 %all_gather.15 = bf16[64,512]{1,0:T(8,128)(2,1)S(1)} all-gather(bf16[32,512]{1,0:T(8,128)(2,1)} %param.4), channel_id=1, replica_groups=mesh['z'=8,'ylo'=2,'core'=2,'x'=4,'yhi'=4] {'ylo'}, dimensions={0}, use_global_device_ids=true | all-gather | bytes 98304 | tf_op jit(solution)/shard_map/all_gather | solution.py:90
  45.7 25.8 %all_gather.16.rows = bf16[512,512]{1,0:T(8,128)(2,1)S(1)} all-gather(bf16[64,512]{1,0:T(8,128)(2,1)S(1)} %all_gather.15), channel_id=1, replica_groups=mesh['z'=8,'ylo'=2,'core'=2,'x'=4,'yhi'=4] {'z'}, dimensions={0}, use_global_device_ids=true | all-gather | bytes 589824 | tf_op jit(solution)/shard_map/all_gather | solution.py:90
  71.6 0.0 collective-permute-done.1.act3
  71.6 3.4 %collective-permute-start.2 = (bf16[4,32,896]{2,1,0:T(8,128)(2,1)S(1)}, bf16[4,32,896]{2,1,0:T(8,128)(2,1)S(1)}, u32[]{:S(2)}, u32[]{:S(2)}) collective-permute-start(bf16[4,32,896]{2,1,0:T(8,128)(2,1)S(1)} %slice.16), channel_id=1, source_target_pairs={{0,4},{4,0},{8,12},{12,8},{1,5},{5,1},{9,13},{13,9},{2,6},{6,2},{1... | collective-permute-start | bytes 688136 | tf_op jit(solution)/shard_map/ppermute | solution.py:33
  75.0 0.0 collective-permute-done.act1
  75.1 2.1 %collective-permute-start.3 = (bf16[4,32,896]{2,1,0:T(8,128)(2,1)S(1)}, bf16[4,32,896]{2,1,0:T(8,128)(2,1)S(1)}, u32[]{:S(2)}, u32[]{:S(2)}) collective-permute-start(bf16[4,32,896]{2,1,0:T(8,128)(2,1)S(1)} %slice.17), channel_id=1, source_target_pairs={{0,12},{4,8},{8,4},{12,0},{1,13},{5,9},{9,5},{13,1},{2,14},{6,10},... | collective-permute-start | bytes 688136 | tf_op jit(solution)/shard_map/ppermute | solution.py:33
  77.2 0.0 collective-permute-done.4
  77.2 0.0 copy-done.1
  77.2 1.7 broadcast_select_fusion
  78.9 0.0 collective-permute-done.2.low2
  78.9 4.1 %collective-permute-done.3.high2 = bf16[4,32,896]{2,1,0:T(8,128)(2,1)S(1)} collective-permute-done((bf16[4,32,896]{2,1,0:T(8,128)(2,1)S(1)}, bf16[4,32,896]{2,1,0:T(8,128)(2,1)S(1)}, u32[]{:S(2)}, u32[]{:S(2)}) %collective-permute-start.3) | collective-permute-done | bytes 229408 | tf_op jit(solution)/shard_map/ppermute | solution.py:33
  83.0 0.0 copy-start
  83.0 2.3 %shard_map.46 = (bf16[16,32,896]{2,1,0:T(8,128)(2,1)S(1)}, f32[8,128]{1,0:T(8,128)S(1)}) custom-call(bf16[8,32,896]{2,1,0:T(8,128)(2,1)S(1)} %all_to_all.10.act0, bf16[8,32,896]{2,1,0:T(8,128)(2,1)S(1)} %collective-permute-done.act1, bf16[4,32,896]{2,1,0:T(8,128)(2,1)S(1)} %collective-permute-done.2.low2, ...), custom_call_target="tpu_custom_call" | custom-call | flops 1644167168 | bytes 5967872 | tf_op jit(solution)/shard_map/pallas_call | solution.py:21
  85.3 0.0 collective-permute-done.5.other
  85.3 0.0 copy-done
  85.3 1.4 shard_map.47
  86.7 0.0 reduce-scatter.3.cloned.1.call-update
  86.8 0.0 reduce-scatter.5.cloned.1.call-start
  86.8 19.9 %all_to_all.11.parts = bf16[16,32,896]{2,1,0:T(8,128)(2,1)S(1)} all-to-all(bf16[16,32,896]{2,1,0:T(8,128)(2,1)S(1)} %get-tuple-element.8), channel_id=1, replica_groups=mesh['z'=8,'ylo'=2,'core'=2,'x'=4,'yhi'=4] {'z','ylo'}, dimensions={0} | all-to-all | bytes 1835008 | tf_op jit(solution)/shard_map/all_to_all | solution.py:102
  106.8 0.1 shard_map.48
  106.9 6.8 %collective-permute-start.7 = (bf16[32,896]{1,0:T(8,128)(2,1)S(1)}, bf16[32,896]{1,0:T(8,128)(2,1)S(1)}, u32[]{:S(2)}, u32[]{:S(2)}) collective-permute-start(bf16[32,896]{1,0:T(8,128)(2,1)S(1)} %shard_map.48), channel_id=1, source_target_pairs={{0,32},{32,0},{1,33},{33,1},{2,34},{34,2},{3,35},{35,3},{4,36},{36... | collective-permute-start | bytes 172040 | tf_op jit(solution)/shard_map/ppermute | solution.py:33
  113.7 0.6 reduce-scatter.3.cloned.1.call-done
  114.3 0.0 reduce-scatter.5.cloned.1.call-update
  114.3 1.2 collective-permute-done.7
  115.5 21.9 %all_gather.19.act_mine = bf16[512,896]{1,0:T(8,128)(2,1)S(1)} all-gather(bf16[64,896]{1,0:T(8,128)(2,1)S(1)} %pad_maximum_fusion.1), channel_id=1, replica_groups=mesh['z'=8,'ylo'=2,'core'=2,'x'=4,'yhi'=4] {'z'}, dimensions={0}, use_global_device_ids=true | all-gather | bytes 1032192 | tf_op jit(solution)/shard_map/all_gather | solution.py:115
  137.5 13.8 %collective-permute-start.8 = (bf16[512,896]{1,0:T(8,128)(2,1)S(1)}, bf16[512,896]{1,0:T(8,128)(2,1)S(1)}, u32[]{:S(2)}, u32[]{:S(2)}) collective-permute-start(bf16[512,896]{1,0:T(8,128)(2,1)S(1)} %all_gather.19.act_mine), channel_id=1, source_target_pairs={{0,16},{16,0},{1,17},{17,1},{2,18},{18,2},{3,19},{19,3},{4,20},{20... | collective-permute-start | bytes 2752520 | tf_op jit(solution)/shard_map/ppermute | solution.py:33
  151.3 0.0 reduce-scatter.5.cloned.1.call-done
  151.3 0.8 convert_element_type.3
  152.2 10.9 %all_gather.17 = bf16[128,512]{1,0:T(8,128)(2,1)S(1)} all-gather(bf16[32,512]{1,0:T(8,128)(2,1)S(1)} %convert_element_type.3), channel_id=1, replica_groups=mesh['z'=8,'ylo'=2,'core'=2,'x'=4,'yhi'=4] {'yhi'}, dimensions={0}, use_global_device_ids=true | all-gather | bytes 163840 | tf_op jit(solution)/shard_map/all_gather | solution.py:117
  163.1 11.3 %all_gather.18 = bf16[512,512]{1,0:T(8,128)(2,1)S(1)} all-gather(bf16[128,512]{1,0:T(8,128)(2,1)S(1)} %all_gather.17), channel_id=1, replica_groups=mesh['z'=8,'ylo'=2,'core'=2,'x'=4,'yhi'=4] {'x'}, dimensions={0}, use_global_device_ids=true | all-gather | bytes 655360 | tf_op jit(solution)/shard_map/all_gather | solution.py:117
  174.5 6.3 %collective-permute-start.6 = (bf16[512,256]{1,0:T(8,128)(2,1)S(1)}, bf16[512,256]{1,0:T(8,128)(2,1)S(1)}, u32[]{:S(2)}, u32[]{:S(2)}) collective-permute-start(bf16[512,256]{1,0:T(8,128)(2,1)S(1)} %get-tuple-element.11), channel_id=1, source_target_pairs={{0,16},{16,0},{1,17},{17,1},{2,18},{18,2},{3,19},{19,3},{4,20},{20... | collective-permute-start | bytes 786440 | tf_op jit(solution)/shard_map/ppermute | solution.py:33
  180.8 0.0 collective-permute-done.8.act_theirs
  180.8 1.1 collective-permute-done.6.grad_theirs
  181.9 1.7 shard_map.49
  (7 shorter events, 0.2 us)
Async XLA Ops:
  6.5 70.7 %copy-start.1 = (bf16[896,896]{1,0:T(8,128)(2,1)S(1)}, bf16[896,896]{1,0:T(8,128)(2,1)}, u32[]{:S(2)}) copy-start(bf16[896,896]{1,0:T(8,128)(2,1)} %param.7) | copy-start | bytes 4816900
  6.5 107.8 %reduce-scatter.3.cloned.1.call-start = ((), (), s32[]{:S(2)}) async-start(), calls=%async_computation.4 | async-start | bytes 1310720 | tf_op jit(solution)/shard_map/reduce_scatter | solution.py:110
  6.5 70.6 %collective-permute-start.4 = (bf16[896,896]{1,0:T(8,128)(2,1)}, bf16[896,896]{1,0:T(8,128)(2,1)}, u32[]{:S(2)}, u32[]{:S(2)}) collective-permute-start(bf16[896,896]{1,0:T(8,128)(2,1)} %param.7), channel_id=1, source_target_pairs={{0,16},{16,0},{1,17},{17,1},{2,18},{18,2},{3,19},{19,3},{4,20},{20... | collective-permute-start | bytes 4816904 | tf_op jit(solution)/shard_map/ppermute | solution.py:33
  33.2 38.3 %collective-permute-start.1 = (bf16[8,32,896]{2,1,0:T(8,128)(2,1)S(1)}, bf16[8,32,896]{2,1,0:T(8,128)(2,1)S(1)}, u32[]{:S(2)}, u32[]{:S(2)}) collective-permute-start(bf16[8,32,896]{2,1,0:T(8,128)(2,1)S(1)} %all_to_all.10.act0), channel_id=1, source_target_pairs={{0,12},{4,8},{8,4},{12,0},{1,13},{5,9},{9,5},{13,1},{2,14},{6,10},... | collective-permute-start | bytes 1376264 | tf_op jit(solution)/shard_map/ppermute | solution.py:33
  37.3 37.8 %collective-permute-start = (bf16[8,32,896]{2,1,0:T(8,128)(2,1)S(1)}, bf16[8,32,896]{2,1,0:T(8,128)(2,1)S(1)}, u32[]{:S(2)}, u32[]{:S(2)}) collective-permute-start(bf16[8,32,896]{2,1,0:T(8,128)(2,1)S(1)} %all_to_all.10.act0), channel_id=1, source_target_pairs={{0,4},{4,0},{8,12},{12,8},{1,5},{5,1},{9,13},{13,9},{2,6},{6,2},{1... | collective-permute-start | bytes 1376264 | tf_op jit(solution)/shard_map/ppermute | solution.py:33
  39.2 46.1 %collective-permute-start.5 = (bf16[512,256]{1,0:T(8,128)(2,1)}, bf16[512,256]{1,0:T(8,128)(2,1)S(1)}, u32[]{:S(2)}, u32[]{:S(2)}) collective-permute-start(bf16[512,256]{1,0:T(8,128)(2,1)} %own.1), channel_id=1, source_target_pairs={{0,16},{16,0},{1,17},{17,1},{2,18},{18,2},{3,19},{19,3},{4,20},{20... | collective-permute-start | bytes 786440 | tf_op jit(solution)/shard_map/ppermute | solution.py:33
  71.6 7.3 %collective-permute-start.2 = (bf16[4,32,896]{2,1,0:T(8,128)(2,1)S(1)}, bf16[4,32,896]{2,1,0:T(8,128)(2,1)S(1)}, u32[]{:S(2)}, u32[]{:S(2)}) collective-permute-start(bf16[4,32,896]{2,1,0:T(8,128)(2,1)S(1)} %slice.16), channel_id=1, source_target_pairs={{0,4},{4,0},{8,12},{12,8},{1,5},{5,1},{9,13},{13,9},{2,6},{6,2},{1... | collective-permute-start | bytes 688136 | tf_op jit(solution)/shard_map/ppermute | solution.py:33
  75.1 8.0 %collective-permute-start.3 = (bf16[4,32,896]{2,1,0:T(8,128)(2,1)S(1)}, bf16[4,32,896]{2,1,0:T(8,128)(2,1)S(1)}, u32[]{:S(2)}, u32[]{:S(2)}) collective-permute-start(bf16[4,32,896]{2,1,0:T(8,128)(2,1)S(1)} %slice.17), channel_id=1, source_target_pairs={{0,12},{4,8},{8,4},{12,0},{1,13},{5,9},{9,5},{13,1},{2,14},{6,10},... | collective-permute-start | bytes 688136 | tf_op jit(solution)/shard_map/ppermute | solution.py:33
  83.0 2.3 %copy-start = (bf16[512,256]{1,0:T(8,128)(2,1)S(1)}, bf16[512,256]{1,0:T(8,128)(2,1)}, u32[]{:S(2)}) copy-start(bf16[512,256]{1,0:T(8,128)(2,1)} %own.1) | copy-start | bytes 786436
  86.8 64.6 %reduce-scatter.5.cloned.1.call-start = ((), (), s32[]{:S(2)}) async-start(), calls=%async_computation.5 | async-start | bytes 327680 | tf_op jit(solution)/shard_map/reduce_scatter | solution.py:111
  106.9 8.6 %collective-permute-start.7 = (bf16[32,896]{1,0:T(8,128)(2,1)S(1)}, bf16[32,896]{1,0:T(8,128)(2,1)S(1)}, u32[]{:S(2)}, u32[]{:S(2)}) collective-permute-start(bf16[32,896]{1,0:T(8,128)(2,1)S(1)} %shard_map.48), channel_id=1, source_target_pairs={{0,32},{32,0},{1,33},{33,1},{2,34},{34,2},{3,35},{35,3},{4,36},{36... | collective-permute-start | bytes 172040 | tf_op jit(solution)/shard_map/ppermute | solution.py:33
  137.5 43.3 %collective-permute-start.8 = (bf16[512,896]{1,0:T(8,128)(2,1)S(1)}, bf16[512,896]{1,0:T(8,128)(2,1)S(1)}, u32[]{:S(2)}, u32[]{:S(2)}) collective-permute-start(bf16[512,896]{1,0:T(8,128)(2,1)S(1)} %all_gather.19.act_mine), channel_id=1, source_target_pairs={{0,16},{16,0},{1,17},{17,1},{2,18},{18,2},{3,19},{19,3},{4,20},{20... | collective-permute-start | bytes 2752520 | tf_op jit(solution)/shard_map/ppermute | solution.py:33
  174.5 7.4 %collective-permute-start.6 = (bf16[512,256]{1,0:T(8,128)(2,1)S(1)}, bf16[512,256]{1,0:T(8,128)(2,1)S(1)}, u32[]{:S(2)}, u32[]{:S(2)}) collective-permute-start(bf16[512,256]{1,0:T(8,128)(2,1)S(1)} %get-tuple-element.11), channel_id=1, source_target_pairs={{0,16},{16,0},{1,17},{17,1},{2,18},{18,2},{3,19},{19,3},{4,20},{20... | collective-permute-start | bytes 786440 | tf_op jit(solution)/shard_map/ppermute | solution.py:33
Sparse Core Ops, SparseCore 0:
  86.9 27.3 reduce-scatter.2
  117.3 27.1 reduce-scatter.4

commit v4 on v1

v4 whole, which is shorter than its diff:
```python
import jax
import jax.numpy as jnp
from jax import lax
from jax.experimental import pallas as pl
from jax.experimental.pallas import tpu as pltpu
from jax.sharding import Mesh, PartitionSpec as P

SEQS = 2
SEQ_LEN = 512
OUT = ("z", "ylo", "core")
INP = ("x", "yhi")
CHIPS = ("z", "ylo")
BF16 = jnp.bfloat16
F32 = jnp.float32
VMEM = pl.BlockSpec(memory_space=pltpu.VMEM)


def kernel_call(body, shapes, args, flops=0):
    moved = sum(a.size * a.dtype.itemsize for a in args) + sum(s.size * s.dtype.itemsize for s in shapes)
    many = len(shapes) > 1
    return pl.pallas_call(
        body,
        out_shape=shapes if many else shapes[0],
        in_specs=[VMEM] * len(args),
        out_specs=[VMEM] * len(shapes) if many else VMEM,
        compiler_params=pltpu.CompilerParams(vmem_limit_bytes=40 * 2**20),
        cost_estimate=pl.CostEstimate(flops=flops, bytes_accessed=moved, transcendentals=0),
    )(*args)


def swap(value, axis, flip):
    size = lax.axis_size(axis)
    return lax.ppermute(value, axis, [(s, s ^ flip) for s in range(size)])


def stack_kernel(*refs):
    blocks, out, done, row = refs[:-2], refs[-2], refs[-1], 0
    for block in blocks:
        out[row:row + block.shape[0], :] = block[...]
        row += block.shape[0]
    done[...] = jnp.zeros_like(done)


def gather_yhi(mine):
    blocks = [mine, swap(mine, "yhi", 1), swap(mine, "yhi", 2), swap(mine, "yhi", 3)]
    rows, columns = mine.shape
    shapes = [jax.ShapeDtypeStruct((4 * rows, columns), mine.dtype), jax.ShapeDtypeStruct((8, 128), F32)]
    return kernel_call(stack_kernel, shapes, blocks)


def act_dot_kernel(act0, act1, low2, high2, act3, own, other, out, done):
    features = own.shape[0]
    rows = jnp.concatenate([act0[...], act1[...], low2[...], high2[...], act3[...]])
    total = jnp.dot(rows[:, :features], own[...], preferred_element_type=F32)
    total += jnp.dot(rows[:, features:], other[...], preferred_element_type=F32)
    out[...] = total.astype(BF16).reshape(out.shape)
    done[...] = jnp.zeros_like(done)


def grad_dot_kernel(done, rows, own, other, out):
    columns = own.shape[1]
    total = jnp.concatenate(
        [jnp.dot(rows[...], basis[...], preferred_element_type=F32) for basis in (own, other)], axis=1
    )
    out[...] = total.astype(BF16).reshape(out.shape)


def sum_parts(parts):
    total = parts[0].astype(F32)
    for index in range(1, parts.shape[0]):
        total += parts[index].astype(F32)
    return total.astype(BF16)


def sum_copies_kernel(parts, out):
    rounded = sum_parts(parts)
    for index in range(out.shape[0]):
        out[index] = rounded


def sum_split_kernel(done, parts, mine, give):
    rounded = sum_parts(parts)
    columns = mine.shape[1]
    mine[...] = rounded[:, :columns]
    give[...] = rounded[:, columns:]


def square_kernel(g0, g1, g2, g3, act_mine, act_theirs, out):
    columns = out.shape[0]
    half = act_mine.shape[0] // SEQS
    grads = (jnp.concatenate([g0[...], g1[...]]), jnp.concatenate([g2[...], g3[...]]))
    total = 0.0
    for seq in range(SEQS):
        rows = slice(seq * half, (seq + 1) * half)
        contract = (((0,), (0,)), ((), ()))
        rotated = lax.dot_general(grads[seq][:, :columns], act_mine[rows, :], contract, preferred_element_type=F32)
        rotated += lax.dot_general(grads[seq][:, columns:], act_theirs[rows, :], contract, preferred_element_type=F32)
        total = total + rotated * rotated
    out[...] = total * (1.0 / (SEQS * SEQ_LEN))


def shards(grads, acts, grad_basis, act_basis):
    core = lax.axis_index("core")
    half, features = acts.shape[0] // 2, acts.shape[1]
    tokens, eig = 16 * half, act_basis.shape[1]
    rows, columns = grads.shape[0], grad_basis.shape[1]

    keep = lax.dynamic_slice_in_dim(acts, core * half, half)
    give = lax.dynamic_slice_in_dim(acts, (1 - core) * half, half)
    act_own = jnp.concatenate([keep, swap(give, "core", 1)], axis=1)
    act_basis_other = swap(act_basis, "core", 1)
    grad_basis_other = swap(grad_basis, "core", 1)

    act0, done = gather_yhi(act_own)
    act1, act3 = swap(act0, "x", 1), swap(act0, "x", 3)
    low2, high2 = swap(act3[:2 * half], "x", 1), swap(act1[2 * half:], "x", 3)

    grad_copies = jnp.broadcast_to(grads[None], (16, *grads.shape))
    grad_rows = lax.all_to_all(grad_copies, CHIPS, 0, 0, tiled=True).reshape(tokens, -1)
    grad_partial = kernel_call(
        grad_dot_kernel,
        [jax.ShapeDtypeStruct((16, rows, 2 * columns), BF16)],
        [done, grad_rows, grad_basis, grad_basis_other],
        flops=2 * tokens * grads.shape[1] * 2 * columns,
    )
    grad_parts = lax.all_to_all(grad_partial, INP, 0, 0, tiled=True)

    blocks = jax.ShapeDtypeStruct((16, half, eig), BF16)
    act_partial, done = kernel_call(
        act_dot_kernel,
        [blocks, jax.ShapeDtypeStruct((8, 128), F32)],
        [act0, act1, low2, high2, act3, act_basis, act_basis_other],
        flops=2 * tokens * 2 * features * eig,
    )
    act_parts = lax.all_to_all(act_partial, CHIPS, 0, 0, tiled=True)

    narrow = jax.ShapeDtypeStruct((rows, columns), BF16)
    grad_mine, grad_give = kernel_call(sum_split_kernel, [narrow, narrow], [done, grad_parts])
    grad_own = jnp.concatenate([grad_mine, swap(grad_give, "core", 1)], axis=1)
    g0, _ = gather_yhi(grad_own)
    act_parts, g0 = lax.optimization_barrier((act_parts, g0))

    act_mine = lax.all_to_all(kernel_call(sum_copies_kernel, [blocks], [act_parts]), CHIPS, 0, 0, tiled=True)
    g1, g2, g3 = swap(g0, "x", 1), swap(g0, "x", 2), swap(g0, "x", 3)
    act_mine, g1, g2, g3 = lax.optimization_barrier((act_mine.reshape(tokens, eig), g1, g2, g3))
    act_theirs = swap(act_mine, "core", 1)

    return kernel_call(
        square_kernel,
        [jax.ShapeDtypeStruct((columns, eig), F32)],
        [g0, g1, g2, g3, act_mine, act_theirs],
        flops=2 * 2 * tokens * columns * eig,
    )


def solution(mesh):
    split = Mesh(mesh.devices.reshape(8, 2, 2, 4, 4), OUT + INP)
    return jax.shard_map(
        shards,
        mesh=split,
        in_specs=(P(OUT, INP), P(INP, OUT), P(INP, OUT), P(OUT, INP)),
        out_specs=P(OUT, INP),
        check_vma=False,
    )
```

time: 176 us -> 158 us (0.90)
  blocking collectives: 29.4 us -> 0 us
  waiting for transfers between devices: 39.2 us -> 51.4 us
  Pallas kernels: 6.63 us -> 9.27 us
  starting transfers between devices: 96.1 us -> 94.3 us
    all_to_all x1 -> x0, blocking collectives: 29.4 us -> none  [gather_chips(): return lax.all_to_all(copies, CHIPS, 0, 0, tiled=True)]
    ppermute x20 -> x18, waiting for transfers between devices: 20.9 us -> 41.8 us  [swap(): return lax.ppermute(value, axis, [(s, s ^ flip) for s in range(size)])]
    ppermute x20 -> x18, starting transfers between devices: 69.9 us -> 59.2 us  [swap(): return lax.ppermute(value, axis, [(s, s ^ flip) for s in range(size)])]
    all_to_all x1, waiting for transfers between devices: 8.36 us -> 0.88 us  [shards(): act_parts = lax.all_to_all(act_partial, CHIPS, 0, 0, tiled=True)]
    all_to_all x2 -> x3, starting transfers between devices: 20.6 us -> 27.1 us  [the longest x1 12 us: shards(): lax.all_to_all(grad_copies, CHIPS, 0, 0, tiled=True).reshape(tokens, -1)]
    pallas_call x6 -> x7, Pallas kernels: 6.63 us -> 9.27 us  [kernel_call(): pl.pallas_call(body, out_shape=shapes if many else shapes[0], in_specs=[V...]
    all_to_all x1, starting transfers between devices: 5.56 us -> 7.94 us  [shards(): act_parts = lax.all_to_all(act_partial, CHIPS, 0, 0, tiled=True)]
    all_to_all x2 -> x3, waiting for transfers between devices: 9.96 us -> 8.74 us  [the longest x1 8.74 us: shards(): lax.all_to_all(kernel_call(sum_copies_kernel, [blocks], [act_parts]), CHI...]
  transfers between devices with their start and end apart: 23 -> 22, of which waited for: 10 -> 13; matrix products, arithmetic and copies ran while one was open for 1% -> 0% of each run, Pallas kernels for 0% -> 4%
where the time goes in v4:
time: 158 us; the launch traced here: 157 us
  starting transfers between devices  94.3 us (60%)
  waiting for transfers between devices  51.4 us (33%)
  Pallas kernels  9.27 us (6%)
  local copies, waits for them, and re-layouts  1.72 us (1%)
    ppermute x18, starting transfers between devices, swap(): return lax.ppermute(value, axis, [(s, s ^ flip) for s in range(size)])  59.2 us
    ppermute x18, waiting for transfers between devices, swap(): return lax.ppermute(value, axis, [(s, s ^ flip) for s in range(size)])  41.8 us
    all_to_all x1, starting transfers between devices, shards(): lax.all_to_all(grad_copies, CHIPS, 0, 0, tiled=True).reshape(tokens, -1)  12 us
    pallas_call x7, Pallas kernels, kernel_call(): pl.pallas_call(body, out_shape=shapes if many else shapes[0], in_specs=[V...  9.27 us
    all_to_all x1, waiting for transfers between devices, shards(): lax.all_to_all(kernel_call(sum_copies_kernel, [blocks], [act_parts]), CHI...  8.74 us
    all_to_all x1, starting transfers between devices, shards(): grad_parts = lax.all_to_all(grad_partial, INP, 0, 0, tiled=True)  8.15 us
    all_to_all x1, starting transfers between devices, shards(): act_parts = lax.all_to_all(act_partial, CHIPS, 0, 0, tiled=True)  7.94 us
    all_to_all x1, starting transfers between devices, shards(): lax.all_to_all(kernel_call(sum_copies_kernel, [blocks], [act_parts]), CHI...  7.01 us
  transfers between devices with their start and end apart: 22, of which 13 were waited for; matrix products, arithmetic and copies ran while one was open for 0% of the time, Pallas kernels for 4%

profile of v4, /device:TPU:1, one launch (start us, length us, event | category | flops | bytes accessed | tf_op | source)
XLA Modules:
  0.0 157.0 jit_solution(8282437164059630539)
XLA Ops:
  0.0 0.0 copy-start.2
  0.0 0.0 copy-start
  0.0 1.7 %broadcast_in_dim.2 = bf16[16,32,512]{2,1,0:T(8,128)(2,1)} broadcast(bf16[32,512]{1,0:T(8,128)(2,1)} %param.4), dimensions={1,2} | broadcast | bytes 557056 | tf_op jit(solution)/shard_map/broadcast_in_dim | solution.py:118
  1.7 12.0 %all-to-all-start.1 = ((bf16[16,32,512]{2,1,0:T(8,128)(2,1)}), bf16[16,32,512]{2,1,0:T(8,128)(2,1)S(1)}, u32[]{:S(2)}, u32[]{:S(2)}) async-start(bf16[16,32,512]{2,1,0:T(8,128)(2,1)} %broadcast_in_dim.2), calls=%async_computation.1 | async-start | bytes 1048576 | tf_op jit(solution)/shard_map/all_to_all | solution.py:119
  13.6 2.9 %collective-permute-start.8 = (bf16[896,896]{1,0:T(8,128)(2,1)}, bf16[896,896]{1,0:T(8,128)(2,1)}, u32[]{:S(2)}, u32[]{:S(2)}) collective-permute-start(bf16[896,896]{1,0:T(8,128)(2,1)} %own.2), channel_id=1, source_target_pairs={{0,16},{16,0},{1,17},{17,1},{2,18},{18,2},{3,19},{19,3},{4,20},{20... | collective-permute-start | bytes 4816904 | tf_op jit(solution)/shard_map/ppermute | solution.py:33
  16.5 0.0 copy-done.2
  16.6 1.9 %collective-permute-start = (bf16[32,896]{1,0:T(8,128)(2,1)S(1)}, bf16[32,896]{1,0:T(8,128)(2,1)S(1)}, u32[]{:S(2)}, u32[]{:S(2)}) collective-permute-start(bf16[32,896]{1,0:T(8,128)(2,1)S(1)} %get-tuple-element.32), channel_id=1, source_target_pairs={{0,16},{16,0},{1,17},{17,1},{2,18},{18,2},{3,19},{19,3},{4,20},{20... | collective-permute-start | bytes 172040 | tf_op jit(solution)/shard_map/ppermute | solution.py:33
  18.5 0.0 copy-done
  18.5 2.4 %collective-permute-start.9 = (bf16[512,256]{1,0:T(8,128)(2,1)S(1)}, bf16[512,256]{1,0:T(8,128)(2,1)S(1)}, u32[]{:S(2)}, u32[]{:S(2)}) collective-permute-start(bf16[512,256]{1,0:T(8,128)(2,1)S(1)} %copy-done), channel_id=1, source_target_pairs={{0,16},{16,0},{1,17},{17,1},{2,18},{18,2},{3,19},{19,3},{4,20},{20... | collective-permute-start | bytes 786440 | tf_op jit(solution)/shard_map/ppermute | solution.py:33
  20.9 0.0 collective-permute-done
  20.9 4.2 %collective-permute-start.1 = (bf16[32,1792]{1,0:T(8,128)(2,1)S(1)}, bf16[32,1792]{1,0:T(8,128)(2,1)S(1)}, u32[]{:S(2)}, u32[]{:S(2)}) collective-permute-start(bf16[32,1792]{1,0:T(8,128)(2,1)S(1)} %pad_maximum_fusion.refs_0_), channel_id=1, source_target_pairs={{0,1},{1,0},{2,3},{3,2},{4,5},{5,4},{6,7},{7,6},{8,9},{9,8},{10,11... | collective-permute-start | bytes 344072 | tf_op jit(solution)/shard_map/ppermute | solution.py:33
  25.2 4.8 %collective-permute-start.2 = (bf16[32,1792]{1,0:T(8,128)(2,1)S(1)}, bf16[32,1792]{1,0:T(8,128)(2,1)S(1)}, u32[]{:S(2)}, u32[]{:S(2)}) collective-permute-start(bf16[32,1792]{1,0:T(8,128)(2,1)S(1)} %pad_maximum_fusion.refs_0_), channel_id=1, source_target_pairs={{0,2},{1,3},{2,0},{3,1},{4,6},{5,7},{6,4},{7,5},{8,10},{9,11},{10,... | collective-permute-start | bytes 344072 | tf_op jit(solution)/shard_map/ppermute | solution.py:33
  29.9 2.4 %collective-permute-start.3 = (bf16[32,1792]{1,0:T(8,128)(2,1)S(1)}, bf16[32,1792]{1,0:T(8,128)(2,1)S(1)}, u32[]{:S(2)}, u32[]{:S(2)}) collective-permute-start(bf16[32,1792]{1,0:T(8,128)(2,1)S(1)} %pad_maximum_fusion.refs_0_), channel_id=1, source_target_pairs={{0,3},{1,2},{2,1},{3,0},{4,7},{5,6},{6,5},{7,4},{8,11},{9,10},{10,... | collective-permute-start | bytes 344072 | tf_op jit(solution)/shard_map/ppermute | solution.py:33
  32.3 0.0 collective-permute-done.1.refs_1_
  32.4 3.1 %collective-permute-done.2.refs_2_ = bf16[32,1792]{1,0:T(8,128)(2,1)S(1)} collective-permute-done((bf16[32,1792]{1,0:T(8,128)(2,1)S(1)}, bf16[32,1792]{1,0:T(8,128)(2,1)S(1)}, u32[]{:S(2)}, u32[]{:S(2)}) %collective-permute-start.2) | collective-permute-done | bytes 114720 | tf_op jit(solution)/shard_map/ppermute | solution.py:33
  35.5 6.0 %collective-permute-done.3.refs_3_ = bf16[32,1792]{1,0:T(8,128)(2,1)S(1)} collective-permute-done((bf16[32,1792]{1,0:T(8,128)(2,1)S(1)}, bf16[32,1792]{1,0:T(8,128)(2,1)S(1)}, u32[]{:S(2)}, u32[]{:S(2)}) %collective-permute-start.3) | collective-permute-done | bytes 114720 | tf_op jit(solution)/shard_map/ppermute | solution.py:33
  41.5 0.0 collective-permute-done.9.other
  41.5 0.0 all-to-all-done.1
  41.6 0.0 copy-start.1
  41.6 1.2 shard_map.48
  42.8 8.2 %all-to-all-start.2 = ((bf16[16,32,512]{2,1,0:T(8,128)(2,1)}), bf16[16,32,512]{2,1,0:T(8,128)(2,1)S(1)}, u32[]{:S(2)}, u32[]{:S(2)}) async-start(bf16[16,32,512]{2,1,0:T(8,128)(2,1)} %shard_map.48), calls=%async_computation.2 | async-start | bytes 1048576 | tf_op jit(solution)/shard_map/all_to_all | solution.py:126
  51.0 4.5 %collective-permute-start.5 = (bf16[128,1792]{1,0:T(8,128)(2,1)S(1)}, bf16[128,1792]{1,0:T(8,128)(2,1)S(1)}, u32[]{:S(2)}, u32[]{:S(2)}) collective-permute-start(bf16[128,1792]{1,0:T(8,128)(2,1)S(1)} %get-tuple-element.18.act0), channel_id=1, source_target_pairs={{0,12},{4,8},{8,4},{12,0},{1,13},{5,9},{9,5},{13,1},{2,14},{6,10},... | collective-permute-start | bytes 1376264 | tf_op jit(solution)/shard_map/ppermute | solution.py:33
  55.5 1.9 %collective-permute-start.4 = (bf16[128,1792]{1,0:T(8,128)(2,1)S(1)}, bf16[128,1792]{1,0:T(8,128)(2,1)S(1)}, u32[]{:S(2)}, u32[]{:S(2)}) collective-permute-start(bf16[128,1792]{1,0:T(8,128)(2,1)S(1)} %get-tuple-element.18.act0), channel_id=1, source_target_pairs={{0,4},{4,0},{8,12},{12,8},{1,5},{5,1},{9,13},{13,9},{2,6},{6,2},{1... | collective-permute-start | bytes 1376264 | tf_op jit(solution)/shard_map/ppermute | solution.py:33
  57.4 13.6 %collective-permute-done.5.act3 = bf16[128,1792]{1,0:T(8,128)(2,1)S(1)} collective-permute-done((bf16[128,1792]{1,0:T(8,128)(2,1)S(1)}, bf16[128,1792]{1,0:T(8,128)(2,1)S(1)}, u32[]{:S(2)}, u32[]{:S(2)}) %collective-permute-start.5) | collective-permute-done | bytes 458784 | tf_op jit(solution)/shard_map/ppermute | solution.py:33
  71.0 1.9 %collective-permute-start.6 = (bf16[64,1792]{1,0:T(8,128)(2,1)S(1)}, bf16[64,1792]{1,0:T(8,128)(2,1)S(1)}, u32[]{:S(2)}, u32[]{:S(2)}) collective-permute-start(bf16[64,1792]{1,0:T(8,128)(2,1)S(1)} %slice.8), channel_id=1, source_target_pairs={{0,4},{4,0},{8,12},{12,8},{1,5},{5,1},{9,13},{13,9},{2,6},{6,2},{1... | collective-permute-start | bytes 688136 | tf_op jit(solution)/shard_map/ppermute | solution.py:33
  72.9 0.0 collective-permute-done.4.act1
  73.0 2.2 %collective-permute-start.7 = (bf16[64,1792]{1,0:T(8,128)(2,1)S(1)}, bf16[64,1792]{1,0:T(8,128)(2,1)S(1)}, u32[]{:S(2)}, u32[]{:S(2)}) collective-permute-start(bf16[64,1792]{1,0:T(8,128)(2,1)S(1)} %slice.9), channel_id=1, source_target_pairs={{0,12},{4,8},{8,4},{12,0},{1,13},{5,9},{9,5},{13,1},{2,14},{6,10},... | collective-permute-start | bytes 688136 | tf_op jit(solution)/shard_map/ppermute | solution.py:33
  75.1 4.3 %collective-permute-done.6.low2 = bf16[64,1792]{1,0:T(8,128)(2,1)S(1)} collective-permute-done((bf16[64,1792]{1,0:T(8,128)(2,1)S(1)}, bf16[64,1792]{1,0:T(8,128)(2,1)S(1)}, u32[]{:S(2)}, u32[]{:S(2)}) %collective-permute-start.6) | collective-permute-done | bytes 229408 | tf_op jit(solution)/shard_map/ppermute | solution.py:33
  79.5 2.8 %collective-permute-done.7.high2 = bf16[64,1792]{1,0:T(8,128)(2,1)S(1)} collective-permute-done((bf16[64,1792]{1,0:T(8,128)(2,1)S(1)}, bf16[64,1792]{1,0:T(8,128)(2,1)S(1)}, u32[]{:S(2)}, u32[]{:S(2)}) %collective-permute-start.7) | collective-permute-done | bytes 229408 | tf_op jit(solution)/shard_map/ppermute | solution.py:33
  82.3 0.0 collective-permute-done.8.other
  82.3 0.0 copy-done.1
  82.3 4.6 %shard_map.47 = (bf16[16,32,896]{2,1,0:T(8,128)(2,1)}, f32[8,128]{1,0:T(8,128)S(1)}) custom-call(bf16[128,1792]{1,0:T(8,128)(2,1)S(1)} %get-tuple-element.18.act0, bf16[128,1792]{1,0:T(8,128)(2,1)S(1)} %collective-permute-done.4.act1, bf16[64,1792]{1,0:T(8,128)(2,1)S(1)} %collective-permute-done.6.low2, bf16[64,1792]{1,0:T(8,128)(2,1)S(1)} %collective-permute-done.7.high2, ...), custom_call_target="tpu_custom_call" | custom-call | flops 1644167168 | bytes 5967872 | tf_op jit(solution)/shard_map/pallas_call | solution.py:21
  86.9 0.0 all-to-all-done.2.parts
  86.9 7.9 %all-to-all-start = ((bf16[16,32,896]{2,1,0:T(8,128)(2,1)}), bf16[16,32,896]{2,1,0:T(8,128)(2,1)S(1)}, u32[]{:S(2)}, u32[]{:S(2)}) async-start(bf16[16,32,896]{2,1,0:T(8,128)(2,1)} %get-tuple-element.19), calls=%async_computation | async-start | bytes 1835008 | tf_op jit(solution)/shard_map/all_to_all | solution.py:135
  94.9 0.1 shard_map.49
  95.0 4.5 %collective-permute-start.10 = (bf16[32,256]{1,0:T(8,128)(2,1)S(1)}, bf16[32,256]{1,0:T(8,128)(2,1)S(1)}, u32[]{:S(2)}, u32[]{:S(2)}) collective-permute-start(bf16[32,256]{1,0:T(8,128)(2,1)S(1)} %get-tuple-element.23), channel_id=1, source_target_pairs={{0,16},{16,0},{1,17},{17,1},{2,18},{18,2},{3,19},{19,3},{4,20},{20... | collective-permute-start | bytes 49160 | tf_op jit(solution)/shard_map/ppermute | solution.py:33
  99.5 0.8 collective-permute-done.10
  100.3 3.0 %collective-permute-start.11 = (bf16[32,512]{1,0:T(8,128)(2,1)S(1)}, bf16[32,512]{1,0:T(8,128)(2,1)S(1)}, u32[]{:S(2)}, u32[]{:S(2)}) collective-permute-start(bf16[32,512]{1,0:T(8,128)(2,1)S(1)} %constant_dynamic-update-slice_fusion.refs_0_), channel_id=1, source_target_pairs={{0,1},{1,0},{2,3},{3,2},{4,5},{5,4},{6,7},{7,6},{8,9},{9,8},{10,11... | collective-permute-start | bytes 98312 | tf_op jit(solution)/shard_map/ppermute | solution.py:33
  103.3 5.8 %collective-permute-start.12 = (bf16[32,512]{1,0:T(8,128)(2,1)S(1)}, bf16[32,512]{1,0:T(8,128)(2,1)S(1)}, u32[]{:S(2)}, u32[]{:S(2)}) collective-permute-start(bf16[32,512]{1,0:T(8,128)(2,1)S(1)} %constant_dynamic-update-slice_fusion.refs_0_), channel_id=1, source_target_pairs={{0,2},{1,3},{2,0},{3,1},{4,6},{5,7},{6,4},{7,5},{8,10},{9,11},{10,... | collective-permute-start | bytes 98312 | tf_op jit(solution)/shard_map/ppermute | solution.py:33
  109.0 2.6 %collective-permute-start.13 = (bf16[32,512]{1,0:T(8,128)(2,1)S(1)}, bf16[32,512]{1,0:T(8,128)(2,1)S(1)}, u32[]{:S(2)}, u32[]{:S(2)}) collective-permute-start(bf16[32,512]{1,0:T(8,128)(2,1)S(1)} %constant_dynamic-update-slice_fusion.refs_0_), channel_id=1, source_target_pairs={{0,3},{1,2},{2,1},{3,0},{4,7},{5,6},{6,5},{7,4},{8,11},{9,10},{10,... | collective-permute-start | bytes 98312 | tf_op jit(solution)/shard_map/ppermute | solution.py:33
  111.7 0.0 collective-permute-done.11.refs_1_
  111.7 0.2 collective-permute-done.12.refs_2_
  111.8 4.3 %collective-permute-done.13.refs_3_ = bf16[32,512]{1,0:T(8,128)(2,1)S(1)} collective-permute-done((bf16[32,512]{1,0:T(8,128)(2,1)S(1)}, bf16[32,512]{1,0:T(8,128)(2,1)S(1)}, u32[]{:S(2)}, u32[]{:S(2)}) %collective-permute-start.13) | collective-permute-done | bytes 32800 | tf_op jit(solution)/shard_map/ppermute | solution.py:33
  116.1 0.6 shard_map.50
  116.7 0.9 all-to-all-done.parts
  117.6 1.1 shard_map.51
  118.6 7.0 %all-to-all-start.3 = ((bf16[16,32,896]{2,1,0:T(8,128)(2,1)}), bf16[16,32,896]{2,1,0:T(8,128)(2,1)S(1)}, u32[]{:S(2)}, u32[]{:S(2)}) async-start(bf16[16,32,896]{2,1,0:T(8,128)(2,1)} %shard_map.51), calls=%async_computation.3 | async-start | bytes 1835008 | tf_op jit(solution)/shard_map/all_to_all | solution.py:143
  125.7 2.2 %collective-permute-start.14 = (bf16[128,512]{1,0:T(8,128)(2,1)S(1)}, bf16[128,512]{1,0:T(8,128)(2,1)S(1)}, u32[]{:S(2)}, u32[]{:S(2)}) collective-permute-start(bf16[128,512]{1,0:T(8,128)(2,1)S(1)} %get-tuple-element.25.g0), channel_id=1, source_target_pairs={{0,4},{4,0},{8,12},{12,8},{1,5},{5,1},{9,13},{13,9},{2,6},{6,2},{1... | collective-permute-start | bytes 393224 | tf_op jit(solution)/shard_map/ppermute | solution.py:33
  127.8 4.4 %collective-permute-start.15 = (bf16[128,512]{1,0:T(8,128)(2,1)S(1)}, bf16[128,512]{1,0:T(8,128)(2,1)S(1)}, u32[]{:S(2)}, u32[]{:S(2)}) collective-permute-start(bf16[128,512]{1,0:T(8,128)(2,1)S(1)} %get-tuple-element.25.g0), channel_id=1, source_target_pairs={{0,8},{4,12},{8,0},{12,4},{1,9},{5,13},{9,1},{13,5},{2,10},{6,14},... | collective-permute-start | bytes 393224 | tf_op jit(solution)/shard_map/ppermute | solution.py:33
  132.2 3.0 %collective-permute-start.16 = (bf16[128,512]{1,0:T(8,128)(2,1)S(1)}, bf16[128,512]{1,0:T(8,128)(2,1)S(1)}, u32[]{:S(2)}, u32[]{:S(2)}) collective-permute-start(bf16[128,512]{1,0:T(8,128)(2,1)S(1)} %get-tuple-element.25.g0), channel_id=1, source_target_pairs={{0,12},{4,8},{8,4},{12,0},{1,13},{5,9},{9,5},{13,1},{2,14},{6,10},... | collective-permute-start | bytes 393224 | tf_op jit(solution)/shard_map/ppermute | solution.py:33
  135.3 0.0 collective-permute-done.14.g1
  135.3 1.0 collective-permute-done.15.g2
  136.3 3.5 %collective-permute-done.16.g3 = bf16[128,512]{1,0:T(8,128)(2,1)S(1)} collective-permute-done((bf16[128,512]{1,0:T(8,128)(2,1)S(1)}, bf16[128,512]{1,0:T(8,128)(2,1)S(1)}, u32[]{:S(2)}, u32[]{:S(2)}) %collective-permute-start.16) | collective-permute-done | bytes 131104 | tf_op jit(solution)/shard_map/ppermute | solution.py:33
  139.8 8.7 %all-to-all-done.3 = bf16[16,32,896]{2,1,0:T(8,128)(2,1)S(1)} async-done(((bf16[16,32,896]{2,1,0:T(8,128)(2,1)}), bf16[16,32,896]{2,1,0:T(8,128)(2,1)S(1)}, u32[]{:S(2)}, u32[]{:S(2)}) %all-to-all-start.3) | async-done | bytes 917536 | tf_op jit(solution)/shard_map/all_to_all | solution.py:143
  148.5 4.7 %collective-permute-start.17 = (bf16[512,896]{1,0:T(8,128)(2,1)S(1)}, bf16[512,896]{1,0:T(8,128)(2,1)S(1)}, u32[]{:S(2)}, u32[]{:S(2)}) collective-permute-start(bf16[512,896]{1,0:T(8,128)(2,1)S(1)} %bitcast.2), channel_id=1, source_target_pairs={{0,16},{16,0},{1,17},{17,1},{2,18},{18,2},{3,19},{19,3},{4,20},{20... | collective-permute-start | bytes 2752520 | tf_op jit(solution)/shard_map/ppermute | solution.py:33
  153.3 2.1 %collective-permute-done.17.act_theirs = bf16[512,896]{1,0:T(8,128)(2,1)S(1)} collective-permute-done((bf16[512,896]{1,0:T(8,128)(2,1)S(1)}, bf16[512,896]{1,0:T(8,128)(2,1)S(1)}, u32[]{:S(2)}, u32[]{:S(2)}) %collective-permute-start.17) | collective-permute-done | bytes 917536 | tf_op jit(solution)/shard_map/ppermute | solution.py:33
  155.4 1.7 %shard_map.52 = f32[256,896]{1,0:T(8,128)} custom-call(bf16[128,512]{1,0:T(8,128)(2,1)S(1)} %get-tuple-element.25.g0, bf16[128,512]{1,0:T(8,128)(2,1)S(1)} %collective-permute-done.14.g1, bf16[128,512]{1,0:T(8,128)(2,1)S(1)} %collective-permute-done.15.g2, bf16[128,512]{1,0:T(8,128)(2,1)S(1)} %collective-permute-done.16.g3, bf16[512,896]{1,0:T(8,128)(2,1)S(1)} %bitcast.3, ...), custom_call_target="tpu_custom_call" | custom-call | flops 469762048 | bytes 3276800 | tf_op jit(solution)/shard_map/pallas_call | solution.py:21
  (7 shorter events, 0.1 us)
Async XLA Ops:
  0.0 16.5 %copy-start.2 = (bf16[64,896]{1,0:T(8,128)(2,1)S(1)}, bf16[64,896]{1,0:T(8,128)(2,1)}, u32[]{:S(2)}) copy-start(bf16[64,896]{1,0:T(8,128)(2,1)} %param.5) | copy-start | bytes 344068
  0.0 18.5 %copy-start = (bf16[512,256]{1,0:T(8,128)(2,1)S(1)}, bf16[512,256]{1,0:T(8,128)(2,1)}, u32[]{:S(2)}) copy-start(bf16[512,256]{1,0:T(8,128)(2,1)} %own.3) | copy-start | bytes 786436
  1.7 39.9 %all-to-all-start.1 = ((bf16[16,32,512]{2,1,0:T(8,128)(2,1)}), bf16[16,32,512]{2,1,0:T(8,128)(2,1)S(1)}, u32[]{:S(2)}, u32[]{:S(2)}) async-start(bf16[16,32,512]{2,1,0:T(8,128)(2,1)} %broadcast_in_dim.2), calls=%async_computation.1 | async-start | bytes 1048576 | tf_op jit(solution)/shard_map/all_to_all | solution.py:119
  13.6 68.7 %collective-permute-start.8 = (bf16[896,896]{1,0:T(8,128)(2,1)}, bf16[896,896]{1,0:T(8,128)(2,1)}, u32[]{:S(2)}, u32[]{:S(2)}) collective-permute-start(bf16[896,896]{1,0:T(8,128)(2,1)} %own.2), channel_id=1, source_target_pairs={{0,16},{16,0},{1,17},{17,1},{2,18},{18,2},{3,19},{19,3},{4,20},{20... | collective-permute-start | bytes 4816904 | tf_op jit(solution)/shard_map/ppermute | solution.py:33
  16.6 4.4 %collective-permute-start = (bf16[32,896]{1,0:T(8,128)(2,1)S(1)}, bf16[32,896]{1,0:T(8,128)(2,1)S(1)}, u32[]{:S(2)}, u32[]{:S(2)}) collective-permute-start(bf16[32,896]{1,0:T(8,128)(2,1)S(1)} %get-tuple-element.32), channel_id=1, source_target_pairs={{0,16},{16,0},{1,17},{17,1},{2,18},{18,2},{3,19},{19,3},{4,20},{20... | collective-permute-start | bytes 172040 | tf_op jit(solution)/shard_map/ppermute | solution.py:33
  18.5 23.0 %collective-permute-start.9 = (bf16[512,256]{1,0:T(8,128)(2,1)S(1)}, bf16[512,256]{1,0:T(8,128)(2,1)S(1)}, u32[]{:S(2)}, u32[]{:S(2)}) collective-permute-start(bf16[512,256]{1,0:T(8,128)(2,1)S(1)} %copy-done), channel_id=1, source_target_pairs={{0,16},{16,0},{1,17},{17,1},{2,18},{18,2},{3,19},{19,3},{4,20},{20... | collective-permute-start | bytes 786440 | tf_op jit(solution)/shard_map/ppermute | solution.py:33
  20.9 11.4 %collective-permute-start.1 = (bf16[32,1792]{1,0:T(8,128)(2,1)S(1)}, bf16[32,1792]{1,0:T(8,128)(2,1)S(1)}, u32[]{:S(2)}, u32[]{:S(2)}) collective-permute-start(bf16[32,1792]{1,0:T(8,128)(2,1)S(1)} %pad_maximum_fusion.refs_0_), channel_id=1, source_target_pairs={{0,1},{1,0},{2,3},{3,2},{4,5},{5,4},{6,7},{7,6},{8,9},{9,8},{10,11... | collective-permute-start | bytes 344072 | tf_op jit(solution)/shard_map/ppermute | solution.py:33
  25.2 10.3 %collective-permute-start.2 = (bf16[32,1792]{1,0:T(8,128)(2,1)S(1)}, bf16[32,1792]{1,0:T(8,128)(2,1)S(1)}, u32[]{:S(2)}, u32[]{:S(2)}) collective-permute-start(bf16[32,1792]{1,0:T(8,128)(2,1)S(1)} %pad_maximum_fusion.refs_0_), channel_id=1, source_target_pairs={{0,2},{1,3},{2,0},{3,1},{4,6},{5,7},{6,4},{7,5},{8,10},{9,11},{10,... | collective-permute-start | bytes 344072 | tf_op jit(solution)/shard_map/ppermute | solution.py:33
  29.9 11.6 %collective-permute-start.3 = (bf16[32,1792]{1,0:T(8,128)(2,1)S(1)}, bf16[32,1792]{1,0:T(8,128)(2,1)S(1)}, u32[]{:S(2)}, u32[]{:S(2)}) collective-permute-start(bf16[32,1792]{1,0:T(8,128)(2,1)S(1)} %pad_maximum_fusion.refs_0_), channel_id=1, source_target_pairs={{0,3},{1,2},{2,1},{3,0},{4,7},{5,6},{6,5},{7,4},{8,11},{9,10},{10,... | collective-permute-start | bytes 344072 | tf_op jit(solution)/shard_map/ppermute | solution.py:33
  41.6 40.8 %copy-start.1 = (bf16[896,896]{1,0:T(8,128)(2,1)S(1)}, bf16[896,896]{1,0:T(8,128)(2,1)}, u32[]{:S(2)}) copy-start(bf16[896,896]{1,0:T(8,128)(2,1)} %own.2) | copy-start | bytes 4816900
  42.8 44.1 %all-to-all-start.2 = ((bf16[16,32,512]{2,1,0:T(8,128)(2,1)}), bf16[16,32,512]{2,1,0:T(8,128)(2,1)S(1)}, u32[]{:S(2)}, u32[]{:S(2)}) async-start(bf16[16,32,512]{2,1,0:T(8,128)(2,1)} %shard_map.48), calls=%async_computation.2 | async-start | bytes 1048576 | tf_op jit(solution)/shard_map/all_to_all | solution.py:126
  51.0 20.0 %collective-permute-start.5 = (bf16[128,1792]{1,0:T(8,128)(2,1)S(1)}, bf16[128,1792]{1,0:T(8,128)(2,1)S(1)}, u32[]{:S(2)}, u32[]{:S(2)}) collective-permute-start(bf16[128,1792]{1,0:T(8,128)(2,1)S(1)} %get-tuple-element.18.act0), channel_id=1, source_target_pairs={{0,12},{4,8},{8,4},{12,0},{1,13},{5,9},{9,5},{13,1},{2,14},{6,10},... | collective-permute-start | bytes 1376264 | tf_op jit(solution)/shard_map/ppermute | solution.py:33
  55.5 17.5 %collective-permute-start.4 = (bf16[128,1792]{1,0:T(8,128)(2,1)S(1)}, bf16[128,1792]{1,0:T(8,128)(2,1)S(1)}, u32[]{:S(2)}, u32[]{:S(2)}) collective-permute-start(bf16[128,1792]{1,0:T(8,128)(2,1)S(1)} %get-tuple-element.18.act0), channel_id=1, source_target_pairs={{0,4},{4,0},{8,12},{12,8},{1,5},{5,1},{9,13},{13,9},{2,6},{6,2},{1... | collective-permute-start | bytes 1376264 | tf_op jit(solution)/shard_map/ppermute | solution.py:33
  71.0 8.5 %collective-permute-start.6 = (bf16[64,1792]{1,0:T(8,128)(2,1)S(1)}, bf16[64,1792]{1,0:T(8,128)(2,1)S(1)}, u32[]{:S(2)}, u32[]{:S(2)}) collective-permute-start(bf16[64,1792]{1,0:T(8,128)(2,1)S(1)} %slice.8), channel_id=1, source_target_pairs={{0,4},{4,0},{8,12},{12,8},{1,5},{5,1},{9,13},{13,9},{2,6},{6,2},{1... | collective-permute-start | bytes 688136 | tf_op jit(solution)/shard_map/ppermute | solution.py:33
  73.0 9.3 %collective-permute-start.7 = (bf16[64,1792]{1,0:T(8,128)(2,1)S(1)}, bf16[64,1792]{1,0:T(8,128)(2,1)S(1)}, u32[]{:S(2)}, u32[]{:S(2)}) collective-permute-start(bf16[64,1792]{1,0:T(8,128)(2,1)S(1)} %slice.9), channel_id=1, source_target_pairs={{0,12},{4,8},{8,4},{12,0},{1,13},{5,9},{9,5},{13,1},{2,14},{6,10},... | collective-permute-start | bytes 688136 | tf_op jit(solution)/shard_map/ppermute | solution.py:33
  86.9 30.6 %all-to-all-start = ((bf16[16,32,896]{2,1,0:T(8,128)(2,1)}), bf16[16,32,896]{2,1,0:T(8,128)(2,1)S(1)}, u32[]{:S(2)}, u32[]{:S(2)}) async-start(bf16[16,32,896]{2,1,0:T(8,128)(2,1)} %get-tuple-element.19), calls=%async_computation | async-start | bytes 1835008 | tf_op jit(solution)/shard_map/all_to_all | solution.py:135
  95.0 5.3 %collective-permute-start.10 = (bf16[32,256]{1,0:T(8,128)(2,1)S(1)}, bf16[32,256]{1,0:T(8,128)(2,1)S(1)}, u32[]{:S(2)}, u32[]{:S(2)}) collective-permute-start(bf16[32,256]{1,0:T(8,128)(2,1)S(1)} %get-tuple-element.23), channel_id=1, source_target_pairs={{0,16},{16,0},{1,17},{17,1},{2,18},{18,2},{3,19},{19,3},{4,20},{20... | collective-permute-start | bytes 49160 | tf_op jit(solution)/shard_map/ppermute | solution.py:33
  100.3 11.4 %collective-permute-start.11 = (bf16[32,512]{1,0:T(8,128)(2,1)S(1)}, bf16[32,512]{1,0:T(8,128)(2,1)S(1)}, u32[]{:S(2)}, u32[]{:S(2)}) collective-permute-start(bf16[32,512]{1,0:T(8,128)(2,1)S(1)} %constant_dynamic-update-slice_fusion.refs_0_), channel_id=1, source_target_pairs={{0,1},{1,0},{2,3},{3,2},{4,5},{5,4},{6,7},{7,6},{8,9},{9,8},{10,11... | collective-permute-start | bytes 98312 | tf_op jit(solution)/shard_map/ppermute | solution.py:33
  103.3 8.6 %collective-permute-start.12 = (bf16[32,512]{1,0:T(8,128)(2,1)S(1)}, bf16[32,512]{1,0:T(8,128)(2,1)S(1)}, u32[]{:S(2)}, u32[]{:S(2)}) collective-permute-start(bf16[32,512]{1,0:T(8,128)(2,1)S(1)} %constant_dynamic-update-slice_fusion.refs_0_), channel_id=1, source_target_pairs={{0,2},{1,3},{2,0},{3,1},{4,6},{5,7},{6,4},{7,5},{8,10},{9,11},{10,... | collective-permute-start | bytes 98312 | tf_op jit(solution)/shard_map/ppermute | solution.py:33
  109.0 7.1 %collective-permute-start.13 = (bf16[32,512]{1,0:T(8,128)(2,1)S(1)}, bf16[32,512]{1,0:T(8,128)(2,1)S(1)}, u32[]{:S(2)}, u32[]{:S(2)}) collective-permute-start(bf16[32,512]{1,0:T(8,128)(2,1)S(1)} %constant_dynamic-update-slice_fusion.refs_0_), channel_id=1, source_target_pairs={{0,3},{1,2},{2,1},{3,0},{4,7},{5,6},{6,5},{7,4},{8,11},{9,10},{10,... | collective-permute-start | bytes 98312 | tf_op jit(solution)/shard_map/ppermute | solution.py:33
  118.6 29.9 %all-to-all-start.3 = ((bf16[16,32,896]{2,1,0:T(8,128)(2,1)}), bf16[16,32,896]{2,1,0:T(8,128)(2,1)S(1)}, u32[]{:S(2)}, u32[]{:S(2)}) async-start(bf16[16,32,896]{2,1,0:T(8,128)(2,1)} %shard_map.51), calls=%async_computation.3 | async-start | bytes 1835008 | tf_op jit(solution)/shard_map/all_to_all | solution.py:143
  125.7 9.6 %collective-permute-start.14 = (bf16[128,512]{1,0:T(8,128)(2,1)S(1)}, bf16[128,512]{1,0:T(8,128)(2,1)S(1)}, u32[]{:S(2)}, u32[]{:S(2)}) collective-permute-start(bf16[128,512]{1,0:T(8,128)(2,1)S(1)} %get-tuple-element.25.g0), channel_id=1, source_target_pairs={{0,4},{4,0},{8,12},{12,8},{1,5},{5,1},{9,13},{13,9},{2,6},{6,2},{1... | collective-permute-start | bytes 393224 | tf_op jit(solution)/shard_map/ppermute | solution.py:33
  127.8 8.5 %collective-permute-start.15 = (bf16[128,512]{1,0:T(8,128)(2,1)S(1)}, bf16[128,512]{1,0:T(8,128)(2,1)S(1)}, u32[]{:S(2)}, u32[]{:S(2)}) collective-permute-start(bf16[128,512]{1,0:T(8,128)(2,1)S(1)} %get-tuple-element.25.g0), channel_id=1, source_target_pairs={{0,8},{4,12},{8,0},{12,4},{1,9},{5,13},{9,1},{13,5},{2,10},{6,14},... | collective-permute-start | bytes 393224 | tf_op jit(solution)/shard_map/ppermute | solution.py:33
  132.2 7.6 %collective-permute-start.16 = (bf16[128,512]{1,0:T(8,128)(2,1)S(1)}, bf16[128,512]{1,0:T(8,128)(2,1)S(1)}, u32[]{:S(2)}, u32[]{:S(2)}) collective-permute-start(bf16[128,512]{1,0:T(8,128)(2,1)S(1)} %get-tuple-element.25.g0), channel_id=1, source_target_pairs={{0,12},{4,8},{8,4},{12,0},{1,13},{5,9},{9,5},{13,1},{2,14},{6,10},... | collective-permute-start | bytes 393224 | tf_op jit(solution)/shard_map/ppermute | solution.py:33
  148.5 6.8 %collective-permute-start.17 = (bf16[512,896]{1,0:T(8,128)(2,1)S(1)}, bf16[512,896]{1,0:T(8,128)(2,1)S(1)}, u32[]{:S(2)}, u32[]{:S(2)}) collective-permute-start(bf16[512,896]{1,0:T(8,128)(2,1)S(1)} %bitcast.2), channel_id=1, source_target_pairs={{0,16},{16,0},{1,17},{17,1},{2,18},{18,2},{3,19},{19,3},{4,20},{20... | collective-permute-start | bytes 2752520 | tf_op jit(solution)/shard_map/ppermute | solution.py:33

commit v5 on v2

v5 whole, which is shorter than its diff:
```python
import jax
import jax.numpy as jnp
from jax import lax
from jax.experimental import pallas as pl
from jax.experimental.pallas import tpu as pltpu
from jax.sharding import Mesh, PartitionSpec as P

SEQS = 2
SEQ_LEN = 512
OUT = ("z", "ylo", "core")
INP = ("x", "yhi")
CHIPS = ("z", "ylo")
BF16 = jnp.bfloat16
F32 = jnp.float32
VMEM = pl.BlockSpec(memory_space=pltpu.VMEM)
SMEM = pl.BlockSpec(memory_space=pltpu.SMEM)
ANY = pl.BlockSpec(memory_space=pl.ANY)


def kernel_call(body, shapes, args, flops=0, scalars=0, unread=0):
    moved = sum(a.size * a.dtype.itemsize for a in args) + sum(s.size * s.dtype.itemsize for s in shapes)
    many = len(shapes) > 1
    return pl.pallas_call(
        body,
        out_shape=shapes if many else shapes[0],
        in_specs=[SMEM] * scalars + [VMEM] * (len(args) - scalars - unread) + [ANY] * unread,
        out_specs=[VMEM] * len(shapes) if many else VMEM,
        compiler_params=pltpu.CompilerParams(vmem_limit_bytes=40 * 2**20),
        cost_estimate=pl.CostEstimate(flops=flops, bytes_accessed=moved, transcendentals=0),
    )(*args)


def swap(value, axis, flip):
    size = lax.axis_size(axis)
    return lax.ppermute(value, axis, [(s, s ^ flip) for s in range(size)])


def act_dot_kernel(acts, basis0, basis1, order, out):
    blocks, block = out.shape[0], out.shape[1]
    total = 0.0
    for core, basis in ((0, basis0), (1, basis1)):
        rows = jnp.concatenate([acts[2 * x + core] for x in range(4)])
        total += jnp.dot(rows, basis[...], preferred_element_type=F32)
    out[...] = total.astype(BF16).reshape(out.shape)


def grad_dot_kernel(rows, own, other, out):
    columns = own.shape[1]
    blocks, block = out.shape[0], out.shape[1]
    for side, basis in ((0, own), (1, other)):
        part = jnp.dot(rows[...], basis[...], preferred_element_type=F32).astype(BF16)
        out[:, :, side * columns:(side + 1) * columns] = part.reshape(blocks, block, columns)


def sum_parts(parts):
    total = parts[0].astype(F32)
    for index in range(1, parts.shape[0]):
        total += parts[index].astype(F32)
    return total.astype(BF16)


def sum_copies_kernel(parts, out):
    rounded = sum_parts(parts)
    for index in range(out.shape[0]):
        out[index] = rounded


def split_kernel(at, parts, order, out):
    core = at[0]
    rounded = sum_parts(parts)
    copies, columns = out.shape[0] // 2, out.shape[2]
    for index in range(copies):
        out[core * copies + index] = rounded[:, :columns]
        out[(1 - core) * copies + index] = rounded[:, columns:]


def square_kernel(at, grads, act_mine, act_theirs, out):
    core = at[0]
    half = act_mine.shape[0] // SEQS
    total = 0.0
    for seq in range(SEQS):
        rotated = 0.0
        for side, act in ((core, act_mine), (1 - core, act_theirs)):
            rotated += lax.dot_general(
                grads[side, seq], act[seq * half:(seq + 1) * half, :], (((0,), (0,)), ((), ())),
                preferred_element_type=F32,
            )
        total = total + rotated * rotated
    out[...] = total * (1.0 / (SEQS * SEQ_LEN))


def both(index, axis, own):
    other = swap(own, axis, 1)
    return jnp.where(index == 0, own, other), jnp.where(index == 0, other, own)


def shards(grads, acts, grad_basis, act_basis):
    core = lax.axis_index("core")
    at = core.astype(jnp.int32).reshape(1)
    half, features = acts.shape[0] // 2, acts.shape[1]
    tokens, eig = 16 * half, act_basis.shape[1]
    rows, columns = grads.shape[0], grad_basis.shape[1]

    copies = jnp.broadcast_to(acts.reshape(2, 1, half, features), (2, 4, half, features))
    act_yhi = lax.all_to_all(copies.reshape(8, half, features), ("core", "yhi"), 0, 0, tiled=True)
    act_basis0, act_basis1 = both(core, "core", act_basis)
    grad_basis_other = swap(grad_basis, "core", 1)

    act_yhi, grads = lax.optimization_barrier((act_yhi, grads))
    act_rows = lax.all_gather(act_yhi.reshape(8 * half, features), "x", axis=0, tiled=True)
    grad_copies = jnp.broadcast_to(grads[None], (16, *grads.shape))
    grad_rows = lax.all_to_all(grad_copies, CHIPS, 0, 0, tiled=True).reshape(tokens, -1)
    grad_partial = kernel_call(
        grad_dot_kernel,
        [jax.ShapeDtypeStruct((16, rows, 2 * columns), BF16)],
        [grad_rows, grad_basis, grad_basis_other],
        flops=2 * tokens * grads.shape[1] * 2 * columns,
    )
    grad_parts = lax.all_to_all(grad_partial, INP, 0, 0, tiled=True)

    blocks = jax.ShapeDtypeStruct((16, half, eig), BF16)
    act_partial = kernel_call(
        act_dot_kernel,
        [blocks],
        [act_rows.reshape(8, 4 * half, features), act_basis0, act_basis1, grad_partial],
        flops=2 * tokens * 2 * features * eig,
        unread=1,
    )
    act_parts = lax.all_to_all(act_partial, CHIPS, 0, 0, tiled=True)
    act_copies = kernel_call(sum_copies_kernel, [blocks], [act_parts])
    act_mine = lax.all_to_all(act_copies, CHIPS, 0, 0, tiled=True).reshape(tokens, eig)
    act_theirs = swap(act_mine, "core", 1)

    split = kernel_call(
        split_kernel,
        [jax.ShapeDtypeStruct((32, rows, columns), BF16)],
        [at, grad_parts, act_mine],
        scalars=1,
        unread=1,
    )
    grad_all = lax.all_to_all(split, ("core", *INP), 0, 0, tiled=True).reshape(2, SEQS, 8 * rows, columns)

    return kernel_call(
        square_kernel,
        [jax.ShapeDtypeStruct((columns, eig), F32)],
        [at, grad_all, act_mine, act_theirs],
        flops=2 * 2 * tokens * columns * eig,
        scalars=1,
    )


def solution(mesh):
    split = Mesh(mesh.devices.reshape(8, 2, 2, 4, 4), OUT + INP)
    return jax.shard_map(
        shards,
        mesh=split,
        in_specs=(P(OUT, INP), P(INP, OUT), P(INP, OUT), P(OUT, INP)),
        out_specs=P(OUT, INP),
        check_vma=False,
    )
```

time: 181 us -> 190 us (1.050)
  the two profiles are of different devices: /device:TPU:9 before, /device:TPU:1 now
where the time goes in v5:
time: 190 us; the launch traced here: 186 us
  blocking collectives  87.1 us (46%)
  waiting for transfers between devices  42.1 us (22%)
  starting transfers between devices  29.5 us (16%)
  between operations  13.5 us (7%)
  Pallas kernels  6.49 us (3%)
  local copies, waits for them, and re-layouts  5.24 us (3%)
  other arithmetic  2.37 us (1%)
    all_to_all x1, blocking collectives, shards(): act_parts = lax.all_to_all(act_partial, CHIPS, 0, 0, tiled=True)  31.7 us
    all_to_all x1, blocking collectives, shards(): lax.all_to_all(act_copies, CHIPS, 0, 0, tiled=True).reshape(tokens, eig)  31 us
    all_to_all x1, blocking collectives, shards(): lax.all_to_all(copies.reshape(8, half, features), ('core', 'yhi'), 0, 0,...  24.4 us
    all_to_all x1, waiting for transfers between devices, shards(): grad_parts = lax.all_to_all(grad_partial, INP, 0, 0, tiled=True)  15.3 us
    all_to_all x1, waiting for transfers between devices, shards(): lax.all_to_all(split, ('core', *INP), 0, 0, tiled=True)  10.3 us
    all_to_all x1, waiting for transfers between devices, shards(): lax.all_to_all(grad_copies, CHIPS, 0, 0, tiled=True).reshape(tokens, -1)  10.1 us
    all_to_all x1, starting transfers between devices, shards(): lax.all_to_all(grad_copies, CHIPS, 0, 0, tiled=True).reshape(tokens, -1)  9.07 us
    ppermute x3, starting transfers between devices, swap(): return lax.ppermute(value, axis, [(s, s ^ flip) for s in range(size)])  6.99 us
  transfers between devices with their start and end apart: 7, of which 5 were waited for; matrix products, arithmetic and copies ran while one was open for 2% of the time, Pallas kernels for 1%

profile of v5, /device:TPU:1, one launch (start us, length us, event | category | flops | bytes accessed | tf_op | source)
XLA Modules:
  0.0 186.3 jit_solution(11858156278450268771)
XLA Ops:
  6.5 0.0 copy-start.5
  6.5 0.0 copy-start.4
  6.5 0.0 all-gather.2.cloned.1.call-start
  6.5 1.1 broadcast_in_dim.14
  7.6 0.0 copy-start.3
  7.6 24.4 %all_to_all.30 = bf16[8,32,896]{2,1,0:T(8,128)(2,1)} all-to-all(bf16[8,32,896]{2,1,0:T(8,128)(2,1)S(1)} %bitcast.14), channel_id=1, replica_groups=mesh['z'=8,'ylo'=2,'core'=2,'x'=4,'yhi'=4] {'core','yhi'}, dimensions={0} | all-to-all | bytes 917504 | tf_op jit(solution)/shard_map/all_to_all | solution.py:105
  32.0 0.0 all-gather.2.cloned.1.call-update
  32.0 0.0 copy-done.4
  32.0 2.3 %collective-permute-start.1 = (bf16[896,896]{1,0:T(8,128)(2,1)S(1)}, bf16[896,896]{1,0:T(8,128)(2,1)}, u32[]{:S(2)}, u32[]{:S(2)}) collective-permute-start(bf16[896,896]{1,0:T(8,128)(2,1)S(1)} %copy-done.4), channel_id=1, source_target_pairs={{0,16},{16,0},{1,17},{17,1},{2,18},{18,2},{3,19},{19,3},{4,20},{20... | collective-permute-start | bytes 4816904 | tf_op jit(solution)/shard_map/ppermute | solution.py:35
  34.3 0.0 copy-done.5
  34.3 0.8 broadcast_in_dim.15
  35.2 9.1 %all-to-all-start.1 = ((bf16[16,32,512]{2,1,0:T(8,128)(2,1)}), bf16[16,32,512]{2,1,0:T(8,128)(2,1)}, u32[]{:S(2)}, u32[]{:S(2)}) async-start(bf16[16,32,512]{2,1,0:T(8,128)(2,1)} %broadcast_in_dim.15), calls=%async_computation.1 | async-start | bytes 1048576 | tf_op jit(solution)/shard_map/all_to_all | solution.py:112
  44.3 0.0 copy-done.3
  44.3 2.6 %collective-permute-start = (bf16[512,256]{1,0:T(8,128)(2,1)S(1)}, bf16[512,256]{1,0:T(8,128)(2,1)}, u32[]{:S(2)}, u32[]{:S(2)}) collective-permute-start(bf16[512,256]{1,0:T(8,128)(2,1)S(1)} %copy-done.3), channel_id=1, source_target_pairs={{0,16},{16,0},{1,17},{17,1},{2,18},{18,2},{3,19},{19,3},{4,20},{20... | collective-permute-start | bytes 786440 | tf_op jit(solution)/shard_map/ppermute | solution.py:35
  46.8 0.0 collective-permute-done.1
  46.9 2.4 %broadcast_select_fusion = (bf16[896,896]{1,0:T(8,128)(2,1)S(1)}, bf16[896,896]{1,0:T(8,128)(2,1)S(1)}) fusion(bf16[896,896]{1,0:T(8,128)(2,1)} %collective-permute-done.1, bf16[896,896]{1,0:T(8,128)(2,1)} %param.7, pred[]{:T(512)S(6)} %eq.4), kind=kLoop, calls=%fused_computation | loop fusion | flops 1605632 | bytes 6422529 | tf_op jit(solution)/shard_map/jit(_where)/select_n | solution.py:94
  49.2 0.0 collective-permute-done.other
  49.2 10.1 %all-to-all-done.1 = bf16[16,32,512]{2,1,0:T(8,128)(2,1)} async-done(((bf16[16,32,512]{2,1,0:T(8,128)(2,1)}), bf16[16,32,512]{2,1,0:T(8,128)(2,1)}, u32[]{:S(2)}, u32[]{:S(2)}) %all-to-all-start.1) | async-done | bytes 524320 | tf_op jit(solution)/shard_map/all_to_all | solution.py:112
  59.3 1.5 shard_map.46.order
  60.9 0.0 copy-start
  60.9 0.8 copy-done
  61.7 4.1 %all-gather.2.cloned.1.call-done = bf16[1024,896]{1,0:T(8,128)(2,1)} async-done(((bf16[256,896]{1,0:T(8,128)(2,1)}), bf16[1024,896]{1,0:T(8,128)(2,1)}) %all-gather.2.cloned.1.call-update) | async-done | bytes 1835024 | tf_op jit(solution)/shard_map/all_gather | solution.py:110
  65.8 0.0 copy-start.1
  65.8 1.0 copy-done.1
  66.8 0.0 copy-start.2
  66.8 1.5 copy-done.2
  68.3 2.3 %shard_map.47 = bf16[16,32,896]{2,1,0:T(8,128)(2,1)S(1)} custom-call(bf16[8,128,896]{2,1,0:T(8,128)(2,1)S(1)} %bitcast.12, bf16[896,896]{1,0:T(8,128)(2,1)S(1)} %get-tuple-element.10.basis0, bf16[896,896]{1,0:T(8,128)(2,1)S(1)} %get-tuple-element.9.basis1, bf16[16,32,512]{2,1,0:T(8,128)(2,1)S(1)} %copy-done.1), custom_call_target="tpu_custom_call" | custom-call | flops 1644167168 | bytes 6488064 | tf_op jit(solution)/shard_map/pallas_call | solution.py:23
  70.6 31.7 %all_to_all.31.parts = bf16[16,32,896]{2,1,0:T(8,128)(2,1)S(1)} all-to-all(bf16[16,32,896]{2,1,0:T(8,128)(2,1)S(1)} %shard_map.47), channel_id=1, replica_groups=mesh['z'=8,'ylo'=2,'core'=2,'x'=4,'yhi'=4] {'z','ylo'}, dimensions={0} | all-to-all | bytes 1835008 | tf_op jit(solution)/shard_map/all_to_all | solution.py:129
  102.2 6.8 %all-to-all-start.2 = ((bf16[16,32,512]{2,1,0:T(8,128)(2,1)}), bf16[16,32,512]{2,1,0:T(8,128)(2,1)S(1)}, u32[]{:S(2)}, u32[]{:S(2)}) async-start(bf16[16,32,512]{2,1,0:T(8,128)(2,1)} %copy-done), calls=%async_computation.2 | async-start | bytes 1048576 | tf_op jit(solution)/shard_map/all_to_all | solution.py:119
  109.0 0.1 shard_map.48
  109.2 15.3 %all-to-all-done.2.parts = bf16[16,32,512]{2,1,0:T(8,128)(2,1)S(1)} async-done(((bf16[16,32,512]{2,1,0:T(8,128)(2,1)}), bf16[16,32,512]{2,1,0:T(8,128)(2,1)S(1)}, u32[]{:S(2)}, u32[]{:S(2)}) %all-to-all-start.2) | async-done | bytes 524320 | tf_op jit(solution)/shard_map/all_to_all | solution.py:119
  124.5 31.0 %all_to_all.32 = bf16[16,32,896]{2,1,0:T(8,128)(2,1)S(1)} all-to-all(bf16[16,32,896]{2,1,0:T(8,128)(2,1)S(1)} %shard_map.48), channel_id=1, replica_groups=mesh['z'=8,'ylo'=2,'core'=2,'x'=4,'yhi'=4] {'z','ylo'}, dimensions={0} | all-to-all | bytes 1835008 | tf_op jit(solution)/shard_map/all_to_all | solution.py:131
  155.5 0.9 shard_map.49
  156.4 6.7 %all-to-all-start.5 = ((bf16[32,32,256]{2,1,0:T(8,128)(2,1)}), bf16[32,32,256]{2,1,0:T(8,128)(2,1)S(1)}, u32[]{:S(2)}, u32[]{:S(2)}) async-start(bf16[32,32,256]{2,1,0:T(8,128)(2,1)} %shard_map.49), calls=%async_computation.5 | async-start | bytes 1048576 | tf_op jit(solution)/shard_map/all_to_all | solution.py:141
  163.1 2.1 %collective-permute-start.2 = (bf16[512,896]{1,0:T(8,128)(2,1)S(1)}, bf16[512,896]{1,0:T(8,128)(2,1)S(1)}, u32[]{:S(2)}, u32[]{:S(2)}) collective-permute-start(bf16[512,896]{1,0:T(8,128)(2,1)S(1)} %bitcast.9), channel_id=1, source_target_pairs={{0,16},{16,0},{1,17},{17,1},{2,18},{18,2},{3,19},{19,3},{4,20},{20... | collective-permute-start | bytes 2752520 | tf_op jit(solution)/shard_map/ppermute | solution.py:35
  165.3 2.2 %collective-permute-done.2.act_theirs = bf16[512,896]{1,0:T(8,128)(2,1)S(1)} collective-permute-done((bf16[512,896]{1,0:T(8,128)(2,1)S(1)}, bf16[512,896]{1,0:T(8,128)(2,1)S(1)}, u32[]{:S(2)}, u32[]{:S(2)}) %collective-permute-start.2) | collective-permute-done | bytes 917536 | tf_op jit(solution)/shard_map/ppermute | solution.py:35
  167.5 10.3 %all-to-all-done.5 = bf16[32,32,256]{2,1,0:T(8,128)(2,1)S(1)} async-done(((bf16[32,32,256]{2,1,0:T(8,128)(2,1)}), bf16[32,32,256]{2,1,0:T(8,128)(2,1)S(1)}, u32[]{:S(2)}, u32[]{:S(2)}) %all-to-all-start.5) | async-done | bytes 524320 | tf_op jit(solution)/shard_map/all_to_all | solution.py:141
  177.8 1.7 shard_map.50
Async XLA Ops:
  6.5 27.8 %copy-start.5 = (bf16[32,512]{1,0:T(8,128)(2,1)S(1)}, bf16[32,512]{1,0:T(8,128)(2,1)}, u32[]{:S(2)}) copy-start(bf16[32,512]{1,0:T(8,128)(2,1)} %param.4) | copy-start | bytes 98308
  6.5 25.5 %copy-start.4 = (bf16[896,896]{1,0:T(8,128)(2,1)S(1)}, bf16[896,896]{1,0:T(8,128)(2,1)}, u32[]{:S(2)}) copy-start(bf16[896,896]{1,0:T(8,128)(2,1)} %param.7) | copy-start | bytes 4816900
  6.5 59.2 %all-gather.2.cloned.1.call-start = ((), (), s32[]{:S(2)}) async-start(), calls=%async_computation.6 | async-start | bytes 2293760 | tf_op jit(solution)/shard_map/all_gather | solution.py:110
  7.6 36.7 %copy-start.3 = (bf16[512,256]{1,0:T(8,128)(2,1)S(1)}, bf16[512,256]{1,0:T(8,128)(2,1)}, u32[]{:S(2)}) copy-start(bf16[512,256]{1,0:T(8,128)(2,1)} %own.1) | copy-start | bytes 786436
  32.0 14.8 %collective-permute-start.1 = (bf16[896,896]{1,0:T(8,128)(2,1)S(1)}, bf16[896,896]{1,0:T(8,128)(2,1)}, u32[]{:S(2)}, u32[]{:S(2)}) collective-permute-start(bf16[896,896]{1,0:T(8,128)(2,1)S(1)} %copy-done.4), channel_id=1, source_target_pairs={{0,16},{16,0},{1,17},{17,1},{2,18},{18,2},{3,19},{19,3},{4,20},{20... | collective-permute-start | bytes 4816904 | tf_op jit(solution)/shard_map/ppermute | solution.py:35
  35.2 24.1 %all-to-all-start.1 = ((bf16[16,32,512]{2,1,0:T(8,128)(2,1)}), bf16[16,32,512]{2,1,0:T(8,128)(2,1)}, u32[]{:S(2)}, u32[]{:S(2)}) async-start(bf16[16,32,512]{2,1,0:T(8,128)(2,1)} %broadcast_in_dim.15), calls=%async_computation.1 | async-start | bytes 1048576 | tf_op jit(solution)/shard_map/all_to_all | solution.py:112
  44.3 5.0 %collective-permute-start = (bf16[512,256]{1,0:T(8,128)(2,1)S(1)}, bf16[512,256]{1,0:T(8,128)(2,1)}, u32[]{:S(2)}, u32[]{:S(2)}) collective-permute-start(bf16[512,256]{1,0:T(8,128)(2,1)S(1)} %copy-done.3), channel_id=1, source_target_pairs={{0,16},{16,0},{1,17},{17,1},{2,18},{18,2},{3,19},{19,3},{4,20},{20... | collective-permute-start | bytes 786440 | tf_op jit(solution)/shard_map/ppermute | solution.py:35
  60.9 0.8 copy-start
  65.8 1.0 copy-start.1
  66.8 1.5 copy-start.2
  102.2 22.3 %all-to-all-start.2 = ((bf16[16,32,512]{2,1,0:T(8,128)(2,1)}), bf16[16,32,512]{2,1,0:T(8,128)(2,1)S(1)}, u32[]{:S(2)}, u32[]{:S(2)}) async-start(bf16[16,32,512]{2,1,0:T(8,128)(2,1)} %copy-done), calls=%async_computation.2 | async-start | bytes 1048576 | tf_op jit(solution)/shard_map/all_to_all | solution.py:119
  156.4 21.4 %all-to-all-start.5 = ((bf16[32,32,256]{2,1,0:T(8,128)(2,1)}), bf16[32,32,256]{2,1,0:T(8,128)(2,1)S(1)}, u32[]{:S(2)}, u32[]{:S(2)}) async-start(bf16[32,32,256]{2,1,0:T(8,128)(2,1)} %shard_map.49), calls=%async_computation.5 | async-start | bytes 1048576 | tf_op jit(solution)/shard_map/all_to_all | solution.py:141
  163.1 4.4 %collective-permute-start.2 = (bf16[512,896]{1,0:T(8,128)(2,1)S(1)}, bf16[512,896]{1,0:T(8,128)(2,1)S(1)}, u32[]{:S(2)}, u32[]{:S(2)}) collective-permute-start(bf16[512,896]{1,0:T(8,128)(2,1)S(1)} %bitcast.9), channel_id=1, source_target_pairs={{0,16},{16,0},{1,17},{17,1},{2,18},{18,2},{3,19},{19,3},{4,20},{20... | collective-permute-start | bytes 2752520 | tf_op jit(solution)/shard_map/ppermute | solution.py:35
Sparse Core Ops, SparseCore 0:
  32.1 33.5 all-gather.1

commit v6 on v5

v6 whole, which is shorter than its diff:
```python
import jax
import jax.numpy as jnp
from jax import lax
from jax.experimental import pallas as pl
from jax.experimental.pallas import tpu as pltpu
from jax.sharding import Mesh, PartitionSpec as P

SEQS = 2
SEQ_LEN = 512
OUT = ("z", "ylo", "core")
INP = ("x", "yhi")
CHIPS = ("z", "ylo")
BF16 = jnp.bfloat16
F32 = jnp.float32
VMEM = pl.BlockSpec(memory_space=pltpu.VMEM)
SMEM = pl.BlockSpec(memory_space=pltpu.SMEM)
ANY = pl.BlockSpec(memory_space=pl.ANY)


def kernel_call(body, shapes, args, flops=0, scalars=0, unread=0, scratch=()):
    moved = sum(a.size * a.dtype.itemsize for a in args) + sum(s.size * s.dtype.itemsize for s in shapes)
    many = len(shapes) > 1
    return pl.pallas_call(
        body,
        out_shape=shapes if many else shapes[0],
        in_specs=[SMEM] * scalars + [VMEM] * (len(args) - scalars - unread) + [ANY] * unread,
        out_specs=[VMEM] * len(shapes) if many else VMEM,
        scratch_shapes=[pltpu.VMEM(s.shape, s.dtype) for s in scratch],
        compiler_params=pltpu.CompilerParams(vmem_limit_bytes=40 * 2**20),
        cost_estimate=pl.CostEstimate(flops=flops, bytes_accessed=moved, transcendentals=0),
    )(*args)


def swap(value, axis, flip):
    size = lax.axis_size(axis)
    return lax.ppermute(value, axis, [(s, s ^ flip) for s in range(size)])


def act_dot_kernel(acts, basis0, basis1, out, done):
    blocks, block = out.shape[0], out.shape[1]
    total = 0.0
    for core, basis in ((0, basis0), (1, basis1)):
        rows = jnp.concatenate([acts[2 * x + core] for x in range(4)])
        total += jnp.dot(rows, basis[...], preferred_element_type=F32)
    out[...] = total.astype(BF16).reshape(out.shape)
    done[...] = jnp.zeros_like(done)


def grad_dot_kernel(at, rows, own, other, order, mine, give1, give2, give3):
    columns = own.shape[1]
    tokens = mine.shape[0]
    for flip, out in enumerate((mine, give1, give2, give3)):
        block = rows[pl.ds(pl.multiple_of((at[1] ^ flip) * tokens, tokens), tokens), :]
        for side, basis in ((0, own), (1, other)):
            part = jnp.dot(block, basis[...], preferred_element_type=F32)
            out[:, side * columns:(side + 1) * columns] = part.astype(out.dtype)


def sum_x_kernel(at, mine, got1, got2, got3, keep, give1, give2, give3, scratch):
    scratch[...] = mine[...] + got1[...].astype(F32) + got2[...].astype(F32) + got3[...].astype(F32)
    tokens = keep.shape[0]
    for flip, out in enumerate((keep, give1, give2, give3)):
        out[...] = scratch[pl.ds(pl.multiple_of((at[2] ^ flip) * tokens, tokens), tokens), :]


def sum_yhi_kernel(mine, got1, got2, got3, keep, give):
    rounded = (mine[...] + got1[...] + got2[...] + got3[...]).astype(BF16)
    columns = keep.shape[1]
    keep[...] = rounded[:, :columns]
    give[...] = rounded[:, columns:]


def stack_kernel(at, block0, block1, block2, block3, out):
    tokens = block0.shape[0]
    for flip, block in enumerate((block0, block1, block2, block3)):
        out[pl.ds(pl.multiple_of((at[2] ^ flip) * tokens, tokens), tokens), :] = block[...]


def sum_copies_kernel(parts, out):
    total = parts[0].astype(F32)
    for index in range(1, parts.shape[0]):
        total += parts[index].astype(F32)
    rounded = total.astype(BF16)
    for index in range(out.shape[0]):
        out[index] = rounded


def square_kernel(at, g0, g1, g2, g3, act_mine, act_theirs, out):
    columns = out.shape[0]
    quarter = act_mine.shape[0] // 4
    total = 0.0
    for pair in (((0, g0), (1, g1)), ((2, g2), (3, g3))):
        rotated = 0.0
        for flip, grad in pair:
            at_row = pl.multiple_of((at[1] ^ flip) * quarter, quarter)
            for side, act in ((0, act_mine), (1, act_theirs)):
                rotated += lax.dot_general(
                    grad[:, side * columns:(side + 1) * columns], act[pl.ds(at_row, quarter), :],
                    (((0,), (0,)), ((), ())), preferred_element_type=F32,
                )
        total = total + rotated * rotated
    out[...] = total * (1.0 / (SEQS * SEQ_LEN))


def both(index, axis, own):
    other = swap(own, axis, 1)
    return jnp.where(index == 0, own, other), jnp.where(index == 0, other, own)


def shards(grads, acts, grad_basis, act_basis):
    core, x, yhi = (lax.axis_index(axis) for axis in ("core", "x", "yhi"))
    at = jnp.stack([core, x, yhi]).astype(jnp.int32)
    half, features = acts.shape[0] // 2, acts.shape[1]
    tokens, eig = 16 * half, act_basis.shape[1]
    rows, columns = grads.shape[0], grad_basis.shape[1]
    shape = jax.ShapeDtypeStruct

    copies = jnp.broadcast_to(acts.reshape(2, 1, half, features), (2, 4, half, features))
    act_yhi = lax.all_to_all(copies.reshape(8, half, features), ("core", "yhi"), 0, 0, tiled=True)
    act_basis0, act_basis1 = both(core, "core", act_basis)
    grad_basis_other = swap(grad_basis, "core", 1)

    act_yhi, grads = lax.optimization_barrier((act_yhi, grads))
    act_rows = lax.all_gather(act_yhi.reshape(8 * half, features), "x", axis=0, tiled=True)
    grad_copies = jnp.broadcast_to(grads[None], (16, *grads.shape))
    grad_rows = lax.all_to_all(grad_copies, CHIPS, 0, 0, tiled=True).reshape(tokens, -1)

    blocks = shape((16, half, eig), BF16)
    act_partial, done = kernel_call(
        act_dot_kernel,
        [blocks, shape((8, 128), F32)],
        [act_rows.reshape(8, 4 * half, features), act_basis0, act_basis1],
        flops=2 * tokens * 2 * features * eig,
    )
    act_parts = lax.all_to_all(act_partial, CHIPS, 0, 0, tiled=True)

    sent, kept = shape((4 * rows, 2 * columns), BF16), shape((4 * rows, 2 * columns), F32)
    mine, *gives = kernel_call(
        grad_dot_kernel,
        [kept, sent, sent, sent],
        [at, grad_rows, grad_basis, grad_basis_other, done],
        flops=2 * tokens * grads.shape[1] * 2 * columns,
        scalars=1,
        unread=1,
    )
    got = [swap(give, "x", flip) for flip, give in zip((1, 2, 3), gives)]
    mine, *gives = kernel_call(
        sum_x_kernel, [shape((rows, 2 * columns), F32)] * 4, [at, mine, *got], scalars=1, scratch=[kept]
    )
    got = [swap(give, "yhi", flip) for flip, give in zip((1, 2, 3), gives)]
    narrow = shape((rows, columns), BF16)
    keep, give = kernel_call(sum_yhi_kernel, [narrow, narrow], [mine, *got])

    grad_own = jnp.concatenate([keep, swap(give, "core", 1)], axis=1)
    got = [swap(grad_own, "yhi", flip) for flip in (1, 2, 3)]
    g0 = kernel_call(stack_kernel, [sent], [at, grad_own, *got], scalars=1)
    g1, g2, g3 = swap(g0, "x", 1), swap(g0, "x", 2), swap(g0, "x", 3)

    act_copies = kernel_call(sum_copies_kernel, [blocks], [act_parts])
    act_mine = lax.all_to_all(act_copies, CHIPS, 0, 0, tiled=True).reshape(tokens, eig)
    act_mine, g1, g2, g3 = lax.optimization_barrier((act_mine, g1, g2, g3))
    act_theirs = swap(act_mine, "core", 1)

    return kernel_call(
        square_kernel,
        [shape((columns, eig), F32)],
        [at, g0, g1, g2, g3, act_mine, act_theirs],
        flops=2 * 2 * tokens * columns * eig,
        scalars=1,
    )


def solution(mesh):
    split = Mesh(mesh.devices.reshape(8, 2, 2, 4, 4), OUT + INP)
    return jax.shard_map(
        shards,
        mesh=split,
        in_specs=(P(OUT, INP), P(INP, OUT), P(INP, OUT), P(OUT, INP)),
        out_specs=P(OUT, INP),
        check_vma=False,
    )
```

time: 190 us -> 216 us (1.14); the launches traced: 186 us -> 215 us
  starting transfers between devices: 29.5 us -> 67.8 us
  blocking collectives: 87.1 us -> 55.9 us
  waiting for transfers between devices: 42.1 us -> 63.5 us
    ppermute x3 -> x16, starting transfers between devices: 6.99 us -> 57.2 us  [swap(): return lax.ppermute(value, axis, [(s, s ^ flip) for s in range(size)])]
    all_to_all x1 -> x0, blocking collectives: 31 us -> none  [shards(): lax.all_to_all(act_copies, CHIPS, 0, 0, tiled=True).reshape(tokens, eig)]
    all_to_all x2 -> x1, waiting for transfers between devices: 25.6 us -> 0.01 us  [shards(): lax.all_to_all(act_copies, CHIPS, 0, 0, tiled=True).reshape(tokens, eig)]
    all_gather x1, waiting for transfers between devices: 4.1 us -> 26 us  [shards(): lax.all_gather(act_yhi.reshape(8 * half, features), 'x', axis=0, tiled=True)]
    ppermute x3 -> x16, waiting for transfers between devices: 2.23 us -> 23.5 us  [swap(): return lax.ppermute(value, axis, [(s, s ^ flip) for s in range(size)])]
    all_to_all x2 -> x1, starting transfers between devices: 13.5 us -> 5.47 us  [shards(): lax.all_to_all(act_copies, CHIPS, 0, 0, tiled=True).reshape(tokens, eig)]
    all_to_all x1, starting transfers between devices: 9.07 us -> 5.1 us  [shards(): lax.all_to_all(grad_copies, CHIPS, 0, 0, tiled=True).reshape(tokens, -1)]
    all_to_all x1, waiting for transfers between devices: 10.1 us -> 13.9 us  [shards(): lax.all_to_all(grad_copies, CHIPS, 0, 0, tiled=True).reshape(tokens, -1)]
  transfers between devices with their start and end apart: 7 -> 19, of which waited for: 5 -> 14; matrix products, arithmetic and copies ran while one was open for 2% -> 1% of each run, Pallas kernels for 1% -> 2%
where the time goes in v6:
time: 216 us; the launch traced here: 215 us
  starting transfers between devices  67.8 us (31%)
  waiting for transfers between devices  63.5 us (29%)
  blocking collectives  55.9 us (26%)
  between operations  13.7 us (6%)
  Pallas kernels  8.11 us (4%)
  local copies, waits for them, and re-layouts  3.44 us (2%)
  other arithmetic  2.28 us (1%)
    ppermute x16, starting transfers between devices, swap(): return lax.ppermute(value, axis, [(s, s ^ flip) for s in range(size)])  57.2 us
    all_to_all x1, blocking collectives, shards(): act_parts = lax.all_to_all(act_partial, CHIPS, 0, 0, tiled=True)  31.7 us
    all_gather x1, waiting for transfers between devices, shards(): lax.all_gather(act_yhi.reshape(8 * half, features), 'x', axis=0, tiled=True)  26 us
    all_to_all x1, blocking collectives, shards(): lax.all_to_all(copies.reshape(8, half, features), ('core', 'yhi'), 0, 0,...  24.2 us
    ppermute x16, waiting for transfers between devices, swap(): return lax.ppermute(value, axis, [(s, s ^ flip) for s in range(size)])  23.5 us
    all_to_all x1, waiting for transfers between devices, shards(): lax.all_to_all(grad_copies, CHIPS, 0, 0, tiled=True).reshape(tokens, -1)  13.9 us
    pallas_call x7, Pallas kernels, kernel_call(): pl.pallas_call(body, out_shape=shapes if many else shapes[0], in_specs=[S...  8.11 us
    all_to_all x1, starting transfers between devices, shards(): lax.all_to_all(act_copies, CHIPS, 0, 0, tiled=True).reshape(tokens, eig)  5.47 us
  transfers between devices with their start and end apart: 19, of which 14 were waited for; matrix products, arithmetic and copies ran while one was open for 1% of the time, Pallas kernels for 2%

profile of v6, /device:TPU:1, one launch (start us, length us, event | category | flops | bytes accessed | tf_op | source)
XLA Modules:
  0.0 214.6 jit_solution(12490480022507098124)
XLA Ops:
  6.5 0.0 copy-start.2
  6.5 0.0 all-gather.2.cloned.1.call-start
  6.5 1.1 broadcast_in_dim.14
  7.6 24.2 %all_to_all.20 = bf16[8,32,896]{2,1,0:T(8,128)(2,1)} all-to-all(bf16[8,32,896]{2,1,0:T(8,128)(2,1)S(1)} %bitcast.14), channel_id=1, replica_groups=mesh['z'=8,'ylo'=2,'core'=2,'x'=4,'yhi'=4] {'core','yhi'}, dimensions={0} | all-to-all | bytes 917504 | tf_op jit(solution)/shard_map/all_to_all | solution.py:119
  31.8 0.0 all-gather.2.cloned.1.call-update
  31.9 0.0 copy-done.2
  31.9 2.3 %collective-permute-start.1 = (bf16[896,896]{1,0:T(8,128)(2,1)S(1)}, bf16[896,896]{1,0:T(8,128)(2,1)}, u32[]{:S(2)}, u32[]{:S(2)}) collective-permute-start(bf16[896,896]{1,0:T(8,128)(2,1)S(1)} %copy-done.2), channel_id=1, source_target_pairs={{0,16},{16,0},{1,17},{17,1},{2,18},{18,2},{3,19},{19,3},{4,20},{20... | collective-permute-start | bytes 4816904 | tf_op jit(solution)/shard_map/ppermute | solution.py:36
  34.2 3.2 %collective-permute-done.1 = bf16[896,896]{1,0:T(8,128)(2,1)} collective-permute-done((bf16[896,896]{1,0:T(8,128)(2,1)S(1)}, bf16[896,896]{1,0:T(8,128)(2,1)}, u32[]{:S(2)}, u32[]{:S(2)}) %collective-permute-start.1) | collective-permute-done | bytes 1605664 | tf_op jit(solution)/shard_map/ppermute | solution.py:36
  37.4 2.2 %broadcast_select_fusion = (bf16[896,896]{1,0:T(8,128)(2,1)S(1)}, bf16[896,896]{1,0:T(8,128)(2,1)S(1)}) fusion(bf16[896,896]{1,0:T(8,128)(2,1)} %collective-permute-done.1, bf16[896,896]{1,0:T(8,128)(2,1)} %param.7, pred[]{:T(512)S(6)} %eq.4), kind=kLoop, calls=%fused_computation | loop fusion | flops 1605632 | bytes 6422529 | tf_op jit(solution)/shard_map/jit(_where)/select_n | solution.py:107
  39.6 26.0 %all-gather.2.cloned.1.call-done = bf16[1024,896]{1,0:T(8,128)(2,1)} async-done(((bf16[256,896]{1,0:T(8,128)(2,1)}), bf16[1024,896]{1,0:T(8,128)(2,1)}) %all-gather.2.cloned.1.call-update) | async-done | bytes 1835024 | tf_op jit(solution)/shard_map/all_gather | solution.py:124
  65.6 0.0 copy-start.1
  65.6 1.5 copy-done.1
  67.1 2.3 %shard_map.46 = (bf16[16,32,896]{2,1,0:T(8,128)(2,1)S(1)}, f32[8,128]{1,0:T(8,128)S(1)}) custom-call(bf16[8,128,896]{2,1,0:T(8,128)(2,1)S(1)} %bitcast.12, bf16[896,896]{1,0:T(8,128)(2,1)S(1)} %get-tuple-element.42.basis0, bf16[896,896]{1,0:T(8,128)(2,1)S(1)} %get-tuple-element.41.basis1), custom_call_target="tpu_custom_call" | custom-call | flops 1644167168 | bytes 5967872 | tf_op jit(solution)/shard_map/pallas_call | solution.py:23
  69.4 0.0 copy-start.3
  69.4 31.7 %all_to_all.21.parts = bf16[16,32,896]{2,1,0:T(8,128)(2,1)S(1)} all-to-all(bf16[16,32,896]{2,1,0:T(8,128)(2,1)S(1)} %get-tuple-element.36), channel_id=1, replica_groups=mesh['z'=8,'ylo'=2,'core'=2,'x'=4,'yhi'=4] {'z','ylo'}, dimensions={0} | all-to-all | bytes 1835008 | tf_op jit(solution)/shard_map/all_to_all | solution.py:135
  101.1 0.0 copy-done.3
  101.1 0.9 broadcast_in_dim.15
  101.9 5.1 %all-to-all-start.1 = ((bf16[16,32,512]{2,1,0:T(8,128)(2,1)}), bf16[16,32,512]{2,1,0:T(8,128)(2,1)S(1)}, u32[]{:S(2)}, u32[]{:S(2)}) async-start(bf16[16,32,512]{2,1,0:T(8,128)(2,1)} %broadcast_in_dim.15), calls=%async_computation.1 | async-start | bytes 1048576 | tf_op jit(solution)/shard_map/all_to_all | solution.py:126
  107.0 0.0 copy-start
  107.1 1.1 shard_map.51
  108.1 13.9 %all-to-all-done.1 = bf16[16,32,512]{2,1,0:T(8,128)(2,1)S(1)} async-done(((bf16[16,32,512]{2,1,0:T(8,128)(2,1)}), bf16[16,32,512]{2,1,0:T(8,128)(2,1)S(1)}, u32[]{:S(2)}, u32[]{:S(2)}) %all-to-all-start.1) | async-done | bytes 524320 | tf_op jit(solution)/shard_map/all_to_all | solution.py:126
  122.0 5.5 %all-to-all-start.3 = ((bf16[16,32,896]{2,1,0:T(8,128)(2,1)}), bf16[16,32,896]{2,1,0:T(8,128)(2,1)S(1)}, u32[]{:S(2)}, u32[]{:S(2)}) async-start(bf16[16,32,896]{2,1,0:T(8,128)(2,1)} %shard_map.51), calls=%async_computation.3 | async-start | bytes 1835008 | tf_op jit(solution)/shard_map/all_to_all | solution.py:160
  127.5 0.0 copy-done
  127.5 3.0 %collective-permute-start = (bf16[512,256]{1,0:T(8,128)(2,1)S(1)}, bf16[512,256]{1,0:T(8,128)(2,1)S(1)}, u32[]{:S(2)}, u32[]{:S(2)}) collective-permute-start(bf16[512,256]{1,0:T(8,128)(2,1)S(1)} %copy-done), channel_id=1, source_target_pairs={{0,16},{16,0},{1,17},{17,1},{2,18},{18,2},{3,19},{19,3},{4,20},{20... | collective-permute-start | bytes 786440 | tf_op jit(solution)/shard_map/ppermute | solution.py:36
  130.5 0.1 pad_add_fusion.at
  130.6 1.1 collective-permute-done.other
  131.6 1.0 shard_map.47
  132.6 2.1 collective-permute-start.2
  134.7 3.5 %collective-permute-start.3 = (bf16[128,512]{1,0:T(8,128)(2,1)S(1)}, bf16[128,512]{1,0:T(8,128)(2,1)S(1)}, u32[]{:S(2)}, u32[]{:S(2)}) collective-permute-start(bf16[128,512]{1,0:T(8,128)(2,1)S(1)} %get-tuple-element.28), channel_id=1, source_target_pairs={{0,8},{4,12},{8,0},{12,4},{1,9},{5,13},{9,1},{13,5},{2,10},{6,14},... | collective-permute-start | bytes 393224 | tf_op jit(solution)/shard_map/ppermute | solution.py:36
  138.2 4.0 %collective-permute-start.4 = (bf16[128,512]{1,0:T(8,128)(2,1)S(1)}, bf16[128,512]{1,0:T(8,128)(2,1)S(1)}, u32[]{:S(2)}, u32[]{:S(2)}) collective-permute-start(bf16[128,512]{1,0:T(8,128)(2,1)S(1)} %get-tuple-element.29), channel_id=1, source_target_pairs={{0,12},{4,8},{8,4},{12,0},{1,13},{5,9},{9,5},{13,1},{2,14},{6,10},... | collective-permute-start | bytes 393224 | tf_op jit(solution)/shard_map/ppermute | solution.py:36
  142.2 0.0 collective-permute-done.2.got1
  142.2 0.3 collective-permute-done.3.got2
  142.5 2.9 %collective-permute-done.4.got3 = bf16[128,512]{1,0:T(8,128)(2,1)S(1)} collective-permute-done((bf16[128,512]{1,0:T(8,128)(2,1)S(1)}, bf16[128,512]{1,0:T(8,128)(2,1)S(1)}, u32[]{:S(2)}, u32[]{:S(2)}) %collective-permute-start.4) | collective-permute-done | bytes 131104 | tf_op jit(solution)/shard_map/ppermute | solution.py:36
  145.4 0.6 shard_map.48
  146.1 4.0 %collective-permute-start.5 = (f32[32,512]{1,0:T(8,128)S(1)}, f32[32,512]{1,0:T(8,128)S(1)}, u32[]{:S(2)}, u32[]{:S(2)}) collective-permute-start(f32[32,512]{1,0:T(8,128)S(1)} %get-tuple-element.31), channel_id=1, source_target_pairs={{0,1},{1,0},{2,3},{3,2},{4,5},{5,4},{6,7},{7,6},{8,9},{9,8},{10,11... | collective-permute-start | bytes 196616 | tf_op jit(solution)/shard_map/ppermute | solution.py:36
  150.1 4.4 %collective-permute-start.6 = (f32[32,512]{1,0:T(8,128)S(1)}, f32[32,512]{1,0:T(8,128)S(1)}, u32[]{:S(2)}, u32[]{:S(2)}) collective-permute-start(f32[32,512]{1,0:T(8,128)S(1)} %get-tuple-element.32), channel_id=1, source_target_pairs={{0,2},{1,3},{2,0},{3,1},{4,6},{5,7},{6,4},{7,5},{8,10},{9,11},{10,... | collective-permute-start | bytes 196616 | tf_op jit(solution)/shard_map/ppermute | solution.py:36
  154.5 2.9 %collective-permute-start.7 = (f32[32,512]{1,0:T(8,128)S(1)}, f32[32,512]{1,0:T(8,128)S(1)}, u32[]{:S(2)}, u32[]{:S(2)}) collective-permute-start(f32[32,512]{1,0:T(8,128)S(1)} %get-tuple-element.33), channel_id=1, source_target_pairs={{0,3},{1,2},{2,1},{3,0},{4,7},{5,6},{6,5},{7,4},{8,11},{9,10},{10,... | collective-permute-start | bytes 196616 | tf_op jit(solution)/shard_map/ppermute | solution.py:36
  157.5 0.0 collective-permute-done.5.got1
  157.5 1.5 collective-permute-done.6.got2
  159.0 3.4 %collective-permute-done.7.got3 = f32[32,512]{1,0:T(8,128)S(1)} collective-permute-done((f32[32,512]{1,0:T(8,128)S(1)}, f32[32,512]{1,0:T(8,128)S(1)}, u32[]{:S(2)}, u32[]{:S(2)}) %collective-permute-start.7) | collective-permute-done | bytes 65568 | tf_op jit(solution)/shard_map/ppermute | solution.py:36
  162.4 4.7 %collective-permute-start.8 = (bf16[32,256]{1,0:T(8,128)(2,1)S(1)}, bf16[32,256]{1,0:T(8,128)(2,1)S(1)}, u32[]{:S(2)}, u32[]{:S(2)}) collective-permute-start(bf16[32,256]{1,0:T(8,128)(2,1)S(1)} %get-tuple-element.35), channel_id=1, source_target_pairs={{0,16},{16,0},{1,17},{17,1},{2,18},{18,2},{3,19},{19,3},{4,20},{20... | collective-permute-start | bytes 49160 | tf_op jit(solution)/shard_map/ppermute | solution.py:36
  167.1 0.8 collective-permute-done.8
  167.9 4.8 %collective-permute-start.10 = (bf16[32,512]{1,0:T(8,128)(2,1)S(1)}, bf16[32,512]{1,0:T(8,128)(2,1)S(1)}, u32[]{:S(2)}, u32[]{:S(2)}) collective-permute-start(bf16[32,512]{1,0:T(8,128)(2,1)S(1)} %constant_dynamic-update-slice_fusion.block0), channel_id=1, source_target_pairs={{0,2},{1,3},{2,0},{3,1},{4,6},{5,7},{6,4},{7,5},{8,10},{9,11},{10,... | collective-permute-start | bytes 98312 | tf_op jit(solution)/shard_map/ppermute | solution.py:36
  172.7 4.3 %collective-permute-start.11 = (bf16[32,512]{1,0:T(8,128)(2,1)S(1)}, bf16[32,512]{1,0:T(8,128)(2,1)S(1)}, u32[]{:S(2)}, u32[]{:S(2)}) collective-permute-start(bf16[32,512]{1,0:T(8,128)(2,1)S(1)} %constant_dynamic-update-slice_fusion.block0), channel_id=1, source_target_pairs={{0,3},{1,2},{2,1},{3,0},{4,7},{5,6},{6,5},{7,4},{8,11},{9,10},{10,... | collective-permute-start | bytes 98312 | tf_op jit(solution)/shard_map/ppermute | solution.py:36
  177.0 2.3 %collective-permute-start.9 = (bf16[32,512]{1,0:T(8,128)(2,1)S(1)}, bf16[32,512]{1,0:T(8,128)(2,1)S(1)}, u32[]{:S(2)}, u32[]{:S(2)}) collective-permute-start(bf16[32,512]{1,0:T(8,128)(2,1)S(1)} %constant_dynamic-update-slice_fusion.block0), channel_id=1, source_target_pairs={{0,1},{1,0},{2,3},{3,2},{4,5},{5,4},{6,7},{7,6},{8,9},{9,8},{10,11... | collective-permute-start | bytes 98312 | tf_op jit(solution)/shard_map/ppermute | solution.py:36
  179.3 0.0 collective-permute-done.10.block2
  179.3 0.2 collective-permute-done.11.block3
  179.5 3.1 %collective-permute-done.9.block1 = bf16[32,512]{1,0:T(8,128)(2,1)S(1)} collective-permute-done((bf16[32,512]{1,0:T(8,128)(2,1)S(1)}, bf16[32,512]{1,0:T(8,128)(2,1)S(1)}, u32[]{:S(2)}, u32[]{:S(2)}) %collective-permute-start.9) | collective-permute-done | bytes 32800 | tf_op jit(solution)/shard_map/ppermute | solution.py:36
  182.6 0.6 shard_map.50.g0
  183.2 3.2 %collective-permute-start.12 = (bf16[128,512]{1,0:T(8,128)(2,1)S(1)}, bf16[128,512]{1,0:T(8,128)(2,1)S(1)}, u32[]{:S(2)}, u32[]{:S(2)}) collective-permute-start(bf16[128,512]{1,0:T(8,128)(2,1)S(1)} %shard_map.50.g0), channel_id=1, source_target_pairs={{0,4},{4,0},{8,12},{12,8},{1,5},{5,1},{9,13},{13,9},{2,6},{6,2},{1... | collective-permute-start | bytes 393224 | tf_op jit(solution)/shard_map/ppermute | solution.py:36
  186.4 3.9 %collective-permute-start.13 = (bf16[128,512]{1,0:T(8,128)(2,1)S(1)}, bf16[128,512]{1,0:T(8,128)(2,1)S(1)}, u32[]{:S(2)}, u32[]{:S(2)}) collective-permute-start(bf16[128,512]{1,0:T(8,128)(2,1)S(1)} %shard_map.50.g0), channel_id=1, source_target_pairs={{0,8},{4,12},{8,0},{12,4},{1,9},{5,13},{9,1},{13,5},{2,10},{6,14},... | collective-permute-start | bytes 393224 | tf_op jit(solution)/shard_map/ppermute | solution.py:36
  190.3 2.5 %collective-permute-start.14 = (bf16[128,512]{1,0:T(8,128)(2,1)S(1)}, bf16[128,512]{1,0:T(8,128)(2,1)S(1)}, u32[]{:S(2)}, u32[]{:S(2)}) collective-permute-start(bf16[128,512]{1,0:T(8,128)(2,1)S(1)} %shard_map.50.g0), channel_id=1, source_target_pairs={{0,12},{4,8},{8,4},{12,0},{1,13},{5,9},{9,5},{13,1},{2,14},{6,10},... | collective-permute-start | bytes 393224 | tf_op jit(solution)/shard_map/ppermute | solution.py:36
  192.8 0.0 collective-permute-done.12.g1
  192.8 2.1 collective-permute-done.13.g2
  194.8 3.0 %collective-permute-done.14.g3 = bf16[128,512]{1,0:T(8,128)(2,1)S(1)} collective-permute-done((bf16[128,512]{1,0:T(8,128)(2,1)S(1)}, bf16[128,512]{1,0:T(8,128)(2,1)S(1)}, u32[]{:S(2)}, u32[]{:S(2)}) %collective-permute-start.14) | collective-permute-done | bytes 131104 | tf_op jit(solution)/shard_map/ppermute | solution.py:36
  197.8 0.0 all-to-all-done.3
  197.8 5.3 %collective-permute-start.15 = (bf16[512,896]{1,0:T(8,128)(2,1)S(1)}, bf16[512,896]{1,0:T(8,128)(2,1)S(1)}, u32[]{:S(2)}, u32[]{:S(2)}) collective-permute-start(bf16[512,896]{1,0:T(8,128)(2,1)S(1)} %bitcast.9), channel_id=1, source_target_pairs={{0,16},{16,0},{1,17},{17,1},{2,18},{18,2},{3,19},{19,3},{4,20},{20... | collective-permute-start | bytes 2752520 | tf_op jit(solution)/shard_map/ppermute | solution.py:36
  203.1 2.1 collective-permute-done.15.act_theirs
  205.2 2.6 %shard_map.52 = f32[256,896]{1,0:T(8,128)} custom-call(s32[3]{0:T(128)S(1)} %pad_add_fusion.at, bf16[128,512]{1,0:T(8,128)(2,1)S(1)} %shard_map.50.g0, bf16[128,512]{1,0:T(8,128)(2,1)S(1)} %collective-permute-done.12.g1, bf16[128,512]{1,0:T(8,128)(2,1)S(1)} %collective-permute-done.13.g2, bf16[128,512]{1,0:T(8,128)(2,1)S(1)} %collective-permute-done.14.g3, ...), custom_call_target="tpu_custom_call" | custom-call | flops 469762048 | bytes 3276812 | tf_op jit(solution)/shard_map/pallas_call | solution.py:23
  (3 shorter events, 0.0 us)
Async XLA Ops:
  6.5 25.3 %copy-start.2 = (bf16[896,896]{1,0:T(8,128)(2,1)S(1)}, bf16[896,896]{1,0:T(8,128)(2,1)}, u32[]{:S(2)}) copy-start(bf16[896,896]{1,0:T(8,128)(2,1)} %param.7) | copy-start | bytes 4816900
  6.5 59.1 %all-gather.2.cloned.1.call-start = ((), (), s32[]{:S(2)}) async-start(), calls=%async_computation.4 | async-start | bytes 2293760 | tf_op jit(solution)/shard_map/all_gather | solution.py:124
  31.9 5.5 %collective-permute-start.1 = (bf16[896,896]{1,0:T(8,128)(2,1)S(1)}, bf16[896,896]{1,0:T(8,128)(2,1)}, u32[]{:S(2)}, u32[]{:S(2)}) collective-permute-start(bf16[896,896]{1,0:T(8,128)(2,1)S(1)} %copy-done.2), channel_id=1, source_target_pairs={{0,16},{16,0},{1,17},{17,1},{2,18},{18,2},{3,19},{19,3},{4,20},{20... | collective-permute-start | bytes 4816904 | tf_op jit(solution)/shard_map/ppermute | solution.py:36
  65.6 1.5 copy-start.1
  69.4 31.7 %copy-start.3 = (bf16[32,512]{1,0:T(8,128)(2,1)S(1)}, bf16[32,512]{1,0:T(8,128)(2,1)}, u32[]{:S(2)}) copy-start(bf16[32,512]{1,0:T(8,128)(2,1)} %param.4) | copy-start | bytes 98308
  101.9 20.1 %all-to-all-start.1 = ((bf16[16,32,512]{2,1,0:T(8,128)(2,1)}), bf16[16,32,512]{2,1,0:T(8,128)(2,1)S(1)}, u32[]{:S(2)}, u32[]{:S(2)}) async-start(bf16[16,32,512]{2,1,0:T(8,128)(2,1)} %broadcast_in_dim.15), calls=%async_computation.1 | async-start | bytes 1048576 | tf_op jit(solution)/shard_map/all_to_all | solution.py:126
  107.0 20.4 %copy-start = (bf16[512,256]{1,0:T(8,128)(2,1)S(1)}, bf16[512,256]{1,0:T(8,128)(2,1)}, u32[]{:S(2)}) copy-start(bf16[512,256]{1,0:T(8,128)(2,1)} %own.1) | copy-start | bytes 786436
  122.0 75.8 %all-to-all-start.3 = ((bf16[16,32,896]{2,1,0:T(8,128)(2,1)}), bf16[16,32,896]{2,1,0:T(8,128)(2,1)S(1)}, u32[]{:S(2)}, u32[]{:S(2)}) async-start(bf16[16,32,896]{2,1,0:T(8,128)(2,1)} %shard_map.51), calls=%async_computation.3 | async-start | bytes 1835008 | tf_op jit(solution)/shard_map/all_to_all | solution.py:160
  127.5 4.2 %collective-permute-start = (bf16[512,256]{1,0:T(8,128)(2,1)S(1)}, bf16[512,256]{1,0:T(8,128)(2,1)S(1)}, u32[]{:S(2)}, u32[]{:S(2)}) collective-permute-start(bf16[512,256]{1,0:T(8,128)(2,1)S(1)} %copy-done), channel_id=1, source_target_pairs={{0,16},{16,0},{1,17},{17,1},{2,18},{18,2},{3,19},{19,3},{4,20},{20... | collective-permute-start | bytes 786440 | tf_op jit(solution)/shard_map/ppermute | solution.py:36
  132.6 9.6 %collective-permute-start.2 = (bf16[128,512]{1,0:T(8,128)(2,1)S(1)}, bf16[128,512]{1,0:T(8,128)(2,1)S(1)}, u32[]{:S(2)}, u32[]{:S(2)}) collective-permute-start(bf16[128,512]{1,0:T(8,128)(2,1)S(1)} %get-tuple-element.27), channel_id=1, source_target_pairs={{0,4},{4,0},{8,12},{12,8},{1,5},{5,1},{9,13},{13,9},{2,6},{6,2},{1... | collective-permute-start | bytes 393224 | tf_op jit(solution)/shard_map/ppermute | solution.py:36
  134.7 7.8 %collective-permute-start.3 = (bf16[128,512]{1,0:T(8,128)(2,1)S(1)}, bf16[128,512]{1,0:T(8,128)(2,1)S(1)}, u32[]{:S(2)}, u32[]{:S(2)}) collective-permute-start(bf16[128,512]{1,0:T(8,128)(2,1)S(1)} %get-tuple-element.28), channel_id=1, source_target_pairs={{0,8},{4,12},{8,0},{12,4},{1,9},{5,13},{9,1},{13,5},{2,10},{6,14},... | collective-permute-start | bytes 393224 | tf_op jit(solution)/shard_map/ppermute | solution.py:36
  138.2 7.2 %collective-permute-start.4 = (bf16[128,512]{1,0:T(8,128)(2,1)S(1)}, bf16[128,512]{1,0:T(8,128)(2,1)S(1)}, u32[]{:S(2)}, u32[]{:S(2)}) collective-permute-start(bf16[128,512]{1,0:T(8,128)(2,1)S(1)} %get-tuple-element.29), channel_id=1, source_target_pairs={{0,12},{4,8},{8,4},{12,0},{1,13},{5,9},{9,5},{13,1},{2,14},{6,10},... | collective-permute-start | bytes 393224 | tf_op jit(solution)/shard_map/ppermute | solution.py:36
  146.1 11.4 %collective-permute-start.5 = (f32[32,512]{1,0:T(8,128)S(1)}, f32[32,512]{1,0:T(8,128)S(1)}, u32[]{:S(2)}, u32[]{:S(2)}) collective-permute-start(f32[32,512]{1,0:T(8,128)S(1)} %get-tuple-element.31), channel_id=1, source_target_pairs={{0,1},{1,0},{2,3},{3,2},{4,5},{5,4},{6,7},{7,6},{8,9},{9,8},{10,11... | collective-permute-start | bytes 196616 | tf_op jit(solution)/shard_map/ppermute | solution.py:36
  150.1 8.9 %collective-permute-start.6 = (f32[32,512]{1,0:T(8,128)S(1)}, f32[32,512]{1,0:T(8,128)S(1)}, u32[]{:S(2)}, u32[]{:S(2)}) collective-permute-start(f32[32,512]{1,0:T(8,128)S(1)} %get-tuple-element.32), channel_id=1, source_target_pairs={{0,2},{1,3},{2,0},{3,1},{4,6},{5,7},{6,4},{7,5},{8,10},{9,11},{10,... | collective-permute-start | bytes 196616 | tf_op jit(solution)/shard_map/ppermute | solution.py:36
  154.5 7.9 %collective-permute-start.7 = (f32[32,512]{1,0:T(8,128)S(1)}, f32[32,512]{1,0:T(8,128)S(1)}, u32[]{:S(2)}, u32[]{:S(2)}) collective-permute-start(f32[32,512]{1,0:T(8,128)S(1)} %get-tuple-element.33), channel_id=1, source_target_pairs={{0,3},{1,2},{2,1},{3,0},{4,7},{5,6},{6,5},{7,4},{8,11},{9,10},{10,... | collective-permute-start | bytes 196616 | tf_op jit(solution)/shard_map/ppermute | solution.py:36
  162.4 5.5 %collective-permute-start.8 = (bf16[32,256]{1,0:T(8,128)(2,1)S(1)}, bf16[32,256]{1,0:T(8,128)(2,1)S(1)}, u32[]{:S(2)}, u32[]{:S(2)}) collective-permute-start(bf16[32,256]{1,0:T(8,128)(2,1)S(1)} %get-tuple-element.35), channel_id=1, source_target_pairs={{0,16},{16,0},{1,17},{17,1},{2,18},{18,2},{3,19},{19,3},{4,20},{20... | collective-permute-start | bytes 49160 | tf_op jit(solution)/shard_map/ppermute | solution.py:36
  167.9 11.4 %collective-permute-start.10 = (bf16[32,512]{1,0:T(8,128)(2,1)S(1)}, bf16[32,512]{1,0:T(8,128)(2,1)S(1)}, u32[]{:S(2)}, u32[]{:S(2)}) collective-permute-start(bf16[32,512]{1,0:T(8,128)(2,1)S(1)} %constant_dynamic-update-slice_fusion.block0), channel_id=1, source_target_pairs={{0,2},{1,3},{2,0},{3,1},{4,6},{5,7},{6,4},{7,5},{8,10},{9,11},{10,... | collective-permute-start | bytes 98312 | tf_op jit(solution)/shard_map/ppermute | solution.py:36
  172.7 6.8 %collective-permute-start.11 = (bf16[32,512]{1,0:T(8,128)(2,1)S(1)}, bf16[32,512]{1,0:T(8,128)(2,1)S(1)}, u32[]{:S(2)}, u32[]{:S(2)}) collective-permute-start(bf16[32,512]{1,0:T(8,128)(2,1)S(1)} %constant_dynamic-update-slice_fusion.block0), channel_id=1, source_target_pairs={{0,3},{1,2},{2,1},{3,0},{4,7},{5,6},{6,5},{7,4},{8,11},{9,10},{10,... | collective-permute-start | bytes 98312 | tf_op jit(solution)/shard_map/ppermute | solution.py:36
  177.0 5.6 %collective-permute-start.9 = (bf16[32,512]{1,0:T(8,128)(2,1)S(1)}, bf16[32,512]{1,0:T(8,128)(2,1)S(1)}, u32[]{:S(2)}, u32[]{:S(2)}) collective-permute-start(bf16[32,512]{1,0:T(8,128)(2,1)S(1)} %constant_dynamic-update-slice_fusion.block0), channel_id=1, source_target_pairs={{0,1},{1,0},{2,3},{3,2},{4,5},{5,4},{6,7},{7,6},{8,9},{9,8},{10,11... | collective-permute-start | bytes 98312 | tf_op jit(solution)/shard_map/ppermute | solution.py:36
  183.2 9.6 %collective-permute-start.12 = (bf16[128,512]{1,0:T(8,128)(2,1)S(1)}, bf16[128,512]{1,0:T(8,128)(2,1)S(1)}, u32[]{:S(2)}, u32[]{:S(2)}) collective-permute-start(bf16[128,512]{1,0:T(8,128)(2,1)S(1)} %shard_map.50.g0), channel_id=1, source_target_pairs={{0,4},{4,0},{8,12},{12,8},{1,5},{5,1},{9,13},{13,9},{2,6},{6,2},{1... | collective-permute-start | bytes 393224 | tf_op jit(solution)/shard_map/ppermute | solution.py:36
  186.4 8.4 %collective-permute-start.13 = (bf16[128,512]{1,0:T(8,128)(2,1)S(1)}, bf16[128,512]{1,0:T(8,128)(2,1)S(1)}, u32[]{:S(2)}, u32[]{:S(2)}) collective-permute-start(bf16[128,512]{1,0:T(8,128)(2,1)S(1)} %shard_map.50.g0), channel_id=1, source_target_pairs={{0,8},{4,12},{8,0},{12,4},{1,9},{5,13},{9,1},{13,5},{2,10},{6,14},... | collective-permute-start | bytes 393224 | tf_op jit(solution)/shard_map/ppermute | solution.py:36
  190.3 7.5 %collective-permute-start.14 = (bf16[128,512]{1,0:T(8,128)(2,1)S(1)}, bf16[128,512]{1,0:T(8,128)(2,1)S(1)}, u32[]{:S(2)}, u32[]{:S(2)}) collective-permute-start(bf16[128,512]{1,0:T(8,128)(2,1)S(1)} %shard_map.50.g0), channel_id=1, source_target_pairs={{0,12},{4,8},{8,4},{12,0},{1,13},{5,9},{9,5},{13,1},{2,14},{6,10},... | collective-permute-start | bytes 393224 | tf_op jit(solution)/shard_map/ppermute | solution.py:36
  197.8 7.4 %collective-permute-start.15 = (bf16[512,896]{1,0:T(8,128)(2,1)S(1)}, bf16[512,896]{1,0:T(8,128)(2,1)S(1)}, u32[]{:S(2)}, u32[]{:S(2)}) collective-permute-start(bf16[512,896]{1,0:T(8,128)(2,1)S(1)} %bitcast.9), channel_id=1, source_target_pairs={{0,16},{16,0},{1,17},{17,1},{2,18},{18,2},{3,19},{19,3},{4,20},{20... | collective-permute-start | bytes 2752520 | tf_op jit(solution)/shard_map/ppermute | solution.py:36
Sparse Core Ops, SparseCore 0:
  32.0 33.5 all-gather.1

commit v7 on v6

v7 whole, which is shorter than its diff:
```python
import functools

import jax
import jax.numpy as jnp
from jax import lax
from jax.experimental import pallas as pl
from jax.experimental.pallas import tpu as pltpu
from jax.sharding import Mesh, PartitionSpec as P

SEQS = 2
SEQ_LEN = 512
OUT = ("z", "ylo", "core")
INP = ("x", "yhi")
CHIPS = ("z", "ylo")
BF16 = jnp.bfloat16
F32 = jnp.float32
VMEM = pl.BlockSpec(memory_space=pltpu.VMEM)
SMEM = pl.BlockSpec(memory_space=pltpu.SMEM)
ANY = pl.BlockSpec(memory_space=pl.ANY)


def kernel_call(body, shapes, args, flops=0, scalars=0, unread=0, scratch=()):
    moved = sum(a.size * a.dtype.itemsize for a in args) + sum(s.size * s.dtype.itemsize for s in shapes)
    many = len(shapes) > 1
    return pl.pallas_call(
        body,
        out_shape=shapes if many else shapes[0],
        in_specs=[SMEM] * scalars + [VMEM] * (len(args) - scalars - unread) + [ANY] * unread,
        out_specs=[VMEM] * len(shapes) if many else VMEM,
        scratch_shapes=[pltpu.VMEM(s.shape, s.dtype) for s in scratch],
        compiler_params=pltpu.CompilerParams(vmem_limit_bytes=40 * 2**20),
        cost_estimate=pl.CostEstimate(flops=flops, bytes_accessed=moved, transcendentals=0),
    )(*args)


def swap(value, axis, flip):
    size = lax.axis_size(axis)
    return lax.ppermute(value, axis, [(s, s ^ flip) for s in range(size)])


def act_dot_kernel(acts, basis0, basis1, order, out, done):
    blocks, block = out.shape[0], out.shape[1]
    total = 0.0
    for core, basis in ((0, basis0), (1, basis1)):
        rows = jnp.concatenate([acts[2 * x + core] for x in range(4)])
        total += jnp.dot(rows, basis[...], preferred_element_type=F32)
    out[...] = total.astype(BF16).reshape(out.shape)
    done[...] = jnp.zeros_like(done)


CORE, X_LOW, X_HIGH, YHI_LOW, YHI_HIGH = range(5)


def half_rows(bit, ref, rows):
    return ref[pl.ds(pl.multiple_of(bit * rows, rows), rows), :]


def grad_dot_kernel(at, rows, own, other, keep, give):
    columns = own.shape[1]
    tokens = keep.shape[0]
    for bit, out in ((at[X_HIGH], keep), (1 - at[X_HIGH], give)):
        block = half_rows(bit, rows, tokens)
        for side, basis in ((0, own), (1, other)):
            part = jnp.dot(block, basis[...], preferred_element_type=F32)
            out[:, side * columns:(side + 1) * columns] = part.astype(out.dtype)


def sum_halves_kernel(which, at, mine, got, order, keep, give, total):
    total[...] = mine[...] + got[...].astype(F32)
    for bit, out in ((at[which], keep), (1 - at[which], give)):
        out[...] = half_rows(bit, total, out.shape[0]).astype(out.dtype)


def sum_columns_kernel(mine, got, keep, give):
    rounded = (mine[...] + got[...]).astype(BF16)
    columns = keep.shape[1]
    keep[...] = rounded[:, :columns]
    give[...] = rounded[:, columns:]


def pair_kernel(which, at, mine, got, order, out):
    rows = mine.shape[0]
    for bit, block in ((at[which], mine), (1 - at[which], got)):
        out[pl.ds(pl.multiple_of(bit * rows, rows), rows), :] = block[...]


def sum_copies_kernel(parts, order, out):
    total = parts[0].astype(F32)
    for index in range(1, parts.shape[0]):
        total += parts[index].astype(F32)
    rounded = total.astype(BF16)
    for index in range(out.shape[0]):
        out[index] = rounded


def square_kernel(at, grad_here, grad_far, act_mine, act_theirs, out):
    columns = out.shape[0]
    half = act_mine.shape[0] // SEQS
    total = 0.0
    for bit, grad in ((at[X_HIGH], grad_here), (1 - at[X_HIGH], grad_far)):
        rotated = 0.0
        for side, act in ((0, act_mine), (1, act_theirs)):
            rotated += lax.dot_general(
                grad[:, side * columns:(side + 1) * columns], half_rows(bit, act, half),
                (((0,), (0,)), ((), ())), preferred_element_type=F32,
            )
        total = total + rotated * rotated
    out[...] = total * (1.0 / (SEQS * SEQ_LEN))


def both(index, axis, own):
    other = swap(own, axis, 1)
    return jnp.where(index == 0, own, other), jnp.where(index == 0, other, own)


def shards(grads, acts, grad_basis, act_basis):
    core, x, yhi = (lax.axis_index(axis) for axis in ("core", "x", "yhi"))
    at = jnp.stack([core, x % 2, x // 2, yhi % 2, yhi // 2]).astype(jnp.int32)
    half, features = acts.shape[0] // 2, acts.shape[1]
    tokens, eig = 16 * half, act_basis.shape[1]
    rows, columns = grads.shape[0], grad_basis.shape[1]
    shape = jax.ShapeDtypeStruct

    copies = jnp.broadcast_to(acts.reshape(2, 1, half, features), (2, 4, half, features))
    act_yhi = lax.all_to_all(copies.reshape(8, half, features), ("core", "yhi"), 0, 0, tiled=True)
    act_basis0, act_basis1 = both(core, "core", act_basis)
    grad_basis_other = swap(grad_basis, "core", 1)

    act_yhi, grads = lax.optimization_barrier((act_yhi, grads))
    act_rows = lax.all_gather(act_yhi.reshape(8 * half, features), "x", axis=0, tiled=True)
    grad_copies = jnp.broadcast_to(grads[None], (16, *grads.shape))
    grad_rows = lax.all_to_all(grad_copies, CHIPS, 0, 0, tiled=True).reshape(tokens, -1)

    wide = lambda count, kind: shape((count * rows, 2 * columns), kind)
    mine, give = kernel_call(
        grad_dot_kernel,
        [wide(8, F32), wide(8, BF16)],
        [at, grad_rows, grad_basis, grad_basis_other],
        flops=2 * tokens * grads.shape[1] * 2 * columns,
        scalars=1,
    )

    blocks = shape((16, half, eig), BF16)
    act_partial, done = kernel_call(
        act_dot_kernel,
        [blocks, shape((8, 128), F32)],
        [act_rows.reshape(8, 4 * half, features), act_basis0, act_basis1, give],
        flops=2 * tokens * 2 * features * eig,
        unread=1,
    )
    act_parts = lax.all_to_all(act_partial, CHIPS, 0, 0, tiled=True)

    for axis, flip, which, count, kind in (("x", 3, X_LOW, 4, BF16), ("x", 1, YHI_HIGH, 2, F32), ("yhi", 3, YHI_LOW, 1, F32)):
        mine, give = kernel_call(
            functools.partial(sum_halves_kernel, which),
            [wide(count, F32), wide(count, kind)],
            [at, mine, swap(give, axis, flip), done],
            scalars=1,
            unread=1,
            scratch=[wide(2 * count, F32)],
        )
    narrow = shape((rows, columns), BF16)
    keep, send = kernel_call(sum_columns_kernel, [narrow, narrow], [mine, swap(give, "yhi", 1)])

    act_copies = kernel_call(sum_copies_kernel, [blocks], [act_parts, mine], unread=1)
    act_mine = lax.all_to_all(act_copies, CHIPS, 0, 0, tiled=True).reshape(tokens, eig)
    here = jnp.concatenate([keep, swap(send, "core", 1)], axis=1)
    for axis, flip, which, count in (("yhi", 1, YHI_LOW, 2), ("yhi", 3, YHI_HIGH, 4), ("x", 1, X_LOW, 8)):
        here = kernel_call(
            functools.partial(pair_kernel, which),
            [wide(count, BF16)],
            [at, here, swap(here, axis, flip), act_copies],
            scalars=1,
            unread=1,
        )
    act_mine, far = lax.optimization_barrier((act_mine, swap(here, "x", 3)))
    act_theirs = swap(act_mine, "core", 1)

    return kernel_call(
        square_kernel,
        [shape((columns, eig), F32)],
        [at, here, far, act_mine, act_theirs],
        flops=2 * 2 * tokens * columns * eig,
        scalars=1,
    )


def solution(mesh):
    split = Mesh(mesh.devices.reshape(8, 2, 2, 4, 4), OUT + INP)
    return jax.shard_map(
        shards,
        mesh=split,
        in_specs=(P(OUT, INP), P(INP, OUT), P(INP, OUT), P(OUT, INP)),
        out_specs=P(OUT, INP),
        check_vma=False,
    )
```

time: 216 us -> 183 us (0.85)
  blocking collectives: 55.9 us -> 24.4 us
  waiting for transfers between devices: 63.5 us -> 49.8 us
  starting transfers between devices: 67.8 us -> 73.6 us
  Pallas kernels: 8.11 us -> 10.9 us
    all_to_all x1 -> x0, blocking collectives: 31.7 us -> none  [shards(): act_parts = lax.all_to_all(act_partial, CHIPS, 0, 0, tiled=True)]
    all_gather x1, waiting for transfers between devices: 26 us -> 5.57 us  [shards(): lax.all_gather(act_yhi.reshape(8 * half, features), 'x', axis=0, tiled=True)]
    ppermute x16 -> x12, waiting for transfers between devices: 23.5 us -> 35.4 us  [swap(): return lax.ppermute(value, axis, [(s, s ^ flip) for s in range(size)])]
    ppermute x16 -> x12, starting transfers between devices: 57.2 us -> 48.4 us  [swap(): return lax.ppermute(value, axis, [(s, s ^ flip) for s in range(size)])]
    all_to_all x0 -> x1, starting transfers between devices: none -> 8.12 us  [shards(): act_parts = lax.all_to_all(act_partial, CHIPS, 0, 0, tiled=True)]
    all_to_all x1, waiting for transfers between devices: 13.9 us -> 8.78 us  [shards(): lax.all_to_all(grad_copies, CHIPS, 0, 0, tiled=True).reshape(tokens, -1)]
    all_to_all x1, starting transfers between devices: 5.1 us -> 9.01 us  [shards(): lax.all_to_all(grad_copies, CHIPS, 0, 0, tiled=True).reshape(tokens, -1)]
    pallas_call x7 -> x11, Pallas kernels: 8.11 us -> 10.9 us  [kernel_call(): pl.pallas_call(body, out_shape=shapes if many else shapes[0], in_specs=[S...]
  transfers between devices with their start and end apart: 19 -> 16, of which waited for: 14 -> 12; matrix products, arithmetic and copies ran while one was open for 1% -> 2% of each run, Pallas kernels for 2% -> 2%
where the time goes in v7:
time: 183 us; the launch traced here: 181 us
  starting transfers between devices  73.6 us (40%)
  waiting for transfers between devices  49.8 us (27%)
  blocking collectives  24.4 us (13%)
  between operations  13.7 us (7%)
  Pallas kernels  10.9 us (6%)
  local copies, waits for them, and re-layouts  4.92 us (3%)
  other arithmetic  3.53 us (2%)
    ppermute x12, starting transfers between devices, swap(): return lax.ppermute(value, axis, [(s, s ^ flip) for s in range(size)])  48.4 us
    ppermute x12, waiting for transfers between devices, swap(): return lax.ppermute(value, axis, [(s, s ^ flip) for s in range(size)])  35.4 us
    all_to_all x1, blocking collectives, shards(): lax.all_to_all(copies.reshape(8, half, features), ('core', 'yhi'), 0, 0,...  24.4 us
    pallas_call x11, Pallas kernels, kernel_call(): pl.pallas_call(body, out_shape=shapes if many else shapes[0], in_specs=[S...  10.9 us
    all_to_all x1, starting transfers between devices, shards(): lax.all_to_all(grad_copies, CHIPS, 0, 0, tiled=True).reshape(tokens, -1)  9.01 us
    all_to_all x1, waiting for transfers between devices, shards(): lax.all_to_all(grad_copies, CHIPS, 0, 0, tiled=True).reshape(tokens, -1)  8.78 us
    all_to_all x1, starting transfers between devices, shards(): lax.all_to_all(act_copies, CHIPS, 0, 0, tiled=True).reshape(tokens, eig)  8.13 us
    all_to_all x1, starting transfers between devices, shards(): act_parts = lax.all_to_all(act_partial, CHIPS, 0, 0, tiled=True)  8.12 us
  transfers between devices with their start and end apart: 16, of which 12 were waited for; matrix products, arithmetic and copies ran while one was open for 2% of the time, Pallas kernels for 2%

profile of v7, /device:TPU:1, one launch (start us, length us, event | category | flops | bytes accessed | tf_op | source)
XLA Modules:
  0.0 180.8 jit_solution(449438628290465051)
XLA Ops:
  6.5 0.0 copy-start.4
  6.5 0.0 copy-start.3
  6.5 0.0 all-gather.2.cloned.1.call-start
  6.5 1.1 broadcast_in_dim.14
  7.6 0.0 copy-start.1
  7.6 24.4 %all_to_all.20 = bf16[8,32,896]{2,1,0:T(8,128)(2,1)} all-to-all(bf16[8,32,896]{2,1,0:T(8,128)(2,1)S(1)} %bitcast.16), channel_id=1, replica_groups=mesh['z'=8,'ylo'=2,'core'=2,'x'=4,'yhi'=4] {'core','yhi'}, dimensions={0} | all-to-all | bytes 917504 | tf_op jit(solution)/shard_map/all_to_all | solution.py:125
  32.0 0.0 all-gather.2.cloned.1.call-update
  32.0 0.0 copy-done.3
  32.0 2.3 %collective-permute-start.2 = (bf16[896,896]{1,0:T(8,128)(2,1)S(1)}, bf16[896,896]{1,0:T(8,128)(2,1)}, u32[]{:S(2)}, u32[]{:S(2)}) collective-permute-start(bf16[896,896]{1,0:T(8,128)(2,1)S(1)} %copy-done.3), channel_id=1, source_target_pairs={{0,16},{16,0},{1,17},{17,1},{2,18},{18,2},{3,19},{19,3},{4,20},{20... | collective-permute-start | bytes 4816904 | tf_op jit(solution)/shard_map/ppermute | solution.py:38
  34.3 0.0 copy-done.4
  34.3 0.8 broadcast_in_dim.15
  35.2 9.0 %all-to-all-start.1 = ((bf16[16,32,512]{2,1,0:T(8,128)(2,1)}), bf16[16,32,512]{2,1,0:T(8,128)(2,1)S(1)}, u32[]{:S(2)}, u32[]{:S(2)}) async-start(bf16[16,32,512]{2,1,0:T(8,128)(2,1)} %broadcast_in_dim.15), calls=%async_computation.1 | async-start | bytes 1048576 | tf_op jit(solution)/shard_map/all_to_all | solution.py:132
  44.2 0.0 copy-done.1
  44.2 2.6 %collective-permute-start = (bf16[512,256]{1,0:T(8,128)(2,1)S(1)}, bf16[512,256]{1,0:T(8,128)(2,1)S(1)}, u32[]{:S(2)}, u32[]{:S(2)}) collective-permute-start(bf16[512,256]{1,0:T(8,128)(2,1)S(1)} %copy-done.1), channel_id=1, source_target_pairs={{0,16},{16,0},{1,17},{17,1},{2,18},{18,2},{3,19},{19,3},{4,20},{20... | collective-permute-start | bytes 786440 | tf_op jit(solution)/shard_map/ppermute | solution.py:38
  46.8 0.1 stack.23.at
  46.9 0.0 collective-permute-done.2
  46.9 3.5 %broadcast_select_fusion = (bf16[896,896]{1,0:T(8,128)(2,1)S(1)}, bf16[896,896]{1,0:T(8,128)(2,1)}) fusion(bf16[896,896]{1,0:T(8,128)(2,1)} %collective-permute-done.2, bf16[896,896]{1,0:T(8,128)(2,1)} %param.7, pred[]{:T(512)S(6)} %eq.7), kind=kLoop, calls=%fused_computation | loop fusion | flops 1605632 | bytes 6422529 | tf_op jit(solution)/shard_map/jit(_where)/select_n | solution.py:113
  50.4 0.0 collective-permute-done.other
  50.4 8.8 %all-to-all-done.1 = bf16[16,32,512]{2,1,0:T(8,128)(2,1)S(1)} async-done(((bf16[16,32,512]{2,1,0:T(8,128)(2,1)}), bf16[16,32,512]{2,1,0:T(8,128)(2,1)S(1)}, u32[]{:S(2)}, u32[]{:S(2)}) %all-to-all-start.1) | async-done | bytes 524320 | tf_op jit(solution)/shard_map/all_to_all | solution.py:132
  59.2 1.0 shard_map.46
  60.2 5.6 %all-gather.2.cloned.1.call-done = bf16[1024,896]{1,0:T(8,128)(2,1)} async-done(((bf16[256,896]{1,0:T(8,128)(2,1)}), bf16[1024,896]{1,0:T(8,128)(2,1)}) %all-gather.2.cloned.1.call-update) | async-done | bytes 1835024 | tf_op jit(solution)/shard_map/all_gather | solution.py:130
  65.8 0.0 copy-start
  65.8 1.4 copy-done
  67.2 0.0 copy-start.2
  67.2 1.5 copy-done.2
  68.7 3.2 %shard_map.47 = (bf16[16,32,896]{2,1,0:T(8,128)(2,1)}, f32[8,128]{1,0:T(8,128)S(1)}) custom-call(bf16[8,128,896]{2,1,0:T(8,128)(2,1)S(1)} %bitcast.14, bf16[896,896]{1,0:T(8,128)(2,1)S(1)} %copy-done, bf16[896,896]{1,0:T(8,128)(2,1)S(1)} %get-tuple-element.37.basis1, bf16[256,512]{1,0:T(8,128)(2,1)S(1)} %get-tuple-element.23.order), custom_call_target="tpu_custom_call" | custom-call | flops 1644167168 | bytes 6230016 | tf_op jit(solution)/shard_map/pallas_call | solution.py:25
  71.9 8.1 %all-to-all-start.2 = ((bf16[16,32,896]{2,1,0:T(8,128)(2,1)}), bf16[16,32,896]{2,1,0:T(8,128)(2,1)S(1)}, u32[]{:S(2)}, u32[]{:S(2)}) async-start(bf16[16,32,896]{2,1,0:T(8,128)(2,1)} %get-tuple-element.34), calls=%async_computation.2 | async-start | bytes 1835008 | tf_op jit(solution)/shard_map/all_to_all | solution.py:151
  80.0 2.5 %collective-permute-start.1 = (bf16[256,512]{1,0:T(8,128)(2,1)S(1)}, bf16[256,512]{1,0:T(8,128)(2,1)S(1)}, u32[]{:S(2)}, u32[]{:S(2)}) collective-permute-start(bf16[256,512]{1,0:T(8,128)(2,1)S(1)} %get-tuple-element.23.order), channel_id=1, source_target_pairs={{0,12},{4,8},{8,4},{12,0},{1,13},{5,9},{9,5},{13,1},{2,14},{6,10},... | collective-permute-start | bytes 786440 | tf_op jit(solution)/shard_map/ppermute | solution.py:38
  82.5 7.5 %collective-permute-done.1.got = bf16[256,512]{1,0:T(8,128)(2,1)S(1)} collective-permute-done((bf16[256,512]{1,0:T(8,128)(2,1)S(1)}, bf16[256,512]{1,0:T(8,128)(2,1)S(1)}, u32[]{:S(2)}, u32[]{:S(2)}) %collective-permute-start.1) | collective-permute-done | bytes 262176 | tf_op jit(solution)/shard_map/ppermute | solution.py:38
  90.0 0.6 shard_map.48
  90.6 1.9 %collective-permute-start.3 = (bf16[128,512]{1,0:T(8,128)(2,1)S(1)}, bf16[128,512]{1,0:T(8,128)(2,1)S(1)}, u32[]{:S(2)}, u32[]{:S(2)}) collective-permute-start(bf16[128,512]{1,0:T(8,128)(2,1)S(1)} %get-tuple-element.27), channel_id=1, source_target_pairs={{0,4},{4,0},{8,12},{12,8},{1,5},{5,1},{9,13},{13,9},{2,6},{6,2},{1... | collective-permute-start | bytes 393224 | tf_op jit(solution)/shard_map/ppermute | solution.py:38
  92.5 4.1 %collective-permute-done.3.got = bf16[128,512]{1,0:T(8,128)(2,1)S(1)} collective-permute-done((bf16[128,512]{1,0:T(8,128)(2,1)S(1)}, bf16[128,512]{1,0:T(8,128)(2,1)S(1)}, u32[]{:S(2)}, u32[]{:S(2)}) %collective-permute-start.3) | collective-permute-done | bytes 131104 | tf_op jit(solution)/shard_map/ppermute | solution.py:38
  96.6 0.6 shard_map.49
  97.2 4.4 %collective-permute-start.4 = (f32[64,512]{1,0:T(8,128)S(1)}, f32[64,512]{1,0:T(8,128)S(1)}, u32[]{:S(2)}, u32[]{:S(2)}) collective-permute-start(f32[64,512]{1,0:T(8,128)S(1)} %get-tuple-element.29), channel_id=1, source_target_pairs={{0,3},{1,2},{2,1},{3,0},{4,7},{5,6},{6,5},{7,4},{8,11},{9,10},{10,... | collective-permute-start | bytes 393224 | tf_op jit(solution)/shard_map/ppermute | solution.py:38
  101.6 3.6 %collective-permute-done.4.got = f32[64,512]{1,0:T(8,128)S(1)} collective-permute-done((f32[64,512]{1,0:T(8,128)S(1)}, f32[64,512]{1,0:T(8,128)S(1)}, u32[]{:S(2)}, u32[]{:S(2)}) %collective-permute-start.4) | collective-permute-done | bytes 131104 | tf_op jit(solution)/shard_map/ppermute | solution.py:38
  105.2 0.6 shard_map.50
  105.8 0.0 all-to-all-done.2.parts
  105.8 1.1 shard_map.52.order
  106.9 8.1 %all-to-all-start.3 = ((bf16[16,32,896]{2,1,0:T(8,128)(2,1)}), bf16[16,32,896]{2,1,0:T(8,128)(2,1)S(1)}, u32[]{:S(2)}, u32[]{:S(2)}) async-start(bf16[16,32,896]{2,1,0:T(8,128)(2,1)} %shard_map.52.order), calls=%async_computation.3 | async-start | bytes 1835008 | tf_op jit(solution)/shard_map/all_to_all | solution.py:166
  115.0 3.4 %collective-permute-start.5 = (f32[32,512]{1,0:T(8,128)S(1)}, f32[32,512]{1,0:T(8,128)S(1)}, u32[]{:S(2)}, u32[]{:S(2)}) collective-permute-start(f32[32,512]{1,0:T(8,128)S(1)} %get-tuple-element.31), channel_id=1, source_target_pairs={{0,1},{1,0},{2,3},{3,2},{4,5},{5,4},{6,7},{7,6},{8,9},{9,8},{10,11... | collective-permute-start | bytes 196616 | tf_op jit(solution)/shard_map/ppermute | solution.py:38
  118.5 4.5 %collective-permute-done.5.got = f32[32,512]{1,0:T(8,128)S(1)} collective-permute-done((f32[32,512]{1,0:T(8,128)S(1)}, f32[32,512]{1,0:T(8,128)S(1)}, u32[]{:S(2)}, u32[]{:S(2)}) %collective-permute-start.5) | collective-permute-done | bytes 65568 | tf_op jit(solution)/shard_map/ppermute | solution.py:38
  122.9 9.2 %collective-permute-start.6 = (bf16[32,256]{1,0:T(8,128)(2,1)S(1)}, bf16[32,256]{1,0:T(8,128)(2,1)S(1)}, u32[]{:S(2)}, u32[]{:S(2)}) collective-permute-start(bf16[32,256]{1,0:T(8,128)(2,1)S(1)} %get-tuple-element.33), channel_id=1, source_target_pairs={{0,16},{16,0},{1,17},{17,1},{2,18},{18,2},{3,19},{19,3},{4,20},{20... | collective-permute-start | bytes 49160 | tf_op jit(solution)/shard_map/ppermute | solution.py:38
  132.2 0.8 collective-permute-done.6
  133.0 5.0 %collective-permute-start.7 = (bf16[32,512]{1,0:T(8,128)(2,1)S(1)}, bf16[32,512]{1,0:T(8,128)(2,1)S(1)}, u32[]{:S(2)}, u32[]{:S(2)}) collective-permute-start(bf16[32,512]{1,0:T(8,128)(2,1)S(1)} %constant_dynamic-update-slice_fusion.mine), channel_id=1, source_target_pairs={{0,1},{1,0},{2,3},{3,2},{4,5},{5,4},{6,7},{7,6},{8,9},{9,8},{10,11... | collective-permute-start | bytes 98312 | tf_op jit(solution)/shard_map/ppermute | solution.py:38
  138.0 1.6 collective-permute-done.7.got
  139.6 0.5 shard_map.53.mine
  140.1 6.2 %collective-permute-start.8 = (bf16[64,512]{1,0:T(8,128)(2,1)S(1)}, bf16[64,512]{1,0:T(8,128)(2,1)S(1)}, u32[]{:S(2)}, u32[]{:S(2)}) collective-permute-start(bf16[64,512]{1,0:T(8,128)(2,1)S(1)} %shard_map.53.mine), channel_id=1, source_target_pairs={{0,3},{1,2},{2,1},{3,0},{4,7},{5,6},{6,5},{7,4},{8,11},{9,10},{10,... | collective-permute-start | bytes 196616 | tf_op jit(solution)/shard_map/ppermute | solution.py:38
  146.3 1.7 collective-permute-done.8.got
  148.0 0.6 shard_map.54.mine
  148.6 1.9 %collective-permute-start.9 = (bf16[128,512]{1,0:T(8,128)(2,1)S(1)}, bf16[128,512]{1,0:T(8,128)(2,1)S(1)}, u32[]{:S(2)}, u32[]{:S(2)}) collective-permute-start(bf16[128,512]{1,0:T(8,128)(2,1)S(1)} %shard_map.54.mine), channel_id=1, source_target_pairs={{0,4},{4,0},{8,12},{12,8},{1,5},{5,1},{9,13},{13,9},{2,6},{6,2},{1... | collective-permute-start | bytes 393224 | tf_op jit(solution)/shard_map/ppermute | solution.py:38
  150.5 3.8 %collective-permute-done.9.got = bf16[128,512]{1,0:T(8,128)(2,1)S(1)} collective-permute-done((bf16[128,512]{1,0:T(8,128)(2,1)S(1)}, bf16[128,512]{1,0:T(8,128)(2,1)S(1)}, u32[]{:S(2)}, u32[]{:S(2)}) %collective-permute-start.9) | collective-permute-done | bytes 131104 | tf_op jit(solution)/shard_map/ppermute | solution.py:38
  154.3 0.6 shard_map.55.grad_here
  154.8 2.4 %collective-permute-start.10 = (bf16[256,512]{1,0:T(8,128)(2,1)S(1)}, bf16[256,512]{1,0:T(8,128)(2,1)S(1)}, u32[]{:S(2)}, u32[]{:S(2)}) collective-permute-start(bf16[256,512]{1,0:T(8,128)(2,1)S(1)} %shard_map.55.grad_here), channel_id=1, source_target_pairs={{0,12},{4,8},{8,4},{12,0},{1,13},{5,9},{9,5},{13,1},{2,14},{6,10},... | collective-permute-start | bytes 786440 | tf_op jit(solution)/shard_map/ppermute | solution.py:38
  157.3 5.9 %collective-permute-done.10.grad_far = bf16[256,512]{1,0:T(8,128)(2,1)S(1)} collective-permute-done((bf16[256,512]{1,0:T(8,128)(2,1)S(1)}, bf16[256,512]{1,0:T(8,128)(2,1)S(1)}, u32[]{:S(2)}, u32[]{:S(2)}) %collective-permute-start.10) | collective-permute-done | bytes 262176 | tf_op jit(solution)/shard_map/ppermute | solution.py:38
  163.2 0.0 all-to-all-done.3
  163.2 6.5 %collective-permute-start.11 = (bf16[512,896]{1,0:T(8,128)(2,1)S(1)}, bf16[512,896]{1,0:T(8,128)(2,1)S(1)}, u32[]{:S(2)}, u32[]{:S(2)}) collective-permute-start(bf16[512,896]{1,0:T(8,128)(2,1)S(1)} %bitcast.11), channel_id=1, source_target_pairs={{0,16},{16,0},{1,17},{17,1},{2,18},{18,2},{3,19},{19,3},{4,20},{20... | collective-permute-start | bytes 2752520 | tf_op jit(solution)/shard_map/ppermute | solution.py:38
  169.7 2.1 %collective-permute-done.11.act_theirs = bf16[512,896]{1,0:T(8,128)(2,1)S(1)} collective-permute-done((bf16[512,896]{1,0:T(8,128)(2,1)S(1)}, bf16[512,896]{1,0:T(8,128)(2,1)S(1)}, u32[]{:S(2)}, u32[]{:S(2)}) %collective-permute-start.11) | collective-permute-done | bytes 917536 | tf_op jit(solution)/shard_map/ppermute | solution.py:38
  171.8 2.2 %shard_map.56 = f32[256,896]{1,0:T(8,128)} custom-call(s32[5]{0:T(128)S(1)} %stack.23.at, bf16[256,512]{1,0:T(8,128)(2,1)S(1)} %shard_map.55.grad_here, bf16[256,512]{1,0:T(8,128)(2,1)S(1)} %collective-permute-done.10.grad_far, bf16[512,896]{1,0:T(8,128)(2,1)S(1)} %bitcast.12, bf16[512,896]{1,0:T(8,128)(2,1)S(1)} %collective-permute-done.11.act_theirs), custom_call_target="tpu_custom_call" | custom-call | flops 469762048 | bytes 3276820 | tf_op jit(solution)/shard_map/pallas_call | solution.py:25
  (3 shorter events, 0.0 us)
Async XLA Ops:
  6.5 27.8 %copy-start.4 = (bf16[32,512]{1,0:T(8,128)(2,1)S(1)}, bf16[32,512]{1,0:T(8,128)(2,1)}, u32[]{:S(2)}) copy-start(bf16[32,512]{1,0:T(8,128)(2,1)} %param.4) | copy-start | bytes 98308
  6.5 25.5 %copy-start.3 = (bf16[896,896]{1,0:T(8,128)(2,1)S(1)}, bf16[896,896]{1,0:T(8,128)(2,1)}, u32[]{:S(2)}) copy-start(bf16[896,896]{1,0:T(8,128)(2,1)} %param.7) | copy-start | bytes 4816900
  6.5 59.2 %all-gather.2.cloned.1.call-start = ((), (), s32[]{:S(2)}) async-start(), calls=%async_computation.4 | async-start | bytes 2293760 | tf_op jit(solution)/shard_map/all_gather | solution.py:130
  7.6 36.6 %copy-start.1 = (bf16[512,256]{1,0:T(8,128)(2,1)S(1)}, bf16[512,256]{1,0:T(8,128)(2,1)}, u32[]{:S(2)}) copy-start(bf16[512,256]{1,0:T(8,128)(2,1)} %own.1) | copy-start | bytes 786436
  32.0 14.9 %collective-permute-start.2 = (bf16[896,896]{1,0:T(8,128)(2,1)S(1)}, bf16[896,896]{1,0:T(8,128)(2,1)}, u32[]{:S(2)}, u32[]{:S(2)}) collective-permute-start(bf16[896,896]{1,0:T(8,128)(2,1)S(1)} %copy-done.3), channel_id=1, source_target_pairs={{0,16},{16,0},{1,17},{17,1},{2,18},{18,2},{3,19},{19,3},{4,20},{20... | collective-permute-start | bytes 4816904 | tf_op jit(solution)/shard_map/ppermute | solution.py:38
  35.2 24.0 %all-to-all-start.1 = ((bf16[16,32,512]{2,1,0:T(8,128)(2,1)}), bf16[16,32,512]{2,1,0:T(8,128)(2,1)S(1)}, u32[]{:S(2)}, u32[]{:S(2)}) async-start(bf16[16,32,512]{2,1,0:T(8,128)(2,1)} %broadcast_in_dim.15), calls=%async_computation.1 | async-start | bytes 1048576 | tf_op jit(solution)/shard_map/all_to_all | solution.py:132
  44.2 6.2 %collective-permute-start = (bf16[512,256]{1,0:T(8,128)(2,1)S(1)}, bf16[512,256]{1,0:T(8,128)(2,1)S(1)}, u32[]{:S(2)}, u32[]{:S(2)}) collective-permute-start(bf16[512,256]{1,0:T(8,128)(2,1)S(1)} %copy-done.1), channel_id=1, source_target_pairs={{0,16},{16,0},{1,17},{17,1},{2,18},{18,2},{3,19},{19,3},{4,20},{20... | collective-permute-start | bytes 786440 | tf_op jit(solution)/shard_map/ppermute | solution.py:38
  65.8 1.4 copy-start
  67.2 1.5 copy-start.2
  71.9 34.0 %all-to-all-start.2 = ((bf16[16,32,896]{2,1,0:T(8,128)(2,1)}), bf16[16,32,896]{2,1,0:T(8,128)(2,1)S(1)}, u32[]{:S(2)}, u32[]{:S(2)}) async-start(bf16[16,32,896]{2,1,0:T(8,128)(2,1)} %get-tuple-element.34), calls=%async_computation.2 | async-start | bytes 1835008 | tf_op jit(solution)/shard_map/all_to_all | solution.py:151
  80.0 10.0 %collective-permute-start.1 = (bf16[256,512]{1,0:T(8,128)(2,1)S(1)}, bf16[256,512]{1,0:T(8,128)(2,1)S(1)}, u32[]{:S(2)}, u32[]{:S(2)}) collective-permute-start(bf16[256,512]{1,0:T(8,128)(2,1)S(1)} %get-tuple-element.23.order), channel_id=1, source_target_pairs={{0,12},{4,8},{8,4},{12,0},{1,13},{5,9},{9,5},{13,1},{2,14},{6,10},... | collective-permute-start | bytes 786440 | tf_op jit(solution)/shard_map/ppermute | solution.py:38
  90.6 6.0 %collective-permute-start.3 = (bf16[128,512]{1,0:T(8,128)(2,1)S(1)}, bf16[128,512]{1,0:T(8,128)(2,1)S(1)}, u32[]{:S(2)}, u32[]{:S(2)}) collective-permute-start(bf16[128,512]{1,0:T(8,128)(2,1)S(1)} %get-tuple-element.27), channel_id=1, source_target_pairs={{0,4},{4,0},{8,12},{12,8},{1,5},{5,1},{9,13},{13,9},{2,6},{6,2},{1... | collective-permute-start | bytes 393224 | tf_op jit(solution)/shard_map/ppermute | solution.py:38
  97.2 8.0 %collective-permute-start.4 = (f32[64,512]{1,0:T(8,128)S(1)}, f32[64,512]{1,0:T(8,128)S(1)}, u32[]{:S(2)}, u32[]{:S(2)}) collective-permute-start(f32[64,512]{1,0:T(8,128)S(1)} %get-tuple-element.29), channel_id=1, source_target_pairs={{0,3},{1,2},{2,1},{3,0},{4,7},{5,6},{6,5},{7,4},{8,11},{9,10},{10,... | collective-permute-start | bytes 393224 | tf_op jit(solution)/shard_map/ppermute | solution.py:38
  106.9 56.3 %all-to-all-start.3 = ((bf16[16,32,896]{2,1,0:T(8,128)(2,1)}), bf16[16,32,896]{2,1,0:T(8,128)(2,1)S(1)}, u32[]{:S(2)}, u32[]{:S(2)}) async-start(bf16[16,32,896]{2,1,0:T(8,128)(2,1)} %shard_map.52.order), calls=%async_computation.3 | async-start | bytes 1835008 | tf_op jit(solution)/shard_map/all_to_all | solution.py:166
  115.0 7.9 %collective-permute-start.5 = (f32[32,512]{1,0:T(8,128)S(1)}, f32[32,512]{1,0:T(8,128)S(1)}, u32[]{:S(2)}, u32[]{:S(2)}) collective-permute-start(f32[32,512]{1,0:T(8,128)S(1)} %get-tuple-element.31), channel_id=1, source_target_pairs={{0,1},{1,0},{2,3},{3,2},{4,5},{5,4},{6,7},{7,6},{8,9},{9,8},{10,11... | collective-permute-start | bytes 196616 | tf_op jit(solution)/shard_map/ppermute | solution.py:38
  122.9 10.0 %collective-permute-start.6 = (bf16[32,256]{1,0:T(8,128)(2,1)S(1)}, bf16[32,256]{1,0:T(8,128)(2,1)S(1)}, u32[]{:S(2)}, u32[]{:S(2)}) collective-permute-start(bf16[32,256]{1,0:T(8,128)(2,1)S(1)} %get-tuple-element.33), channel_id=1, source_target_pairs={{0,16},{16,0},{1,17},{17,1},{2,18},{18,2},{3,19},{19,3},{4,20},{20... | collective-permute-start | bytes 49160 | tf_op jit(solution)/shard_map/ppermute | solution.py:38
  133.0 6.6 %collective-permute-start.7 = (bf16[32,512]{1,0:T(8,128)(2,1)S(1)}, bf16[32,512]{1,0:T(8,128)(2,1)S(1)}, u32[]{:S(2)}, u32[]{:S(2)}) collective-permute-start(bf16[32,512]{1,0:T(8,128)(2,1)S(1)} %constant_dynamic-update-slice_fusion.mine), channel_id=1, source_target_pairs={{0,1},{1,0},{2,3},{3,2},{4,5},{5,4},{6,7},{7,6},{8,9},{9,8},{10,11... | collective-permute-start | bytes 98312 | tf_op jit(solution)/shard_map/ppermute | solution.py:38
  140.1 7.9 %collective-permute-start.8 = (bf16[64,512]{1,0:T(8,128)(2,1)S(1)}, bf16[64,512]{1,0:T(8,128)(2,1)S(1)}, u32[]{:S(2)}, u32[]{:S(2)}) collective-permute-start(bf16[64,512]{1,0:T(8,128)(2,1)S(1)} %shard_map.53.mine), channel_id=1, source_target_pairs={{0,3},{1,2},{2,1},{3,0},{4,7},{5,6},{6,5},{7,4},{8,11},{9,10},{10,... | collective-permute-start | bytes 196616 | tf_op jit(solution)/shard_map/ppermute | solution.py:38
  148.6 5.7 %collective-permute-start.9 = (bf16[128,512]{1,0:T(8,128)(2,1)S(1)}, bf16[128,512]{1,0:T(8,128)(2,1)S(1)}, u32[]{:S(2)}, u32[]{:S(2)}) collective-permute-start(bf16[128,512]{1,0:T(8,128)(2,1)S(1)} %shard_map.54.mine), channel_id=1, source_target_pairs={{0,4},{4,0},{8,12},{12,8},{1,5},{5,1},{9,13},{13,9},{2,6},{6,2},{1... | collective-permute-start | bytes 393224 | tf_op jit(solution)/shard_map/ppermute | solution.py:38
  154.8 8.3 %collective-permute-start.10 = (bf16[256,512]{1,0:T(8,128)(2,1)S(1)}, bf16[256,512]{1,0:T(8,128)(2,1)S(1)}, u32[]{:S(2)}, u32[]{:S(2)}) collective-permute-start(bf16[256,512]{1,0:T(8,128)(2,1)S(1)} %shard_map.55.grad_here), channel_id=1, source_target_pairs={{0,12},{4,8},{8,4},{12,0},{1,13},{5,9},{9,5},{13,1},{2,14},{6,10},... | collective-permute-start | bytes 786440 | tf_op jit(solution)/shard_map/ppermute | solution.py:38
  163.2 8.6 %collective-permute-start.11 = (bf16[512,896]{1,0:T(8,128)(2,1)S(1)}, bf16[512,896]{1,0:T(8,128)(2,1)S(1)}, u32[]{:S(2)}, u32[]{:S(2)}) collective-permute-start(bf16[512,896]{1,0:T(8,128)(2,1)S(1)} %bitcast.11), channel_id=1, source_target_pairs={{0,16},{16,0},{1,17},{17,1},{2,18},{18,2},{3,19},{19,3},{4,20},{20... | collective-permute-start | bytes 2752520 | tf_op jit(solution)/shard_map/ppermute | solution.py:38
Sparse Core Ops, SparseCore 0:
  32.1 33.5 all-gather.1

commit v8 on v4

--- a/solution.py
+++ b/solution.py
@@ -12,16 +12,17 @@
 CHIPS = ("z", "ylo")
 BF16 = jnp.bfloat16
 F32 = jnp.float32
+SMEM = pl.BlockSpec(memory_space=pltpu.SMEM)
 VMEM = pl.BlockSpec(memory_space=pltpu.VMEM)
 
 
-def kernel_call(body, shapes, args, flops=0):
+def kernel_call(body, shapes, args, flops=0, scalars=0):
     moved = sum(a.size * a.dtype.itemsize for a in args) + sum(s.size * s.dtype.itemsize for s in shapes)
     many = len(shapes) > 1
     return pl.pallas_call(
         body,
         out_shape=shapes if many else shapes[0],
-        in_specs=[VMEM] * len(args),
+        in_specs=[SMEM] * scalars + [VMEM] * (len(args) - scalars),
         out_specs=[VMEM] * len(shapes) if many else VMEM,
         compiler_params=pltpu.CompilerParams(vmem_limit_bytes=40 * 2**20),
         cost_estimate=pl.CostEstimate(flops=flops, bytes_accessed=moved, transcendentals=0),
@@ -42,17 +43,23 @@
 
 
 def gather_yhi(mine):
-    blocks = [mine, swap(mine, "yhi", 1), swap(mine, "yhi", 2), swap(mine, "yhi", 3)]
-    rows, columns = mine.shape
-    shapes = [jax.ShapeDtypeStruct((4 * rows, columns), mine.dtype), jax.ShapeDtypeStruct((8, 128), F32)]
+    return [mine, swap(mine, "yhi", 1), swap(mine, "yhi", 2), swap(mine, "yhi", 3)]
+
+
+def stack(blocks):
+    rows, columns = blocks[0].shape
+    shapes = [jax.ShapeDtypeStruct((len(blocks) * rows, columns), BF16), jax.ShapeDtypeStruct((8, 128), F32)]
     return kernel_call(stack_kernel, shapes, blocks)
 
 
-def act_dot_kernel(act0, act1, low2, high2, act3, own, other, out, done):
+def act_dot_kernel(at, acts, last0, last1, last2, last3, own, other, out, done):
     features = own.shape[0]
-    rows = jnp.concatenate([act0[...], act1[...], low2[...], high2[...], act3[...]])
-    total = jnp.dot(rows[:, :features], own[...], preferred_element_type=F32)
-    total += jnp.dot(rows[:, features:], other[...], preferred_element_type=F32)
+    total = 0.0
+    for side, basis in ((0, own), (1, other)):
+        rows = []
+        for flip, last in enumerate((last0, last1, last2, last3)):
+            rows += [ref[..., side * features:(side + 1) * features] for ref in (acts.at[at[0] ^ flip], last)]
+        total += jnp.dot(jnp.concatenate(rows), basis[...], preferred_element_type=F32)
     out[...] = total.astype(BF16).reshape(out.shape)
     done[...] = jnp.zeros_like(done)
 
@@ -100,7 +107,7 @@
 
 
 def shards(grads, acts, grad_basis, act_basis):
-    core = lax.axis_index("core")
+    core, x = lax.axis_index("core"), lax.axis_index("x").astype(jnp.int32).reshape(1)
     half, features = acts.shape[0] // 2, acts.shape[1]
     tokens, eig = 16 * half, act_basis.shape[1]
     rows, columns = grads.shape[0], grad_basis.shape[1]
@@ -111,9 +118,10 @@
     act_basis_other = swap(act_basis, "core", 1)
     grad_basis_other = swap(grad_basis, "core", 1)
 
-    act0, done = gather_yhi(act_own)
-    act1, act3 = swap(act0, "x", 1), swap(act0, "x", 3)
-    low2, high2 = swap(act3[:2 * half], "x", 1), swap(act1[2 * half:], "x", 3)
+    *first, last = gather_yhi(act_own)
+    act_first, done = stack(first)
+    act_rows = lax.all_gather(act_first, "x")
+    lasts = [last, swap(last, "x", 1), swap(last, "x", 2), swap(last, "x", 3)]
 
     grad_copies = jnp.broadcast_to(grads[None], (16, *grads.shape))
     grad_rows = lax.all_to_all(grad_copies, CHIPS, 0, 0, tiled=True).reshape(tokens, -1)
@@ -129,15 +137,16 @@
     act_partial, done = kernel_call(
         act_dot_kernel,
         [blocks, jax.ShapeDtypeStruct((8, 128), F32)],
-        [act0, act1, low2, high2, act3, act_basis, act_basis_other],
+        [x, act_rows, *lasts, act_basis, act_basis_other],
         flops=2 * tokens * 2 * features * eig,
+        scalars=1,
     )
     act_parts = lax.all_to_all(act_partial, CHIPS, 0, 0, tiled=True)
 
     narrow = jax.ShapeDtypeStruct((rows, columns), BF16)
     grad_mine, grad_give = kernel_call(sum_split_kernel, [narrow, narrow], [done, grad_parts])
     grad_own = jnp.concatenate([grad_mine, swap(grad_give, "core", 1)], axis=1)
-    g0, _ = gather_yhi(grad_own)
+    g0, _ = stack(gather_yhi(grad_own))
     act_parts, g0 = lax.optimization_barrier((act_parts, g0))
 
     act_mine = lax.all_to_all(kernel_call(sum_copies_kernel, [blocks], [act_parts]), CHIPS, 0, 0, tiled=True)

time: 158 us -> 181 us (1.15)
  between operations: 0.31 us -> 13.6 us
  waiting for transfers between devices: 51.4 us -> 58.5 us
  local copies, waits for them, and re-layouts: 1.72 us -> 3.95 us
    all_to_all x1, waiting for transfers between devices: 0.01 us -> 8.81 us  [shards(): lax.all_to_all(grad_copies, CHIPS, 0, 0, tiled=True).reshape(tokens, -1)]
    ppermute x18 -> x17, waiting for transfers between devices: 41.8 us -> 35.4 us  [swap(): return lax.ppermute(value, axis, [(s, s ^ flip) for s in range(size)])]
    all_to_all x1, starting transfers between devices: 8.15 us -> 4.12 us  [shards(): grad_parts = lax.all_to_all(grad_partial, INP, 0, 0, tiled=True)]
    all_to_all x1, waiting for transfers between devices: 0.88 us -> 3.83 us  [shards(): act_parts = lax.all_to_all(act_partial, CHIPS, 0, 0, tiled=True)]
    ppermute x18 -> x17, starting transfers between devices: 59.2 us -> 62 us  [swap(): return lax.ppermute(value, axis, [(s, s ^ flip) for s in range(size)])]
  transfers between devices with their start and end apart: 22 -> 22, of which waited for: 13 -> 16; matrix products, arithmetic and copies ran while one was open for 0% -> 1% of each run, Pallas kernels for 4% -> 4%
where the time goes in v8:
time: 181 us; the launch traced here: 180 us
  starting transfers between devices  93.8 us (52%)
  waiting for transfers between devices  58.5 us (32%)
  between operations  13.6 us (8%)
  Pallas kernels  9.96 us (6%)
  local copies, waits for them, and re-layouts  3.95 us (2%)
    ppermute x17, starting transfers between devices, swap(): return lax.ppermute(value, axis, [(s, s ^ flip) for s in range(size)])  62 us
    ppermute x17, waiting for transfers between devices, swap(): return lax.ppermute(value, axis, [(s, s ^ flip) for s in range(size)])  35.4 us
    all_to_all x1, starting transfers between devices, shards(): lax.all_to_all(grad_copies, CHIPS, 0, 0, tiled=True).reshape(tokens, -1)  12.5 us
    all_to_all x1, waiting for transfers between devices, shards(): lax.all_to_all(kernel_call(sum_copies_kernel, [blocks], [act_parts]), CHI...  10.4 us
    pallas_call x7, Pallas kernels, kernel_call(): pl.pallas_call(body, out_shape=shapes if many else shapes[0], in_specs=[S...  9.96 us
    all_to_all x1, starting transfers between devices, shards(): act_parts = lax.all_to_all(act_partial, CHIPS, 0, 0, tiled=True)  9.05 us
    all_to_all x1, waiting for transfers between devices, shards(): lax.all_to_all(grad_copies, CHIPS, 0, 0, tiled=True).reshape(tokens, -1)  8.81 us
    all_to_all x1, starting transfers between devices, shards(): lax.all_to_all(kernel_call(sum_copies_kernel, [blocks], [act_parts]), CHI...  6.11 us
  transfers between devices with their start and end apart: 22, of which 16 were waited for; matrix products, arithmetic and copies ran while one was open for 1% of the time, Pallas kernels for 4%

profile of v8, /device:TPU:1, one launch (start us, length us, event | category | flops | bytes accessed | tf_op | source)
XLA Modules:
  0.0 179.8 jit_solution(17376498613408170821)
XLA Ops:
  6.5 0.0 copy-start.1
  6.5 0.0 copy-start
  6.5 0.0 all-gather.3.cloned.1.call-start
  6.5 1.0 constant_dynamic-slice_fusion.1
  7.5 8.8 %collective-permute-start = (bf16[32,896]{1,0:T(8,128)(2,1)S(1)}, bf16[32,896]{1,0:T(8,128)(2,1)S(1)}, u32[]{:S(2)}, u32[]{:S(2)}) collective-permute-start(bf16[32,896]{1,0:T(8,128)(2,1)S(1)} %get-tuple-element.32), channel_id=1, source_target_pairs={{0,16},{16,0},{1,17},{17,1},{2,18},{18,2},{3,19},{19,3},{4,20},{20... | collective-permute-start | bytes 172040 | tf_op jit(solution)/shard_map/ppermute | solution.py:34
  16.3 0.9 collective-permute-done
  17.2 1.9 %collective-permute-start.1 = (bf16[32,1792]{1,0:T(8,128)(2,1)S(1)}, bf16[32,1792]{1,0:T(8,128)(2,1)S(1)}, u32[]{:S(2)}, u32[]{:S(2)}) collective-permute-start(bf16[32,1792]{1,0:T(8,128)(2,1)S(1)} %pad_maximum_fusion.refs_0_), channel_id=1, source_target_pairs={{0,1},{1,0},{2,3},{3,2},{4,5},{5,4},{6,7},{7,6},{8,9},{9,8},{10,11... | collective-permute-start | bytes 344072 | tf_op jit(solution)/shard_map/ppermute | solution.py:34
  19.1 2.6 %collective-permute-start.2 = (bf16[32,1792]{1,0:T(8,128)(2,1)S(1)}, bf16[32,1792]{1,0:T(8,128)(2,1)S(1)}, u32[]{:S(2)}, u32[]{:S(2)}) collective-permute-start(bf16[32,1792]{1,0:T(8,128)(2,1)S(1)} %pad_maximum_fusion.refs_0_), channel_id=1, source_target_pairs={{0,2},{1,3},{2,0},{3,1},{4,6},{5,7},{6,4},{7,5},{8,10},{9,11},{10,... | collective-permute-start | bytes 344072 | tf_op jit(solution)/shard_map/ppermute | solution.py:34
  21.7 2.7 %collective-permute-done.1.refs_1_ = bf16[32,1792]{1,0:T(8,128)(2,1)S(1)} collective-permute-done((bf16[32,1792]{1,0:T(8,128)(2,1)S(1)}, bf16[32,1792]{1,0:T(8,128)(2,1)S(1)}, u32[]{:S(2)}, u32[]{:S(2)}) %collective-permute-start.1) | collective-permute-done | bytes 114720 | tf_op jit(solution)/shard_map/ppermute | solution.py:34
  24.4 5.6 %collective-permute-done.2.refs_2_ = bf16[32,1792]{1,0:T(8,128)(2,1)S(1)} collective-permute-done((bf16[32,1792]{1,0:T(8,128)(2,1)S(1)}, bf16[32,1792]{1,0:T(8,128)(2,1)S(1)}, u32[]{:S(2)}, u32[]{:S(2)}) %collective-permute-start.2) | collective-permute-done | bytes 114720 | tf_op jit(solution)/shard_map/ppermute | solution.py:34
  30.0 0.7 shard_map.46
  30.7 0.0 all-gather.3.cloned.1.call-update
  30.7 1.6 broadcast_in_dim.2
  32.3 12.5 %all-to-all-start.1 = ((bf16[16,32,512]{2,1,0:T(8,128)(2,1)}), bf16[16,32,512]{2,1,0:T(8,128)(2,1)S(1)}, u32[]{:S(2)}, u32[]{:S(2)}) async-start(bf16[16,32,512]{2,1,0:T(8,128)(2,1)} %broadcast_in_dim.2), calls=%async_computation.1 | async-start | bytes 1048576 | tf_op jit(solution)/shard_map/all_to_all | solution.py:127
  44.8 0.0 copy-done.1
  44.9 2.7 %collective-permute-start.7 = (bf16[896,896]{1,0:T(8,128)(2,1)S(1)}, bf16[896,896]{1,0:T(8,128)(2,1)}, u32[]{:S(2)}, u32[]{:S(2)}) collective-permute-start(bf16[896,896]{1,0:T(8,128)(2,1)S(1)} %copy-done.1), channel_id=1, source_target_pairs={{0,16},{16,0},{1,17},{17,1},{2,18},{18,2},{3,19},{19,3},{4,20},{20... | collective-permute-start | bytes 4816904 | tf_op jit(solution)/shard_map/ppermute | solution.py:34
  47.5 0.0 copy-done
  47.6 1.9 %collective-permute-start.8 = (bf16[512,256]{1,0:T(8,128)(2,1)S(1)}, bf16[512,256]{1,0:T(8,128)(2,1)S(1)}, u32[]{:S(2)}, u32[]{:S(2)}) collective-permute-start(bf16[512,256]{1,0:T(8,128)(2,1)S(1)} %copy-done), channel_id=1, source_target_pairs={{0,16},{16,0},{1,17},{17,1},{2,18},{18,2},{3,19},{19,3},{4,20},{20... | collective-permute-start | bytes 786440 | tf_op jit(solution)/shard_map/ppermute | solution.py:34
  49.5 1.5 collective-permute-done.8.other
  51.0 8.8 %all-to-all-done.1 = bf16[16,32,512]{2,1,0:T(8,128)(2,1)S(1)} async-done(((bf16[16,32,512]{2,1,0:T(8,128)(2,1)}), bf16[16,32,512]{2,1,0:T(8,128)(2,1)S(1)}, u32[]{:S(2)}, u32[]{:S(2)}) %all-to-all-start.1) | async-done | bytes 524320 | tf_op jit(solution)/shard_map/all_to_all | solution.py:127
  59.8 1.2 shard_map.48
  61.0 4.1 %all-to-all-start.2 = ((bf16[16,32,512]{2,1,0:T(8,128)(2,1)}), bf16[16,32,512]{2,1,0:T(8,128)(2,1)S(1)}, u32[]{:S(2)}, u32[]{:S(2)}) async-start(bf16[16,32,512]{2,1,0:T(8,128)(2,1)} %shard_map.48), calls=%async_computation.2 | async-start | bytes 1048576 | tf_op jit(solution)/shard_map/all_to_all | solution.py:134
  65.2 5.4 %collective-permute-start.3 = (bf16[32,1792]{1,0:T(8,128)(2,1)S(1)}, bf16[32,1792]{1,0:T(8,128)(2,1)S(1)}, u32[]{:S(2)}, u32[]{:S(2)}) collective-permute-start(bf16[32,1792]{1,0:T(8,128)(2,1)S(1)} %pad_maximum_fusion.refs_0_), channel_id=1, source_target_pairs={{0,3},{1,2},{2,1},{3,0},{4,7},{5,6},{6,5},{7,4},{8,11},{9,10},{10,... | collective-permute-start | bytes 344072 | tf_op jit(solution)/shard_map/ppermute | solution.py:34
  70.5 12.0 %collective-permute-done.3.last0 = bf16[32,1792]{1,0:T(8,128)(2,1)S(1)} collective-permute-done((bf16[32,1792]{1,0:T(8,128)(2,1)S(1)}, bf16[32,1792]{1,0:T(8,128)(2,1)S(1)}, u32[]{:S(2)}, u32[]{:S(2)}) %collective-permute-start.3) | collective-permute-done | bytes 114720 | tf_op jit(solution)/shard_map/ppermute | solution.py:34
  82.6 3.1 %collective-permute-start.4 = (bf16[32,1792]{1,0:T(8,128)(2,1)S(1)}, bf16[32,1792]{1,0:T(8,128)(2,1)S(1)}, u32[]{:S(2)}, u32[]{:S(2)}) collective-permute-start(bf16[32,1792]{1,0:T(8,128)(2,1)S(1)} %collective-permute-done.3.last0), channel_id=1, source_target_pairs={{0,4},{4,0},{8,12},{12,8},{1,5},{5,1},{9,13},{13,9},{2,6},{6,2},{1... | collective-permute-start | bytes 344072 | tf_op jit(solution)/shard_map/ppermute | solution.py:34
  85.6 4.3 %collective-permute-start.5 = (bf16[32,1792]{1,0:T(8,128)(2,1)S(1)}, bf16[32,1792]{1,0:T(8,128)(2,1)S(1)}, u32[]{:S(2)}, u32[]{:S(2)}) collective-permute-start(bf16[32,1792]{1,0:T(8,128)(2,1)S(1)} %collective-permute-done.3.last0), channel_id=1, source_target_pairs={{0,8},{4,12},{8,0},{12,4},{1,9},{5,13},{9,1},{13,5},{2,10},{6,14},... | collective-permute-start | bytes 344072 | tf_op jit(solution)/shard_map/ppermute | solution.py:34
  90.0 2.2 %collective-permute-start.6 = (bf16[32,1792]{1,0:T(8,128)(2,1)S(1)}, bf16[32,1792]{1,0:T(8,128)(2,1)S(1)}, u32[]{:S(2)}, u32[]{:S(2)}) collective-permute-start(bf16[32,1792]{1,0:T(8,128)(2,1)S(1)} %collective-permute-done.3.last0), channel_id=1, source_target_pairs={{0,12},{4,8},{8,4},{12,0},{1,13},{5,9},{9,5},{13,1},{2,14},{6,10},... | collective-permute-start | bytes 344072 | tf_op jit(solution)/shard_map/ppermute | solution.py:34
  92.2 0.0 collective-permute-done.4.last1
  92.2 1.5 collective-permute-done.5.last2
  93.7 3.0 %collective-permute-done.6.last3 = bf16[32,1792]{1,0:T(8,128)(2,1)S(1)} collective-permute-done((bf16[32,1792]{1,0:T(8,128)(2,1)S(1)}, bf16[32,1792]{1,0:T(8,128)(2,1)S(1)}, u32[]{:S(2)}, u32[]{:S(2)}) %collective-permute-start.6) | collective-permute-done | bytes 114720 | tf_op jit(solution)/shard_map/ppermute | solution.py:34
  96.7 0.0 collective-permute-done.7.other
  96.7 0.0 all-gather.3.cloned.1.call-done
  96.7 0.0 copy-start.2
  96.7 1.3 copy-done.2
  98.0 4.6 %shard_map.47 = (bf16[16,32,896]{2,1,0:T(8,128)(2,1)}, f32[8,128]{1,0:T(8,128)S(1)}) custom-call(s32[1]{0:T(128)} %bitcast.at, bf16[4,96,1792]{2,1,0:T(8,128)(2,1)S(1)} %bitcast.7, bf16[32,1792]{1,0:T(8,128)(2,1)S(1)} %collective-permute-done.3.last0, bf16[32,1792]{1,0:T(8,128)(2,1)S(1)} %collective-permute-done.4.last1, ...), custom_call_target="tpu_custom_call" | custom-call | flops 1644167168 | bytes 5967876 | tf_op jit(solution)/shard_map/pallas_call | solution.py:22
  102.6 0.0 all-to-all-done.2.parts
  102.7 9.1 %all-to-all-start = ((bf16[16,32,896]{2,1,0:T(8,128)(2,1)}), bf16[16,32,896]{2,1,0:T(8,128)(2,1)S(1)}, u32[]{:S(2)}, u32[]{:S(2)}) async-start(bf16[16,32,896]{2,1,0:T(8,128)(2,1)} %get-tuple-element.19), calls=%async_computation | async-start | bytes 1835008 | tf_op jit(solution)/shard_map/all_to_all | solution.py:144
  111.7 0.1 shard_map.49
  111.8 4.4 %collective-permute-start.9 = (bf16[32,256]{1,0:T(8,128)(2,1)S(1)}, bf16[32,256]{1,0:T(8,128)(2,1)S(1)}, u32[]{:S(2)}, u32[]{:S(2)}) collective-permute-start(bf16[32,256]{1,0:T(8,128)(2,1)S(1)} %get-tuple-element.23), channel_id=1, source_target_pairs={{0,16},{16,0},{1,17},{17,1},{2,18},{18,2},{3,19},{19,3},{4,20},{20... | collective-permute-start | bytes 49160 | tf_op jit(solution)/shard_map/ppermute | solution.py:34
  116.2 0.8 collective-permute-done.9
  117.0 3.1 %collective-permute-start.10 = (bf16[32,512]{1,0:T(8,128)(2,1)S(1)}, bf16[32,512]{1,0:T(8,128)(2,1)S(1)}, u32[]{:S(2)}, u32[]{:S(2)}) collective-permute-start(bf16[32,512]{1,0:T(8,128)(2,1)S(1)} %constant_dynamic-update-slice_fusion.refs_0_), channel_id=1, source_target_pairs={{0,1},{1,0},{2,3},{3,2},{4,5},{5,4},{6,7},{7,6},{8,9},{9,8},{10,11... | collective-permute-start | bytes 98312 | tf_op jit(solution)/shard_map/ppermute | solution.py:34
  120.1 2.8 %collective-permute-start.11 = (bf16[32,512]{1,0:T(8,128)(2,1)S(1)}, bf16[32,512]{1,0:T(8,128)(2,1)S(1)}, u32[]{:S(2)}, u32[]{:S(2)}) collective-permute-start(bf16[32,512]{1,0:T(8,128)(2,1)S(1)} %constant_dynamic-update-slice_fusion.refs_0_), channel_id=1, source_target_pairs={{0,2},{1,3},{2,0},{3,1},{4,6},{5,7},{6,4},{7,5},{8,10},{9,11},{10,... | collective-permute-start | bytes 98312 | tf_op jit(solution)/shard_map/ppermute | solution.py:34
  122.9 5.5 %collective-permute-start.12 = (bf16[32,512]{1,0:T(8,128)(2,1)S(1)}, bf16[32,512]{1,0:T(8,128)(2,1)S(1)}, u32[]{:S(2)}, u32[]{:S(2)}) collective-permute-start(bf16[32,512]{1,0:T(8,128)(2,1)S(1)} %constant_dynamic-update-slice_fusion.refs_0_), channel_id=1, source_target_pairs={{0,3},{1,2},{2,1},{3,0},{4,7},{5,6},{6,5},{7,4},{8,11},{9,10},{10,... | collective-permute-start | bytes 98312 | tf_op jit(solution)/shard_map/ppermute | solution.py:34
  128.4 0.0 collective-permute-done.10.refs_1_
  128.4 0.3 collective-permute-done.11.refs_2_
  128.7 1.3 collective-permute-done.12.refs_3_
  130.0 0.6 shard_map.50
  130.6 3.8 %all-to-all-done.parts = bf16[16,32,896]{2,1,0:T(8,128)(2,1)S(1)} async-done(((bf16[16,32,896]{2,1,0:T(8,128)(2,1)}), bf16[16,32,896]{2,1,0:T(8,128)(2,1)S(1)}, u32[]{:S(2)}, u32[]{:S(2)}) %all-to-all-start) | async-done | bytes 917536 | tf_op jit(solution)/shard_map/all_to_all | solution.py:144
  134.5 1.1 shard_map.51
  135.5 6.1 %all-to-all-start.3 = ((bf16[16,32,896]{2,1,0:T(8,128)(2,1)}), bf16[16,32,896]{2,1,0:T(8,128)(2,1)S(1)}, u32[]{:S(2)}, u32[]{:S(2)}) async-start(bf16[16,32,896]{2,1,0:T(8,128)(2,1)} %shard_map.51), calls=%async_computation.3 | async-start | bytes 1835008 | tf_op jit(solution)/shard_map/all_to_all | solution.py:152
  141.6 1.9 %collective-permute-start.13 = (bf16[128,512]{1,0:T(8,128)(2,1)S(1)}, bf16[128,512]{1,0:T(8,128)(2,1)S(1)}, u32[]{:S(2)}, u32[]{:S(2)}) collective-permute-start(bf16[128,512]{1,0:T(8,128)(2,1)S(1)} %get-tuple-element.25.g0), channel_id=1, source_target_pairs={{0,4},{4,0},{8,12},{12,8},{1,5},{5,1},{9,13},{13,9},{2,6},{6,2},{1... | collective-permute-start | bytes 393224 | tf_op jit(solution)/shard_map/ppermute | solution.py:34
  143.6 4.2 %collective-permute-start.14 = (bf16[128,512]{1,0:T(8,128)(2,1)S(1)}, bf16[128,512]{1,0:T(8,128)(2,1)S(1)}, u32[]{:S(2)}, u32[]{:S(2)}) collective-permute-start(bf16[128,512]{1,0:T(8,128)(2,1)S(1)} %get-tuple-element.25.g0), channel_id=1, source_target_pairs={{0,8},{4,12},{8,0},{12,4},{1,9},{5,13},{9,1},{13,5},{2,10},{6,14},... | collective-permute-start | bytes 393224 | tf_op jit(solution)/shard_map/ppermute | solution.py:34
  147.7 3.5 %collective-permute-start.15 = (bf16[128,512]{1,0:T(8,128)(2,1)S(1)}, bf16[128,512]{1,0:T(8,128)(2,1)S(1)}, u32[]{:S(2)}, u32[]{:S(2)}) collective-permute-start(bf16[128,512]{1,0:T(8,128)(2,1)S(1)} %get-tuple-element.25.g0), channel_id=1, source_target_pairs={{0,12},{4,8},{8,4},{12,0},{1,13},{5,9},{9,5},{13,1},{2,14},{6,10},... | collective-permute-start | bytes 393224 | tf_op jit(solution)/shard_map/ppermute | solution.py:34
  151.2 0.0 collective-permute-done.13.g1
  151.2 0.3 collective-permute-done.14.g2
  151.6 3.4 %collective-permute-done.15.g3 = bf16[128,512]{1,0:T(8,128)(2,1)S(1)} collective-permute-done((bf16[128,512]{1,0:T(8,128)(2,1)S(1)}, bf16[128,512]{1,0:T(8,128)(2,1)S(1)}, u32[]{:S(2)}, u32[]{:S(2)}) %collective-permute-start.15) | collective-permute-done | bytes 131104 | tf_op jit(solution)/shard_map/ppermute | solution.py:34
  154.9 10.4 %all-to-all-done.3 = bf16[16,32,896]{2,1,0:T(8,128)(2,1)S(1)} async-done(((bf16[16,32,896]{2,1,0:T(8,128)(2,1)}), bf16[16,32,896]{2,1,0:T(8,128)(2,1)S(1)}, u32[]{:S(2)}, u32[]{:S(2)}) %all-to-all-start.3) | async-done | bytes 917536 | tf_op jit(solution)/shard_map/all_to_all | solution.py:152
  165.4 3.8 %collective-permute-start.16 = (bf16[512,896]{1,0:T(8,128)(2,1)S(1)}, bf16[512,896]{1,0:T(8,128)(2,1)S(1)}, u32[]{:S(2)}, u32[]{:S(2)}) collective-permute-start(bf16[512,896]{1,0:T(8,128)(2,1)S(1)} %bitcast.4), channel_id=1, source_target_pairs={{0,16},{16,0},{1,17},{17,1},{2,18},{18,2},{3,19},{19,3},{4,20},{20... | collective-permute-start | bytes 2752520 | tf_op jit(solution)/shard_map/ppermute | solution.py:34
  169.2 2.1 %collective-permute-done.16.act_theirs = bf16[512,896]{1,0:T(8,128)(2,1)S(1)} collective-permute-done((bf16[512,896]{1,0:T(8,128)(2,1)S(1)}, bf16[512,896]{1,0:T(8,128)(2,1)S(1)}, u32[]{:S(2)}, u32[]{:S(2)}) %collective-permute-start.16) | collective-permute-done | bytes 917536 | tf_op jit(solution)/shard_map/ppermute | solution.py:34
  171.3 1.7 shard_map.52
  (3 shorter events, 0.0 us)
Async XLA Ops:
  6.5 38.3 %copy-start.1 = (bf16[896,896]{1,0:T(8,128)(2,1)S(1)}, bf16[896,896]{1,0:T(8,128)(2,1)}, u32[]{:S(2)}) copy-start(bf16[896,896]{1,0:T(8,128)(2,1)} %own.2) | copy-start | bytes 4816900
  6.5 41.0 %copy-start = (bf16[512,256]{1,0:T(8,128)(2,1)S(1)}, bf16[512,256]{1,0:T(8,128)(2,1)}, u32[]{:S(2)}) copy-start(bf16[512,256]{1,0:T(8,128)(2,1)} %own.3) | copy-start | bytes 786436
  6.5 90.2 %all-gather.3.cloned.1.call-start = ((), (), s32[]{:S(2)}) async-start(), calls=%async_computation.4 | async-start | bytes 1720320 | tf_op jit(solution)/shard_map/all_gather | solution.py:123
  7.5 9.7 %collective-permute-start = (bf16[32,896]{1,0:T(8,128)(2,1)S(1)}, bf16[32,896]{1,0:T(8,128)(2,1)S(1)}, u32[]{:S(2)}, u32[]{:S(2)}) collective-permute-start(bf16[32,896]{1,0:T(8,128)(2,1)S(1)} %get-tuple-element.32), channel_id=1, source_target_pairs={{0,16},{16,0},{1,17},{17,1},{2,18},{18,2},{3,19},{19,3},{4,20},{20... | collective-permute-start | bytes 172040 | tf_op jit(solution)/shard_map/ppermute | solution.py:34
  17.2 7.2 %collective-permute-start.1 = (bf16[32,1792]{1,0:T(8,128)(2,1)S(1)}, bf16[32,1792]{1,0:T(8,128)(2,1)S(1)}, u32[]{:S(2)}, u32[]{:S(2)}) collective-permute-start(bf16[32,1792]{1,0:T(8,128)(2,1)S(1)} %pad_maximum_fusion.refs_0_), channel_id=1, source_target_pairs={{0,1},{1,0},{2,3},{3,2},{4,5},{5,4},{6,7},{7,6},{8,9},{9,8},{10,11... | collective-permute-start | bytes 344072 | tf_op jit(solution)/shard_map/ppermute | solution.py:34
  19.1 10.8 %collective-permute-start.2 = (bf16[32,1792]{1,0:T(8,128)(2,1)S(1)}, bf16[32,1792]{1,0:T(8,128)(2,1)S(1)}, u32[]{:S(2)}, u32[]{:S(2)}) collective-permute-start(bf16[32,1792]{1,0:T(8,128)(2,1)S(1)} %pad_maximum_fusion.refs_0_), channel_id=1, source_target_pairs={{0,2},{1,3},{2,0},{3,1},{4,6},{5,7},{6,4},{7,5},{8,10},{9,11},{10,... | collective-permute-start | bytes 344072 | tf_op jit(solution)/shard_map/ppermute | solution.py:34
  32.3 27.4 %all-to-all-start.1 = ((bf16[16,32,512]{2,1,0:T(8,128)(2,1)}), bf16[16,32,512]{2,1,0:T(8,128)(2,1)S(1)}, u32[]{:S(2)}, u32[]{:S(2)}) async-start(bf16[16,32,512]{2,1,0:T(8,128)(2,1)} %broadcast_in_dim.2), calls=%async_computation.1 | async-start | bytes 1048576 | tf_op jit(solution)/shard_map/all_to_all | solution.py:127
  44.9 51.8 %collective-permute-start.7 = (bf16[896,896]{1,0:T(8,128)(2,1)S(1)}, bf16[896,896]{1,0:T(8,128)(2,1)}, u32[]{:S(2)}, u32[]{:S(2)}) collective-permute-start(bf16[896,896]{1,0:T(8,128)(2,1)S(1)} %copy-done.1), channel_id=1, source_target_pairs={{0,16},{16,0},{1,17},{17,1},{2,18},{18,2},{3,19},{19,3},{4,20},{20... | collective-permute-start | bytes 4816904 | tf_op jit(solution)/shard_map/ppermute | solution.py:34
  47.6 3.4 %collective-permute-start.8 = (bf16[512,256]{1,0:T(8,128)(2,1)S(1)}, bf16[512,256]{1,0:T(8,128)(2,1)S(1)}, u32[]{:S(2)}, u32[]{:S(2)}) collective-permute-start(bf16[512,256]{1,0:T(8,128)(2,1)S(1)} %copy-done), channel_id=1, source_target_pairs={{0,16},{16,0},{1,17},{17,1},{2,18},{18,2},{3,19},{19,3},{4,20},{20... | collective-permute-start | bytes 786440 | tf_op jit(solution)/shard_map/ppermute | solution.py:34
  61.0 41.6 %all-to-all-start.2 = ((bf16[16,32,512]{2,1,0:T(8,128)(2,1)}), bf16[16,32,512]{2,1,0:T(8,128)(2,1)S(1)}, u32[]{:S(2)}, u32[]{:S(2)}) async-start(bf16[16,32,512]{2,1,0:T(8,128)(2,1)} %shard_map.48), calls=%async_computation.2 | async-start | bytes 1048576 | tf_op jit(solution)/shard_map/all_to_all | solution.py:134
  65.2 17.4 %collective-permute-start.3 = (bf16[32,1792]{1,0:T(8,128)(2,1)S(1)}, bf16[32,1792]{1,0:T(8,128)(2,1)S(1)}, u32[]{:S(2)}, u32[]{:S(2)}) collective-permute-start(bf16[32,1792]{1,0:T(8,128)(2,1)S(1)} %pad_maximum_fusion.refs_0_), channel_id=1, source_target_pairs={{0,3},{1,2},{2,1},{3,0},{4,7},{5,6},{6,5},{7,4},{8,11},{9,10},{10,... | collective-permute-start | bytes 344072 | tf_op jit(solution)/shard_map/ppermute | solution.py:34
  82.6 9.6 %collective-permute-start.4 = (bf16[32,1792]{1,0:T(8,128)(2,1)S(1)}, bf16[32,1792]{1,0:T(8,128)(2,1)S(1)}, u32[]{:S(2)}, u32[]{:S(2)}) collective-permute-start(bf16[32,1792]{1,0:T(8,128)(2,1)S(1)} %collective-permute-done.3.last0), channel_id=1, source_target_pairs={{0,4},{4,0},{8,12},{12,8},{1,5},{5,1},{9,13},{13,9},{2,6},{6,2},{1... | collective-permute-start | bytes 344072 | tf_op jit(solution)/shard_map/ppermute | solution.py:34
  85.6 8.1 %collective-permute-start.5 = (bf16[32,1792]{1,0:T(8,128)(2,1)S(1)}, bf16[32,1792]{1,0:T(8,128)(2,1)S(1)}, u32[]{:S(2)}, u32[]{:S(2)}) collective-permute-start(bf16[32,1792]{1,0:T(8,128)(2,1)S(1)} %collective-permute-done.3.last0), channel_id=1, source_target_pairs={{0,8},{4,12},{8,0},{12,4},{1,9},{5,13},{9,1},{13,5},{2,10},{6,14},... | collective-permute-start | bytes 344072 | tf_op jit(solution)/shard_map/ppermute | solution.py:34
  90.0 6.7 %collective-permute-start.6 = (bf16[32,1792]{1,0:T(8,128)(2,1)S(1)}, bf16[32,1792]{1,0:T(8,128)(2,1)S(1)}, u32[]{:S(2)}, u32[]{:S(2)}) collective-permute-start(bf16[32,1792]{1,0:T(8,128)(2,1)S(1)} %collective-permute-done.3.last0), channel_id=1, source_target_pairs={{0,12},{4,8},{8,4},{12,0},{1,13},{5,9},{9,5},{13,1},{2,14},{6,10},... | collective-permute-start | bytes 344072 | tf_op jit(solution)/shard_map/ppermute | solution.py:34
  96.7 1.3 copy-start.2
  102.7 31.8 %all-to-all-start = ((bf16[16,32,896]{2,1,0:T(8,128)(2,1)}), bf16[16,32,896]{2,1,0:T(8,128)(2,1)S(1)}, u32[]{:S(2)}, u32[]{:S(2)}) async-start(bf16[16,32,896]{2,1,0:T(8,128)(2,1)} %get-tuple-element.19), calls=%async_computation | async-start | bytes 1835008 | tf_op jit(solution)/shard_map/all_to_all | solution.py:144
  111.8 5.2 %collective-permute-start.9 = (bf16[32,256]{1,0:T(8,128)(2,1)S(1)}, bf16[32,256]{1,0:T(8,128)(2,1)S(1)}, u32[]{:S(2)}, u32[]{:S(2)}) collective-permute-start(bf16[32,256]{1,0:T(8,128)(2,1)S(1)} %get-tuple-element.23), channel_id=1, source_target_pairs={{0,16},{16,0},{1,17},{17,1},{2,18},{18,2},{3,19},{19,3},{4,20},{20... | collective-permute-start | bytes 49160 | tf_op jit(solution)/shard_map/ppermute | solution.py:34
  117.0 11.4 %collective-permute-start.10 = (bf16[32,512]{1,0:T(8,128)(2,1)S(1)}, bf16[32,512]{1,0:T(8,128)(2,1)S(1)}, u32[]{:S(2)}, u32[]{:S(2)}) collective-permute-start(bf16[32,512]{1,0:T(8,128)(2,1)S(1)} %constant_dynamic-update-slice_fusion.refs_0_), channel_id=1, source_target_pairs={{0,1},{1,0},{2,3},{3,2},{4,5},{5,4},{6,7},{7,6},{8,9},{9,8},{10,11... | collective-permute-start | bytes 98312 | tf_op jit(solution)/shard_map/ppermute | solution.py:34
  120.1 8.6 %collective-permute-start.11 = (bf16[32,512]{1,0:T(8,128)(2,1)S(1)}, bf16[32,512]{1,0:T(8,128)(2,1)S(1)}, u32[]{:S(2)}, u32[]{:S(2)}) collective-permute-start(bf16[32,512]{1,0:T(8,128)(2,1)S(1)} %constant_dynamic-update-slice_fusion.refs_0_), channel_id=1, source_target_pairs={{0,2},{1,3},{2,0},{3,1},{4,6},{5,7},{6,4},{7,5},{8,10},{9,11},{10,... | collective-permute-start | bytes 98312 | tf_op jit(solution)/shard_map/ppermute | solution.py:34
  122.9 7.1 %collective-permute-start.12 = (bf16[32,512]{1,0:T(8,128)(2,1)S(1)}, bf16[32,512]{1,0:T(8,128)(2,1)S(1)}, u32[]{:S(2)}, u32[]{:S(2)}) collective-permute-start(bf16[32,512]{1,0:T(8,128)(2,1)S(1)} %constant_dynamic-update-slice_fusion.refs_0_), channel_id=1, source_target_pairs={{0,3},{1,2},{2,1},{3,0},{4,7},{5,6},{6,5},{7,4},{8,11},{9,10},{10,... | collective-permute-start | bytes 98312 | tf_op jit(solution)/shard_map/ppermute | solution.py:34
  135.5 29.9 %all-to-all-start.3 = ((bf16[16,32,896]{2,1,0:T(8,128)(2,1)}), bf16[16,32,896]{2,1,0:T(8,128)(2,1)S(1)}, u32[]{:S(2)}, u32[]{:S(2)}) async-start(bf16[16,32,896]{2,1,0:T(8,128)(2,1)} %shard_map.51), calls=%async_computation.3 | async-start | bytes 1835008 | tf_op jit(solution)/shard_map/all_to_all | solution.py:152
  141.6 9.6 %collective-permute-start.13 = (bf16[128,512]{1,0:T(8,128)(2,1)S(1)}, bf16[128,512]{1,0:T(8,128)(2,1)S(1)}, u32[]{:S(2)}, u32[]{:S(2)}) collective-permute-start(bf16[128,512]{1,0:T(8,128)(2,1)S(1)} %get-tuple-element.25.g0), channel_id=1, source_target_pairs={{0,4},{4,0},{8,12},{12,8},{1,5},{5,1},{9,13},{13,9},{2,6},{6,2},{1... | collective-permute-start | bytes 393224 | tf_op jit(solution)/shard_map/ppermute | solution.py:34
  143.6 8.0 %collective-permute-start.14 = (bf16[128,512]{1,0:T(8,128)(2,1)S(1)}, bf16[128,512]{1,0:T(8,128)(2,1)S(1)}, u32[]{:S(2)}, u32[]{:S(2)}) collective-permute-start(bf16[128,512]{1,0:T(8,128)(2,1)S(1)} %get-tuple-element.25.g0), channel_id=1, source_target_pairs={{0,8},{4,12},{8,0},{12,4},{1,9},{5,13},{9,1},{13,5},{2,10},{6,14},... | collective-permute-start | bytes 393224 | tf_op jit(solution)/shard_map/ppermute | solution.py:34
  147.7 7.2 %collective-permute-start.15 = (bf16[128,512]{1,0:T(8,128)(2,1)S(1)}, bf16[128,512]{1,0:T(8,128)(2,1)S(1)}, u32[]{:S(2)}, u32[]{:S(2)}) collective-permute-start(bf16[128,512]{1,0:T(8,128)(2,1)S(1)} %get-tuple-element.25.g0), channel_id=1, source_target_pairs={{0,12},{4,8},{8,4},{12,0},{1,13},{5,9},{9,5},{13,1},{2,14},{6,10},... | collective-permute-start | bytes 393224 | tf_op jit(solution)/shard_map/ppermute | solution.py:34
  165.4 5.9 %collective-permute-start.16 = (bf16[512,896]{1,0:T(8,128)(2,1)S(1)}, bf16[512,896]{1,0:T(8,128)(2,1)S(1)}, u32[]{:S(2)}, u32[]{:S(2)}) collective-permute-start(bf16[512,896]{1,0:T(8,128)(2,1)S(1)} %bitcast.4), channel_id=1, source_target_pairs={{0,16},{16,0},{1,17},{17,1},{2,18},{18,2},{3,19},{19,3},{4,20},{20... | collective-permute-start | bytes 2752520 | tf_op jit(solution)/shard_map/ppermute | solution.py:34
Sparse Core Ops, SparseCore 0:
  30.9 31.5 all-gather.2

commit v9 on v8

v9 whole, which is shorter than its diff:
```python
import jax
import jax.numpy as jnp
from jax import lax
from jax.experimental import pallas as pl
from jax.experimental.pallas import tpu as pltpu
from jax.sharding import Mesh, PartitionSpec as P

SEQS = 2
SEQ_LEN = 512
OUT = ("z", "ylo", "core")
INP = ("x", "yhi")
CHIPS = ("z", "ylo")
BF16 = jnp.bfloat16
F32 = jnp.float32
SMEM = pl.BlockSpec(memory_space=pltpu.SMEM)
ANY = pl.BlockSpec(memory_space=pl.ANY)
VMEM = pl.BlockSpec(memory_space=pltpu.VMEM)


def kernel_call(body, shapes, args, flops=0, scalars=0, unread=0):
    moved = sum(a.size * a.dtype.itemsize for a in args) + sum(s.size * s.dtype.itemsize for s in shapes)
    many = len(shapes) > 1
    return pl.pallas_call(
        body,
        out_shape=shapes if many else shapes[0],
        in_specs=[SMEM] * scalars + [VMEM] * (len(args) - scalars - unread) + [ANY] * unread,
        out_specs=[VMEM] * len(shapes) if many else VMEM,
        compiler_params=pltpu.CompilerParams(vmem_limit_bytes=40 * 2**20),
        cost_estimate=pl.CostEstimate(flops=flops, bytes_accessed=moved, transcendentals=0),
    )(*args)


def swap(value, axis, flip):
    size = lax.axis_size(axis)
    return lax.ppermute(value, axis, [(s, s ^ flip) for s in range(size)])


def gather_yhi(mine):
    return [mine, swap(mine, "yhi", 1), swap(mine, "yhi", 2), swap(mine, "yhi", 3)]


def stack_acts_kernel(block0, block1, block2, block3, order, out, done):
    rows, features = block0.shape[0], out.shape[2]
    for index, block in enumerate((block0, block1, block2, block3)):
        for side in range(2):
            out[side, index * rows:(index + 1) * rows, :] = block[:, side * features:(side + 1) * features]
    done[...] = jnp.zeros_like(done)


def stack_kernel(block0, block1, block2, block3, out):
    rows = block0.shape[0]
    for index, block in enumerate((block0, block1, block2, block3)):
        out[index * rows:(index + 1) * rows, :] = block[...]


def place_kernel(x, block0, block1, block2, block3, out):
    rows = block0.shape[0]
    for flip, block in enumerate((block0, block1, block2, block3)):
        out[pl.ds(pl.multiple_of((x[0] ^ flip) * rows, rows), rows), :] = block[...]


def act_dot_kernel(acts, own, other, out, done):
    total = 0.0
    for side, basis in ((0, own), (1, other)):
        rows = jnp.concatenate([acts[x, side] for x in range(acts.shape[0])])
        total += jnp.dot(rows, basis[...], preferred_element_type=F32)
    out[...] = total.astype(BF16).reshape(out.shape)
    done[...] = jnp.zeros_like(done)


def grad_dot_kernel(done, rows, own, other, out):
    columns = own.shape[1]
    total = jnp.concatenate(
        [jnp.dot(rows[...], basis[...], preferred_element_type=F32) for basis in (own, other)], axis=1
    )
    out[...] = total.astype(BF16).reshape(out.shape)


def sum_parts(parts):
    total = parts[0].astype(F32)
    for index in range(1, parts.shape[0]):
        total += parts[index].astype(F32)
    return total.astype(BF16)


def sum_copies_kernel(parts, out):
    rounded = sum_parts(parts)
    for index in range(out.shape[0]):
        out[index] = rounded


def sum_split_kernel(done, parts, mine, give):
    rounded = sum_parts(parts)
    columns = mine.shape[1]
    mine[...] = rounded[:, :columns]
    give[...] = rounded[:, columns:]


def square_kernel(grads, act_mine, act_theirs, out):
    columns = out.shape[0]
    half = act_mine.shape[0] // SEQS
    total = 0.0
    for seq in range(SEQS):
        rows = slice(seq * half, (seq + 1) * half)
        rotated = 0.0
        for side, act in ((0, act_mine), (1, act_theirs)):
            rotated += lax.dot_general(
                grads[rows, side * columns:(side + 1) * columns], act[rows, :], (((0,), (0,)), ((), ())),
                preferred_element_type=F32,
            )
        total = total + rotated * rotated
    out[...] = total * (1.0 / (SEQS * SEQ_LEN))


def shards(grads, acts, grad_basis, act_basis):
    core, x = lax.axis_index("core"), lax.axis_index("x").astype(jnp.int32).reshape(1)
    half, features = acts.shape[0] // 2, acts.shape[1]
    tokens, eig = 16 * half, act_basis.shape[1]
    rows, columns = grads.shape[0], grad_basis.shape[1]

    keep = lax.dynamic_slice_in_dim(acts, core * half, half)
    give = lax.dynamic_slice_in_dim(acts, (1 - core) * half, half)
    act_own = jnp.concatenate([keep, swap(give, "core", 1)], axis=1)
    act_basis_other = swap(act_basis, "core", 1)
    grad_basis_other = swap(grad_basis, "core", 1)

    grad_copies = jnp.broadcast_to(grads[None], (16, *grads.shape))
    grad_rows = lax.all_to_all(grad_copies, CHIPS, 0, 0, tiled=True).reshape(tokens, -1)
    act_yhi, done = kernel_call(
        stack_acts_kernel,
        [jax.ShapeDtypeStruct((2, 4 * half, features), BF16), jax.ShapeDtypeStruct((8, 128), F32)],
        [*gather_yhi(act_own), grad_rows],
        unread=1,
    )
    act_rows = lax.all_gather(act_yhi, "x")

    grad_partial = kernel_call(
        grad_dot_kernel,
        [jax.ShapeDtypeStruct((16, rows, 2 * columns), BF16)],
        [done, grad_rows, grad_basis, grad_basis_other],
        flops=2 * tokens * grads.shape[1] * 2 * columns,
    )
    grad_parts = lax.all_to_all(grad_partial, INP, 0, 0, tiled=True)

    blocks = jax.ShapeDtypeStruct((16, half, eig), BF16)
    act_partial, done = kernel_call(
        act_dot_kernel,
        [blocks, jax.ShapeDtypeStruct((8, 128), F32)],
        [act_rows, act_basis, act_basis_other],
        flops=2 * tokens * 2 * features * eig,
    )
    act_parts = lax.all_to_all(act_partial, CHIPS, 0, 0, tiled=True)

    narrow = jax.ShapeDtypeStruct((rows, columns), BF16)
    grad_mine, grad_give = kernel_call(sum_split_kernel, [narrow, narrow], [done, grad_parts])
    grad_own = jnp.concatenate([grad_mine, swap(grad_give, "core", 1)], axis=1)
    g0 = kernel_call(stack_kernel, [jax.ShapeDtypeStruct((4 * rows, 2 * columns), BF16)], gather_yhi(grad_own))
    act_parts, g0 = lax.optimization_barrier((act_parts, g0))

    act_mine = lax.all_to_all(kernel_call(sum_copies_kernel, [blocks], [act_parts]), CHIPS, 0, 0, tiled=True)
    grad_blocks = [g0, swap(g0, "x", 1), swap(g0, "x", 2), swap(g0, "x", 3)]
    grad_all = kernel_call(
        place_kernel, [jax.ShapeDtypeStruct((tokens, 2 * columns), BF16)], [x, *grad_blocks], scalars=1
    )
    act_mine, grad_all = lax.optimization_barrier((act_mine.reshape(tokens, eig), grad_all))
    act_theirs = swap(act_mine, "core", 1)

    return kernel_call(
        square_kernel,
        [jax.ShapeDtypeStruct((columns, eig), F32)],
        [grad_all, act_mine, act_theirs],
        flops=2 * 2 * tokens * columns * eig,
    )


def solution(mesh):
    split = Mesh(mesh.devices.reshape(8, 2, 2, 4, 4), OUT + INP)
    return jax.shard_map(
        shards,
        mesh=split,
        in_specs=(P(OUT, INP), P(INP, OUT), P(INP, OUT), P(OUT, INP)),
        out_specs=P(OUT, INP),
        check_vma=False,
    )
```

time: 181 us -> 169 us (0.934)
  starting transfers between devices: 93.8 us -> 78.6 us
  waiting for transfers between devices: 58.5 us -> 63.2 us
    all_gather x1, waiting for transfers between devices: 0.01 us -> 24.5 us  [shards(): act_rows = lax.all_gather(act_yhi, 'x')]
    ppermute x17 -> x14, starting transfers between devices: 62 us -> 46.9 us  [swap(): return lax.ppermute(value, axis, [(s, s ^ flip) for s in range(size)])]
    ppermute x17 -> x14, waiting for transfers between devices: 35.4 us -> 24.7 us  [swap(): return lax.ppermute(value, axis, [(s, s ^ flip) for s in range(size)])]
    all_to_all x1, waiting for transfers between devices: 8.81 us -> 0.01 us  [shards(): lax.all_to_all(grad_copies, CHIPS, 0, 0, tiled=True).reshape(tokens, -1)]
    all_to_all x1, starting transfers between devices: 4.12 us -> 7.46 us  [shards(): grad_parts = lax.all_to_all(grad_partial, INP, 0, 0, tiled=True)]
    all_to_all x1, starting transfers between devices: 9.05 us -> 6.74 us  [shards(): act_parts = lax.all_to_all(act_partial, CHIPS, 0, 0, tiled=True)]
    pallas_call x7 -> x8, Pallas kernels: 9.96 us -> 9.48 us  [kernel_call(): pl.pallas_call(body, out_shape=shapes if many else shapes[0], in_specs=[S...]
  transfers between devices with their start and end apart: 22 -> 19, of which waited for: 16 -> 13; matrix products, arithmetic and copies ran while one was open for 1% -> 0% of each run, Pallas kernels for 4% -> 4%
where the time goes in v9:
time: 169 us; the launch traced here: 168 us
  starting transfers between devices  78.6 us (47%)
  waiting for transfers between devices  63.2 us (37%)
  between operations  13.6 us (8%)
  Pallas kernels  9.48 us (6%)
  local copies, waits for them, and re-layouts  3.17 us (2%)
    ppermute x14, starting transfers between devices, swap(): return lax.ppermute(value, axis, [(s, s ^ flip) for s in range(size)])  46.9 us
    ppermute x14, waiting for transfers between devices, swap(): return lax.ppermute(value, axis, [(s, s ^ flip) for s in range(size)])  24.7 us
    all_gather x1, waiting for transfers between devices, shards(): act_rows = lax.all_gather(act_yhi, 'x')  24.5 us
    all_to_all x1, starting transfers between devices, shards(): lax.all_to_all(grad_copies, CHIPS, 0, 0, tiled=True).reshape(tokens, -1)  12.1 us
    all_to_all x1, waiting for transfers between devices, shards(): lax.all_to_all(kernel_call(sum_copies_kernel, [blocks], [act_parts]), CHI...  10.4 us
    pallas_call x8, Pallas kernels, kernel_call(): pl.pallas_call(body, out_shape=shapes if many else shapes[0], in_specs=[S...  9.48 us
    all_to_all x1, starting transfers between devices, shards(): grad_parts = lax.all_to_all(grad_partial, INP, 0, 0, tiled=True)  7.46 us
    all_to_all x1, starting transfers between devices, shards(): act_parts = lax.all_to_all(act_partial, CHIPS, 0, 0, tiled=True)  6.74 us
  transfers between devices with their start and end apart: 19, of which 13 were waited for; matrix products, arithmetic and copies ran while one was open for 0% of the time, Pallas kernels for 4%

profile of v9, /device:TPU:1, one launch (start us, length us, event | category | flops | bytes accessed | tf_op | source)
XLA Modules:
  0.0 168.1 jit_solution(4479696568823617610)
XLA Ops:
  6.5 0.0 copy-start.3
  6.5 1.6 broadcast_in_dim.2
  8.2 0.0 copy-start.2
  8.2 0.0 copy-start
  8.2 12.1 %all-to-all-start = ((bf16[16,32,512]{2,1,0:T(8,128)(2,1)}), bf16[16,32,512]{2,1,0:T(8,128)(2,1)S(1)}, u32[]{:S(2)}, u32[]{:S(2)}) async-start(bf16[16,32,512]{2,1,0:T(8,128)(2,1)} %broadcast_in_dim.2), calls=%async_computation | async-start | bytes 1048576 | tf_op jit(solution)/shard_map/all_to_all | solution.py:128
  20.3 0.0 all-gather.3.cloned.1.call-start
  20.4 0.0 copy-done.3
  20.4 2.9 %collective-permute-start = (bf16[32,896]{1,0:T(8,128)(2,1)S(1)}, bf16[32,896]{1,0:T(8,128)(2,1)S(1)}, u32[]{:S(2)}, u32[]{:S(2)}) collective-permute-start(bf16[32,896]{1,0:T(8,128)(2,1)S(1)} %get-tuple-element.26), channel_id=1, source_target_pairs={{0,16},{16,0},{1,17},{17,1},{2,18},{18,2},{3,19},{19,3},{4,20},{20... | collective-permute-start | bytes 172040 | tf_op jit(solution)/shard_map/ppermute | solution.py:35
  23.3 0.9 collective-permute-done
  24.1 5.0 %collective-permute-start.3 = (bf16[32,1792]{1,0:T(8,128)(2,1)S(1)}, bf16[32,1792]{1,0:T(8,128)(2,1)S(1)}, u32[]{:S(2)}, u32[]{:S(2)}) collective-permute-start(bf16[32,1792]{1,0:T(8,128)(2,1)S(1)} %pad_maximum_fusion.block0), channel_id=1, source_target_pairs={{0,3},{1,2},{2,1},{3,0},{4,7},{5,6},{6,5},{7,4},{8,11},{9,10},{10,... | collective-permute-start | bytes 344072 | tf_op jit(solution)/shard_map/ppermute | solution.py:35
  29.1 4.4 %collective-permute-start.2 = (bf16[32,1792]{1,0:T(8,128)(2,1)S(1)}, bf16[32,1792]{1,0:T(8,128)(2,1)S(1)}, u32[]{:S(2)}, u32[]{:S(2)}) collective-permute-start(bf16[32,1792]{1,0:T(8,128)(2,1)S(1)} %pad_maximum_fusion.block0), channel_id=1, source_target_pairs={{0,2},{1,3},{2,0},{3,1},{4,6},{5,7},{6,4},{7,5},{8,10},{9,11},{10,... | collective-permute-start | bytes 344072 | tf_op jit(solution)/shard_map/ppermute | solution.py:35
  33.6 2.0 %collective-permute-start.1 = (bf16[32,1792]{1,0:T(8,128)(2,1)S(1)}, bf16[32,1792]{1,0:T(8,128)(2,1)S(1)}, u32[]{:S(2)}, u32[]{:S(2)}) collective-permute-start(bf16[32,1792]{1,0:T(8,128)(2,1)S(1)} %pad_maximum_fusion.block0), channel_id=1, source_target_pairs={{0,1},{1,0},{2,3},{3,2},{4,5},{5,4},{6,7},{7,6},{8,9},{9,8},{10,11... | collective-permute-start | bytes 344072 | tf_op jit(solution)/shard_map/ppermute | solution.py:35
  35.5 0.0 collective-permute-done.3.block3
  35.6 9.1 %collective-permute-done.2.block2 = bf16[32,1792]{1,0:T(8,128)(2,1)S(1)} collective-permute-done((bf16[32,1792]{1,0:T(8,128)(2,1)S(1)}, bf16[32,1792]{1,0:T(8,128)(2,1)S(1)}, u32[]{:S(2)}, u32[]{:S(2)}) %collective-permute-start.2) | collective-permute-done | bytes 114720 | tf_op jit(solution)/shard_map/ppermute | solution.py:35
  44.7 2.3 %collective-permute-done.1.block1 = bf16[32,1792]{1,0:T(8,128)(2,1)S(1)} collective-permute-done((bf16[32,1792]{1,0:T(8,128)(2,1)S(1)}, bf16[32,1792]{1,0:T(8,128)(2,1)S(1)}, u32[]{:S(2)}, u32[]{:S(2)}) %collective-permute-start.1) | collective-permute-done | bytes 114720 | tf_op jit(solution)/shard_map/ppermute | solution.py:35
  47.0 0.0 all-to-all-done
  47.0 0.8 shard_map.46
  47.8 0.0 all-gather.3.cloned.1.call-update
  47.8 0.0 copy-done.2
  47.8 2.4 %collective-permute-start.4 = (bf16[896,896]{1,0:T(8,128)(2,1)S(1)}, bf16[896,896]{1,0:T(8,128)(2,1)}, u32[]{:S(2)}, u32[]{:S(2)}) collective-permute-start(bf16[896,896]{1,0:T(8,128)(2,1)S(1)} %copy-done.2), channel_id=1, source_target_pairs={{0,16},{16,0},{1,17},{17,1},{2,18},{18,2},{3,19},{19,3},{4,20},{20... | collective-permute-start | bytes 4816904 | tf_op jit(solution)/shard_map/ppermute | solution.py:35
  50.2 0.0 copy-done
  50.2 1.9 %collective-permute-start.5 = (bf16[512,256]{1,0:T(8,128)(2,1)S(1)}, bf16[512,256]{1,0:T(8,128)(2,1)S(1)}, u32[]{:S(2)}, u32[]{:S(2)}) collective-permute-start(bf16[512,256]{1,0:T(8,128)(2,1)S(1)} %copy-done), channel_id=1, source_target_pairs={{0,16},{16,0},{1,17},{17,1},{2,18},{18,2},{3,19},{19,3},{4,20},{20... | collective-permute-start | bytes 786440 | tf_op jit(solution)/shard_map/ppermute | solution.py:35
  52.2 1.5 collective-permute-done.5.other
  53.7 1.2 shard_map.48
  54.9 7.5 %all-to-all-start.2 = ((bf16[16,32,512]{2,1,0:T(8,128)(2,1)}), bf16[16,32,512]{2,1,0:T(8,128)(2,1)S(1)}, u32[]{:S(2)}, u32[]{:S(2)}) async-start(bf16[16,32,512]{2,1,0:T(8,128)(2,1)} %shard_map.48), calls=%async_computation.2 | async-start | bytes 1048576 | tf_op jit(solution)/shard_map/all_to_all | solution.py:143
  62.4 0.0 collective-permute-done.4.other
  62.4 24.5 %all-gather.3.cloned.1.call-done = bf16[8,128,896]{2,1,0:T(8,128)(2,1)} async-done(((bf16[2,128,896]{2,1,0:T(8,128)(2,1)}), bf16[8,128,896]{2,1,0:T(8,128)(2,1)}) %all-gather.3.cloned.1.call-update) | async-done | bytes 1835024 | tf_op jit(solution)/shard_map/all_gather | solution.py:135
  86.9 0.0 copy-start.1
  86.9 1.5 copy-done.1
  88.4 4.6 %shard_map.47 = (bf16[16,32,896]{2,1,0:T(8,128)(2,1)}, f32[8,128]{1,0:T(8,128)S(1)}) custom-call(bf16[4,2,128,896]{3,2,1,0:T(8,128)(2,1)S(1)} %bitcast.8, bf16[896,896]{1,0:T(8,128)(2,1)S(1)} %copy-done.2, bf16[896,896]{1,0:T(8,128)(2,1)} %collective-permute-done.4.other), custom_call_target="tpu_custom_call" | custom-call | flops 1644167168 | bytes 5967872 | tf_op jit(solution)/shard_map/pallas_call | solution.py:23
  93.0 0.0 all-to-all-done.2.parts
  93.0 6.7 %all-to-all-start.1 = ((bf16[16,32,896]{2,1,0:T(8,128)(2,1)}), bf16[16,32,896]{2,1,0:T(8,128)(2,1)S(1)}, u32[]{:S(2)}, u32[]{:S(2)}) async-start(bf16[16,32,896]{2,1,0:T(8,128)(2,1)} %get-tuple-element.16), calls=%async_computation.1 | async-start | bytes 1835008 | tf_op jit(solution)/shard_map/all_to_all | solution.py:152
  99.8 0.1 shard_map.49
  99.8 2.8 %collective-permute-start.6 = (bf16[32,256]{1,0:T(8,128)(2,1)S(1)}, bf16[32,256]{1,0:T(8,128)(2,1)S(1)}, u32[]{:S(2)}, u32[]{:S(2)}) collective-permute-start(bf16[32,256]{1,0:T(8,128)(2,1)S(1)} %get-tuple-element.20), channel_id=1, source_target_pairs={{0,16},{16,0},{1,17},{17,1},{2,18},{18,2},{3,19},{19,3},{4,20},{20... | collective-permute-start | bytes 49160 | tf_op jit(solution)/shard_map/ppermute | solution.py:35
  102.7 0.8 collective-permute-done.6
  103.5 5.3 %collective-permute-start.9 = (bf16[32,512]{1,0:T(8,128)(2,1)S(1)}, bf16[32,512]{1,0:T(8,128)(2,1)S(1)}, u32[]{:S(2)}, u32[]{:S(2)}) collective-permute-start(bf16[32,512]{1,0:T(8,128)(2,1)S(1)} %constant_dynamic-update-slice_fusion.block0), channel_id=1, source_target_pairs={{0,3},{1,2},{2,1},{3,0},{4,7},{5,6},{6,5},{7,4},{8,11},{9,10},{10,... | collective-permute-start | bytes 98312 | tf_op jit(solution)/shard_map/ppermute | solution.py:35
  108.8 3.9 %collective-permute-start.8 = (bf16[32,512]{1,0:T(8,128)(2,1)S(1)}, bf16[32,512]{1,0:T(8,128)(2,1)S(1)}, u32[]{:S(2)}, u32[]{:S(2)}) collective-permute-start(bf16[32,512]{1,0:T(8,128)(2,1)S(1)} %constant_dynamic-update-slice_fusion.block0), channel_id=1, source_target_pairs={{0,2},{1,3},{2,0},{3,1},{4,6},{5,7},{6,4},{7,5},{8,10},{9,11},{10,... | collective-permute-start | bytes 98312 | tf_op jit(solution)/shard_map/ppermute | solution.py:35
  112.7 2.2 %collective-permute-start.7 = (bf16[32,512]{1,0:T(8,128)(2,1)S(1)}, bf16[32,512]{1,0:T(8,128)(2,1)S(1)}, u32[]{:S(2)}, u32[]{:S(2)}) collective-permute-start(bf16[32,512]{1,0:T(8,128)(2,1)S(1)} %constant_dynamic-update-slice_fusion.block0), channel_id=1, source_target_pairs={{0,1},{1,0},{2,3},{3,2},{4,5},{5,4},{6,7},{7,6},{8,9},{9,8},{10,11... | collective-permute-start | bytes 98312 | tf_op jit(solution)/shard_map/ppermute | solution.py:35
  114.9 2.6 %collective-permute-done.9.block3 = bf16[32,512]{1,0:T(8,128)(2,1)S(1)} collective-permute-done((bf16[32,512]{1,0:T(8,128)(2,1)S(1)}, bf16[32,512]{1,0:T(8,128)(2,1)S(1)}, u32[]{:S(2)}, u32[]{:S(2)}) %collective-permute-start.9) | collective-permute-done | bytes 32800 | tf_op jit(solution)/shard_map/ppermute | solution.py:35
  117.5 2.2 %collective-permute-done.8.block2 = bf16[32,512]{1,0:T(8,128)(2,1)S(1)} collective-permute-done((bf16[32,512]{1,0:T(8,128)(2,1)S(1)}, bf16[32,512]{1,0:T(8,128)(2,1)S(1)}, u32[]{:S(2)}, u32[]{:S(2)}) %collective-permute-start.8) | collective-permute-done | bytes 32800 | tf_op jit(solution)/shard_map/ppermute | solution.py:35
  119.7 0.0 collective-permute-done.7.block1
  119.7 3.6 %all-to-all-done.1.parts = bf16[16,32,896]{2,1,0:T(8,128)(2,1)S(1)} async-done(((bf16[16,32,896]{2,1,0:T(8,128)(2,1)}), bf16[16,32,896]{2,1,0:T(8,128)(2,1)S(1)}, u32[]{:S(2)}, u32[]{:S(2)}) %all-to-all-start.1) | async-done | bytes 917536 | tf_op jit(solution)/shard_map/all_to_all | solution.py:152
  123.3 1.1 shard_map.51
  124.4 5.3 %all-to-all-start.3 = ((bf16[16,32,896]{2,1,0:T(8,128)(2,1)}), bf16[16,32,896]{2,1,0:T(8,128)(2,1)S(1)}, u32[]{:S(2)}, u32[]{:S(2)}) async-start(bf16[16,32,896]{2,1,0:T(8,128)(2,1)} %shard_map.51), calls=%async_computation.3 | async-start | bytes 1835008 | tf_op jit(solution)/shard_map/all_to_all | solution.py:160
  129.7 2.6 %collective-permute-start.12 = (bf16[128,512]{1,0:T(8,128)(2,1)S(1)}, bf16[128,512]{1,0:T(8,128)(2,1)S(1)}, u32[]{:S(2)}, u32[]{:S(2)}) collective-permute-start(bf16[128,512]{1,0:T(8,128)(2,1)S(1)} %shard_map.50.block0), channel_id=1, source_target_pairs={{0,12},{4,8},{8,4},{12,0},{1,13},{5,9},{9,5},{13,1},{2,14},{6,10},... | collective-permute-start | bytes 393224 | tf_op jit(solution)/shard_map/ppermute | solution.py:35
  132.3 3.3 %collective-permute-start.11 = (bf16[128,512]{1,0:T(8,128)(2,1)S(1)}, bf16[128,512]{1,0:T(8,128)(2,1)S(1)}, u32[]{:S(2)}, u32[]{:S(2)}) collective-permute-start(bf16[128,512]{1,0:T(8,128)(2,1)S(1)} %shard_map.50.block0), channel_id=1, source_target_pairs={{0,8},{4,12},{8,0},{12,4},{1,9},{5,13},{9,1},{13,5},{2,10},{6,14},... | collective-permute-start | bytes 393224 | tf_op jit(solution)/shard_map/ppermute | solution.py:35
  135.6 3.0 %collective-permute-start.10 = (bf16[128,512]{1,0:T(8,128)(2,1)S(1)}, bf16[128,512]{1,0:T(8,128)(2,1)S(1)}, u32[]{:S(2)}, u32[]{:S(2)}) collective-permute-start(bf16[128,512]{1,0:T(8,128)(2,1)S(1)} %shard_map.50.block0), channel_id=1, source_target_pairs={{0,4},{4,0},{8,12},{12,8},{1,5},{5,1},{9,13},{13,9},{2,6},{6,2},{1... | collective-permute-start | bytes 393224 | tf_op jit(solution)/shard_map/ppermute | solution.py:35
  138.7 0.0 collective-permute-done.12.block3
  138.7 0.9 collective-permute-done.11.block2
  139.6 2.3 %collective-permute-done.10.block1 = bf16[128,512]{1,0:T(8,128)(2,1)S(1)} collective-permute-done((bf16[128,512]{1,0:T(8,128)(2,1)S(1)}, bf16[128,512]{1,0:T(8,128)(2,1)S(1)}, u32[]{:S(2)}, u32[]{:S(2)}) %collective-permute-start.10) | collective-permute-done | bytes 131104 | tf_op jit(solution)/shard_map/ppermute | solution.py:35
  141.9 10.4 %all-to-all-done.3 = bf16[16,32,896]{2,1,0:T(8,128)(2,1)S(1)} async-done(((bf16[16,32,896]{2,1,0:T(8,128)(2,1)}), bf16[16,32,896]{2,1,0:T(8,128)(2,1)S(1)}, u32[]{:S(2)}, u32[]{:S(2)}) %all-to-all-start.3) | async-done | bytes 917536 | tf_op jit(solution)/shard_map/all_to_all | solution.py:160
  152.3 5.2 %collective-permute-start.13 = (bf16[512,896]{1,0:T(8,128)(2,1)S(1)}, bf16[512,896]{1,0:T(8,128)(2,1)S(1)}, u32[]{:S(2)}, u32[]{:S(2)}) collective-permute-start(bf16[512,896]{1,0:T(8,128)(2,1)S(1)} %bitcast.6), channel_id=1, source_target_pairs={{0,16},{16,0},{1,17},{17,1},{2,18},{18,2},{3,19},{19,3},{4,20},{20... | collective-permute-start | bytes 2752520 | tf_op jit(solution)/shard_map/ppermute | solution.py:35
  157.5 2.1 %collective-permute-done.13.act_theirs = bf16[512,896]{1,0:T(8,128)(2,1)S(1)} collective-permute-done((bf16[512,896]{1,0:T(8,128)(2,1)S(1)}, bf16[512,896]{1,0:T(8,128)(2,1)S(1)}, u32[]{:S(2)}, u32[]{:S(2)}) %collective-permute-start.13) | collective-permute-done | bytes 917536 | tf_op jit(solution)/shard_map/ppermute | solution.py:35
  159.6 1.7 shard_map.53
  (6 shorter events, 0.1 us)
Async XLA Ops:
  6.5 13.8 %copy-start.3 = (bf16[64,896]{1,0:T(8,128)(2,1)S(1)}, bf16[64,896]{1,0:T(8,128)(2,1)}, u32[]{:S(2)}) copy-start(bf16[64,896]{1,0:T(8,128)(2,1)} %param.5) | copy-start | bytes 344068
  8.2 39.6 %copy-start.2 = (bf16[896,896]{1,0:T(8,128)(2,1)S(1)}, bf16[896,896]{1,0:T(8,128)(2,1)}, u32[]{:S(2)}) copy-start(bf16[896,896]{1,0:T(8,128)(2,1)} %own.2) | copy-start | bytes 4816900
  8.2 42.1 %copy-start = (bf16[512,256]{1,0:T(8,128)(2,1)S(1)}, bf16[512,256]{1,0:T(8,128)(2,1)}, u32[]{:S(2)}) copy-start(bf16[512,256]{1,0:T(8,128)(2,1)} %own.3) | copy-start | bytes 786436
  8.2 38.8 %all-to-all-start = ((bf16[16,32,512]{2,1,0:T(8,128)(2,1)}), bf16[16,32,512]{2,1,0:T(8,128)(2,1)S(1)}, u32[]{:S(2)}, u32[]{:S(2)}) async-start(bf16[16,32,512]{2,1,0:T(8,128)(2,1)} %broadcast_in_dim.2), calls=%async_computation | async-start | bytes 1048576 | tf_op jit(solution)/shard_map/all_to_all | solution.py:128
  20.3 66.6 %all-gather.3.cloned.1.call-start = ((), (), s32[]{:S(2)}) async-start(), calls=%async_computation.4 | async-start | bytes 2293760 | tf_op jit(solution)/shard_map/all_gather | solution.py:135
  20.4 3.7 %collective-permute-start = (bf16[32,896]{1,0:T(8,128)(2,1)S(1)}, bf16[32,896]{1,0:T(8,128)(2,1)S(1)}, u32[]{:S(2)}, u32[]{:S(2)}) collective-permute-start(bf16[32,896]{1,0:T(8,128)(2,1)S(1)} %get-tuple-element.26), channel_id=1, source_target_pairs={{0,16},{16,0},{1,17},{17,1},{2,18},{18,2},{3,19},{19,3},{4,20},{20... | collective-permute-start | bytes 172040 | tf_op jit(solution)/shard_map/ppermute | solution.py:35
  24.1 11.4 %collective-permute-start.3 = (bf16[32,1792]{1,0:T(8,128)(2,1)S(1)}, bf16[32,1792]{1,0:T(8,128)(2,1)S(1)}, u32[]{:S(2)}, u32[]{:S(2)}) collective-permute-start(bf16[32,1792]{1,0:T(8,128)(2,1)S(1)} %pad_maximum_fusion.block0), channel_id=1, source_target_pairs={{0,3},{1,2},{2,1},{3,0},{4,7},{5,6},{6,5},{7,4},{8,11},{9,10},{10,... | collective-permute-start | bytes 344072 | tf_op jit(solution)/shard_map/ppermute | solution.py:35
  29.1 15.6 %collective-permute-start.2 = (bf16[32,1792]{1,0:T(8,128)(2,1)S(1)}, bf16[32,1792]{1,0:T(8,128)(2,1)S(1)}, u32[]{:S(2)}, u32[]{:S(2)}) collective-permute-start(bf16[32,1792]{1,0:T(8,128)(2,1)S(1)} %pad_maximum_fusion.block0), channel_id=1, source_target_pairs={{0,2},{1,3},{2,0},{3,1},{4,6},{5,7},{6,4},{7,5},{8,10},{9,11},{10,... | collective-permute-start | bytes 344072 | tf_op jit(solution)/shard_map/ppermute | solution.py:35
  33.6 13.4 %collective-permute-start.1 = (bf16[32,1792]{1,0:T(8,128)(2,1)S(1)}, bf16[32,1792]{1,0:T(8,128)(2,1)S(1)}, u32[]{:S(2)}, u32[]{:S(2)}) collective-permute-start(bf16[32,1792]{1,0:T(8,128)(2,1)S(1)} %pad_maximum_fusion.block0), channel_id=1, source_target_pairs={{0,1},{1,0},{2,3},{3,2},{4,5},{5,4},{6,7},{7,6},{8,9},{9,8},{10,11... | collective-permute-start | bytes 344072 | tf_op jit(solution)/shard_map/ppermute | solution.py:35
  47.8 14.6 %collective-permute-start.4 = (bf16[896,896]{1,0:T(8,128)(2,1)S(1)}, bf16[896,896]{1,0:T(8,128)(2,1)}, u32[]{:S(2)}, u32[]{:S(2)}) collective-permute-start(bf16[896,896]{1,0:T(8,128)(2,1)S(1)} %copy-done.2), channel_id=1, source_target_pairs={{0,16},{16,0},{1,17},{17,1},{2,18},{18,2},{3,19},{19,3},{4,20},{20... | collective-permute-start | bytes 4816904 | tf_op jit(solution)/shard_map/ppermute | solution.py:35
  50.2 3.4 %collective-permute-start.5 = (bf16[512,256]{1,0:T(8,128)(2,1)S(1)}, bf16[512,256]{1,0:T(8,128)(2,1)S(1)}, u32[]{:S(2)}, u32[]{:S(2)}) collective-permute-start(bf16[512,256]{1,0:T(8,128)(2,1)S(1)} %copy-done), channel_id=1, source_target_pairs={{0,16},{16,0},{1,17},{17,1},{2,18},{18,2},{3,19},{19,3},{4,20},{20... | collective-permute-start | bytes 786440 | tf_op jit(solution)/shard_map/ppermute | solution.py:35
  54.9 38.1 %all-to-all-start.2 = ((bf16[16,32,512]{2,1,0:T(8,128)(2,1)}), bf16[16,32,512]{2,1,0:T(8,128)(2,1)S(1)}, u32[]{:S(2)}, u32[]{:S(2)}) async-start(bf16[16,32,512]{2,1,0:T(8,128)(2,1)} %shard_map.48), calls=%async_computation.2 | async-start | bytes 1048576 | tf_op jit(solution)/shard_map/all_to_all | solution.py:143
  86.9 1.5 copy-start.1
  93.0 30.3 %all-to-all-start.1 = ((bf16[16,32,896]{2,1,0:T(8,128)(2,1)}), bf16[16,32,896]{2,1,0:T(8,128)(2,1)S(1)}, u32[]{:S(2)}, u32[]{:S(2)}) async-start(bf16[16,32,896]{2,1,0:T(8,128)(2,1)} %get-tuple-element.16), calls=%async_computation.1 | async-start | bytes 1835008 | tf_op jit(solution)/shard_map/all_to_all | solution.py:152
  99.8 3.6 %collective-permute-start.6 = (bf16[32,256]{1,0:T(8,128)(2,1)S(1)}, bf16[32,256]{1,0:T(8,128)(2,1)S(1)}, u32[]{:S(2)}, u32[]{:S(2)}) collective-permute-start(bf16[32,256]{1,0:T(8,128)(2,1)S(1)} %get-tuple-element.20), channel_id=1, source_target_pairs={{0,16},{16,0},{1,17},{17,1},{2,18},{18,2},{3,19},{19,3},{4,20},{20... | collective-permute-start | bytes 49160 | tf_op jit(solution)/shard_map/ppermute | solution.py:35
  103.5 14.0 %collective-permute-start.9 = (bf16[32,512]{1,0:T(8,128)(2,1)S(1)}, bf16[32,512]{1,0:T(8,128)(2,1)S(1)}, u32[]{:S(2)}, u32[]{:S(2)}) collective-permute-start(bf16[32,512]{1,0:T(8,128)(2,1)S(1)} %constant_dynamic-update-slice_fusion.block0), channel_id=1, source_target_pairs={{0,3},{1,2},{2,1},{3,0},{4,7},{5,6},{6,5},{7,4},{8,11},{9,10},{10,... | collective-permute-start | bytes 98312 | tf_op jit(solution)/shard_map/ppermute | solution.py:35
  108.8 10.9 %collective-permute-start.8 = (bf16[32,512]{1,0:T(8,128)(2,1)S(1)}, bf16[32,512]{1,0:T(8,128)(2,1)S(1)}, u32[]{:S(2)}, u32[]{:S(2)}) collective-permute-start(bf16[32,512]{1,0:T(8,128)(2,1)S(1)} %constant_dynamic-update-slice_fusion.block0), channel_id=1, source_target_pairs={{0,2},{1,3},{2,0},{3,1},{4,6},{5,7},{6,4},{7,5},{8,10},{9,11},{10,... | collective-permute-start | bytes 98312 | tf_op jit(solution)/shard_map/ppermute | solution.py:35
  112.7 7.0 %collective-permute-start.7 = (bf16[32,512]{1,0:T(8,128)(2,1)S(1)}, bf16[32,512]{1,0:T(8,128)(2,1)S(1)}, u32[]{:S(2)}, u32[]{:S(2)}) collective-permute-start(bf16[32,512]{1,0:T(8,128)(2,1)S(1)} %constant_dynamic-update-slice_fusion.block0), channel_id=1, source_target_pairs={{0,1},{1,0},{2,3},{3,2},{4,5},{5,4},{6,7},{7,6},{8,9},{9,8},{10,11... | collective-permute-start | bytes 98312 | tf_op jit(solution)/shard_map/ppermute | solution.py:35
  124.4 28.0 %all-to-all-start.3 = ((bf16[16,32,896]{2,1,0:T(8,128)(2,1)}), bf16[16,32,896]{2,1,0:T(8,128)(2,1)S(1)}, u32[]{:S(2)}, u32[]{:S(2)}) async-start(bf16[16,32,896]{2,1,0:T(8,128)(2,1)} %shard_map.51), calls=%async_computation.3 | async-start | bytes 1835008 | tf_op jit(solution)/shard_map/all_to_all | solution.py:160
  129.7 9.0 %collective-permute-start.12 = (bf16[128,512]{1,0:T(8,128)(2,1)S(1)}, bf16[128,512]{1,0:T(8,128)(2,1)S(1)}, u32[]{:S(2)}, u32[]{:S(2)}) collective-permute-start(bf16[128,512]{1,0:T(8,128)(2,1)S(1)} %shard_map.50.block0), channel_id=1, source_target_pairs={{0,12},{4,8},{8,4},{12,0},{1,13},{5,9},{9,5},{13,1},{2,14},{6,10},... | collective-permute-start | bytes 393224 | tf_op jit(solution)/shard_map/ppermute | solution.py:35
  132.3 7.3 %collective-permute-start.11 = (bf16[128,512]{1,0:T(8,128)(2,1)S(1)}, bf16[128,512]{1,0:T(8,128)(2,1)S(1)}, u32[]{:S(2)}, u32[]{:S(2)}) collective-permute-start(bf16[128,512]{1,0:T(8,128)(2,1)S(1)} %shard_map.50.block0), channel_id=1, source_target_pairs={{0,8},{4,12},{8,0},{12,4},{1,9},{5,13},{9,1},{13,5},{2,10},{6,14},... | collective-permute-start | bytes 393224 | tf_op jit(solution)/shard_map/ppermute | solution.py:35
  135.6 6.3 %collective-permute-start.10 = (bf16[128,512]{1,0:T(8,128)(2,1)S(1)}, bf16[128,512]{1,0:T(8,128)(2,1)S(1)}, u32[]{:S(2)}, u32[]{:S(2)}) collective-permute-start(bf16[128,512]{1,0:T(8,128)(2,1)S(1)} %shard_map.50.block0), channel_id=1, source_target_pairs={{0,4},{4,0},{8,12},{12,8},{1,5},{5,1},{9,13},{13,9},{2,6},{6,2},{1... | collective-permute-start | bytes 393224 | tf_op jit(solution)/shard_map/ppermute | solution.py:35
  152.3 7.2 %collective-permute-start.13 = (bf16[512,896]{1,0:T(8,128)(2,1)S(1)}, bf16[512,896]{1,0:T(8,128)(2,1)S(1)}, u32[]{:S(2)}, u32[]{:S(2)}) collective-permute-start(bf16[512,896]{1,0:T(8,128)(2,1)S(1)} %bitcast.6), channel_id=1, source_target_pairs={{0,16},{16,0},{1,17},{17,1},{2,18},{18,2},{3,19},{19,3},{4,20},{20... | collective-permute-start | bytes 2752520 | tf_op jit(solution)/shard_map/ppermute | solution.py:35
Sparse Core Ops, SparseCore 0:
  47.9 38.9 all-gather.2

commit v10 on v9

v10 whole, which is shorter than its diff:
```python
import jax
import jax.numpy as jnp
from jax import lax
from jax.experimental import pallas as pl
from jax.experimental.pallas import tpu as pltpu
from jax.sharding import Mesh, PartitionSpec as P

SEQS = 2
SEQ_LEN = 512
OUT = ("z", "ylo", "core")
INP = ("x", "yhi")
CHIPS = ("z", "ylo")
BF16 = jnp.bfloat16
F32 = jnp.float32
ANY = pl.BlockSpec(memory_space=pl.ANY)
VMEM = pl.BlockSpec(memory_space=pltpu.VMEM)


def kernel_call(body, shapes, args, flops=0, unread=0):
    moved = sum(a.size * a.dtype.itemsize for a in args) + sum(s.size * s.dtype.itemsize for s in shapes)
    many = len(shapes) > 1
    return pl.pallas_call(
        body,
        out_shape=shapes if many else shapes[0],
        in_specs=[VMEM] * (len(args) - unread) + [ANY] * unread,
        out_specs=[VMEM] * len(shapes) if many else VMEM,
        compiler_params=pltpu.CompilerParams(vmem_limit_bytes=40 * 2**20),
        cost_estimate=pl.CostEstimate(flops=flops, bytes_accessed=moved, transcendentals=0),
    )(*args)


def swap(value, axis, flip):
    size = lax.axis_size(axis)
    return lax.ppermute(value, axis, [(s, s ^ flip) for s in range(size)])


def gather_yhi(mine):
    return [mine, swap(mine, "yhi", 1), swap(mine, "yhi", 2), swap(mine, "yhi", 3)]


def stack_acts_kernel(block0, block1, block2, block3, order, out):
    rows, features = block0.shape[0], out.shape[2]
    for index, block in enumerate((block0, block1, block2, block3)):
        for side in range(2):
            out[side, index * rows:(index + 1) * rows, :] = block[:, side * features:(side + 1) * features]


def stack_kernel(block0, block1, block2, block3, out):
    rows = block0.shape[0]
    for index, block in enumerate((block0, block1, block2, block3)):
        out[index * rows:(index + 1) * rows, :] = block[...]


def act_dot_kernel(act0, act1, low2, high2, act3, basis0, basis1, out, done):
    first = [act0[0], act1[0], low2[...], act3[0]]
    second = [act0[1], act1[1], high2[...], act3[1]]
    total = 0.0
    for rows, basis in ((first, basis0), (second, basis1)):
        total += jnp.dot(jnp.concatenate(rows), basis[...], preferred_element_type=F32)
    out[...] = total.astype(BF16).reshape(out.shape)
    done[...] = jnp.zeros_like(done)


def grad_dot_kernel(rows, own, other, order, out):
    columns = own.shape[1]
    total = jnp.concatenate(
        [jnp.dot(rows[...], basis[...], preferred_element_type=F32) for basis in (own, other)], axis=1
    )
    out[...] = total.astype(BF16).reshape(out.shape)


def sum_parts(parts):
    total = parts[0].astype(F32)
    for index in range(1, parts.shape[0]):
        total += parts[index].astype(F32)
    return total.astype(BF16)


def sum_copies_kernel(parts, out):
    rounded = sum_parts(parts)
    for index in range(out.shape[0]):
        out[index] = rounded


def sum_split_kernel(done, parts, mine, give):
    rounded = sum_parts(parts)
    columns = mine.shape[1]
    mine[...] = rounded[:, :columns]
    give[...] = rounded[:, columns:]


def square_kernel(g0, g1, g2, g3, act_mine, act_theirs, out):
    columns = out.shape[0]
    half = act_mine.shape[0] // SEQS
    grads = (jnp.concatenate([g0[...], g1[...]]), jnp.concatenate([g2[...], g3[...]]))
    total = 0.0
    for seq in range(SEQS):
        rows = slice(seq * half, (seq + 1) * half)
        contract = (((0,), (0,)), ((), ()))
        rotated = lax.dot_general(grads[seq][:, :columns], act_mine[rows, :], contract, preferred_element_type=F32)
        rotated += lax.dot_general(grads[seq][:, columns:], act_theirs[rows, :], contract, preferred_element_type=F32)
        total = total + rotated * rotated
    out[...] = total * (1.0 / (SEQS * SEQ_LEN))


def both(index, own, other):
    return jnp.where(index == 0, own, other), jnp.where(index == 0, other, own)


def shards(grads, acts, grad_basis, act_basis):
    core = lax.axis_index("core")
    half, features = acts.shape[0] // 2, acts.shape[1]
    tokens, eig = 16 * half, act_basis.shape[1]
    rows, columns = grads.shape[0], grad_basis.shape[1]

    keep = lax.dynamic_slice_in_dim(acts, core * half, half)
    give = lax.dynamic_slice_in_dim(acts, (1 - core) * half, half)
    act_own = jnp.concatenate(both(core, keep, swap(give, "core", 1)), axis=1)
    act_basis0, act_basis1 = both(core, act_basis, swap(act_basis, "core", 1))
    grad_basis_other = swap(grad_basis, "core", 1)

    grad_copies = jnp.broadcast_to(grads[None], (16, *grads.shape))
    grad_rows = lax.all_to_all(grad_copies, CHIPS, 0, 0, tiled=True).reshape(tokens, -1)
    act0 = kernel_call(
        stack_acts_kernel,
        [jax.ShapeDtypeStruct((2, 4 * half, features), BF16)],
        [*gather_yhi(act_own), grad_rows],
        unread=1,
    )
    act1, act3 = swap(act0, "x", 1), swap(act0, "x", 3)
    low2, high2 = swap(act3[0], "x", 1), swap(act1[1], "x", 3)

    grad_partial = kernel_call(
        grad_dot_kernel,
        [jax.ShapeDtypeStruct((16, rows, 2 * columns), BF16)],
        [grad_rows, grad_basis, grad_basis_other, act1],
        flops=2 * tokens * grads.shape[1] * 2 * columns,
        unread=1,
    )
    grad_parts = lax.all_to_all(grad_partial, INP, 0, 0, tiled=True)

    blocks = jax.ShapeDtypeStruct((16, half, eig), BF16)
    act_partial, done = kernel_call(
        act_dot_kernel,
        [blocks, jax.ShapeDtypeStruct((8, 128), F32)],
        [act0, act1, low2, high2, act3, act_basis0, act_basis1],
        flops=2 * tokens * 2 * features * eig,
    )
    act_parts = lax.all_to_all(act_partial, CHIPS, 0, 0, tiled=True)

    narrow = jax.ShapeDtypeStruct((rows, columns), BF16)
    grad_mine, grad_give = kernel_call(sum_split_kernel, [narrow, narrow], [done, grad_parts])
    grad_own = jnp.concatenate([grad_mine, swap(grad_give, "core", 1)], axis=1)
    g0 = kernel_call(stack_kernel, [jax.ShapeDtypeStruct((4 * rows, 2 * columns), BF16)], gather_yhi(grad_own))
    act_parts, g0 = lax.optimization_barrier((act_parts, g0))

    act_mine = lax.all_to_all(kernel_call(sum_copies_kernel, [blocks], [act_parts]), CHIPS, 0, 0, tiled=True)
    g1, g2, g3 = swap(g0, "x", 1), swap(g0, "x", 2), swap(g0, "x", 3)
    act_mine, g1, g2, g3 = lax.optimization_barrier((act_mine.reshape(tokens, eig), g1, g2, g3))
    act_theirs = swap(act_mine, "core", 1)

    return kernel_call(
        square_kernel,
        [jax.ShapeDtypeStruct((columns, eig), F32)],
        [g0, g1, g2, g3, act_mine, act_theirs],
        flops=2 * 2 * tokens * columns * eig,
    )


def solution(mesh):
    split = Mesh(mesh.devices.reshape(8, 2, 2, 4, 4), OUT + INP)
    return jax.shard_map(
        shards,
        mesh=split,
        in_specs=(P(OUT, INP), P(INP, OUT), P(INP, OUT), P(OUT, INP)),
        out_specs=P(OUT, INP),
        check_vma=False,
    )
```

time: 169 us -> 153 us (0.905)
  waiting for transfers between devices: 63.2 us -> 45.4 us
  starting transfers between devices: 78.6 us -> 94.8 us
  between operations: 13.6 us -> 0.32 us
  Pallas kernels: 9.48 us -> 7.24 us
  other arithmetic: 0.01 us -> 2.24 us
    all_gather x1 -> x0, waiting for transfers between devices: 24.5 us -> none  [shards(): act_rows = lax.all_gather(act_yhi, 'x')]
    ppermute x14 -> x18, starting transfers between devices: 46.9 us -> 62.7 us  [swap(): return lax.ppermute(value, axis, [(s, s ^ flip) for s in range(size)])]
    ppermute x14 -> x18, waiting for transfers between devices: 24.7 us -> 33.9 us  [swap(): return lax.ppermute(value, axis, [(s, s ^ flip) for s in range(size)])]
    pallas_call x8 -> x7, Pallas kernels: 9.48 us -> 7.24 us  [kernel_call(): pl.pallas_call(body, out_shape=shapes if many else shapes[0], in_specs=[V...]
    select_n x0 -> x2, other arithmetic: none -> 2.23 us  [the longest x1 2.21 us: both(): jnp.where(index == 0, other, own)]
    all_to_all x1, waiting for transfers between devices: 3.56 us -> 1.83 us  [shards(): act_parts = lax.all_to_all(act_partial, CHIPS, 0, 0, tiled=True)]
  transfers between devices with their start and end apart: 19 -> 22, of which waited for: 13 -> 14; matrix products, arithmetic and copies ran while one was open for 0% -> 2% of each run, Pallas kernels for 4% -> 3%
where the time goes in v10:
time: 153 us; the launch traced here: 152 us
  starting transfers between devices  94.8 us (62%)
  waiting for transfers between devices  45.4 us (30%)
  Pallas kernels  7.24 us (5%)
  other arithmetic  2.24 us (1%)
  local copies, waits for them, and re-layouts  1.7 us (1%)
    ppermute x18, starting transfers between devices, swap(): return lax.ppermute(value, axis, [(s, s ^ flip) for s in range(size)])  62.7 us
    ppermute x18, waiting for transfers between devices, swap(): return lax.ppermute(value, axis, [(s, s ^ flip) for s in range(size)])  33.9 us
    all_to_all x1, starting transfers between devices, shards(): lax.all_to_all(grad_copies, CHIPS, 0, 0, tiled=True).reshape(tokens, -1)  12.1 us
    all_to_all x1, waiting for transfers between devices, shards(): lax.all_to_all(kernel_call(sum_copies_kernel, [blocks], [act_parts]), CHI...  9.73 us
    all_to_all x1, starting transfers between devices, shards(): grad_parts = lax.all_to_all(grad_partial, INP, 0, 0, tiled=True)  7.46 us
    pallas_call x7, Pallas kernels, kernel_call(): pl.pallas_call(body, out_shape=shapes if many else shapes[0], in_specs=[V...  7.24 us
    all_to_all x1, starting transfers between devices, shards(): act_parts = lax.all_to_all(act_partial, CHIPS, 0, 0, tiled=True)  6.44 us
    all_to_all x1, starting transfers between devices, shards(): lax.all_to_all(kernel_call(sum_copies_kernel, [blocks], [act_parts]), CHI...  6.09 us
  transfers between devices with their start and end apart: 22, of which 14 were waited for; matrix products, arithmetic and copies ran while one was open for 2% of the time, Pallas kernels for 3%

profile of v10, /device:TPU:1, one launch (start us, length us, event | category | flops | bytes accessed | tf_op | source)
XLA Modules:
  0.0 151.7 jit_solution(16258523882512943453)
XLA Ops:
  0.0 0.0 copy-start.1
  0.0 1.6 %broadcast_in_dim.2 = bf16[16,32,512]{2,1,0:T(8,128)(2,1)} broadcast(bf16[32,512]{1,0:T(8,128)(2,1)} %param.4), dimensions={1,2} | broadcast | bytes 557056 | tf_op jit(solution)/shard_map/broadcast_in_dim | solution.py:122
  1.6 0.0 copy-start
  1.6 12.1 %all-to-all-start = ((bf16[16,32,512]{2,1,0:T(8,128)(2,1)}), bf16[16,32,512]{2,1,0:T(8,128)(2,1)S(1)}, u32[]{:S(2)}, u32[]{:S(2)}) async-start(bf16[16,32,512]{2,1,0:T(8,128)(2,1)} %broadcast_in_dim.2), calls=%async_computation | async-start | bytes 1048576 | tf_op jit(solution)/shard_map/all_to_all | solution.py:123
  13.8 2.9 %collective-permute-start.8 = (bf16[896,896]{1,0:T(8,128)(2,1)}, bf16[896,896]{1,0:T(8,128)(2,1)}, u32[]{:S(2)}, u32[]{:S(2)}) collective-permute-start(bf16[896,896]{1,0:T(8,128)(2,1)} %param.7), channel_id=1, source_target_pairs={{0,16},{16,0},{1,17},{17,1},{2,18},{18,2},{3,19},{19,3},{4,20},{20... | collective-permute-start | bytes 4816904 | tf_op jit(solution)/shard_map/ppermute | solution.py:34
  16.6 0.0 copy-done.1
  16.7 1.9 %collective-permute-start = (bf16[32,896]{1,0:T(8,128)(2,1)S(1)}, bf16[32,896]{1,0:T(8,128)(2,1)S(1)}, u32[]{:S(2)}, u32[]{:S(2)}) collective-permute-start(bf16[32,896]{1,0:T(8,128)(2,1)S(1)} %constant_dynamic-slice_fusion), channel_id=1, source_target_pairs={{0,16},{16,0},{1,17},{17,1},{2,18},{18,2},{3,19},{19,3},{4,20},{20... | collective-permute-start | bytes 172040 | tf_op jit(solution)/shard_map/ppermute | solution.py:34
  18.6 1.2 collective-permute-done
  19.9 5.0 %collective-permute-start.3 = (bf16[32,1792]{1,0:T(8,128)(2,1)S(1)}, bf16[32,1792]{1,0:T(8,128)(2,1)S(1)}, u32[]{:S(2)}, u32[]{:S(2)}) collective-permute-start(bf16[32,1792]{1,0:T(8,128)(2,1)S(1)} %pad_maximum_fusion.block0), channel_id=1, source_target_pairs={{0,3},{1,2},{2,1},{3,0},{4,7},{5,6},{6,5},{7,4},{8,11},{9,10},{10,... | collective-permute-start | bytes 344072 | tf_op jit(solution)/shard_map/ppermute | solution.py:34
  24.8 4.4 %collective-permute-start.2 = (bf16[32,1792]{1,0:T(8,128)(2,1)S(1)}, bf16[32,1792]{1,0:T(8,128)(2,1)S(1)}, u32[]{:S(2)}, u32[]{:S(2)}) collective-permute-start(bf16[32,1792]{1,0:T(8,128)(2,1)S(1)} %pad_maximum_fusion.block0), channel_id=1, source_target_pairs={{0,2},{1,3},{2,0},{3,1},{4,6},{5,7},{6,4},{7,5},{8,10},{9,11},{10,... | collective-permute-start | bytes 344072 | tf_op jit(solution)/shard_map/ppermute | solution.py:34
  29.3 2.0 %collective-permute-start.1 = (bf16[32,1792]{1,0:T(8,128)(2,1)S(1)}, bf16[32,1792]{1,0:T(8,128)(2,1)S(1)}, u32[]{:S(2)}, u32[]{:S(2)}) collective-permute-start(bf16[32,1792]{1,0:T(8,128)(2,1)S(1)} %pad_maximum_fusion.block0), channel_id=1, source_target_pairs={{0,1},{1,0},{2,3},{3,2},{4,5},{5,4},{6,7},{7,6},{8,9},{9,8},{10,11... | collective-permute-start | bytes 344072 | tf_op jit(solution)/shard_map/ppermute | solution.py:34
  31.3 0.0 collective-permute-done.3.block3
  31.3 9.1 %collective-permute-done.2.block2 = bf16[32,1792]{1,0:T(8,128)(2,1)S(1)} collective-permute-done((bf16[32,1792]{1,0:T(8,128)(2,1)S(1)}, bf16[32,1792]{1,0:T(8,128)(2,1)S(1)}, u32[]{:S(2)}, u32[]{:S(2)}) %collective-permute-start.2) | collective-permute-done | bytes 114720 | tf_op jit(solution)/shard_map/ppermute | solution.py:34
  40.4 2.3 %collective-permute-done.1.block1 = bf16[32,1792]{1,0:T(8,128)(2,1)S(1)} collective-permute-done((bf16[32,1792]{1,0:T(8,128)(2,1)S(1)}, bf16[32,1792]{1,0:T(8,128)(2,1)S(1)}, u32[]{:S(2)}, u32[]{:S(2)}) %collective-permute-start.1) | collective-permute-done | bytes 114720 | tf_op jit(solution)/shard_map/ppermute | solution.py:34
  42.7 0.0 all-to-all-done
  42.7 3.1 %collective-permute-start.4 = (bf16[2,128,896]{2,1,0:T(8,128)(2,1)S(1)}, bf16[2,128,896]{2,1,0:T(8,128)(2,1)S(1)}, u32[]{:S(2)}, u32[]{:S(2)}) collective-permute-start(bf16[2,128,896]{2,1,0:T(8,128)(2,1)S(1)} %shard_map.46.act0), channel_id=1, source_target_pairs={{0,4},{4,0},{8,12},{12,8},{1,5},{5,1},{9,13},{13,9},{2,6},{6,2},{1... | collective-permute-start | bytes 1376264 | tf_op jit(solution)/shard_map/ppermute | solution.py:34
  45.9 3.7 %collective-permute-start.5 = (bf16[2,128,896]{2,1,0:T(8,128)(2,1)S(1)}, bf16[2,128,896]{2,1,0:T(8,128)(2,1)S(1)}, u32[]{:S(2)}, u32[]{:S(2)}) collective-permute-start(bf16[2,128,896]{2,1,0:T(8,128)(2,1)S(1)} %shard_map.46.act0), channel_id=1, source_target_pairs={{0,12},{4,8},{8,4},{12,0},{1,13},{5,9},{9,5},{13,1},{2,14},{6,10},... | collective-permute-start | bytes 1376264 | tf_op jit(solution)/shard_map/ppermute | solution.py:34
  49.6 0.0 copy-done
  49.6 3.0 %collective-permute-start.9 = (bf16[512,256]{1,0:T(8,128)(2,1)S(1)}, bf16[512,256]{1,0:T(8,128)(2,1)S(1)}, u32[]{:S(2)}, u32[]{:S(2)}) collective-permute-start(bf16[512,256]{1,0:T(8,128)(2,1)S(1)} %copy-done), channel_id=1, source_target_pairs={{0,16},{16,0},{1,17},{17,1},{2,18},{18,2},{3,19},{19,3},{4,20},{20... | collective-permute-start | bytes 786440 | tf_op jit(solution)/shard_map/ppermute | solution.py:34
  52.6 1.1 collective-permute-done.9.other
  53.7 2.5 %collective-permute-done.4.act1.order = bf16[2,128,896]{2,1,0:T(8,128)(2,1)S(1)} collective-permute-done((bf16[2,128,896]{2,1,0:T(8,128)(2,1)S(1)}, bf16[2,128,896]{2,1,0:T(8,128)(2,1)S(1)}, u32[]{:S(2)}, u32[]{:S(2)}) %collective-permute-start.4) | collective-permute-done | bytes 458784 | tf_op jit(solution)/shard_map/ppermute | solution.py:34
  56.2 1.2 shard_map.48
  57.5 7.5 %all-to-all-start.2 = ((bf16[16,32,512]{2,1,0:T(8,128)(2,1)}), bf16[16,32,512]{2,1,0:T(8,128)(2,1)S(1)}, u32[]{:S(2)}, u32[]{:S(2)}) async-start(bf16[16,32,512]{2,1,0:T(8,128)(2,1)} %shard_map.48), calls=%async_computation.2 | async-start | bytes 1048576 | tf_op jit(solution)/shard_map/all_to_all | solution.py:140
  64.9 0.0 collective-permute-done.5.act3
  65.0 3.3 %collective-permute-start.6 = (bf16[128,896]{1,0:T(8,128)(2,1)S(1)}, bf16[128,896]{1,0:T(8,128)(2,1)S(1)}, u32[]{:S(2)}, u32[]{:S(2)}) collective-permute-start(bf16[128,896]{1,0:T(8,128)(2,1)S(1)} %slice_bitcast_fusion.1), channel_id=1, source_target_pairs={{0,4},{4,0},{8,12},{12,8},{1,5},{5,1},{9,13},{13,9},{2,6},{6,2},{1... | collective-permute-start | bytes 688136 | tf_op jit(solution)/shard_map/ppermute | solution.py:34
  68.3 3.7 %collective-permute-start.7 = (bf16[128,896]{1,0:T(8,128)(2,1)S(1)}, bf16[128,896]{1,0:T(8,128)(2,1)S(1)}, u32[]{:S(2)}, u32[]{:S(2)}) collective-permute-start(bf16[128,896]{1,0:T(8,128)(2,1)S(1)} %slice_bitcast_fusion), channel_id=1, source_target_pairs={{0,12},{4,8},{8,4},{12,0},{1,13},{5,9},{9,5},{13,1},{2,14},{6,10},... | collective-permute-start | bytes 688136 | tf_op jit(solution)/shard_map/ppermute | solution.py:34
  72.0 0.0 collective-permute-done.8
  72.0 2.2 %broadcast_select_fusion = (bf16[896,896]{1,0:T(8,128)(2,1)S(1)}, bf16[896,896]{1,0:T(8,128)(2,1)S(1)}) fusion(bf16[896,896]{1,0:T(8,128)(2,1)} %collective-permute-done.8, bf16[896,896]{1,0:T(8,128)(2,1)} %param.7, pred[]{:T(512)S(6)} %eq.2), kind=kLoop, calls=%fused_computation | loop fusion | flops 1605632 | bytes 6422529 | tf_op jit(solution)/shard_map/jit(_where)/select_n | solution.py:107
  74.2 0.0 collective-permute-done.6.low2
  74.2 6.7 %collective-permute-done.7.high2 = bf16[128,896]{1,0:T(8,128)(2,1)S(1)} collective-permute-done((bf16[128,896]{1,0:T(8,128)(2,1)S(1)}, bf16[128,896]{1,0:T(8,128)(2,1)S(1)}, u32[]{:S(2)}, u32[]{:S(2)}) %collective-permute-start.7) | collective-permute-done | bytes 229408 | tf_op jit(solution)/shard_map/ppermute | solution.py:34
  80.9 3.2 %shard_map.47 = (bf16[16,32,896]{2,1,0:T(8,128)(2,1)}, f32[8,128]{1,0:T(8,128)S(1)}) custom-call(bf16[2,128,896]{2,1,0:T(8,128)(2,1)S(1)} %shard_map.46.act0, bf16[2,128,896]{2,1,0:T(8,128)(2,1)S(1)} %collective-permute-done.4.act1.order, bf16[128,896]{1,0:T(8,128)(2,1)S(1)} %collective-permute-done.6.low2, ...), custom_call_target="tpu_custom_call" | custom-call | flops 1644167168 | bytes 5967872 | tf_op jit(solution)/shard_map/pallas_call | solution.py:22
  84.1 0.0 all-to-all-done.2.parts
  84.1 6.4 %all-to-all-start.1 = ((bf16[16,32,896]{2,1,0:T(8,128)(2,1)}), bf16[16,32,896]{2,1,0:T(8,128)(2,1)S(1)}, u32[]{:S(2)}, u32[]{:S(2)}) async-start(bf16[16,32,896]{2,1,0:T(8,128)(2,1)} %get-tuple-element.15), calls=%async_computation.1 | async-start | bytes 1835008 | tf_op jit(solution)/shard_map/all_to_all | solution.py:149
  90.5 0.1 shard_map.49
  90.6 5.1 %collective-permute-start.10 = (bf16[32,256]{1,0:T(8,128)(2,1)S(1)}, bf16[32,256]{1,0:T(8,128)(2,1)S(1)}, u32[]{:S(2)}, u32[]{:S(2)}) collective-permute-start(bf16[32,256]{1,0:T(8,128)(2,1)S(1)} %get-tuple-element.18), channel_id=1, source_target_pairs={{0,16},{16,0},{1,17},{17,1},{2,18},{18,2},{3,19},{19,3},{4,20},{20... | collective-permute-start | bytes 49160 | tf_op jit(solution)/shard_map/ppermute | solution.py:34
  95.7 0.8 collective-permute-done.10
  96.5 4.2 %collective-permute-start.13 = (bf16[32,512]{1,0:T(8,128)(2,1)S(1)}, bf16[32,512]{1,0:T(8,128)(2,1)S(1)}, u32[]{:S(2)}, u32[]{:S(2)}) collective-permute-start(bf16[32,512]{1,0:T(8,128)(2,1)S(1)} %constant_dynamic-update-slice_fusion.block0), channel_id=1, source_target_pairs={{0,3},{1,2},{2,1},{3,0},{4,7},{5,6},{6,5},{7,4},{8,11},{9,10},{10,... | collective-permute-start | bytes 98312 | tf_op jit(solution)/shard_map/ppermute | solution.py:34
  100.7 4.6 %collective-permute-start.12 = (bf16[32,512]{1,0:T(8,128)(2,1)S(1)}, bf16[32,512]{1,0:T(8,128)(2,1)S(1)}, u32[]{:S(2)}, u32[]{:S(2)}) collective-permute-start(bf16[32,512]{1,0:T(8,128)(2,1)S(1)} %constant_dynamic-update-slice_fusion.block0), channel_id=1, source_target_pairs={{0,2},{1,3},{2,0},{3,1},{4,6},{5,7},{6,4},{7,5},{8,10},{9,11},{10,... | collective-permute-start | bytes 98312 | tf_op jit(solution)/shard_map/ppermute | solution.py:34
  105.3 2.5 %collective-permute-start.11 = (bf16[32,512]{1,0:T(8,128)(2,1)S(1)}, bf16[32,512]{1,0:T(8,128)(2,1)S(1)}, u32[]{:S(2)}, u32[]{:S(2)}) collective-permute-start(bf16[32,512]{1,0:T(8,128)(2,1)S(1)} %constant_dynamic-update-slice_fusion.block0), channel_id=1, source_target_pairs={{0,1},{1,0},{2,3},{3,2},{4,5},{5,4},{6,7},{7,6},{8,9},{9,8},{10,11... | collective-permute-start | bytes 98312 | tf_op jit(solution)/shard_map/ppermute | solution.py:34
  107.9 0.0 collective-permute-done.13.block3
  107.9 1.4 collective-permute-done.12.block2
  109.3 2.1 %collective-permute-done.11.block1 = bf16[32,512]{1,0:T(8,128)(2,1)S(1)} collective-permute-done((bf16[32,512]{1,0:T(8,128)(2,1)S(1)}, bf16[32,512]{1,0:T(8,128)(2,1)S(1)}, u32[]{:S(2)}, u32[]{:S(2)}) %collective-permute-start.11) | collective-permute-done | bytes 32800 | tf_op jit(solution)/shard_map/ppermute | solution.py:34
  111.4 1.8 %all-to-all-done.1.parts = bf16[16,32,896]{2,1,0:T(8,128)(2,1)S(1)} async-done(((bf16[16,32,896]{2,1,0:T(8,128)(2,1)}), bf16[16,32,896]{2,1,0:T(8,128)(2,1)S(1)}, u32[]{:S(2)}, u32[]{:S(2)}) %all-to-all-start.1) | async-done | bytes 917536 | tf_op jit(solution)/shard_map/all_to_all | solution.py:149
  113.3 1.1 shard_map.51
  114.3 6.1 %all-to-all-start.3 = ((bf16[16,32,896]{2,1,0:T(8,128)(2,1)}), bf16[16,32,896]{2,1,0:T(8,128)(2,1)S(1)}, u32[]{:S(2)}, u32[]{:S(2)}) async-start(bf16[16,32,896]{2,1,0:T(8,128)(2,1)} %shard_map.51), calls=%async_computation.3 | async-start | bytes 1835008 | tf_op jit(solution)/shard_map/all_to_all | solution.py:157
  120.4 4.2 %collective-permute-start.16 = (bf16[128,512]{1,0:T(8,128)(2,1)S(1)}, bf16[128,512]{1,0:T(8,128)(2,1)S(1)}, u32[]{:S(2)}, u32[]{:S(2)}) collective-permute-start(bf16[128,512]{1,0:T(8,128)(2,1)S(1)} %shard_map.50.g0), channel_id=1, source_target_pairs={{0,12},{4,8},{8,4},{12,0},{1,13},{5,9},{9,5},{13,1},{2,14},{6,10},... | collective-permute-start | bytes 393224 | tf_op jit(solution)/shard_map/ppermute | solution.py:34
  124.6 1.9 %collective-permute-start.15 = (bf16[128,512]{1,0:T(8,128)(2,1)S(1)}, bf16[128,512]{1,0:T(8,128)(2,1)S(1)}, u32[]{:S(2)}, u32[]{:S(2)}) collective-permute-start(bf16[128,512]{1,0:T(8,128)(2,1)S(1)} %shard_map.50.g0), channel_id=1, source_target_pairs={{0,8},{4,12},{8,0},{12,4},{1,9},{5,13},{9,1},{13,5},{2,10},{6,14},... | collective-permute-start | bytes 393224 | tf_op jit(solution)/shard_map/ppermute | solution.py:34
  126.6 2.9 %collective-permute-start.14 = (bf16[128,512]{1,0:T(8,128)(2,1)S(1)}, bf16[128,512]{1,0:T(8,128)(2,1)S(1)}, u32[]{:S(2)}, u32[]{:S(2)}) collective-permute-start(bf16[128,512]{1,0:T(8,128)(2,1)S(1)} %shard_map.50.g0), channel_id=1, source_target_pairs={{0,4},{4,0},{8,12},{12,8},{1,5},{5,1},{9,13},{13,9},{2,6},{6,2},{1... | collective-permute-start | bytes 393224 | tf_op jit(solution)/shard_map/ppermute | solution.py:34
  129.4 0.0 collective-permute-done.16.g3
  129.4 2.7 %collective-permute-done.15.g2 = bf16[128,512]{1,0:T(8,128)(2,1)S(1)} collective-permute-done((bf16[128,512]{1,0:T(8,128)(2,1)S(1)}, bf16[128,512]{1,0:T(8,128)(2,1)S(1)}, u32[]{:S(2)}, u32[]{:S(2)}) %collective-permute-start.15) | collective-permute-done | bytes 131104 | tf_op jit(solution)/shard_map/ppermute | solution.py:34
  132.2 1.8 %collective-permute-done.14.g1 = bf16[128,512]{1,0:T(8,128)(2,1)S(1)} collective-permute-done((bf16[128,512]{1,0:T(8,128)(2,1)S(1)}, bf16[128,512]{1,0:T(8,128)(2,1)S(1)}, u32[]{:S(2)}, u32[]{:S(2)}) %collective-permute-start.14) | collective-permute-done | bytes 131104 | tf_op jit(solution)/shard_map/ppermute | solution.py:34
  133.9 9.7 %all-to-all-done.3 = bf16[16,32,896]{2,1,0:T(8,128)(2,1)S(1)} async-done(((bf16[16,32,896]{2,1,0:T(8,128)(2,1)}), bf16[16,32,896]{2,1,0:T(8,128)(2,1)S(1)}, u32[]{:S(2)}, u32[]{:S(2)}) %all-to-all-start.3) | async-done | bytes 917536 | tf_op jit(solution)/shard_map/all_to_all | solution.py:157
  143.7 4.3 %collective-permute-start.17 = (bf16[512,896]{1,0:T(8,128)(2,1)S(1)}, bf16[512,896]{1,0:T(8,128)(2,1)S(1)}, u32[]{:S(2)}, u32[]{:S(2)}) collective-permute-start(bf16[512,896]{1,0:T(8,128)(2,1)S(1)} %bitcast.8), channel_id=1, source_target_pairs={{0,16},{16,0},{1,17},{17,1},{2,18},{18,2},{3,19},{19,3},{4,20},{20... | collective-permute-start | bytes 2752520 | tf_op jit(solution)/shard_map/ppermute | solution.py:34
  148.0 2.1 %collective-permute-done.17.act_theirs = bf16[512,896]{1,0:T(8,128)(2,1)S(1)} collective-permute-done((bf16[512,896]{1,0:T(8,128)(2,1)S(1)}, bf16[512,896]{1,0:T(8,128)(2,1)S(1)}, u32[]{:S(2)}, u32[]{:S(2)}) %collective-permute-start.17) | collective-permute-done | bytes 917536 | tf_op jit(solution)/shard_map/ppermute | solution.py:34
  150.1 1.7 %shard_map.52 = f32[256,896]{1,0:T(8,128)} custom-call(bf16[128,512]{1,0:T(8,128)(2,1)S(1)} %shard_map.50.g0, bf16[128,512]{1,0:T(8,128)(2,1)S(1)} %collective-permute-done.14.g1, bf16[128,512]{1,0:T(8,128)(2,1)S(1)} %collective-permute-done.15.g2, bf16[128,512]{1,0:T(8,128)(2,1)S(1)} %collective-permute-done.16.g3, bf16[512,896]{1,0:T(8,128)(2,1)S(1)} %bitcast.9, ...), custom_call_target="tpu_custom_call" | custom-call | flops 469762048 | bytes 3276800 | tf_op jit(solution)/shard_map/pallas_call | solution.py:22
  (9 shorter events, 0.1 us)
Async XLA Ops:
  0.0 16.6 %copy-start.1 = (bf16[64,896]{1,0:T(8,128)(2,1)S(1)}, bf16[64,896]{1,0:T(8,128)(2,1)}, u32[]{:S(2)}) copy-start(bf16[64,896]{1,0:T(8,128)(2,1)} %param.5) | copy-start | bytes 344068
  1.6 48.0 %copy-start = (bf16[512,256]{1,0:T(8,128)(2,1)S(1)}, bf16[512,256]{1,0:T(8,128)(2,1)}, u32[]{:S(2)}) copy-start(bf16[512,256]{1,0:T(8,128)(2,1)} %own.1) | copy-start | bytes 786436
  1.6 41.1 %all-to-all-start = ((bf16[16,32,512]{2,1,0:T(8,128)(2,1)}), bf16[16,32,512]{2,1,0:T(8,128)(2,1)S(1)}, u32[]{:S(2)}, u32[]{:S(2)}) async-start(bf16[16,32,512]{2,1,0:T(8,128)(2,1)} %broadcast_in_dim.2), calls=%async_computation | async-start | bytes 1048576 | tf_op jit(solution)/shard_map/all_to_all | solution.py:123
  13.8 58.2 %collective-permute-start.8 = (bf16[896,896]{1,0:T(8,128)(2,1)}, bf16[896,896]{1,0:T(8,128)(2,1)}, u32[]{:S(2)}, u32[]{:S(2)}) collective-permute-start(bf16[896,896]{1,0:T(8,128)(2,1)} %param.7), channel_id=1, source_target_pairs={{0,16},{16,0},{1,17},{17,1},{2,18},{18,2},{3,19},{19,3},{4,20},{20... | collective-permute-start | bytes 4816904 | tf_op jit(solution)/shard_map/ppermute | solution.py:34
  16.7 3.1 %collective-permute-start = (bf16[32,896]{1,0:T(8,128)(2,1)S(1)}, bf16[32,896]{1,0:T(8,128)(2,1)S(1)}, u32[]{:S(2)}, u32[]{:S(2)}) collective-permute-start(bf16[32,896]{1,0:T(8,128)(2,1)S(1)} %constant_dynamic-slice_fusion), channel_id=1, source_target_pairs={{0,16},{16,0},{1,17},{17,1},{2,18},{18,2},{3,19},{19,3},{4,20},{20... | collective-permute-start | bytes 172040 | tf_op jit(solution)/shard_map/ppermute | solution.py:34
  19.9 11.4 %collective-permute-start.3 = (bf16[32,1792]{1,0:T(8,128)(2,1)S(1)}, bf16[32,1792]{1,0:T(8,128)(2,1)S(1)}, u32[]{:S(2)}, u32[]{:S(2)}) collective-permute-start(bf16[32,1792]{1,0:T(8,128)(2,1)S(1)} %pad_maximum_fusion.block0), channel_id=1, source_target_pairs={{0,3},{1,2},{2,1},{3,0},{4,7},{5,6},{6,5},{7,4},{8,11},{9,10},{10,... | collective-permute-start | bytes 344072 | tf_op jit(solution)/shard_map/ppermute | solution.py:34
  24.8 15.6 %collective-permute-start.2 = (bf16[32,1792]{1,0:T(8,128)(2,1)S(1)}, bf16[32,1792]{1,0:T(8,128)(2,1)S(1)}, u32[]{:S(2)}, u32[]{:S(2)}) collective-permute-start(bf16[32,1792]{1,0:T(8,128)(2,1)S(1)} %pad_maximum_fusion.block0), channel_id=1, source_target_pairs={{0,2},{1,3},{2,0},{3,1},{4,6},{5,7},{6,4},{7,5},{8,10},{9,11},{10,... | collective-permute-start | bytes 344072 | tf_op jit(solution)/shard_map/ppermute | solution.py:34
  29.3 13.4 %collective-permute-start.1 = (bf16[32,1792]{1,0:T(8,128)(2,1)S(1)}, bf16[32,1792]{1,0:T(8,128)(2,1)S(1)}, u32[]{:S(2)}, u32[]{:S(2)}) collective-permute-start(bf16[32,1792]{1,0:T(8,128)(2,1)S(1)} %pad_maximum_fusion.block0), channel_id=1, source_target_pairs={{0,1},{1,0},{2,3},{3,2},{4,5},{5,4},{6,7},{7,6},{8,9},{9,8},{10,11... | collective-permute-start | bytes 344072 | tf_op jit(solution)/shard_map/ppermute | solution.py:34
  42.7 13.5 %collective-permute-start.4 = (bf16[2,128,896]{2,1,0:T(8,128)(2,1)S(1)}, bf16[2,128,896]{2,1,0:T(8,128)(2,1)S(1)}, u32[]{:S(2)}, u32[]{:S(2)}) collective-permute-start(bf16[2,128,896]{2,1,0:T(8,128)(2,1)S(1)} %shard_map.46.act0), channel_id=1, source_target_pairs={{0,4},{4,0},{8,12},{12,8},{1,5},{5,1},{9,13},{13,9},{2,6},{6,2},{1... | collective-permute-start | bytes 1376264 | tf_op jit(solution)/shard_map/ppermute | solution.py:34
  45.9 19.1 %collective-permute-start.5 = (bf16[2,128,896]{2,1,0:T(8,128)(2,1)S(1)}, bf16[2,128,896]{2,1,0:T(8,128)(2,1)S(1)}, u32[]{:S(2)}, u32[]{:S(2)}) collective-permute-start(bf16[2,128,896]{2,1,0:T(8,128)(2,1)S(1)} %shard_map.46.act0), channel_id=1, source_target_pairs={{0,12},{4,8},{8,4},{12,0},{1,13},{5,9},{9,5},{13,1},{2,14},{6,10},... | collective-permute-start | bytes 1376264 | tf_op jit(solution)/shard_map/ppermute | solution.py:34
  49.6 4.1 %collective-permute-start.9 = (bf16[512,256]{1,0:T(8,128)(2,1)S(1)}, bf16[512,256]{1,0:T(8,128)(2,1)S(1)}, u32[]{:S(2)}, u32[]{:S(2)}) collective-permute-start(bf16[512,256]{1,0:T(8,128)(2,1)S(1)} %copy-done), channel_id=1, source_target_pairs={{0,16},{16,0},{1,17},{17,1},{2,18},{18,2},{3,19},{19,3},{4,20},{20... | collective-permute-start | bytes 786440 | tf_op jit(solution)/shard_map/ppermute | solution.py:34
  57.5 26.6 %all-to-all-start.2 = ((bf16[16,32,512]{2,1,0:T(8,128)(2,1)}), bf16[16,32,512]{2,1,0:T(8,128)(2,1)S(1)}, u32[]{:S(2)}, u32[]{:S(2)}) async-start(bf16[16,32,512]{2,1,0:T(8,128)(2,1)} %shard_map.48), calls=%async_computation.2 | async-start | bytes 1048576 | tf_op jit(solution)/shard_map/all_to_all | solution.py:140
  65.0 9.2 %collective-permute-start.6 = (bf16[128,896]{1,0:T(8,128)(2,1)S(1)}, bf16[128,896]{1,0:T(8,128)(2,1)S(1)}, u32[]{:S(2)}, u32[]{:S(2)}) collective-permute-start(bf16[128,896]{1,0:T(8,128)(2,1)S(1)} %slice_bitcast_fusion.1), channel_id=1, source_target_pairs={{0,4},{4,0},{8,12},{12,8},{1,5},{5,1},{9,13},{13,9},{2,6},{6,2},{1... | collective-permute-start | bytes 688136 | tf_op jit(solution)/shard_map/ppermute | solution.py:34
  68.3 12.6 %collective-permute-start.7 = (bf16[128,896]{1,0:T(8,128)(2,1)S(1)}, bf16[128,896]{1,0:T(8,128)(2,1)S(1)}, u32[]{:S(2)}, u32[]{:S(2)}) collective-permute-start(bf16[128,896]{1,0:T(8,128)(2,1)S(1)} %slice_bitcast_fusion), channel_id=1, source_target_pairs={{0,12},{4,8},{8,4},{12,0},{1,13},{5,9},{9,5},{13,1},{2,14},{6,10},... | collective-permute-start | bytes 688136 | tf_op jit(solution)/shard_map/ppermute | solution.py:34
  84.1 29.2 %all-to-all-start.1 = ((bf16[16,32,896]{2,1,0:T(8,128)(2,1)}), bf16[16,32,896]{2,1,0:T(8,128)(2,1)S(1)}, u32[]{:S(2)}, u32[]{:S(2)}) async-start(bf16[16,32,896]{2,1,0:T(8,128)(2,1)} %get-tuple-element.15), calls=%async_computation.1 | async-start | bytes 1835008 | tf_op jit(solution)/shard_map/all_to_all | solution.py:149
  90.6 5.9 %collective-permute-start.10 = (bf16[32,256]{1,0:T(8,128)(2,1)S(1)}, bf16[32,256]{1,0:T(8,128)(2,1)S(1)}, u32[]{:S(2)}, u32[]{:S(2)}) collective-permute-start(bf16[32,256]{1,0:T(8,128)(2,1)S(1)} %get-tuple-element.18), channel_id=1, source_target_pairs={{0,16},{16,0},{1,17},{17,1},{2,18},{18,2},{3,19},{19,3},{4,20},{20... | collective-permute-start | bytes 49160 | tf_op jit(solution)/shard_map/ppermute | solution.py:34
  96.5 11.4 %collective-permute-start.13 = (bf16[32,512]{1,0:T(8,128)(2,1)S(1)}, bf16[32,512]{1,0:T(8,128)(2,1)S(1)}, u32[]{:S(2)}, u32[]{:S(2)}) collective-permute-start(bf16[32,512]{1,0:T(8,128)(2,1)S(1)} %constant_dynamic-update-slice_fusion.block0), channel_id=1, source_target_pairs={{0,3},{1,2},{2,1},{3,0},{4,7},{5,6},{6,5},{7,4},{8,11},{9,10},{10,... | collective-permute-start | bytes 98312 | tf_op jit(solution)/shard_map/ppermute | solution.py:34
  100.7 8.6 %collective-permute-start.12 = (bf16[32,512]{1,0:T(8,128)(2,1)S(1)}, bf16[32,512]{1,0:T(8,128)(2,1)S(1)}, u32[]{:S(2)}, u32[]{:S(2)}) collective-permute-start(bf16[32,512]{1,0:T(8,128)(2,1)S(1)} %constant_dynamic-update-slice_fusion.block0), channel_id=1, source_target_pairs={{0,2},{1,3},{2,0},{3,1},{4,6},{5,7},{6,4},{7,5},{8,10},{9,11},{10,... | collective-permute-start | bytes 98312 | tf_op jit(solution)/shard_map/ppermute | solution.py:34
  105.3 6.1 %collective-permute-start.11 = (bf16[32,512]{1,0:T(8,128)(2,1)S(1)}, bf16[32,512]{1,0:T(8,128)(2,1)S(1)}, u32[]{:S(2)}, u32[]{:S(2)}) collective-permute-start(bf16[32,512]{1,0:T(8,128)(2,1)S(1)} %constant_dynamic-update-slice_fusion.block0), channel_id=1, source_target_pairs={{0,1},{1,0},{2,3},{3,2},{4,5},{5,4},{6,7},{7,6},{8,9},{9,8},{10,11... | collective-permute-start | bytes 98312 | tf_op jit(solution)/shard_map/ppermute | solution.py:34
  114.3 29.3 %all-to-all-start.3 = ((bf16[16,32,896]{2,1,0:T(8,128)(2,1)}), bf16[16,32,896]{2,1,0:T(8,128)(2,1)S(1)}, u32[]{:S(2)}, u32[]{:S(2)}) async-start(bf16[16,32,896]{2,1,0:T(8,128)(2,1)} %shard_map.51), calls=%async_computation.3 | async-start | bytes 1835008 | tf_op jit(solution)/shard_map/all_to_all | solution.py:157
  120.4 9.0 %collective-permute-start.16 = (bf16[128,512]{1,0:T(8,128)(2,1)S(1)}, bf16[128,512]{1,0:T(8,128)(2,1)S(1)}, u32[]{:S(2)}, u32[]{:S(2)}) collective-permute-start(bf16[128,512]{1,0:T(8,128)(2,1)S(1)} %shard_map.50.g0), channel_id=1, source_target_pairs={{0,12},{4,8},{8,4},{12,0},{1,13},{5,9},{9,5},{13,1},{2,14},{6,10},... | collective-permute-start | bytes 393224 | tf_op jit(solution)/shard_map/ppermute | solution.py:34
  124.6 7.5 %collective-permute-start.15 = (bf16[128,512]{1,0:T(8,128)(2,1)S(1)}, bf16[128,512]{1,0:T(8,128)(2,1)S(1)}, u32[]{:S(2)}, u32[]{:S(2)}) collective-permute-start(bf16[128,512]{1,0:T(8,128)(2,1)S(1)} %shard_map.50.g0), channel_id=1, source_target_pairs={{0,8},{4,12},{8,0},{12,4},{1,9},{5,13},{9,1},{13,5},{2,10},{6,14},... | collective-permute-start | bytes 393224 | tf_op jit(solution)/shard_map/ppermute | solution.py:34
  126.6 7.4 %collective-permute-start.14 = (bf16[128,512]{1,0:T(8,128)(2,1)S(1)}, bf16[128,512]{1,0:T(8,128)(2,1)S(1)}, u32[]{:S(2)}, u32[]{:S(2)}) collective-permute-start(bf16[128,512]{1,0:T(8,128)(2,1)S(1)} %shard_map.50.g0), channel_id=1, source_target_pairs={{0,4},{4,0},{8,12},{12,8},{1,5},{5,1},{9,13},{13,9},{2,6},{6,2},{1... | collective-permute-start | bytes 393224 | tf_op jit(solution)/shard_map/ppermute | solution.py:34
  143.7 6.4 %collective-permute-start.17 = (bf16[512,896]{1,0:T(8,128)(2,1)S(1)}, bf16[512,896]{1,0:T(8,128)(2,1)S(1)}, u32[]{:S(2)}, u32[]{:S(2)}) collective-permute-start(bf16[512,896]{1,0:T(8,128)(2,1)S(1)} %bitcast.8), channel_id=1, source_target_pairs={{0,16},{16,0},{1,17},{17,1},{2,18},{18,2},{3,19},{19,3},{4,20},{20... | collective-permute-start | bytes 2752520 | tf_op jit(solution)/shard_map/ppermute | solution.py:34

commit v11 on v10

--- a/solution.py
+++ b/solution.py
@@ -38,11 +38,13 @@
     return [mine, swap(mine, "yhi", 1), swap(mine, "yhi", 2), swap(mine, "yhi", 3)]
 
 
-def stack_acts_kernel(block0, block1, block2, block3, order, out):
-    rows, features = block0.shape[0], out.shape[2]
-    for index, block in enumerate((block0, block1, block2, block3)):
-        for side in range(2):
-            out[side, index * rows:(index + 1) * rows, :] = block[:, side * features:(side + 1) * features]
+def stack_acts_kernel(block0, block1, low2, high2, block3, order, out0, out1):
+    features, row = out0.shape[1], 0
+    for block in (block0, block1, low2, high2, block3):
+        rows = block.shape[0]
+        for side, out in enumerate((out0, out1)):
+            out[row:row + rows, :] = block[:, side * features:(side + 1) * features]
+        row += rows
 
 
 def stack_kernel(block0, block1, block2, block3, out):
@@ -51,9 +53,9 @@
         out[index * rows:(index + 1) * rows, :] = block[...]
 
 
-def act_dot_kernel(act0, act1, low2, high2, act3, basis0, basis1, out, done):
-    first = [act0[0], act1[0], low2[...], act3[0]]
-    second = [act0[1], act1[1], high2[...], act3[1]]
+def act_dot_kernel(own0, own1, near0, near1, low2, high2, back0, back1, basis0, basis1, out, done):
+    first = [own0[...], near0[...], low2[...], back0[...]]
+    second = [own1[...], near1[...], high2[...], back1[...]]
     total = 0.0
     for rows, basis in ((first, basis0), (second, basis1)):
         total += jnp.dot(jnp.concatenate(rows), basis[...], preferred_element_type=F32)
@@ -121,19 +123,22 @@
 
     grad_copies = jnp.broadcast_to(grads[None], (16, *grads.shape))
     grad_rows = lax.all_to_all(grad_copies, CHIPS, 0, 0, tiled=True).reshape(tokens, -1)
-    act0 = kernel_call(
+    near, back = swap(act_own, "yhi", 1), swap(act_own, "yhi", 3)
+    low, high = swap(back[:half // 2], "yhi", 1), swap(near[half // 2:], "yhi", 3)
+    own0, own1 = kernel_call(
         stack_acts_kernel,
-        [jax.ShapeDtypeStruct((2, 4 * half, features), BF16)],
-        [*gather_yhi(act_own), grad_rows],
+        [jax.ShapeDtypeStruct((4 * half, features), BF16)] * 2,
+        [act_own, near, low, high, back, grad_rows],
         unread=1,
     )
-    act1, act3 = swap(act0, "x", 1), swap(act0, "x", 3)
-    low2, high2 = swap(act3[0], "x", 1), swap(act1[1], "x", 3)
+    near1, back0 = swap(own1, "x", 1), swap(own0, "x", 3)
+    low2, high2 = swap(back0, "x", 1), swap(near1, "x", 3)
+    near0, back1 = swap(own0, "x", 1), swap(own1, "x", 3)
 
     grad_partial = kernel_call(
         grad_dot_kernel,
         [jax.ShapeDtypeStruct((16, rows, 2 * columns), BF16)],
-        [grad_rows, grad_basis, grad_basis_other, act1],
+        [grad_rows, grad_basis, grad_basis_other, near1],
         flops=2 * tokens * grads.shape[1] * 2 * columns,
         unread=1,
     )
@@ -143,7 +148,7 @@
     act_partial, done = kernel_call(
         act_dot_kernel,
         [blocks, jax.ShapeDtypeStruct((8, 128), F32)],
-        [act0, act1, low2, high2, act3, act_basis0, act_basis1],
+        [own0, own1, near0, near1, low2, high2, back0, back1, act_basis0, act_basis1],
         flops=2 * tokens * 2 * features * eig,
     )
     act_parts = lax.all_to_all(act_partial, CHIPS, 0, 0, tiled=True)

time: 153 us -> 157 us (1.026)
  starting transfers between devices: 94.8 us -> 107 us
  waiting for transfers between devices: 45.4 us -> 38.1 us
    ppermute x18 -> x21, waiting for transfers between devices: 33.9 us -> 23.4 us  [swap(): return lax.ppermute(value, axis, [(s, s ^ flip) for s in range(size)])]
    ppermute x18 -> x21, starting transfers between devices: 62.7 us -> 71.7 us  [swap(): return lax.ppermute(value, axis, [(s, s ^ flip) for s in range(size)])]
    all_to_all x1, starting transfers between devices: 6.44 us -> 10.5 us  [shards(): act_parts = lax.all_to_all(act_partial, CHIPS, 0, 0, tiled=True)]
    all_to_all x1, waiting for transfers between devices: 1.83 us -> 3.99 us  [shards(): act_parts = lax.all_to_all(act_partial, CHIPS, 0, 0, tiled=True)]
  transfers between devices with their start and end apart: 22 -> 25, of which waited for: 14 -> 14; matrix products, arithmetic and copies ran while one was open for 2% -> 1% of each run, Pallas kernels for 3% -> 3%
where the time goes in v11:
time: 157 us; the launch traced here: 156 us
  starting transfers between devices  107 us (68%)
  waiting for transfers between devices  38.1 us (24%)
  Pallas kernels  7.26 us (5%)
  other arithmetic  1.76 us (1%)
  local copies, waits for them, and re-layouts  1.69 us (1%)
    ppermute x21, starting transfers between devices, swap(): return lax.ppermute(value, axis, [(s, s ^ flip) for s in range(size)])  71.7 us
    ppermute x21, waiting for transfers between devices, swap(): return lax.ppermute(value, axis, [(s, s ^ flip) for s in range(size)])  23.4 us
    all_to_all x1, starting transfers between devices, shards(): lax.all_to_all(grad_copies, CHIPS, 0, 0, tiled=True).reshape(tokens, -1)  12 us
    all_to_all x1, waiting for transfers between devices, shards(): lax.all_to_all(kernel_call(sum_copies_kernel, [blocks], [act_parts]), CHI...  10.7 us
    all_to_all x1, starting transfers between devices, shards(): act_parts = lax.all_to_all(act_partial, CHIPS, 0, 0, tiled=True)  10.5 us
    all_to_all x1, starting transfers between devices, shards(): grad_parts = lax.all_to_all(grad_partial, INP, 0, 0, tiled=True)  7.28 us
    pallas_call x7, Pallas kernels, kernel_call(): pl.pallas_call(body, out_shape=shapes if many else shapes[0], in_specs=[V...  7.26 us
    all_to_all x1, starting transfers between devices, shards(): lax.all_to_all(kernel_call(sum_copies_kernel, [blocks], [act_parts]), CHI...  5.45 us
  transfers between devices with their start and end apart: 25, of which 14 were waited for; matrix products, arithmetic and copies ran while one was open for 1% of the time, Pallas kernels for 3%

profile of v11, /device:TPU:1, one launch (start us, length us, event | category | flops | bytes accessed | tf_op | source)
XLA Modules:
  0.0 156.2 jit_solution(910525617105928930)
XLA Ops:
  0.0 0.0 copy-start.2
  0.0 0.0 copy-start
  0.0 1.7 %broadcast_in_dim.2 = bf16[16,32,512]{2,1,0:T(8,128)(2,1)} broadcast(bf16[32,512]{1,0:T(8,128)(2,1)} %param.4), dimensions={1,2} | broadcast | bytes 557056 | tf_op jit(solution)/shard_map/broadcast_in_dim | solution.py:124
  1.7 12.0 %all-to-all-start = ((bf16[16,32,512]{2,1,0:T(8,128)(2,1)}), bf16[16,32,512]{2,1,0:T(8,128)(2,1)S(1)}, u32[]{:S(2)}, u32[]{:S(2)}) async-start(bf16[16,32,512]{2,1,0:T(8,128)(2,1)} %broadcast_in_dim.2), calls=%async_computation | async-start | bytes 1048576 | tf_op jit(solution)/shard_map/all_to_all | solution.py:125
  13.6 2.9 %collective-permute-start.11 = (bf16[896,896]{1,0:T(8,128)(2,1)}, bf16[896,896]{1,0:T(8,128)(2,1)}, u32[]{:S(2)}, u32[]{:S(2)}) collective-permute-start(bf16[896,896]{1,0:T(8,128)(2,1)} %param.7), channel_id=1, source_target_pairs={{0,16},{16,0},{1,17},{17,1},{2,18},{18,2},{3,19},{19,3},{4,20},{20... | collective-permute-start | bytes 4816904 | tf_op jit(solution)/shard_map/ppermute | solution.py:34
  16.5 0.0 copy-done.2
  16.6 1.9 %collective-permute-start = (bf16[32,896]{1,0:T(8,128)(2,1)S(1)}, bf16[32,896]{1,0:T(8,128)(2,1)S(1)}, u32[]{:S(2)}, u32[]{:S(2)}) collective-permute-start(bf16[32,896]{1,0:T(8,128)(2,1)S(1)} %constant_dynamic-slice_fusion), channel_id=1, source_target_pairs={{0,16},{16,0},{1,17},{17,1},{2,18},{18,2},{3,19},{19,3},{4,20},{20... | collective-permute-start | bytes 172040 | tf_op jit(solution)/shard_map/ppermute | solution.py:34
  18.5 1.2 collective-permute-done
  19.7 5.0 %collective-permute-start.2 = (bf16[32,1792]{1,0:T(8,128)(2,1)S(1)}, bf16[32,1792]{1,0:T(8,128)(2,1)S(1)}, u32[]{:S(2)}, u32[]{:S(2)}) collective-permute-start(bf16[32,1792]{1,0:T(8,128)(2,1)S(1)} %pad_maximum_fusion.block0), channel_id=1, source_target_pairs={{0,3},{1,2},{2,1},{3,0},{4,7},{5,6},{6,5},{7,4},{8,11},{9,10},{10,... | collective-permute-start | bytes 344072 | tf_op jit(solution)/shard_map/ppermute | solution.py:34
  24.7 3.8 %collective-permute-start.1 = (bf16[32,1792]{1,0:T(8,128)(2,1)S(1)}, bf16[32,1792]{1,0:T(8,128)(2,1)S(1)}, u32[]{:S(2)}, u32[]{:S(2)}) collective-permute-start(bf16[32,1792]{1,0:T(8,128)(2,1)S(1)} %pad_maximum_fusion.block0), channel_id=1, source_target_pairs={{0,1},{1,0},{2,3},{3,2},{4,5},{5,4},{6,7},{7,6},{8,9},{9,8},{10,11... | collective-permute-start | bytes 344072 | tf_op jit(solution)/shard_map/ppermute | solution.py:34
  28.5 0.0 collective-permute-done.2.block3
  28.5 6.3 %collective-permute-start.3 = (bf16[16,1792]{1,0:T(8,128)(2,1)S(1)}, bf16[16,1792]{1,0:T(8,128)(2,1)S(1)}, u32[]{:S(2)}, u32[]{:S(2)}) collective-permute-start(bf16[16,1792]{1,0:T(8,128)(2,1)S(1)} %slice.8), channel_id=1, source_target_pairs={{0,1},{1,0},{2,3},{3,2},{4,5},{5,4},{6,7},{7,6},{8,9},{9,8},{10,11... | collective-permute-start | bytes 172040 | tf_op jit(solution)/shard_map/ppermute | solution.py:34
  34.8 0.0 collective-permute-done.1.block1
  34.8 2.7 %collective-permute-start.4 = (bf16[16,1792]{1,0:T(8,128)(2,1)S(1)}, bf16[16,1792]{1,0:T(8,128)(2,1)S(1)}, u32[]{:S(2)}, u32[]{:S(2)}) collective-permute-start(bf16[16,1792]{1,0:T(8,128)(2,1)S(1)} %slice.9), channel_id=1, source_target_pairs={{0,3},{1,2},{2,1},{3,0},{4,7},{5,6},{6,5},{7,4},{8,11},{9,10},{10,... | collective-permute-start | bytes 172040 | tf_op jit(solution)/shard_map/ppermute | solution.py:34
  37.5 0.0 copy-done
  37.5 3.5 %collective-permute-start.12 = (bf16[512,256]{1,0:T(8,128)(2,1)S(1)}, bf16[512,256]{1,0:T(8,128)(2,1)S(1)}, u32[]{:S(2)}, u32[]{:S(2)}) collective-permute-start(bf16[512,256]{1,0:T(8,128)(2,1)S(1)} %copy-done), channel_id=1, source_target_pairs={{0,16},{16,0},{1,17},{17,1},{2,18},{18,2},{3,19},{19,3},{4,20},{20... | collective-permute-start | bytes 786440 | tf_op jit(solution)/shard_map/ppermute | solution.py:34
  41.0 0.0 collective-permute-done.3.low2
  41.0 0.9 collective-permute-done.4.high2
  42.0 0.0 all-to-all-done
  42.0 0.0 copy-start.1
  42.0 3.3 %collective-permute-start.6 = (bf16[128,896]{1,0:T(8,128)(2,1)S(1)}, bf16[128,896]{1,0:T(8,128)(2,1)S(1)}, u32[]{:S(2)}, u32[]{:S(2)}) collective-permute-start(bf16[128,896]{1,0:T(8,128)(2,1)S(1)} %get-tuple-element.18.own1), channel_id=1, source_target_pairs={{0,4},{4,0},{8,12},{12,8},{1,5},{5,1},{9,13},{13,9},{2,6},{6,2},{1... | collective-permute-start | bytes 688136 | tf_op jit(solution)/shard_map/ppermute | solution.py:34
  45.3 0.0 collective-permute-done.12.other
  45.3 3.6 %collective-permute-done.6.near1.order = bf16[128,896]{1,0:T(8,128)(2,1)S(1)} collective-permute-done((bf16[128,896]{1,0:T(8,128)(2,1)S(1)}, bf16[128,896]{1,0:T(8,128)(2,1)S(1)}, u32[]{:S(2)}, u32[]{:S(2)}) %collective-permute-start.6) | collective-permute-done | bytes 229408 | tf_op jit(solution)/shard_map/ppermute | solution.py:34
  48.9 1.2 shard_map.48
  50.2 7.3 %all-to-all-start.2 = ((bf16[16,32,512]{2,1,0:T(8,128)(2,1)}), bf16[16,32,512]{2,1,0:T(8,128)(2,1)S(1)}, u32[]{:S(2)}, u32[]{:S(2)}) async-start(bf16[16,32,512]{2,1,0:T(8,128)(2,1)} %shard_map.48), calls=%async_computation.2 | async-start | bytes 1048576 | tf_op jit(solution)/shard_map/all_to_all | solution.py:145
  57.4 4.5 %collective-permute-start.7 = (bf16[128,896]{1,0:T(8,128)(2,1)S(1)}, bf16[128,896]{1,0:T(8,128)(2,1)S(1)}, u32[]{:S(2)}, u32[]{:S(2)}) collective-permute-start(bf16[128,896]{1,0:T(8,128)(2,1)S(1)} %get-tuple-element.17.own0), channel_id=1, source_target_pairs={{0,12},{4,8},{8,4},{12,0},{1,13},{5,9},{9,5},{13,1},{2,14},{6,10},... | collective-permute-start | bytes 688136 | tf_op jit(solution)/shard_map/ppermute | solution.py:34
  61.9 1.9 %collective-permute-start.5 = (bf16[128,896]{1,0:T(8,128)(2,1)S(1)}, bf16[128,896]{1,0:T(8,128)(2,1)S(1)}, u32[]{:S(2)}, u32[]{:S(2)}) collective-permute-start(bf16[128,896]{1,0:T(8,128)(2,1)S(1)} %get-tuple-element.17.own0), channel_id=1, source_target_pairs={{0,4},{4,0},{8,12},{12,8},{1,5},{5,1},{9,13},{13,9},{2,6},{6,2},{1... | collective-permute-start | bytes 688136 | tf_op jit(solution)/shard_map/ppermute | solution.py:34
  63.9 2.8 %collective-permute-start.10 = (bf16[128,896]{1,0:T(8,128)(2,1)S(1)}, bf16[128,896]{1,0:T(8,128)(2,1)S(1)}, u32[]{:S(2)}, u32[]{:S(2)}) collective-permute-start(bf16[128,896]{1,0:T(8,128)(2,1)S(1)} %get-tuple-element.18.own1), channel_id=1, source_target_pairs={{0,12},{4,8},{8,4},{12,0},{1,13},{5,9},{9,5},{13,1},{2,14},{6,10},... | collective-permute-start | bytes 688136 | tf_op jit(solution)/shard_map/ppermute | solution.py:34
  66.6 3.7 %collective-permute-start.9 = (bf16[128,896]{1,0:T(8,128)(2,1)S(1)}, bf16[128,896]{1,0:T(8,128)(2,1)S(1)}, u32[]{:S(2)}, u32[]{:S(2)}) collective-permute-start(bf16[128,896]{1,0:T(8,128)(2,1)S(1)} %collective-permute-done.6.near1.order), channel_id=1, source_target_pairs={{0,12},{4,8},{8,4},{12,0},{1,13},{5,9},{9,5},{13,1},{2,14},{6,10},... | collective-permute-start | bytes 688136 | tf_op jit(solution)/shard_map/ppermute | solution.py:34
  70.4 0.0 collective-permute-done.7.back0
  70.4 2.2 %collective-permute-start.8 = (bf16[128,896]{1,0:T(8,128)(2,1)S(1)}, bf16[128,896]{1,0:T(8,128)(2,1)S(1)}, u32[]{:S(2)}, u32[]{:S(2)}) collective-permute-start(bf16[128,896]{1,0:T(8,128)(2,1)S(1)} %collective-permute-done.7.back0), channel_id=1, source_target_pairs={{0,4},{4,0},{8,12},{12,8},{1,5},{5,1},{9,13},{13,9},{2,6},{6,2},{1... | collective-permute-start | bytes 688136 | tf_op jit(solution)/shard_map/ppermute | solution.py:34
  72.5 0.0 collective-permute-done.11
  72.6 0.0 copy-done.1
  72.6 1.7 %broadcast_select_fusion = (bf16[896,896]{1,0:T(8,128)(2,1)S(1)}, bf16[896,896]{1,0:T(8,128)(2,1)S(1)}) fusion(bf16[896,896]{1,0:T(8,128)(2,1)} %collective-permute-done.11, bf16[896,896]{1,0:T(8,128)(2,1)S(1)} %copy-done.1, pred[]{:T(512)S(6)} %eq.2), kind=kLoop, calls=%fused_computation | loop fusion | flops 1605632 | bytes 6422529 | tf_op jit(solution)/shard_map/jit(_where)/select_n | solution.py:109
  74.3 0.0 collective-permute-done.5.near0
  74.3 2.0 %collective-permute-done.10.back1 = bf16[128,896]{1,0:T(8,128)(2,1)S(1)} collective-permute-done((bf16[128,896]{1,0:T(8,128)(2,1)S(1)}, bf16[128,896]{1,0:T(8,128)(2,1)S(1)}, u32[]{:S(2)}, u32[]{:S(2)}) %collective-permute-start.10) | collective-permute-done | bytes 229408 | tf_op jit(solution)/shard_map/ppermute | solution.py:34
  76.3 1.1 collective-permute-done.8.low2
  77.4 3.8 %collective-permute-done.9.high2 = bf16[128,896]{1,0:T(8,128)(2,1)S(1)} collective-permute-done((bf16[128,896]{1,0:T(8,128)(2,1)S(1)}, bf16[128,896]{1,0:T(8,128)(2,1)S(1)}, u32[]{:S(2)}, u32[]{:S(2)}) %collective-permute-start.9) | collective-permute-done | bytes 229408 | tf_op jit(solution)/shard_map/ppermute | solution.py:34
  81.2 3.2 %shard_map.47 = (bf16[16,32,896]{2,1,0:T(8,128)(2,1)}, f32[8,128]{1,0:T(8,128)S(1)}) custom-call(bf16[128,896]{1,0:T(8,128)(2,1)S(1)} %get-tuple-element.17.own0, bf16[128,896]{1,0:T(8,128)(2,1)S(1)} %get-tuple-element.18.own1, bf16[128,896]{1,0:T(8,128)(2,1)S(1)} %collective-permute-done.5.near0, bf16[128,896]{1,0:T(8,128)(2,1)S(1)} %collective-permute-done.6.near1.order, ...), custom_call_target="tpu_custom_call" | custom-call | flops 1644167168 | bytes 5967872 | tf_op jit(solution)/shard_map/pallas_call | solution.py:22
  84.4 0.0 all-to-all-done.2.parts
  84.4 10.5 %all-to-all-start.1 = ((bf16[16,32,896]{2,1,0:T(8,128)(2,1)}), bf16[16,32,896]{2,1,0:T(8,128)(2,1)S(1)}, u32[]{:S(2)}, u32[]{:S(2)}) async-start(bf16[16,32,896]{2,1,0:T(8,128)(2,1)} %get-tuple-element.19), calls=%async_computation.1 | async-start | bytes 1835008 | tf_op jit(solution)/shard_map/all_to_all | solution.py:154
  94.9 0.1 shard_map.49
  95.0 3.3 %collective-permute-start.13 = (bf16[32,256]{1,0:T(8,128)(2,1)S(1)}, bf16[32,256]{1,0:T(8,128)(2,1)S(1)}, u32[]{:S(2)}, u32[]{:S(2)}) collective-permute-start(bf16[32,256]{1,0:T(8,128)(2,1)S(1)} %get-tuple-element.22), channel_id=1, source_target_pairs={{0,16},{16,0},{1,17},{17,1},{2,18},{18,2},{3,19},{19,3},{4,20},{20... | collective-permute-start | bytes 49160 | tf_op jit(solution)/shard_map/ppermute | solution.py:34
  98.3 0.8 collective-permute-done.13
  99.1 5.3 %collective-permute-start.16 = (bf16[32,512]{1,0:T(8,128)(2,1)S(1)}, bf16[32,512]{1,0:T(8,128)(2,1)S(1)}, u32[]{:S(2)}, u32[]{:S(2)}) collective-permute-start(bf16[32,512]{1,0:T(8,128)(2,1)S(1)} %constant_dynamic-update-slice_fusion.block0), channel_id=1, source_target_pairs={{0,3},{1,2},{2,1},{3,0},{4,7},{5,6},{6,5},{7,4},{8,11},{9,10},{10,... | collective-permute-start | bytes 98312 | tf_op jit(solution)/shard_map/ppermute | solution.py:34
  104.5 4.0 %collective-permute-start.15 = (bf16[32,512]{1,0:T(8,128)(2,1)S(1)}, bf16[32,512]{1,0:T(8,128)(2,1)S(1)}, u32[]{:S(2)}, u32[]{:S(2)}) collective-permute-start(bf16[32,512]{1,0:T(8,128)(2,1)S(1)} %constant_dynamic-update-slice_fusion.block0), channel_id=1, source_target_pairs={{0,2},{1,3},{2,0},{3,1},{4,6},{5,7},{6,4},{7,5},{8,10},{9,11},{10,... | collective-permute-start | bytes 98312 | tf_op jit(solution)/shard_map/ppermute | solution.py:34
  108.5 2.0 %collective-permute-start.14 = (bf16[32,512]{1,0:T(8,128)(2,1)S(1)}, bf16[32,512]{1,0:T(8,128)(2,1)S(1)}, u32[]{:S(2)}, u32[]{:S(2)}) collective-permute-start(bf16[32,512]{1,0:T(8,128)(2,1)S(1)} %constant_dynamic-update-slice_fusion.block0), channel_id=1, source_target_pairs={{0,1},{1,0},{2,3},{3,2},{4,5},{5,4},{6,7},{7,6},{8,9},{9,8},{10,11... | collective-permute-start | bytes 98312 | tf_op jit(solution)/shard_map/ppermute | solution.py:34
  110.5 0.0 collective-permute-done.16.block3
  110.5 2.7 %collective-permute-done.15.block2 = bf16[32,512]{1,0:T(8,128)(2,1)S(1)} collective-permute-done((bf16[32,512]{1,0:T(8,128)(2,1)S(1)}, bf16[32,512]{1,0:T(8,128)(2,1)S(1)}, u32[]{:S(2)}, u32[]{:S(2)}) %collective-permute-start.15) | collective-permute-done | bytes 32800 | tf_op jit(solution)/shard_map/ppermute | solution.py:34
  113.2 1.1 collective-permute-done.14.block1
  114.3 4.0 %all-to-all-done.1.parts = bf16[16,32,896]{2,1,0:T(8,128)(2,1)S(1)} async-done(((bf16[16,32,896]{2,1,0:T(8,128)(2,1)}), bf16[16,32,896]{2,1,0:T(8,128)(2,1)S(1)}, u32[]{:S(2)}, u32[]{:S(2)}) %all-to-all-start.1) | async-done | bytes 917536 | tf_op jit(solution)/shard_map/all_to_all | solution.py:154
  118.3 1.1 shard_map.51
  119.4 5.4 %all-to-all-start.3 = ((bf16[16,32,896]{2,1,0:T(8,128)(2,1)}), bf16[16,32,896]{2,1,0:T(8,128)(2,1)S(1)}, u32[]{:S(2)}, u32[]{:S(2)}) async-start(bf16[16,32,896]{2,1,0:T(8,128)(2,1)} %shard_map.51), calls=%async_computation.3 | async-start | bytes 1835008 | tf_op jit(solution)/shard_map/all_to_all | solution.py:162
  124.8 2.7 %collective-permute-start.19 = (bf16[128,512]{1,0:T(8,128)(2,1)S(1)}, bf16[128,512]{1,0:T(8,128)(2,1)S(1)}, u32[]{:S(2)}, u32[]{:S(2)}) collective-permute-start(bf16[128,512]{1,0:T(8,128)(2,1)S(1)} %shard_map.50.g0), channel_id=1, source_target_pairs={{0,12},{4,8},{8,4},{12,0},{1,13},{5,9},{9,5},{13,1},{2,14},{6,10},... | collective-permute-start | bytes 393224 | tf_op jit(solution)/shard_map/ppermute | solution.py:34
  127.6 3.0 %collective-permute-start.18 = (bf16[128,512]{1,0:T(8,128)(2,1)S(1)}, bf16[128,512]{1,0:T(8,128)(2,1)S(1)}, u32[]{:S(2)}, u32[]{:S(2)}) collective-permute-start(bf16[128,512]{1,0:T(8,128)(2,1)S(1)} %shard_map.50.g0), channel_id=1, source_target_pairs={{0,8},{4,12},{8,0},{12,4},{1,9},{5,13},{9,1},{13,5},{2,10},{6,14},... | collective-permute-start | bytes 393224 | tf_op jit(solution)/shard_map/ppermute | solution.py:34
  130.6 3.2 %collective-permute-start.17 = (bf16[128,512]{1,0:T(8,128)(2,1)S(1)}, bf16[128,512]{1,0:T(8,128)(2,1)S(1)}, u32[]{:S(2)}, u32[]{:S(2)}) collective-permute-start(bf16[128,512]{1,0:T(8,128)(2,1)S(1)} %shard_map.50.g0), channel_id=1, source_target_pairs={{0,4},{4,0},{8,12},{12,8},{1,5},{5,1},{9,13},{13,9},{2,6},{6,2},{1... | collective-permute-start | bytes 393224 | tf_op jit(solution)/shard_map/ppermute | solution.py:34
  133.8 0.0 collective-permute-done.19.g3
  133.8 1.2 collective-permute-done.18.g2
  135.1 2.8 %collective-permute-done.17.g1 = bf16[128,512]{1,0:T(8,128)(2,1)S(1)} collective-permute-done((bf16[128,512]{1,0:T(8,128)(2,1)S(1)}, bf16[128,512]{1,0:T(8,128)(2,1)S(1)}, u32[]{:S(2)}, u32[]{:S(2)}) %collective-permute-start.17) | collective-permute-done | bytes 131104 | tf_op jit(solution)/shard_map/ppermute | solution.py:34
  137.9 10.7 %all-to-all-done.3 = bf16[16,32,896]{2,1,0:T(8,128)(2,1)S(1)} async-done(((bf16[16,32,896]{2,1,0:T(8,128)(2,1)}), bf16[16,32,896]{2,1,0:T(8,128)(2,1)S(1)}, u32[]{:S(2)}, u32[]{:S(2)}) %all-to-all-start.3) | async-done | bytes 917536 | tf_op jit(solution)/shard_map/all_to_all | solution.py:162
  148.6 3.8 %collective-permute-start.20 = (bf16[512,896]{1,0:T(8,128)(2,1)S(1)}, bf16[512,896]{1,0:T(8,128)(2,1)S(1)}, u32[]{:S(2)}, u32[]{:S(2)}) collective-permute-start(bf16[512,896]{1,0:T(8,128)(2,1)S(1)} %bitcast.4), channel_id=1, source_target_pairs={{0,16},{16,0},{1,17},{17,1},{2,18},{18,2},{3,19},{19,3},{4,20},{20... | collective-permute-start | bytes 2752520 | tf_op jit(solution)/shard_map/ppermute | solution.py:34
  152.4 2.1 %collective-permute-done.20.act_theirs = bf16[512,896]{1,0:T(8,128)(2,1)S(1)} collective-permute-done((bf16[512,896]{1,0:T(8,128)(2,1)S(1)}, bf16[512,896]{1,0:T(8,128)(2,1)S(1)}, u32[]{:S(2)}, u32[]{:S(2)}) %collective-permute-start.20) | collective-permute-done | bytes 917536 | tf_op jit(solution)/shard_map/ppermute | solution.py:34
  154.5 1.7 %shard_map.52 = f32[256,896]{1,0:T(8,128)} custom-call(bf16[128,512]{1,0:T(8,128)(2,1)S(1)} %shard_map.50.g0, bf16[128,512]{1,0:T(8,128)(2,1)S(1)} %collective-permute-done.17.g1, bf16[128,512]{1,0:T(8,128)(2,1)S(1)} %collective-permute-done.18.g2, bf16[128,512]{1,0:T(8,128)(2,1)S(1)} %collective-permute-done.19.g3, bf16[512,896]{1,0:T(8,128)(2,1)S(1)} %bitcast.5, ...), custom_call_target="tpu_custom_call" | custom-call | flops 469762048 | bytes 3276800 | tf_op jit(solution)/shard_map/pallas_call | solution.py:22
  (9 shorter events, 0.1 us)
Async XLA Ops:
  0.0 16.5 %copy-start.2 = (bf16[64,896]{1,0:T(8,128)(2,1)S(1)}, bf16[64,896]{1,0:T(8,128)(2,1)}, u32[]{:S(2)}) copy-start(bf16[64,896]{1,0:T(8,128)(2,1)} %param.5) | copy-start | bytes 344068
  0.0 37.5 %copy-start = (bf16[512,256]{1,0:T(8,128)(2,1)S(1)}, bf16[512,256]{1,0:T(8,128)(2,1)}, u32[]{:S(2)}) copy-start(bf16[512,256]{1,0:T(8,128)(2,1)} %own.1) | copy-start | bytes 786436
  1.7 40.3 %all-to-all-start = ((bf16[16,32,512]{2,1,0:T(8,128)(2,1)}), bf16[16,32,512]{2,1,0:T(8,128)(2,1)S(1)}, u32[]{:S(2)}, u32[]{:S(2)}) async-start(bf16[16,32,512]{2,1,0:T(8,128)(2,1)} %broadcast_in_dim.2), calls=%async_computation | async-start | bytes 1048576 | tf_op jit(solution)/shard_map/all_to_all | solution.py:125
  13.6 58.9 %collective-permute-start.11 = (bf16[896,896]{1,0:T(8,128)(2,1)}, bf16[896,896]{1,0:T(8,128)(2,1)}, u32[]{:S(2)}, u32[]{:S(2)}) collective-permute-start(bf16[896,896]{1,0:T(8,128)(2,1)} %param.7), channel_id=1, source_target_pairs={{0,16},{16,0},{1,17},{17,1},{2,18},{18,2},{3,19},{19,3},{4,20},{20... | collective-permute-start | bytes 4816904 | tf_op jit(solution)/shard_map/ppermute | solution.py:34
  16.6 3.1 %collective-permute-start = (bf16[32,896]{1,0:T(8,128)(2,1)S(1)}, bf16[32,896]{1,0:T(8,128)(2,1)S(1)}, u32[]{:S(2)}, u32[]{:S(2)}) collective-permute-start(bf16[32,896]{1,0:T(8,128)(2,1)S(1)} %constant_dynamic-slice_fusion), channel_id=1, source_target_pairs={{0,16},{16,0},{1,17},{17,1},{2,18},{18,2},{3,19},{19,3},{4,20},{20... | collective-permute-start | bytes 172040 | tf_op jit(solution)/shard_map/ppermute | solution.py:34
  19.7 8.8 %collective-permute-start.2 = (bf16[32,1792]{1,0:T(8,128)(2,1)S(1)}, bf16[32,1792]{1,0:T(8,128)(2,1)S(1)}, u32[]{:S(2)}, u32[]{:S(2)}) collective-permute-start(bf16[32,1792]{1,0:T(8,128)(2,1)S(1)} %pad_maximum_fusion.block0), channel_id=1, source_target_pairs={{0,3},{1,2},{2,1},{3,0},{4,7},{5,6},{6,5},{7,4},{8,11},{9,10},{10,... | collective-permute-start | bytes 344072 | tf_op jit(solution)/shard_map/ppermute | solution.py:34
  24.7 10.1 %collective-permute-start.1 = (bf16[32,1792]{1,0:T(8,128)(2,1)S(1)}, bf16[32,1792]{1,0:T(8,128)(2,1)S(1)}, u32[]{:S(2)}, u32[]{:S(2)}) collective-permute-start(bf16[32,1792]{1,0:T(8,128)(2,1)S(1)} %pad_maximum_fusion.block0), channel_id=1, source_target_pairs={{0,1},{1,0},{2,3},{3,2},{4,5},{5,4},{6,7},{7,6},{8,9},{9,8},{10,11... | collective-permute-start | bytes 344072 | tf_op jit(solution)/shard_map/ppermute | solution.py:34
  28.5 12.5 %collective-permute-start.3 = (bf16[16,1792]{1,0:T(8,128)(2,1)S(1)}, bf16[16,1792]{1,0:T(8,128)(2,1)S(1)}, u32[]{:S(2)}, u32[]{:S(2)}) collective-permute-start(bf16[16,1792]{1,0:T(8,128)(2,1)S(1)} %slice.8), channel_id=1, source_target_pairs={{0,1},{1,0},{2,3},{3,2},{4,5},{5,4},{6,7},{7,6},{8,9},{9,8},{10,11... | collective-permute-start | bytes 172040 | tf_op jit(solution)/shard_map/ppermute | solution.py:34
  34.8 7.1 %collective-permute-start.4 = (bf16[16,1792]{1,0:T(8,128)(2,1)S(1)}, bf16[16,1792]{1,0:T(8,128)(2,1)S(1)}, u32[]{:S(2)}, u32[]{:S(2)}) collective-permute-start(bf16[16,1792]{1,0:T(8,128)(2,1)S(1)} %slice.9), channel_id=1, source_target_pairs={{0,3},{1,2},{2,1},{3,0},{4,7},{5,6},{6,5},{7,4},{8,11},{9,10},{10,... | collective-permute-start | bytes 172040 | tf_op jit(solution)/shard_map/ppermute | solution.py:34
  37.5 7.7 %collective-permute-start.12 = (bf16[512,256]{1,0:T(8,128)(2,1)S(1)}, bf16[512,256]{1,0:T(8,128)(2,1)S(1)}, u32[]{:S(2)}, u32[]{:S(2)}) collective-permute-start(bf16[512,256]{1,0:T(8,128)(2,1)S(1)} %copy-done), channel_id=1, source_target_pairs={{0,16},{16,0},{1,17},{17,1},{2,18},{18,2},{3,19},{19,3},{4,20},{20... | collective-permute-start | bytes 786440 | tf_op jit(solution)/shard_map/ppermute | solution.py:34
  42.0 30.5 %copy-start.1 = (bf16[896,896]{1,0:T(8,128)(2,1)S(1)}, bf16[896,896]{1,0:T(8,128)(2,1)}, u32[]{:S(2)}) copy-start(bf16[896,896]{1,0:T(8,128)(2,1)} %param.7) | copy-start | bytes 4816900
  42.0 6.9 %collective-permute-start.6 = (bf16[128,896]{1,0:T(8,128)(2,1)S(1)}, bf16[128,896]{1,0:T(8,128)(2,1)S(1)}, u32[]{:S(2)}, u32[]{:S(2)}) collective-permute-start(bf16[128,896]{1,0:T(8,128)(2,1)S(1)} %get-tuple-element.18.own1), channel_id=1, source_target_pairs={{0,4},{4,0},{8,12},{12,8},{1,5},{5,1},{9,13},{13,9},{2,6},{6,2},{1... | collective-permute-start | bytes 688136 | tf_op jit(solution)/shard_map/ppermute | solution.py:34
  50.2 34.3 %all-to-all-start.2 = ((bf16[16,32,512]{2,1,0:T(8,128)(2,1)}), bf16[16,32,512]{2,1,0:T(8,128)(2,1)S(1)}, u32[]{:S(2)}, u32[]{:S(2)}) async-start(bf16[16,32,512]{2,1,0:T(8,128)(2,1)} %shard_map.48), calls=%async_computation.2 | async-start | bytes 1048576 | tf_op jit(solution)/shard_map/all_to_all | solution.py:145
  57.4 12.9 %collective-permute-start.7 = (bf16[128,896]{1,0:T(8,128)(2,1)S(1)}, bf16[128,896]{1,0:T(8,128)(2,1)S(1)}, u32[]{:S(2)}, u32[]{:S(2)}) collective-permute-start(bf16[128,896]{1,0:T(8,128)(2,1)S(1)} %get-tuple-element.17.own0), channel_id=1, source_target_pairs={{0,12},{4,8},{8,4},{12,0},{1,13},{5,9},{9,5},{13,1},{2,14},{6,10},... | collective-permute-start | bytes 688136 | tf_op jit(solution)/shard_map/ppermute | solution.py:34
  61.9 12.4 %collective-permute-start.5 = (bf16[128,896]{1,0:T(8,128)(2,1)S(1)}, bf16[128,896]{1,0:T(8,128)(2,1)S(1)}, u32[]{:S(2)}, u32[]{:S(2)}) collective-permute-start(bf16[128,896]{1,0:T(8,128)(2,1)S(1)} %get-tuple-element.17.own0), channel_id=1, source_target_pairs={{0,4},{4,0},{8,12},{12,8},{1,5},{5,1},{9,13},{13,9},{2,6},{6,2},{1... | collective-permute-start | bytes 688136 | tf_op jit(solution)/shard_map/ppermute | solution.py:34
  63.9 12.4 %collective-permute-start.10 = (bf16[128,896]{1,0:T(8,128)(2,1)S(1)}, bf16[128,896]{1,0:T(8,128)(2,1)S(1)}, u32[]{:S(2)}, u32[]{:S(2)}) collective-permute-start(bf16[128,896]{1,0:T(8,128)(2,1)S(1)} %get-tuple-element.18.own1), channel_id=1, source_target_pairs={{0,12},{4,8},{8,4},{12,0},{1,13},{5,9},{9,5},{13,1},{2,14},{6,10},... | collective-permute-start | bytes 688136 | tf_op jit(solution)/shard_map/ppermute | solution.py:34
  66.6 14.6 %collective-permute-start.9 = (bf16[128,896]{1,0:T(8,128)(2,1)S(1)}, bf16[128,896]{1,0:T(8,128)(2,1)S(1)}, u32[]{:S(2)}, u32[]{:S(2)}) collective-permute-start(bf16[128,896]{1,0:T(8,128)(2,1)S(1)} %collective-permute-done.6.near1.order), channel_id=1, source_target_pairs={{0,12},{4,8},{8,4},{12,0},{1,13},{5,9},{9,5},{13,1},{2,14},{6,10},... | collective-permute-start | bytes 688136 | tf_op jit(solution)/shard_map/ppermute | solution.py:34
  70.4 7.1 %collective-permute-start.8 = (bf16[128,896]{1,0:T(8,128)(2,1)S(1)}, bf16[128,896]{1,0:T(8,128)(2,1)S(1)}, u32[]{:S(2)}, u32[]{:S(2)}) collective-permute-start(bf16[128,896]{1,0:T(8,128)(2,1)S(1)} %collective-permute-done.7.back0), channel_id=1, source_target_pairs={{0,4},{4,0},{8,12},{12,8},{1,5},{5,1},{9,13},{13,9},{2,6},{6,2},{1... | collective-permute-start | bytes 688136 | tf_op jit(solution)/shard_map/ppermute | solution.py:34
  84.4 33.9 %all-to-all-start.1 = ((bf16[16,32,896]{2,1,0:T(8,128)(2,1)}), bf16[16,32,896]{2,1,0:T(8,128)(2,1)S(1)}, u32[]{:S(2)}, u32[]{:S(2)}) async-start(bf16[16,32,896]{2,1,0:T(8,128)(2,1)} %get-tuple-element.19), calls=%async_computation.1 | async-start | bytes 1835008 | tf_op jit(solution)/shard_map/all_to_all | solution.py:154
  95.0 4.1 %collective-permute-start.13 = (bf16[32,256]{1,0:T(8,128)(2,1)S(1)}, bf16[32,256]{1,0:T(8,128)(2,1)S(1)}, u32[]{:S(2)}, u32[]{:S(2)}) collective-permute-start(bf16[32,256]{1,0:T(8,128)(2,1)S(1)} %get-tuple-element.22), channel_id=1, source_target_pairs={{0,16},{16,0},{1,17},{17,1},{2,18},{18,2},{3,19},{19,3},{4,20},{20... | collective-permute-start | bytes 49160 | tf_op jit(solution)/shard_map/ppermute | solution.py:34
  99.1 11.4 %collective-permute-start.16 = (bf16[32,512]{1,0:T(8,128)(2,1)S(1)}, bf16[32,512]{1,0:T(8,128)(2,1)S(1)}, u32[]{:S(2)}, u32[]{:S(2)}) collective-permute-start(bf16[32,512]{1,0:T(8,128)(2,1)S(1)} %constant_dynamic-update-slice_fusion.block0), channel_id=1, source_target_pairs={{0,3},{1,2},{2,1},{3,0},{4,7},{5,6},{6,5},{7,4},{8,11},{9,10},{10,... | collective-permute-start | bytes 98312 | tf_op jit(solution)/shard_map/ppermute | solution.py:34
  104.5 8.8 %collective-permute-start.15 = (bf16[32,512]{1,0:T(8,128)(2,1)S(1)}, bf16[32,512]{1,0:T(8,128)(2,1)S(1)}, u32[]{:S(2)}, u32[]{:S(2)}) collective-permute-start(bf16[32,512]{1,0:T(8,128)(2,1)S(1)} %constant_dynamic-update-slice_fusion.block0), channel_id=1, source_target_pairs={{0,2},{1,3},{2,0},{3,1},{4,6},{5,7},{6,4},{7,5},{8,10},{9,11},{10,... | collective-permute-start | bytes 98312 | tf_op jit(solution)/shard_map/ppermute | solution.py:34
  108.5 5.9 %collective-permute-start.14 = (bf16[32,512]{1,0:T(8,128)(2,1)S(1)}, bf16[32,512]{1,0:T(8,128)(2,1)S(1)}, u32[]{:S(2)}, u32[]{:S(2)}) collective-permute-start(bf16[32,512]{1,0:T(8,128)(2,1)S(1)} %constant_dynamic-update-slice_fusion.block0), channel_id=1, source_target_pairs={{0,1},{1,0},{2,3},{3,2},{4,5},{5,4},{6,7},{7,6},{8,9},{9,8},{10,11... | collective-permute-start | bytes 98312 | tf_op jit(solution)/shard_map/ppermute | solution.py:34
  119.4 29.2 %all-to-all-start.3 = ((bf16[16,32,896]{2,1,0:T(8,128)(2,1)}), bf16[16,32,896]{2,1,0:T(8,128)(2,1)S(1)}, u32[]{:S(2)}, u32[]{:S(2)}) async-start(bf16[16,32,896]{2,1,0:T(8,128)(2,1)} %shard_map.51), calls=%async_computation.3 | async-start | bytes 1835008 | tf_op jit(solution)/shard_map/all_to_all | solution.py:162
  124.8 9.0 %collective-permute-start.19 = (bf16[128,512]{1,0:T(8,128)(2,1)S(1)}, bf16[128,512]{1,0:T(8,128)(2,1)S(1)}, u32[]{:S(2)}, u32[]{:S(2)}) collective-permute-start(bf16[128,512]{1,0:T(8,128)(2,1)S(1)} %shard_map.50.g0), channel_id=1, source_target_pairs={{0,12},{4,8},{8,4},{12,0},{1,13},{5,9},{9,5},{13,1},{2,14},{6,10},... | collective-permute-start | bytes 393224 | tf_op jit(solution)/shard_map/ppermute | solution.py:34
  127.6 7.5 %collective-permute-start.18 = (bf16[128,512]{1,0:T(8,128)(2,1)S(1)}, bf16[128,512]{1,0:T(8,128)(2,1)S(1)}, u32[]{:S(2)}, u32[]{:S(2)}) collective-permute-start(bf16[128,512]{1,0:T(8,128)(2,1)S(1)} %shard_map.50.g0), channel_id=1, source_target_pairs={{0,8},{4,12},{8,0},{12,4},{1,9},{5,13},{9,1},{13,5},{2,10},{6,14},... | collective-permute-start | bytes 393224 | tf_op jit(solution)/shard_map/ppermute | solution.py:34
  130.6 7.3 %collective-permute-start.17 = (bf16[128,512]{1,0:T(8,128)(2,1)S(1)}, bf16[128,512]{1,0:T(8,128)(2,1)S(1)}, u32[]{:S(2)}, u32[]{:S(2)}) collective-permute-start(bf16[128,512]{1,0:T(8,128)(2,1)S(1)} %shard_map.50.g0), channel_id=1, source_target_pairs={{0,4},{4,0},{8,12},{12,8},{1,5},{5,1},{9,13},{13,9},{2,6},{6,2},{1... | collective-permute-start | bytes 393224 | tf_op jit(solution)/shard_map/ppermute | solution.py:34
  148.6 5.9 %collective-permute-start.20 = (bf16[512,896]{1,0:T(8,128)(2,1)S(1)}, bf16[512,896]{1,0:T(8,128)(2,1)S(1)}, u32[]{:S(2)}, u32[]{:S(2)}) collective-permute-start(bf16[512,896]{1,0:T(8,128)(2,1)S(1)} %bitcast.4), channel_id=1, source_target_pairs={{0,16},{16,0},{1,17},{17,1},{2,18},{18,2},{3,19},{19,3},{4,20},{20... | collective-permute-start | bytes 2752520 | tf_op jit(solution)/shard_map/ppermute | solution.py:34

commit v12 on v10

--- a/solution.py
+++ b/solution.py
@@ -36,6 +36,11 @@
 
 def gather_yhi(mine):
     return [mine, swap(mine, "yhi", 1), swap(mine, "yhi", 2), swap(mine, "yhi", 3)]
+
+
+def copies_kernel(block, order, out):
+    for index in range(out.shape[0]):
+        out[index] = block[...]
 
 
 def stack_acts_kernel(block0, block1, block2, block3, order, out):
@@ -119,7 +124,9 @@
     act_basis0, act_basis1 = both(core, act_basis, swap(act_basis, "core", 1))
     grad_basis_other = swap(grad_basis, "core", 1)
 
-    grad_copies = jnp.broadcast_to(grads[None], (16, *grads.shape))
+    grad_copies = kernel_call(
+        copies_kernel, [jax.ShapeDtypeStruct((16, *grads.shape), BF16)], [grads, act_own], unread=1
+    )
     grad_rows = lax.all_to_all(grad_copies, CHIPS, 0, 0, tiled=True).reshape(tokens, -1)
     act0 = kernel_call(
         stack_acts_kernel,

time: 153 us -> 155 us (1.013)
    ppermute x18, starting transfers between devices: 62.7 us -> 69.7 us  [swap(): return lax.ppermute(value, axis, [(s, s ^ flip) for s in range(size)])]
    all_to_all x1, starting transfers between devices: 12.1 us -> 5.78 us  [shards(): lax.all_to_all(grad_copies, CHIPS, 0, 0, tiled=True).reshape(tokens, -1)]
    ppermute x18, waiting for transfers between devices: 33.9 us -> 31.6 us  [swap(): return lax.ppermute(value, axis, [(s, s ^ flip) for s in range(size)])]
    broadcast_in_dim x1 -> x0, local copies, waits for them, and re-layouts: 1.64 us -> none  [shards(): grad_copies = jnp.broadcast_to(grads[None], (16, *grads.shape))]
    pallas_call x7 -> x8, Pallas kernels: 7.24 us -> 8.07 us  [kernel_call(): pl.pallas_call(body, out_shape=shapes if many else shapes[0], in_specs=[V...]
  transfers between devices with their start and end apart: 22 -> 22, of which waited for: 14 -> 14; matrix products, arithmetic and copies ran while one was open for 2% -> 1% of each run, Pallas kernels for 3% -> 3%
where the time goes in v12:
time: 155 us; the launch traced here: 153 us
  starting transfers between devices  95.7 us (62%)
  waiting for transfers between devices  44.1 us (28%)
  Pallas kernels  8.07 us (5%)
  other arithmetic  3.06 us (2%)
  local copies, waits for them, and re-layouts  1.63 us (1%)
    ppermute x18, starting transfers between devices, swap(): return lax.ppermute(value, axis, [(s, s ^ flip) for s in range(size)])  69.7 us
    ppermute x18, waiting for transfers between devices, swap(): return lax.ppermute(value, axis, [(s, s ^ flip) for s in range(size)])  31.6 us
    all_to_all x1, waiting for transfers between devices, shards(): lax.all_to_all(kernel_call(sum_copies_kernel, [blocks], [act_parts]), CHI...  10.9 us
    pallas_call x8, Pallas kernels, kernel_call(): pl.pallas_call(body, out_shape=shapes if many else shapes[0], in_specs=[V...  8.07 us
    all_to_all x1, starting transfers between devices, shards(): grad_parts = lax.all_to_all(grad_partial, INP, 0, 0, tiled=True)  8.04 us
    all_to_all x1, starting transfers between devices, shards(): lax.all_to_all(kernel_call(sum_copies_kernel, [blocks], [act_parts]), CHI...  6.13 us
    all_to_all x1, starting transfers between devices, shards(): act_parts = lax.all_to_all(act_partial, CHIPS, 0, 0, tiled=True)  6.04 us
    all_to_all x1, starting transfers between devices, shards(): lax.all_to_all(grad_copies, CHIPS, 0, 0, tiled=True).reshape(tokens, -1)  5.78 us
  transfers between devices with their start and end apart: 22, of which 14 were waited for; matrix products, arithmetic and copies ran while one was open for 1% of the time, Pallas kernels for 3%

profile of v12, /device:TPU:1, one launch (start us, length us, event | category | flops | bytes accessed | tf_op | source)
XLA Modules:
  0.0 152.8 jit_solution(6725521542379984196)
XLA Ops:
  0.0 0.8 constant_dynamic-slice_fusion
  0.8 8.8 %collective-permute-start = (bf16[32,896]{1,0:T(8,128)(2,1)S(1)}, bf16[32,896]{1,0:T(8,128)(2,1)S(1)}, u32[]{:S(2)}, u32[]{:S(2)}) collective-permute-start(bf16[32,896]{1,0:T(8,128)(2,1)S(1)} %constant_dynamic-slice_fusion), channel_id=1, source_target_pairs={{0,16},{16,0},{1,17},{17,1},{2,18},{18,2},{3,19},{19,3},{4,20},{20... | collective-permute-start | bytes 172040 | tf_op jit(solution)/shard_map/ppermute | solution.py:34
  9.6 0.9 collective-permute-done
  10.5 0.8 broadcast_select_fusion.3
  11.3 0.0 copy-start.1
  11.4 0.7 copy-done.1
  12.1 0.0 copy-start
  12.1 0.8 shard_map.46
  12.9 5.8 %all-to-all-start = ((bf16[16,32,512]{2,1,0:T(8,128)(2,1)}), bf16[16,32,512]{2,1,0:T(8,128)(2,1)S(1)}, u32[]{:S(2)}, u32[]{:S(2)}) async-start(bf16[16,32,512]{2,1,0:T(8,128)(2,1)} %shard_map.46), calls=%async_computation | async-start | bytes 1048576 | tf_op jit(solution)/shard_map/all_to_all | solution.py:130
  18.7 2.5 %collective-permute-start.8 = (bf16[896,896]{1,0:T(8,128)(2,1)}, bf16[896,896]{1,0:T(8,128)(2,1)}, u32[]{:S(2)}, u32[]{:S(2)}) collective-permute-start(bf16[896,896]{1,0:T(8,128)(2,1)} %param.7), channel_id=1, source_target_pairs={{0,16},{16,0},{1,17},{17,1},{2,18},{18,2},{3,19},{19,3},{4,20},{20... | collective-permute-start | bytes 4816904 | tf_op jit(solution)/shard_map/ppermute | solution.py:34
  21.3 5.0 %collective-permute-start.3 = (bf16[32,1792]{1,0:T(8,128)(2,1)S(1)}, bf16[32,1792]{1,0:T(8,128)(2,1)S(1)}, u32[]{:S(2)}, u32[]{:S(2)}) collective-permute-start(bf16[32,1792]{1,0:T(8,128)(2,1)S(1)} %pad_maximum_fusion.order.block0), channel_id=1, source_target_pairs={{0,3},{1,2},{2,1},{3,0},{4,7},{5,6},{6,5},{7,4},{8,11},{9,10},{10,... | collective-permute-start | bytes 344072 | tf_op jit(solution)/shard_map/ppermute | solution.py:34
  26.3 4.4 %collective-permute-start.2 = (bf16[32,1792]{1,0:T(8,128)(2,1)S(1)}, bf16[32,1792]{1,0:T(8,128)(2,1)S(1)}, u32[]{:S(2)}, u32[]{:S(2)}) collective-permute-start(bf16[32,1792]{1,0:T(8,128)(2,1)S(1)} %pad_maximum_fusion.order.block0), channel_id=1, source_target_pairs={{0,2},{1,3},{2,0},{3,1},{4,6},{5,7},{6,4},{7,5},{8,10},{9,11},{10,... | collective-permute-start | bytes 344072 | tf_op jit(solution)/shard_map/ppermute | solution.py:34
  30.7 2.0 %collective-permute-start.1 = (bf16[32,1792]{1,0:T(8,128)(2,1)S(1)}, bf16[32,1792]{1,0:T(8,128)(2,1)S(1)}, u32[]{:S(2)}, u32[]{:S(2)}) collective-permute-start(bf16[32,1792]{1,0:T(8,128)(2,1)S(1)} %pad_maximum_fusion.order.block0), channel_id=1, source_target_pairs={{0,1},{1,0},{2,3},{3,2},{4,5},{5,4},{6,7},{7,6},{8,9},{9,8},{10,11... | collective-permute-start | bytes 344072 | tf_op jit(solution)/shard_map/ppermute | solution.py:34
  32.7 0.0 collective-permute-done.3.block3
  32.7 9.1 %collective-permute-done.2.block2 = bf16[32,1792]{1,0:T(8,128)(2,1)S(1)} collective-permute-done((bf16[32,1792]{1,0:T(8,128)(2,1)S(1)}, bf16[32,1792]{1,0:T(8,128)(2,1)S(1)}, u32[]{:S(2)}, u32[]{:S(2)}) %collective-permute-start.2) | collective-permute-done | bytes 114720 | tf_op jit(solution)/shard_map/ppermute | solution.py:34
  41.8 1.7 %collective-permute-done.1.block1 = bf16[32,1792]{1,0:T(8,128)(2,1)S(1)} collective-permute-done((bf16[32,1792]{1,0:T(8,128)(2,1)S(1)}, bf16[32,1792]{1,0:T(8,128)(2,1)S(1)}, u32[]{:S(2)}, u32[]{:S(2)}) %collective-permute-start.1) | collective-permute-done | bytes 114720 | tf_op jit(solution)/shard_map/ppermute | solution.py:34
  43.5 0.0 all-to-all-done
  43.6 3.1 %collective-permute-start.4 = (bf16[2,128,896]{2,1,0:T(8,128)(2,1)S(1)}, bf16[2,128,896]{2,1,0:T(8,128)(2,1)S(1)}, u32[]{:S(2)}, u32[]{:S(2)}) collective-permute-start(bf16[2,128,896]{2,1,0:T(8,128)(2,1)S(1)} %shard_map.47.act0), channel_id=1, source_target_pairs={{0,4},{4,0},{8,12},{12,8},{1,5},{5,1},{9,13},{13,9},{2,6},{6,2},{1... | collective-permute-start | bytes 1376264 | tf_op jit(solution)/shard_map/ppermute | solution.py:34
  46.7 3.7 %collective-permute-start.5 = (bf16[2,128,896]{2,1,0:T(8,128)(2,1)S(1)}, bf16[2,128,896]{2,1,0:T(8,128)(2,1)S(1)}, u32[]{:S(2)}, u32[]{:S(2)}) collective-permute-start(bf16[2,128,896]{2,1,0:T(8,128)(2,1)S(1)} %shard_map.47.act0), channel_id=1, source_target_pairs={{0,12},{4,8},{8,4},{12,0},{1,13},{5,9},{9,5},{13,1},{2,14},{6,10},... | collective-permute-start | bytes 1376264 | tf_op jit(solution)/shard_map/ppermute | solution.py:34
  50.4 0.0 copy-done
  50.4 3.0 %collective-permute-start.9 = (bf16[512,256]{1,0:T(8,128)(2,1)S(1)}, bf16[512,256]{1,0:T(8,128)(2,1)S(1)}, u32[]{:S(2)}, u32[]{:S(2)}) collective-permute-start(bf16[512,256]{1,0:T(8,128)(2,1)S(1)} %copy-done), channel_id=1, source_target_pairs={{0,16},{16,0},{1,17},{17,1},{2,18},{18,2},{3,19},{19,3},{4,20},{20... | collective-permute-start | bytes 786440 | tf_op jit(solution)/shard_map/ppermute | solution.py:34
  53.4 1.1 collective-permute-done.9.other
  54.5 2.5 %collective-permute-done.4.act1.order = bf16[2,128,896]{2,1,0:T(8,128)(2,1)S(1)} collective-permute-done((bf16[2,128,896]{2,1,0:T(8,128)(2,1)S(1)}, bf16[2,128,896]{2,1,0:T(8,128)(2,1)S(1)}, u32[]{:S(2)}, u32[]{:S(2)}) %collective-permute-start.4) | collective-permute-done | bytes 458784 | tf_op jit(solution)/shard_map/ppermute | solution.py:34
  57.1 1.2 shard_map.49
  58.3 8.0 %all-to-all-start.2 = ((bf16[16,32,512]{2,1,0:T(8,128)(2,1)}), bf16[16,32,512]{2,1,0:T(8,128)(2,1)S(1)}, u32[]{:S(2)}, u32[]{:S(2)}) async-start(bf16[16,32,512]{2,1,0:T(8,128)(2,1)} %shard_map.49), calls=%async_computation.2 | async-start | bytes 1048576 | tf_op jit(solution)/shard_map/all_to_all | solution.py:147
  66.3 0.0 collective-permute-done.5.act3
  66.4 3.3 %collective-permute-start.6 = (bf16[128,896]{1,0:T(8,128)(2,1)S(1)}, bf16[128,896]{1,0:T(8,128)(2,1)S(1)}, u32[]{:S(2)}, u32[]{:S(2)}) collective-permute-start(bf16[128,896]{1,0:T(8,128)(2,1)S(1)} %slice_bitcast_fusion.1), channel_id=1, source_target_pairs={{0,4},{4,0},{8,12},{12,8},{1,5},{5,1},{9,13},{13,9},{2,6},{6,2},{1... | collective-permute-start | bytes 688136 | tf_op jit(solution)/shard_map/ppermute | solution.py:34
  69.7 3.7 %collective-permute-start.7 = (bf16[128,896]{1,0:T(8,128)(2,1)S(1)}, bf16[128,896]{1,0:T(8,128)(2,1)S(1)}, u32[]{:S(2)}, u32[]{:S(2)}) collective-permute-start(bf16[128,896]{1,0:T(8,128)(2,1)S(1)} %slice_bitcast_fusion), channel_id=1, source_target_pairs={{0,12},{4,8},{8,4},{12,0},{1,13},{5,9},{9,5},{13,1},{2,14},{6,10},... | collective-permute-start | bytes 688136 | tf_op jit(solution)/shard_map/ppermute | solution.py:34
  73.4 0.0 collective-permute-done.8
  73.4 2.2 %broadcast_select_fusion = (bf16[896,896]{1,0:T(8,128)(2,1)S(1)}, bf16[896,896]{1,0:T(8,128)(2,1)S(1)}) fusion(bf16[896,896]{1,0:T(8,128)(2,1)} %collective-permute-done.8, bf16[896,896]{1,0:T(8,128)(2,1)} %param.7, pred[]{:T(512)S(6)} %eq.2), kind=kLoop, calls=%fused_computation | loop fusion | flops 1605632 | bytes 6422529 | tf_op jit(solution)/shard_map/jit(_where)/select_n | solution.py:112
  75.6 0.0 collective-permute-done.6.low2
  75.6 6.4 %collective-permute-done.7.high2 = bf16[128,896]{1,0:T(8,128)(2,1)S(1)} collective-permute-done((bf16[128,896]{1,0:T(8,128)(2,1)S(1)}, bf16[128,896]{1,0:T(8,128)(2,1)S(1)}, u32[]{:S(2)}, u32[]{:S(2)}) %collective-permute-start.7) | collective-permute-done | bytes 229408 | tf_op jit(solution)/shard_map/ppermute | solution.py:34
  82.0 3.2 %shard_map.48 = (bf16[16,32,896]{2,1,0:T(8,128)(2,1)}, f32[8,128]{1,0:T(8,128)S(1)}) custom-call(bf16[2,128,896]{2,1,0:T(8,128)(2,1)S(1)} %shard_map.47.act0, bf16[2,128,896]{2,1,0:T(8,128)(2,1)S(1)} %collective-permute-done.4.act1.order, bf16[128,896]{1,0:T(8,128)(2,1)S(1)} %collective-permute-done.6.low2, ...), custom_call_target="tpu_custom_call" | custom-call | flops 1644167168 | bytes 5967872 | tf_op jit(solution)/shard_map/pallas_call | solution.py:22
  85.2 0.0 all-to-all-done.2.parts
  85.2 6.0 %all-to-all-start.1 = ((bf16[16,32,896]{2,1,0:T(8,128)(2,1)}), bf16[16,32,896]{2,1,0:T(8,128)(2,1)S(1)}, u32[]{:S(2)}, u32[]{:S(2)}) async-start(bf16[16,32,896]{2,1,0:T(8,128)(2,1)} %get-tuple-element.15), calls=%async_computation.1 | async-start | bytes 1835008 | tf_op jit(solution)/shard_map/all_to_all | solution.py:156
  91.3 0.1 shard_map.50
  91.3 5.4 %collective-permute-start.10 = (bf16[32,256]{1,0:T(8,128)(2,1)S(1)}, bf16[32,256]{1,0:T(8,128)(2,1)S(1)}, u32[]{:S(2)}, u32[]{:S(2)}) collective-permute-start(bf16[32,256]{1,0:T(8,128)(2,1)S(1)} %get-tuple-element.18), channel_id=1, source_target_pairs={{0,16},{16,0},{1,17},{17,1},{2,18},{18,2},{3,19},{19,3},{4,20},{20... | collective-permute-start | bytes 49160 | tf_op jit(solution)/shard_map/ppermute | solution.py:34
  96.8 0.8 collective-permute-done.10
  97.6 5.0 %collective-permute-start.13 = (bf16[32,512]{1,0:T(8,128)(2,1)S(1)}, bf16[32,512]{1,0:T(8,128)(2,1)S(1)}, u32[]{:S(2)}, u32[]{:S(2)}) collective-permute-start(bf16[32,512]{1,0:T(8,128)(2,1)S(1)} %constant_dynamic-update-slice_fusion.block0), channel_id=1, source_target_pairs={{0,3},{1,2},{2,1},{3,0},{4,7},{5,6},{6,5},{7,4},{8,11},{9,10},{10,... | collective-permute-start | bytes 98312 | tf_op jit(solution)/shard_map/ppermute | solution.py:34
  102.5 4.2 %collective-permute-start.12 = (bf16[32,512]{1,0:T(8,128)(2,1)S(1)}, bf16[32,512]{1,0:T(8,128)(2,1)S(1)}, u32[]{:S(2)}, u32[]{:S(2)}) collective-permute-start(bf16[32,512]{1,0:T(8,128)(2,1)S(1)} %constant_dynamic-update-slice_fusion.block0), channel_id=1, source_target_pairs={{0,2},{1,3},{2,0},{3,1},{4,6},{5,7},{6,4},{7,5},{8,10},{9,11},{10,... | collective-permute-start | bytes 98312 | tf_op jit(solution)/shard_map/ppermute | solution.py:34
  106.8 2.2 %collective-permute-start.11 = (bf16[32,512]{1,0:T(8,128)(2,1)S(1)}, bf16[32,512]{1,0:T(8,128)(2,1)S(1)}, u32[]{:S(2)}, u32[]{:S(2)}) collective-permute-start(bf16[32,512]{1,0:T(8,128)(2,1)S(1)} %constant_dynamic-update-slice_fusion.block0), channel_id=1, source_target_pairs={{0,1},{1,0},{2,3},{3,2},{4,5},{5,4},{6,7},{7,6},{8,9},{9,8},{10,11... | collective-permute-start | bytes 98312 | tf_op jit(solution)/shard_map/ppermute | solution.py:34
  109.0 0.0 collective-permute-done.13.block3
  109.0 3.3 %collective-permute-done.12.block2 = bf16[32,512]{1,0:T(8,128)(2,1)S(1)} collective-permute-done((bf16[32,512]{1,0:T(8,128)(2,1)S(1)}, bf16[32,512]{1,0:T(8,128)(2,1)S(1)}, u32[]{:S(2)}, u32[]{:S(2)}) %collective-permute-start.12) | collective-permute-done | bytes 32800 | tf_op jit(solution)/shard_map/ppermute | solution.py:34
  112.3 0.5 collective-permute-done.11.block1
  112.8 1.6 %all-to-all-done.1.parts = bf16[16,32,896]{2,1,0:T(8,128)(2,1)S(1)} async-done(((bf16[16,32,896]{2,1,0:T(8,128)(2,1)}), bf16[16,32,896]{2,1,0:T(8,128)(2,1)S(1)}, u32[]{:S(2)}, u32[]{:S(2)}) %all-to-all-start.1) | async-done | bytes 917536 | tf_op jit(solution)/shard_map/all_to_all | solution.py:156
  114.3 1.1 shard_map.52
  115.4 6.1 %all-to-all-start.3 = ((bf16[16,32,896]{2,1,0:T(8,128)(2,1)}), bf16[16,32,896]{2,1,0:T(8,128)(2,1)S(1)}, u32[]{:S(2)}, u32[]{:S(2)}) async-start(bf16[16,32,896]{2,1,0:T(8,128)(2,1)} %shard_map.52), calls=%async_computation.3 | async-start | bytes 1835008 | tf_op jit(solution)/shard_map/all_to_all | solution.py:164
  121.5 3.6 %collective-permute-start.16 = (bf16[128,512]{1,0:T(8,128)(2,1)S(1)}, bf16[128,512]{1,0:T(8,128)(2,1)S(1)}, u32[]{:S(2)}, u32[]{:S(2)}) collective-permute-start(bf16[128,512]{1,0:T(8,128)(2,1)S(1)} %shard_map.51.g0), channel_id=1, source_target_pairs={{0,12},{4,8},{8,4},{12,0},{1,13},{5,9},{9,5},{13,1},{2,14},{6,10},... | collective-permute-start | bytes 393224 | tf_op jit(solution)/shard_map/ppermute | solution.py:34
  125.2 1.9 %collective-permute-start.15 = (bf16[128,512]{1,0:T(8,128)(2,1)S(1)}, bf16[128,512]{1,0:T(8,128)(2,1)S(1)}, u32[]{:S(2)}, u32[]{:S(2)}) collective-permute-start(bf16[128,512]{1,0:T(8,128)(2,1)S(1)} %shard_map.51.g0), channel_id=1, source_target_pairs={{0,8},{4,12},{8,0},{12,4},{1,9},{5,13},{9,1},{13,5},{2,10},{6,14},... | collective-permute-start | bytes 393224 | tf_op jit(solution)/shard_map/ppermute | solution.py:34
  127.1 3.4 %collective-permute-start.14 = (bf16[128,512]{1,0:T(8,128)(2,1)S(1)}, bf16[128,512]{1,0:T(8,128)(2,1)S(1)}, u32[]{:S(2)}, u32[]{:S(2)}) collective-permute-start(bf16[128,512]{1,0:T(8,128)(2,1)S(1)} %shard_map.51.g0), channel_id=1, source_target_pairs={{0,4},{4,0},{8,12},{12,8},{1,5},{5,1},{9,13},{13,9},{2,6},{6,2},{1... | collective-permute-start | bytes 393224 | tf_op jit(solution)/shard_map/ppermute | solution.py:34
  130.5 0.0 collective-permute-done.16.g3
  130.5 2.2 %collective-permute-done.15.g2 = bf16[128,512]{1,0:T(8,128)(2,1)S(1)} collective-permute-done((bf16[128,512]{1,0:T(8,128)(2,1)S(1)}, bf16[128,512]{1,0:T(8,128)(2,1)S(1)}, u32[]{:S(2)}, u32[]{:S(2)}) %collective-permute-start.15) | collective-permute-done | bytes 131104 | tf_op jit(solution)/shard_map/ppermute | solution.py:34
  132.7 1.0 collective-permute-done.14.g1
  133.7 10.9 %all-to-all-done.3 = bf16[16,32,896]{2,1,0:T(8,128)(2,1)S(1)} async-done(((bf16[16,32,896]{2,1,0:T(8,128)(2,1)}), bf16[16,32,896]{2,1,0:T(8,128)(2,1)S(1)}, u32[]{:S(2)}, u32[]{:S(2)}) %all-to-all-start.3) | async-done | bytes 917536 | tf_op jit(solution)/shard_map/all_to_all | solution.py:164
  144.6 4.5 %collective-permute-start.17 = (bf16[512,896]{1,0:T(8,128)(2,1)S(1)}, bf16[512,896]{1,0:T(8,128)(2,1)S(1)}, u32[]{:S(2)}, u32[]{:S(2)}) collective-permute-start(bf16[512,896]{1,0:T(8,128)(2,1)S(1)} %bitcast.8), channel_id=1, source_target_pairs={{0,16},{16,0},{1,17},{17,1},{2,18},{18,2},{3,19},{19,3},{4,20},{20... | collective-permute-start | bytes 2752520 | tf_op jit(solution)/shard_map/ppermute | solution.py:34
  149.1 2.1 %collective-permute-done.17.act_theirs = bf16[512,896]{1,0:T(8,128)(2,1)S(1)} collective-permute-done((bf16[512,896]{1,0:T(8,128)(2,1)S(1)}, bf16[512,896]{1,0:T(8,128)(2,1)S(1)}, u32[]{:S(2)}, u32[]{:S(2)}) %collective-permute-start.17) | collective-permute-done | bytes 917536 | tf_op jit(solution)/shard_map/ppermute | solution.py:34
  151.2 1.7 %shard_map.53 = f32[256,896]{1,0:T(8,128)} custom-call(bf16[128,512]{1,0:T(8,128)(2,1)S(1)} %shard_map.51.g0, bf16[128,512]{1,0:T(8,128)(2,1)S(1)} %collective-permute-done.14.g1, bf16[128,512]{1,0:T(8,128)(2,1)S(1)} %collective-permute-done.15.g2, bf16[128,512]{1,0:T(8,128)(2,1)S(1)} %collective-permute-done.16.g3, bf16[512,896]{1,0:T(8,128)(2,1)S(1)} %bitcast.9, ...), custom_call_target="tpu_custom_call" | custom-call | flops 469762048 | bytes 3276800 | tf_op jit(solution)/shard_map/pallas_call | solution.py:22
  (7 shorter events, 0.1 us)
Async XLA Ops:
  0.8 9.7 %collective-permute-start = (bf16[32,896]{1,0:T(8,128)(2,1)S(1)}, bf16[32,896]{1,0:T(8,128)(2,1)S(1)}, u32[]{:S(2)}, u32[]{:S(2)}) collective-permute-start(bf16[32,896]{1,0:T(8,128)(2,1)S(1)} %constant_dynamic-slice_fusion), channel_id=1, source_target_pairs={{0,16},{16,0},{1,17},{17,1},{2,18},{18,2},{3,19},{19,3},{4,20},{20... | collective-permute-start | bytes 172040 | tf_op jit(solution)/shard_map/ppermute | solution.py:34
  11.3 0.8 copy-start.1
  12.1 38.3 %copy-start = (bf16[512,256]{1,0:T(8,128)(2,1)S(1)}, bf16[512,256]{1,0:T(8,128)(2,1)}, u32[]{:S(2)}) copy-start(bf16[512,256]{1,0:T(8,128)(2,1)} %own.1) | copy-start | bytes 786436
  12.9 30.6 %all-to-all-start = ((bf16[16,32,512]{2,1,0:T(8,128)(2,1)}), bf16[16,32,512]{2,1,0:T(8,128)(2,1)S(1)}, u32[]{:S(2)}, u32[]{:S(2)}) async-start(bf16[16,32,512]{2,1,0:T(8,128)(2,1)} %shard_map.46), calls=%async_computation | async-start | bytes 1048576 | tf_op jit(solution)/shard_map/all_to_all | solution.py:130
  18.7 54.7 %collective-permute-start.8 = (bf16[896,896]{1,0:T(8,128)(2,1)}, bf16[896,896]{1,0:T(8,128)(2,1)}, u32[]{:S(2)}, u32[]{:S(2)}) collective-permute-start(bf16[896,896]{1,0:T(8,128)(2,1)} %param.7), channel_id=1, source_target_pairs={{0,16},{16,0},{1,17},{17,1},{2,18},{18,2},{3,19},{19,3},{4,20},{20... | collective-permute-start | bytes 4816904 | tf_op jit(solution)/shard_map/ppermute | solution.py:34
  21.3 11.4 %collective-permute-start.3 = (bf16[32,1792]{1,0:T(8,128)(2,1)S(1)}, bf16[32,1792]{1,0:T(8,128)(2,1)S(1)}, u32[]{:S(2)}, u32[]{:S(2)}) collective-permute-start(bf16[32,1792]{1,0:T(8,128)(2,1)S(1)} %pad_maximum_fusion.order.block0), channel_id=1, source_target_pairs={{0,3},{1,2},{2,1},{3,0},{4,7},{5,6},{6,5},{7,4},{8,11},{9,10},{10,... | collective-permute-start | bytes 344072 | tf_op jit(solution)/shard_map/ppermute | solution.py:34
  26.3 15.6 %collective-permute-start.2 = (bf16[32,1792]{1,0:T(8,128)(2,1)S(1)}, bf16[32,1792]{1,0:T(8,128)(2,1)S(1)}, u32[]{:S(2)}, u32[]{:S(2)}) collective-permute-start(bf16[32,1792]{1,0:T(8,128)(2,1)S(1)} %pad_maximum_fusion.order.block0), channel_id=1, source_target_pairs={{0,2},{1,3},{2,0},{3,1},{4,6},{5,7},{6,4},{7,5},{8,10},{9,11},{10,... | collective-permute-start | bytes 344072 | tf_op jit(solution)/shard_map/ppermute | solution.py:34
  30.7 12.8 %collective-permute-start.1 = (bf16[32,1792]{1,0:T(8,128)(2,1)S(1)}, bf16[32,1792]{1,0:T(8,128)(2,1)S(1)}, u32[]{:S(2)}, u32[]{:S(2)}) collective-permute-start(bf16[32,1792]{1,0:T(8,128)(2,1)S(1)} %pad_maximum_fusion.order.block0), channel_id=1, source_target_pairs={{0,1},{1,0},{2,3},{3,2},{4,5},{5,4},{6,7},{7,6},{8,9},{9,8},{10,11... | collective-permute-start | bytes 344072 | tf_op jit(solution)/shard_map/ppermute | solution.py:34
  43.6 13.5 %collective-permute-start.4 = (bf16[2,128,896]{2,1,0:T(8,128)(2,1)S(1)}, bf16[2,128,896]{2,1,0:T(8,128)(2,1)S(1)}, u32[]{:S(2)}, u32[]{:S(2)}) collective-permute-start(bf16[2,128,896]{2,1,0:T(8,128)(2,1)S(1)} %shard_map.47.act0), channel_id=1, source_target_pairs={{0,4},{4,0},{8,12},{12,8},{1,5},{5,1},{9,13},{13,9},{2,6},{6,2},{1... | collective-permute-start | bytes 1376264 | tf_op jit(solution)/shard_map/ppermute | solution.py:34
  46.7 19.6 %collective-permute-start.5 = (bf16[2,128,896]{2,1,0:T(8,128)(2,1)S(1)}, bf16[2,128,896]{2,1,0:T(8,128)(2,1)S(1)}, u32[]{:S(2)}, u32[]{:S(2)}) collective-permute-start(bf16[2,128,896]{2,1,0:T(8,128)(2,1)S(1)} %shard_map.47.act0), channel_id=1, source_target_pairs={{0,12},{4,8},{8,4},{12,0},{1,13},{5,9},{9,5},{13,1},{2,14},{6,10},... | collective-permute-start | bytes 1376264 | tf_op jit(solution)/shard_map/ppermute | solution.py:34
  50.4 4.1 %collective-permute-start.9 = (bf16[512,256]{1,0:T(8,128)(2,1)S(1)}, bf16[512,256]{1,0:T(8,128)(2,1)S(1)}, u32[]{:S(2)}, u32[]{:S(2)}) collective-permute-start(bf16[512,256]{1,0:T(8,128)(2,1)S(1)} %copy-done), channel_id=1, source_target_pairs={{0,16},{16,0},{1,17},{17,1},{2,18},{18,2},{3,19},{19,3},{4,20},{20... | collective-permute-start | bytes 786440 | tf_op jit(solution)/shard_map/ppermute | solution.py:34
  58.3 26.9 %all-to-all-start.2 = ((bf16[16,32,512]{2,1,0:T(8,128)(2,1)}), bf16[16,32,512]{2,1,0:T(8,128)(2,1)S(1)}, u32[]{:S(2)}, u32[]{:S(2)}) async-start(bf16[16,32,512]{2,1,0:T(8,128)(2,1)} %shard_map.49), calls=%async_computation.2 | async-start | bytes 1048576 | tf_op jit(solution)/shard_map/all_to_all | solution.py:147
  66.4 9.2 %collective-permute-start.6 = (bf16[128,896]{1,0:T(8,128)(2,1)S(1)}, bf16[128,896]{1,0:T(8,128)(2,1)S(1)}, u32[]{:S(2)}, u32[]{:S(2)}) collective-permute-start(bf16[128,896]{1,0:T(8,128)(2,1)S(1)} %slice_bitcast_fusion.1), channel_id=1, source_target_pairs={{0,4},{4,0},{8,12},{12,8},{1,5},{5,1},{9,13},{13,9},{2,6},{6,2},{1... | collective-permute-start | bytes 688136 | tf_op jit(solution)/shard_map/ppermute | solution.py:34
  69.7 12.3 %collective-permute-start.7 = (bf16[128,896]{1,0:T(8,128)(2,1)S(1)}, bf16[128,896]{1,0:T(8,128)(2,1)S(1)}, u32[]{:S(2)}, u32[]{:S(2)}) collective-permute-start(bf16[128,896]{1,0:T(8,128)(2,1)S(1)} %slice_bitcast_fusion), channel_id=1, source_target_pairs={{0,12},{4,8},{8,4},{12,0},{1,13},{5,9},{9,5},{13,1},{2,14},{6,10},... | collective-permute-start | bytes 688136 | tf_op jit(solution)/shard_map/ppermute | solution.py:34
  85.2 29.1 %all-to-all-start.1 = ((bf16[16,32,896]{2,1,0:T(8,128)(2,1)}), bf16[16,32,896]{2,1,0:T(8,128)(2,1)S(1)}, u32[]{:S(2)}, u32[]{:S(2)}) async-start(bf16[16,32,896]{2,1,0:T(8,128)(2,1)} %get-tuple-element.15), calls=%async_computation.1 | async-start | bytes 1835008 | tf_op jit(solution)/shard_map/all_to_all | solution.py:156
  91.3 6.2 %collective-permute-start.10 = (bf16[32,256]{1,0:T(8,128)(2,1)S(1)}, bf16[32,256]{1,0:T(8,128)(2,1)S(1)}, u32[]{:S(2)}, u32[]{:S(2)}) collective-permute-start(bf16[32,256]{1,0:T(8,128)(2,1)S(1)} %get-tuple-element.18), channel_id=1, source_target_pairs={{0,16},{16,0},{1,17},{17,1},{2,18},{18,2},{3,19},{19,3},{4,20},{20... | collective-permute-start | bytes 49160 | tf_op jit(solution)/shard_map/ppermute | solution.py:34
  97.6 11.4 %collective-permute-start.13 = (bf16[32,512]{1,0:T(8,128)(2,1)S(1)}, bf16[32,512]{1,0:T(8,128)(2,1)S(1)}, u32[]{:S(2)}, u32[]{:S(2)}) collective-permute-start(bf16[32,512]{1,0:T(8,128)(2,1)S(1)} %constant_dynamic-update-slice_fusion.block0), channel_id=1, source_target_pairs={{0,3},{1,2},{2,1},{3,0},{4,7},{5,6},{6,5},{7,4},{8,11},{9,10},{10,... | collective-permute-start | bytes 98312 | tf_op jit(solution)/shard_map/ppermute | solution.py:34
  102.5 9.7 %collective-permute-start.12 = (bf16[32,512]{1,0:T(8,128)(2,1)S(1)}, bf16[32,512]{1,0:T(8,128)(2,1)S(1)}, u32[]{:S(2)}, u32[]{:S(2)}) collective-permute-start(bf16[32,512]{1,0:T(8,128)(2,1)S(1)} %constant_dynamic-update-slice_fusion.block0), channel_id=1, source_target_pairs={{0,2},{1,3},{2,0},{3,1},{4,6},{5,7},{6,4},{7,5},{8,10},{9,11},{10,... | collective-permute-start | bytes 98312 | tf_op jit(solution)/shard_map/ppermute | solution.py:34
  106.8 6.0 %collective-permute-start.11 = (bf16[32,512]{1,0:T(8,128)(2,1)S(1)}, bf16[32,512]{1,0:T(8,128)(2,1)S(1)}, u32[]{:S(2)}, u32[]{:S(2)}) collective-permute-start(bf16[32,512]{1,0:T(8,128)(2,1)S(1)} %constant_dynamic-update-slice_fusion.block0), channel_id=1, source_target_pairs={{0,1},{1,0},{2,3},{3,2},{4,5},{5,4},{6,7},{7,6},{8,9},{9,8},{10,11... | collective-permute-start | bytes 98312 | tf_op jit(solution)/shard_map/ppermute | solution.py:34
  115.4 29.2 %all-to-all-start.3 = ((bf16[16,32,896]{2,1,0:T(8,128)(2,1)}), bf16[16,32,896]{2,1,0:T(8,128)(2,1)S(1)}, u32[]{:S(2)}, u32[]{:S(2)}) async-start(bf16[16,32,896]{2,1,0:T(8,128)(2,1)} %shard_map.52), calls=%async_computation.3 | async-start | bytes 1835008 | tf_op jit(solution)/shard_map/all_to_all | solution.py:164
  121.5 9.0 %collective-permute-start.16 = (bf16[128,512]{1,0:T(8,128)(2,1)S(1)}, bf16[128,512]{1,0:T(8,128)(2,1)S(1)}, u32[]{:S(2)}, u32[]{:S(2)}) collective-permute-start(bf16[128,512]{1,0:T(8,128)(2,1)S(1)} %shard_map.51.g0), channel_id=1, source_target_pairs={{0,12},{4,8},{8,4},{12,0},{1,13},{5,9},{9,5},{13,1},{2,14},{6,10},... | collective-permute-start | bytes 393224 | tf_op jit(solution)/shard_map/ppermute | solution.py:34
  125.2 7.5 %collective-permute-start.15 = (bf16[128,512]{1,0:T(8,128)(2,1)S(1)}, bf16[128,512]{1,0:T(8,128)(2,1)S(1)}, u32[]{:S(2)}, u32[]{:S(2)}) collective-permute-start(bf16[128,512]{1,0:T(8,128)(2,1)S(1)} %shard_map.51.g0), channel_id=1, source_target_pairs={{0,8},{4,12},{8,0},{12,4},{1,9},{5,13},{9,1},{13,5},{2,10},{6,14},... | collective-permute-start | bytes 393224 | tf_op jit(solution)/shard_map/ppermute | solution.py:34
  127.1 6.6 %collective-permute-start.14 = (bf16[128,512]{1,0:T(8,128)(2,1)S(1)}, bf16[128,512]{1,0:T(8,128)(2,1)S(1)}, u32[]{:S(2)}, u32[]{:S(2)}) collective-permute-start(bf16[128,512]{1,0:T(8,128)(2,1)S(1)} %shard_map.51.g0), channel_id=1, source_target_pairs={{0,4},{4,0},{8,12},{12,8},{1,5},{5,1},{9,13},{13,9},{2,6},{6,2},{1... | collective-permute-start | bytes 393224 | tf_op jit(solution)/shard_map/ppermute | solution.py:34
  144.6 6.5 %collective-permute-start.17 = (bf16[512,896]{1,0:T(8,128)(2,1)S(1)}, bf16[512,896]{1,0:T(8,128)(2,1)S(1)}, u32[]{:S(2)}, u32[]{:S(2)}) collective-permute-start(bf16[512,896]{1,0:T(8,128)(2,1)S(1)} %bitcast.8), channel_id=1, source_target_pairs={{0,16},{16,0},{1,17},{17,1},{2,18},{18,2},{3,19},{19,3},{4,20},{20... | collective-permute-start | bytes 2752520 | tf_op jit(solution)/shard_map/ppermute | solution.py:34

commit v13 on v12

--- a/solution.py
+++ b/solution.py
@@ -43,7 +43,7 @@
         out[index] = block[...]
 
 
-def stack_acts_kernel(block0, block1, block2, block3, order, out):
+def stack_acts_kernel(block0, block1, block2, block3, out):
     rows, features = block0.shape[0], out.shape[2]
     for index, block in enumerate((block0, block1, block2, block3)):
         for side in range(2):
@@ -131,8 +131,7 @@
     act0 = kernel_call(
         stack_acts_kernel,
         [jax.ShapeDtypeStruct((2, 4 * half, features), BF16)],
-        [*gather_yhi(act_own), grad_rows],
-        unread=1,
+        gather_yhi(act_own),
     )
     act1, act3 = swap(act0, "x", 1), swap(act0, "x", 3)
     low2, high2 = swap(act3[0], "x", 1), swap(act1[1], "x", 3)

time: 155 us -> 153 us (0.987)
  waiting for transfers between devices: 44.1 us -> 38.3 us
  starting transfers between devices: 95.7 us -> 101 us
    ppermute x18, waiting for transfers between devices: 31.6 us -> 29.4 us  [swap(): return lax.ppermute(value, axis, [(s, s ^ flip) for s in range(size)])]
    all_to_all x1, starting transfers between devices: 6.04 us -> 8.12 us  [shards(): act_parts = lax.all_to_all(act_partial, CHIPS, 0, 0, tiled=True)]
    all_to_all x1, waiting for transfers between devices: 10.9 us -> 8.87 us  [shards(): lax.all_to_all(kernel_call(sum_copies_kernel, [blocks], [act_parts]), CHI...]
    all_to_all x1, starting transfers between devices: 6.13 us -> 7.87 us  [shards(): lax.all_to_all(kernel_call(sum_copies_kernel, [blocks], [act_parts]), CHI...]
  transfers between devices with their start and end apart: 22 -> 22, of which waited for: 14 -> 13; matrix products, arithmetic and copies ran while one was open for 1% -> 2% of each run, Pallas kernels for 3% -> 4%
where the time goes in v13:
time: 153 us; the launch traced here: 152 us
  starting transfers between devices  101 us (66%)
  waiting for transfers between devices  38.3 us (25%)
  Pallas kernels  8.07 us (5%)
  other arithmetic  3.06 us (2%)
  local copies, waits for them, and re-layouts  1.67 us (1%)
    ppermute x18, starting transfers between devices, swap(): return lax.ppermute(value, axis, [(s, s ^ flip) for s in range(size)])  70.4 us
    ppermute x18, waiting for transfers between devices, swap(): return lax.ppermute(value, axis, [(s, s ^ flip) for s in range(size)])  29.4 us
    all_to_all x1, waiting for transfers between devices, shards(): lax.all_to_all(kernel_call(sum_copies_kernel, [blocks], [act_parts]), CHI...  8.87 us
    all_to_all x1, starting transfers between devices, shards(): grad_parts = lax.all_to_all(grad_partial, INP, 0, 0, tiled=True)  8.7 us
    all_to_all x1, starting transfers between devices, shards(): act_parts = lax.all_to_all(act_partial, CHIPS, 0, 0, tiled=True)  8.12 us
    pallas_call x8, Pallas kernels, kernel_call(): pl.pallas_call(body, out_shape=shapes if many else shapes[0], in_specs=[V...  8.07 us
    all_to_all x1, starting transfers between devices, shards(): lax.all_to_all(kernel_call(sum_copies_kernel, [blocks], [act_parts]), CHI...  7.87 us
    all_to_all x1, starting transfers between devices, shards(): lax.all_to_all(grad_copies, CHIPS, 0, 0, tiled=True).reshape(tokens, -1)  5.78 us
  transfers between devices with their start and end apart: 22, of which 13 were waited for; matrix products, arithmetic and copies ran while one was open for 2% of the time, Pallas kernels for 4%

profile of v13, /device:TPU:1, one launch (start us, length us, event | category | flops | bytes accessed | tf_op | source)
XLA Modules:
  0.0 152.3 jit_solution(2182873502970337902)
XLA Ops:
  0.0 0.0 copy-start
  0.0 0.9 constant_dynamic-slice_fusion
  0.9 8.8 %collective-permute-start = (bf16[32,896]{1,0:T(8,128)(2,1)S(1)}, bf16[32,896]{1,0:T(8,128)(2,1)S(1)}, u32[]{:S(2)}, u32[]{:S(2)}) collective-permute-start(bf16[32,896]{1,0:T(8,128)(2,1)S(1)} %constant_dynamic-slice_fusion), channel_id=1, source_target_pairs={{0,16},{16,0},{1,17},{17,1},{2,18},{18,2},{3,19},{19,3},{4,20},{20... | collective-permute-start | bytes 172040 | tf_op jit(solution)/shard_map/ppermute | solution.py:34
  9.7 1.9 %collective-permute-start.8 = (bf16[896,896]{1,0:T(8,128)(2,1)}, bf16[896,896]{1,0:T(8,128)(2,1)}, u32[]{:S(2)}, u32[]{:S(2)}) collective-permute-start(bf16[896,896]{1,0:T(8,128)(2,1)} %param.7), channel_id=1, source_target_pairs={{0,16},{16,0},{1,17},{17,1},{2,18},{18,2},{3,19},{19,3},{4,20},{20... | collective-permute-start | bytes 4816904 | tf_op jit(solution)/shard_map/ppermute | solution.py:34
  11.6 0.0 collective-permute-done
  11.6 0.8 broadcast_select_fusion.3
  12.5 0.0 copy-start.1
  12.5 0.7 copy-done.1
  13.2 0.8 shard_map.48
  14.1 5.8 %all-to-all-start.1 = ((bf16[16,32,512]{2,1,0:T(8,128)(2,1)}), bf16[16,32,512]{2,1,0:T(8,128)(2,1)S(1)}, u32[]{:S(2)}, u32[]{:S(2)}) async-start(bf16[16,32,512]{2,1,0:T(8,128)(2,1)} %shard_map.48), calls=%async_computation.1 | async-start | bytes 1048576 | tf_op jit(solution)/shard_map/all_to_all | solution.py:130
  19.8 4.2 %collective-permute-start.1 = (bf16[32,1792]{1,0:T(8,128)(2,1)S(1)}, bf16[32,1792]{1,0:T(8,128)(2,1)S(1)}, u32[]{:S(2)}, u32[]{:S(2)}) collective-permute-start(bf16[32,1792]{1,0:T(8,128)(2,1)S(1)} %pad_maximum_fusion.block0.order), channel_id=1, source_target_pairs={{0,1},{1,0},{2,3},{3,2},{4,5},{5,4},{6,7},{7,6},{8,9},{9,8},{10,11... | collective-permute-start | bytes 344072 | tf_op jit(solution)/shard_map/ppermute | solution.py:34
  24.1 4.8 %collective-permute-start.2 = (bf16[32,1792]{1,0:T(8,128)(2,1)S(1)}, bf16[32,1792]{1,0:T(8,128)(2,1)S(1)}, u32[]{:S(2)}, u32[]{:S(2)}) collective-permute-start(bf16[32,1792]{1,0:T(8,128)(2,1)S(1)} %pad_maximum_fusion.block0.order), channel_id=1, source_target_pairs={{0,2},{1,3},{2,0},{3,1},{4,6},{5,7},{6,4},{7,5},{8,10},{9,11},{10,... | collective-permute-start | bytes 344072 | tf_op jit(solution)/shard_map/ppermute | solution.py:34
  28.8 2.4 %collective-permute-start.3 = (bf16[32,1792]{1,0:T(8,128)(2,1)S(1)}, bf16[32,1792]{1,0:T(8,128)(2,1)S(1)}, u32[]{:S(2)}, u32[]{:S(2)}) collective-permute-start(bf16[32,1792]{1,0:T(8,128)(2,1)S(1)} %pad_maximum_fusion.block0.order), channel_id=1, source_target_pairs={{0,3},{1,2},{2,1},{3,0},{4,7},{5,6},{6,5},{7,4},{8,11},{9,10},{10,... | collective-permute-start | bytes 344072 | tf_op jit(solution)/shard_map/ppermute | solution.py:34
  31.3 0.0 collective-permute-done.1.block1
  31.3 4.2 %collective-permute-done.2.block2 = bf16[32,1792]{1,0:T(8,128)(2,1)S(1)} collective-permute-done((bf16[32,1792]{1,0:T(8,128)(2,1)S(1)}, bf16[32,1792]{1,0:T(8,128)(2,1)S(1)}, u32[]{:S(2)}, u32[]{:S(2)}) %collective-permute-start.2) | collective-permute-done | bytes 114720 | tf_op jit(solution)/shard_map/ppermute | solution.py:34
  35.5 4.5 %collective-permute-done.3.block3 = bf16[32,1792]{1,0:T(8,128)(2,1)S(1)} collective-permute-done((bf16[32,1792]{1,0:T(8,128)(2,1)S(1)}, bf16[32,1792]{1,0:T(8,128)(2,1)S(1)}, u32[]{:S(2)}, u32[]{:S(2)}) %collective-permute-start.3) | collective-permute-done | bytes 114720 | tf_op jit(solution)/shard_map/ppermute | solution.py:34
  40.1 3.1 %collective-permute-start.4 = (bf16[2,128,896]{2,1,0:T(8,128)(2,1)S(1)}, bf16[2,128,896]{2,1,0:T(8,128)(2,1)S(1)}, u32[]{:S(2)}, u32[]{:S(2)}) collective-permute-start(bf16[2,128,896]{2,1,0:T(8,128)(2,1)S(1)} %shard_map.46.act0), channel_id=1, source_target_pairs={{0,4},{4,0},{8,12},{12,8},{1,5},{5,1},{9,13},{13,9},{2,6},{6,2},{1... | collective-permute-start | bytes 1376264 | tf_op jit(solution)/shard_map/ppermute | solution.py:34
  43.2 3.7 %collective-permute-start.5 = (bf16[2,128,896]{2,1,0:T(8,128)(2,1)S(1)}, bf16[2,128,896]{2,1,0:T(8,128)(2,1)S(1)}, u32[]{:S(2)}, u32[]{:S(2)}) collective-permute-start(bf16[2,128,896]{2,1,0:T(8,128)(2,1)S(1)} %shard_map.46.act0), channel_id=1, source_target_pairs={{0,12},{4,8},{8,4},{12,0},{1,13},{5,9},{9,5},{13,1},{2,14},{6,10},... | collective-permute-start | bytes 1376264 | tf_op jit(solution)/shard_map/ppermute | solution.py:34
  46.9 0.0 copy-done
  46.9 3.2 %collective-permute-start.9 = (bf16[512,256]{1,0:T(8,128)(2,1)S(1)}, bf16[512,256]{1,0:T(8,128)(2,1)S(1)}, u32[]{:S(2)}, u32[]{:S(2)}) collective-permute-start(bf16[512,256]{1,0:T(8,128)(2,1)S(1)} %copy-done), channel_id=1, source_target_pairs={{0,16},{16,0},{1,17},{17,1},{2,18},{18,2},{3,19},{19,3},{4,20},{20... | collective-permute-start | bytes 786440 | tf_op jit(solution)/shard_map/ppermute | solution.py:34
  50.1 1.1 collective-permute-done.9.other
  51.3 2.0 %collective-permute-done.4.act1.order = bf16[2,128,896]{2,1,0:T(8,128)(2,1)S(1)} collective-permute-done((bf16[2,128,896]{2,1,0:T(8,128)(2,1)S(1)}, bf16[2,128,896]{2,1,0:T(8,128)(2,1)S(1)}, u32[]{:S(2)}, u32[]{:S(2)}) %collective-permute-start.4) | collective-permute-done | bytes 458784 | tf_op jit(solution)/shard_map/ppermute | solution.py:34
  53.3 0.0 all-to-all-done.1
  53.3 1.2 shard_map.49
  54.5 8.7 %all-to-all-start.2 = ((bf16[16,32,512]{2,1,0:T(8,128)(2,1)}), bf16[16,32,512]{2,1,0:T(8,128)(2,1)S(1)}, u32[]{:S(2)}, u32[]{:S(2)}) async-start(bf16[16,32,512]{2,1,0:T(8,128)(2,1)} %shard_map.49), calls=%async_computation.2 | async-start | bytes 1048576 | tf_op jit(solution)/shard_map/all_to_all | solution.py:146
  63.2 0.0 collective-permute-done.5.act3
  63.3 3.3 %collective-permute-start.6 = (bf16[128,896]{1,0:T(8,128)(2,1)S(1)}, bf16[128,896]{1,0:T(8,128)(2,1)S(1)}, u32[]{:S(2)}, u32[]{:S(2)}) collective-permute-start(bf16[128,896]{1,0:T(8,128)(2,1)S(1)} %slice_bitcast_fusion.1), channel_id=1, source_target_pairs={{0,4},{4,0},{8,12},{12,8},{1,5},{5,1},{9,13},{13,9},{2,6},{6,2},{1... | collective-permute-start | bytes 688136 | tf_op jit(solution)/shard_map/ppermute | solution.py:34
  66.6 3.7 %collective-permute-start.7 = (bf16[128,896]{1,0:T(8,128)(2,1)S(1)}, bf16[128,896]{1,0:T(8,128)(2,1)S(1)}, u32[]{:S(2)}, u32[]{:S(2)}) collective-permute-start(bf16[128,896]{1,0:T(8,128)(2,1)S(1)} %slice_bitcast_fusion), channel_id=1, source_target_pairs={{0,12},{4,8},{8,4},{12,0},{1,13},{5,9},{9,5},{13,1},{2,14},{6,10},... | collective-permute-start | bytes 688136 | tf_op jit(solution)/shard_map/ppermute | solution.py:34
  70.3 0.0 collective-permute-done.8
  70.3 2.2 %broadcast_select_fusion = (bf16[896,896]{1,0:T(8,128)(2,1)S(1)}, bf16[896,896]{1,0:T(8,128)(2,1)S(1)}) fusion(bf16[896,896]{1,0:T(8,128)(2,1)} %collective-permute-done.8, bf16[896,896]{1,0:T(8,128)(2,1)} %param.7, pred[]{:T(512)S(6)} %eq.2), kind=kLoop, calls=%fused_computation | loop fusion | flops 1605632 | bytes 6422529 | tf_op jit(solution)/shard_map/jit(_where)/select_n | solution.py:112
  72.5 4.1 %collective-permute-done.6.low2 = bf16[128,896]{1,0:T(8,128)(2,1)S(1)} collective-permute-done((bf16[128,896]{1,0:T(8,128)(2,1)S(1)}, bf16[128,896]{1,0:T(8,128)(2,1)S(1)}, u32[]{:S(2)}, u32[]{:S(2)}) %collective-permute-start.6) | collective-permute-done | bytes 229408 | tf_op jit(solution)/shard_map/ppermute | solution.py:34
  76.6 1.3 collective-permute-done.7.high2
  77.9 3.2 %shard_map.47 = (bf16[16,32,896]{2,1,0:T(8,128)(2,1)}, f32[8,128]{1,0:T(8,128)S(1)}) custom-call(bf16[2,128,896]{2,1,0:T(8,128)(2,1)S(1)} %shard_map.46.act0, bf16[2,128,896]{2,1,0:T(8,128)(2,1)S(1)} %collective-permute-done.4.act1.order, bf16[128,896]{1,0:T(8,128)(2,1)S(1)} %collective-permute-done.6.low2, ...), custom_call_target="tpu_custom_call" | custom-call | flops 1644167168 | bytes 5967872 | tf_op jit(solution)/shard_map/pallas_call | solution.py:22
  81.1 0.0 all-to-all-done.2.parts
  81.1 8.1 %all-to-all-start = ((bf16[16,32,896]{2,1,0:T(8,128)(2,1)}), bf16[16,32,896]{2,1,0:T(8,128)(2,1)S(1)}, u32[]{:S(2)}, u32[]{:S(2)}) async-start(bf16[16,32,896]{2,1,0:T(8,128)(2,1)} %get-tuple-element.15), calls=%async_computation | async-start | bytes 1835008 | tf_op jit(solution)/shard_map/all_to_all | solution.py:155
  89.3 0.1 shard_map.50
  89.3 5.0 %collective-permute-start.10 = (bf16[32,256]{1,0:T(8,128)(2,1)S(1)}, bf16[32,256]{1,0:T(8,128)(2,1)S(1)}, u32[]{:S(2)}, u32[]{:S(2)}) collective-permute-start(bf16[32,256]{1,0:T(8,128)(2,1)S(1)} %get-tuple-element.18), channel_id=1, source_target_pairs={{0,16},{16,0},{1,17},{17,1},{2,18},{18,2},{3,19},{19,3},{4,20},{20... | collective-permute-start | bytes 49160 | tf_op jit(solution)/shard_map/ppermute | solution.py:34
  94.3 0.8 collective-permute-done.10
  95.1 4.9 %collective-permute-start.11 = (bf16[32,512]{1,0:T(8,128)(2,1)S(1)}, bf16[32,512]{1,0:T(8,128)(2,1)S(1)}, u32[]{:S(2)}, u32[]{:S(2)}) collective-permute-start(bf16[32,512]{1,0:T(8,128)(2,1)S(1)} %constant_dynamic-update-slice_fusion.block0), channel_id=1, source_target_pairs={{0,1},{1,0},{2,3},{3,2},{4,5},{5,4},{6,7},{7,6},{8,9},{9,8},{10,11... | collective-permute-start | bytes 98312 | tf_op jit(solution)/shard_map/ppermute | solution.py:34
  100.1 4.8 %collective-permute-start.12 = (bf16[32,512]{1,0:T(8,128)(2,1)S(1)}, bf16[32,512]{1,0:T(8,128)(2,1)S(1)}, u32[]{:S(2)}, u32[]{:S(2)}) collective-permute-start(bf16[32,512]{1,0:T(8,128)(2,1)S(1)} %constant_dynamic-update-slice_fusion.block0), channel_id=1, source_target_pairs={{0,2},{1,3},{2,0},{3,1},{4,6},{5,7},{6,4},{7,5},{8,10},{9,11},{10,... | collective-permute-start | bytes 98312 | tf_op jit(solution)/shard_map/ppermute | solution.py:34
  104.9 2.3 %collective-permute-start.13 = (bf16[32,512]{1,0:T(8,128)(2,1)S(1)}, bf16[32,512]{1,0:T(8,128)(2,1)S(1)}, u32[]{:S(2)}, u32[]{:S(2)}) collective-permute-start(bf16[32,512]{1,0:T(8,128)(2,1)S(1)} %constant_dynamic-update-slice_fusion.block0), channel_id=1, source_target_pairs={{0,3},{1,2},{2,1},{3,0},{4,7},{5,6},{6,5},{7,4},{8,11},{9,10},{10,... | collective-permute-start | bytes 98312 | tf_op jit(solution)/shard_map/ppermute | solution.py:34
  107.2 0.0 collective-permute-done.11.block1
  107.2 1.4 collective-permute-done.12.block2
  108.6 3.3 %collective-permute-done.13.block3 = bf16[32,512]{1,0:T(8,128)(2,1)S(1)} collective-permute-done((bf16[32,512]{1,0:T(8,128)(2,1)S(1)}, bf16[32,512]{1,0:T(8,128)(2,1)S(1)}, u32[]{:S(2)}, u32[]{:S(2)}) %collective-permute-start.13) | collective-permute-done | bytes 32800 | tf_op jit(solution)/shard_map/ppermute | solution.py:34
  112.0 0.0 all-to-all-done.parts
  112.0 1.1 shard_map.52
  113.1 7.9 %all-to-all-start.3 = ((bf16[16,32,896]{2,1,0:T(8,128)(2,1)}), bf16[16,32,896]{2,1,0:T(8,128)(2,1)S(1)}, u32[]{:S(2)}, u32[]{:S(2)}) async-start(bf16[16,32,896]{2,1,0:T(8,128)(2,1)} %shard_map.52), calls=%async_computation.3 | async-start | bytes 1835008 | tf_op jit(solution)/shard_map/all_to_all | solution.py:163
  120.9 1.9 %collective-permute-start.14 = (bf16[128,512]{1,0:T(8,128)(2,1)S(1)}, bf16[128,512]{1,0:T(8,128)(2,1)S(1)}, u32[]{:S(2)}, u32[]{:S(2)}) collective-permute-start(bf16[128,512]{1,0:T(8,128)(2,1)S(1)} %shard_map.51.g0), channel_id=1, source_target_pairs={{0,4},{4,0},{8,12},{12,8},{1,5},{5,1},{9,13},{13,9},{2,6},{6,2},{1... | collective-permute-start | bytes 393224 | tf_op jit(solution)/shard_map/ppermute | solution.py:34
  122.9 4.9 %collective-permute-start.15 = (bf16[128,512]{1,0:T(8,128)(2,1)S(1)}, bf16[128,512]{1,0:T(8,128)(2,1)S(1)}, u32[]{:S(2)}, u32[]{:S(2)}) collective-permute-start(bf16[128,512]{1,0:T(8,128)(2,1)S(1)} %shard_map.51.g0), channel_id=1, source_target_pairs={{0,8},{4,12},{8,0},{12,4},{1,9},{5,13},{9,1},{13,5},{2,10},{6,14},... | collective-permute-start | bytes 393224 | tf_op jit(solution)/shard_map/ppermute | solution.py:34
  127.7 2.8 %collective-permute-start.16 = (bf16[128,512]{1,0:T(8,128)(2,1)S(1)}, bf16[128,512]{1,0:T(8,128)(2,1)S(1)}, u32[]{:S(2)}, u32[]{:S(2)}) collective-permute-start(bf16[128,512]{1,0:T(8,128)(2,1)S(1)} %shard_map.51.g0), channel_id=1, source_target_pairs={{0,12},{4,8},{8,4},{12,0},{1,13},{5,9},{9,5},{13,1},{2,14},{6,10},... | collective-permute-start | bytes 393224 | tf_op jit(solution)/shard_map/ppermute | solution.py:34
  130.5 0.0 collective-permute-done.14.g1
  130.6 0.1 collective-permute-done.15.g2
  130.6 4.3 %collective-permute-done.16.g3 = bf16[128,512]{1,0:T(8,128)(2,1)S(1)} collective-permute-done((bf16[128,512]{1,0:T(8,128)(2,1)S(1)}, bf16[128,512]{1,0:T(8,128)(2,1)S(1)}, u32[]{:S(2)}, u32[]{:S(2)}) %collective-permute-start.16) | collective-permute-done | bytes 131104 | tf_op jit(solution)/shard_map/ppermute | solution.py:34
  135.0 8.9 %all-to-all-done.3 = bf16[16,32,896]{2,1,0:T(8,128)(2,1)S(1)} async-done(((bf16[16,32,896]{2,1,0:T(8,128)(2,1)}), bf16[16,32,896]{2,1,0:T(8,128)(2,1)S(1)}, u32[]{:S(2)}, u32[]{:S(2)}) %all-to-all-start.3) | async-done | bytes 917536 | tf_op jit(solution)/shard_map/all_to_all | solution.py:163
  143.8 4.7 %collective-permute-start.17 = (bf16[512,896]{1,0:T(8,128)(2,1)S(1)}, bf16[512,896]{1,0:T(8,128)(2,1)S(1)}, u32[]{:S(2)}, u32[]{:S(2)}) collective-permute-start(bf16[512,896]{1,0:T(8,128)(2,1)S(1)} %bitcast.6), channel_id=1, source_target_pairs={{0,16},{16,0},{1,17},{17,1},{2,18},{18,2},{3,19},{19,3},{4,20},{20... | collective-permute-start | bytes 2752520 | tf_op jit(solution)/shard_map/ppermute | solution.py:34
  148.6 2.1 %collective-permute-done.17.act_theirs = bf16[512,896]{1,0:T(8,128)(2,1)S(1)} collective-permute-done((bf16[512,896]{1,0:T(8,128)(2,1)S(1)}, bf16[512,896]{1,0:T(8,128)(2,1)S(1)}, u32[]{:S(2)}, u32[]{:S(2)}) %collective-permute-start.17) | collective-permute-done | bytes 917536 | tf_op jit(solution)/shard_map/ppermute | solution.py:34
  150.6 1.7 %shard_map.53 = f32[256,896]{1,0:T(8,128)} custom-call(bf16[128,512]{1,0:T(8,128)(2,1)S(1)} %shard_map.51.g0, bf16[128,512]{1,0:T(8,128)(2,1)S(1)} %collective-permute-done.14.g1, bf16[128,512]{1,0:T(8,128)(2,1)S(1)} %collective-permute-done.15.g2, bf16[128,512]{1,0:T(8,128)(2,1)S(1)} %collective-permute-done.16.g3, bf16[512,896]{1,0:T(8,128)(2,1)S(1)} %bitcast.7, ...), custom_call_target="tpu_custom_call" | custom-call | flops 469762048 | bytes 3276800 | tf_op jit(solution)/shard_map/pallas_call | solution.py:22
  (7 shorter events, 0.1 us)
Async XLA Ops:
  0.0 46.9 %copy-start = (bf16[512,256]{1,0:T(8,128)(2,1)S(1)}, bf16[512,256]{1,0:T(8,128)(2,1)}, u32[]{:S(2)}) copy-start(bf16[512,256]{1,0:T(8,128)(2,1)} %own.1) | copy-start | bytes 786436
  0.9 10.7 %collective-permute-start = (bf16[32,896]{1,0:T(8,128)(2,1)S(1)}, bf16[32,896]{1,0:T(8,128)(2,1)S(1)}, u32[]{:S(2)}, u32[]{:S(2)}) collective-permute-start(bf16[32,896]{1,0:T(8,128)(2,1)S(1)} %constant_dynamic-slice_fusion), channel_id=1, source_target_pairs={{0,16},{16,0},{1,17},{17,1},{2,18},{18,2},{3,19},{19,3},{4,20},{20... | collective-permute-start | bytes 172040 | tf_op jit(solution)/shard_map/ppermute | solution.py:34
  9.7 60.6 %collective-permute-start.8 = (bf16[896,896]{1,0:T(8,128)(2,1)}, bf16[896,896]{1,0:T(8,128)(2,1)}, u32[]{:S(2)}, u32[]{:S(2)}) collective-permute-start(bf16[896,896]{1,0:T(8,128)(2,1)} %param.7), channel_id=1, source_target_pairs={{0,16},{16,0},{1,17},{17,1},{2,18},{18,2},{3,19},{19,3},{4,20},{20... | collective-permute-start | bytes 4816904 | tf_op jit(solution)/shard_map/ppermute | solution.py:34
  12.5 0.8 copy-start.1
  14.1 39.2 %all-to-all-start.1 = ((bf16[16,32,512]{2,1,0:T(8,128)(2,1)}), bf16[16,32,512]{2,1,0:T(8,128)(2,1)S(1)}, u32[]{:S(2)}, u32[]{:S(2)}) async-start(bf16[16,32,512]{2,1,0:T(8,128)(2,1)} %shard_map.48), calls=%async_computation.1 | async-start | bytes 1048576 | tf_op jit(solution)/shard_map/all_to_all | solution.py:130
  19.8 11.4 %collective-permute-start.1 = (bf16[32,1792]{1,0:T(8,128)(2,1)S(1)}, bf16[32,1792]{1,0:T(8,128)(2,1)S(1)}, u32[]{:S(2)}, u32[]{:S(2)}) collective-permute-start(bf16[32,1792]{1,0:T(8,128)(2,1)S(1)} %pad_maximum_fusion.block0.order), channel_id=1, source_target_pairs={{0,1},{1,0},{2,3},{3,2},{4,5},{5,4},{6,7},{7,6},{8,9},{9,8},{10,11... | collective-permute-start | bytes 344072 | tf_op jit(solution)/shard_map/ppermute | solution.py:34
  24.1 11.4 %collective-permute-start.2 = (bf16[32,1792]{1,0:T(8,128)(2,1)S(1)}, bf16[32,1792]{1,0:T(8,128)(2,1)S(1)}, u32[]{:S(2)}, u32[]{:S(2)}) collective-permute-start(bf16[32,1792]{1,0:T(8,128)(2,1)S(1)} %pad_maximum_fusion.block0.order), channel_id=1, source_target_pairs={{0,2},{1,3},{2,0},{3,1},{4,6},{5,7},{6,4},{7,5},{8,10},{9,11},{10,... | collective-permute-start | bytes 344072 | tf_op jit(solution)/shard_map/ppermute | solution.py:34
  28.8 11.2 %collective-permute-start.3 = (bf16[32,1792]{1,0:T(8,128)(2,1)S(1)}, bf16[32,1792]{1,0:T(8,128)(2,1)S(1)}, u32[]{:S(2)}, u32[]{:S(2)}) collective-permute-start(bf16[32,1792]{1,0:T(8,128)(2,1)S(1)} %pad_maximum_fusion.block0.order), channel_id=1, source_target_pairs={{0,3},{1,2},{2,1},{3,0},{4,7},{5,6},{6,5},{7,4},{8,11},{9,10},{10,... | collective-permute-start | bytes 344072 | tf_op jit(solution)/shard_map/ppermute | solution.py:34
  40.1 13.2 %collective-permute-start.4 = (bf16[2,128,896]{2,1,0:T(8,128)(2,1)S(1)}, bf16[2,128,896]{2,1,0:T(8,128)(2,1)S(1)}, u32[]{:S(2)}, u32[]{:S(2)}) collective-permute-start(bf16[2,128,896]{2,1,0:T(8,128)(2,1)S(1)} %shard_map.46.act0), channel_id=1, source_target_pairs={{0,4},{4,0},{8,12},{12,8},{1,5},{5,1},{9,13},{13,9},{2,6},{6,2},{1... | collective-permute-start | bytes 1376264 | tf_op jit(solution)/shard_map/ppermute | solution.py:34
  43.2 20.1 %collective-permute-start.5 = (bf16[2,128,896]{2,1,0:T(8,128)(2,1)S(1)}, bf16[2,128,896]{2,1,0:T(8,128)(2,1)S(1)}, u32[]{:S(2)}, u32[]{:S(2)}) collective-permute-start(bf16[2,128,896]{2,1,0:T(8,128)(2,1)S(1)} %shard_map.46.act0), channel_id=1, source_target_pairs={{0,12},{4,8},{8,4},{12,0},{1,13},{5,9},{9,5},{13,1},{2,14},{6,10},... | collective-permute-start | bytes 1376264 | tf_op jit(solution)/shard_map/ppermute | solution.py:34
  46.9 4.3 %collective-permute-start.9 = (bf16[512,256]{1,0:T(8,128)(2,1)S(1)}, bf16[512,256]{1,0:T(8,128)(2,1)S(1)}, u32[]{:S(2)}, u32[]{:S(2)}) collective-permute-start(bf16[512,256]{1,0:T(8,128)(2,1)S(1)} %copy-done), channel_id=1, source_target_pairs={{0,16},{16,0},{1,17},{17,1},{2,18},{18,2},{3,19},{19,3},{4,20},{20... | collective-permute-start | bytes 786440 | tf_op jit(solution)/shard_map/ppermute | solution.py:34
  54.5 26.6 %all-to-all-start.2 = ((bf16[16,32,512]{2,1,0:T(8,128)(2,1)}), bf16[16,32,512]{2,1,0:T(8,128)(2,1)S(1)}, u32[]{:S(2)}, u32[]{:S(2)}) async-start(bf16[16,32,512]{2,1,0:T(8,128)(2,1)} %shard_map.49), calls=%async_computation.2 | async-start | bytes 1048576 | tf_op jit(solution)/shard_map/all_to_all | solution.py:146
  63.3 13.4 %collective-permute-start.6 = (bf16[128,896]{1,0:T(8,128)(2,1)S(1)}, bf16[128,896]{1,0:T(8,128)(2,1)S(1)}, u32[]{:S(2)}, u32[]{:S(2)}) collective-permute-start(bf16[128,896]{1,0:T(8,128)(2,1)S(1)} %slice_bitcast_fusion.1), channel_id=1, source_target_pairs={{0,4},{4,0},{8,12},{12,8},{1,5},{5,1},{9,13},{13,9},{2,6},{6,2},{1... | collective-permute-start | bytes 688136 | tf_op jit(solution)/shard_map/ppermute | solution.py:34
  66.6 11.4 %collective-permute-start.7 = (bf16[128,896]{1,0:T(8,128)(2,1)S(1)}, bf16[128,896]{1,0:T(8,128)(2,1)S(1)}, u32[]{:S(2)}, u32[]{:S(2)}) collective-permute-start(bf16[128,896]{1,0:T(8,128)(2,1)S(1)} %slice_bitcast_fusion), channel_id=1, source_target_pairs={{0,12},{4,8},{8,4},{12,0},{1,13},{5,9},{9,5},{13,1},{2,14},{6,10},... | collective-permute-start | bytes 688136 | tf_op jit(solution)/shard_map/ppermute | solution.py:34
  81.1 30.9 %all-to-all-start = ((bf16[16,32,896]{2,1,0:T(8,128)(2,1)}), bf16[16,32,896]{2,1,0:T(8,128)(2,1)S(1)}, u32[]{:S(2)}, u32[]{:S(2)}) async-start(bf16[16,32,896]{2,1,0:T(8,128)(2,1)} %get-tuple-element.15), calls=%async_computation | async-start | bytes 1835008 | tf_op jit(solution)/shard_map/all_to_all | solution.py:155
  89.3 5.8 %collective-permute-start.10 = (bf16[32,256]{1,0:T(8,128)(2,1)S(1)}, bf16[32,256]{1,0:T(8,128)(2,1)S(1)}, u32[]{:S(2)}, u32[]{:S(2)}) collective-permute-start(bf16[32,256]{1,0:T(8,128)(2,1)S(1)} %get-tuple-element.18), channel_id=1, source_target_pairs={{0,16},{16,0},{1,17},{17,1},{2,18},{18,2},{3,19},{19,3},{4,20},{20... | collective-permute-start | bytes 49160 | tf_op jit(solution)/shard_map/ppermute | solution.py:34
  95.1 12.1 %collective-permute-start.11 = (bf16[32,512]{1,0:T(8,128)(2,1)S(1)}, bf16[32,512]{1,0:T(8,128)(2,1)S(1)}, u32[]{:S(2)}, u32[]{:S(2)}) collective-permute-start(bf16[32,512]{1,0:T(8,128)(2,1)S(1)} %constant_dynamic-update-slice_fusion.block0), channel_id=1, source_target_pairs={{0,1},{1,0},{2,3},{3,2},{4,5},{5,4},{6,7},{7,6},{8,9},{9,8},{10,11... | collective-permute-start | bytes 98312 | tf_op jit(solution)/shard_map/ppermute | solution.py:34
  100.1 8.6 %collective-permute-start.12 = (bf16[32,512]{1,0:T(8,128)(2,1)S(1)}, bf16[32,512]{1,0:T(8,128)(2,1)S(1)}, u32[]{:S(2)}, u32[]{:S(2)}) collective-permute-start(bf16[32,512]{1,0:T(8,128)(2,1)S(1)} %constant_dynamic-update-slice_fusion.block0), channel_id=1, source_target_pairs={{0,2},{1,3},{2,0},{3,1},{4,6},{5,7},{6,4},{7,5},{8,10},{9,11},{10,... | collective-permute-start | bytes 98312 | tf_op jit(solution)/shard_map/ppermute | solution.py:34
  104.9 7.1 %collective-permute-start.13 = (bf16[32,512]{1,0:T(8,128)(2,1)S(1)}, bf16[32,512]{1,0:T(8,128)(2,1)S(1)}, u32[]{:S(2)}, u32[]{:S(2)}) collective-permute-start(bf16[32,512]{1,0:T(8,128)(2,1)S(1)} %constant_dynamic-update-slice_fusion.block0), channel_id=1, source_target_pairs={{0,3},{1,2},{2,1},{3,0},{4,7},{5,6},{6,5},{7,4},{8,11},{9,10},{10,... | collective-permute-start | bytes 98312 | tf_op jit(solution)/shard_map/ppermute | solution.py:34
  113.1 30.8 %all-to-all-start.3 = ((bf16[16,32,896]{2,1,0:T(8,128)(2,1)}), bf16[16,32,896]{2,1,0:T(8,128)(2,1)S(1)}, u32[]{:S(2)}, u32[]{:S(2)}) async-start(bf16[16,32,896]{2,1,0:T(8,128)(2,1)} %shard_map.52), calls=%async_computation.3 | async-start | bytes 1835008 | tf_op jit(solution)/shard_map/all_to_all | solution.py:163
  120.9 9.6 %collective-permute-start.14 = (bf16[128,512]{1,0:T(8,128)(2,1)S(1)}, bf16[128,512]{1,0:T(8,128)(2,1)S(1)}, u32[]{:S(2)}, u32[]{:S(2)}) collective-permute-start(bf16[128,512]{1,0:T(8,128)(2,1)S(1)} %shard_map.51.g0), channel_id=1, source_target_pairs={{0,4},{4,0},{8,12},{12,8},{1,5},{5,1},{9,13},{13,9},{2,6},{6,2},{1... | collective-permute-start | bytes 393224 | tf_op jit(solution)/shard_map/ppermute | solution.py:34
  122.9 7.8 %collective-permute-start.15 = (bf16[128,512]{1,0:T(8,128)(2,1)S(1)}, bf16[128,512]{1,0:T(8,128)(2,1)S(1)}, u32[]{:S(2)}, u32[]{:S(2)}) collective-permute-start(bf16[128,512]{1,0:T(8,128)(2,1)S(1)} %shard_map.51.g0), channel_id=1, source_target_pairs={{0,8},{4,12},{8,0},{12,4},{1,9},{5,13},{9,1},{13,5},{2,10},{6,14},... | collective-permute-start | bytes 393224 | tf_op jit(solution)/shard_map/ppermute | solution.py:34
  127.7 7.2 %collective-permute-start.16 = (bf16[128,512]{1,0:T(8,128)(2,1)S(1)}, bf16[128,512]{1,0:T(8,128)(2,1)S(1)}, u32[]{:S(2)}, u32[]{:S(2)}) collective-permute-start(bf16[128,512]{1,0:T(8,128)(2,1)S(1)} %shard_map.51.g0), channel_id=1, source_target_pairs={{0,12},{4,8},{8,4},{12,0},{1,13},{5,9},{9,5},{13,1},{2,14},{6,10},... | collective-permute-start | bytes 393224 | tf_op jit(solution)/shard_map/ppermute | solution.py:34
  143.8 6.8 %collective-permute-start.17 = (bf16[512,896]{1,0:T(8,128)(2,1)S(1)}, bf16[512,896]{1,0:T(8,128)(2,1)S(1)}, u32[]{:S(2)}, u32[]{:S(2)}) collective-permute-start(bf16[512,896]{1,0:T(8,128)(2,1)S(1)} %bitcast.6), channel_id=1, source_target_pairs={{0,16},{16,0},{1,17},{17,1},{2,18},{18,2},{3,19},{19,3},{4,20},{20... | collective-permute-start | bytes 2752520 | tf_op jit(solution)/shard_map/ppermute | solution.py:34
